TPU v7x, 32 devices: a whole 2x2x4 slice. The times are simulated.
32 devices in a mesh: seq: 4 (over y, x), item: 8 (over z, core).
Axes of the slice: x: 2, y: 2, z: 4, core: 2. Of those that a mesh axis runs over, the one named last changes fastest.
Arguments:
- hidden: float32 [8, 4096, 768], P('item', 'seq'), may hold values from -6 to 6
- block_lists: int32 [8, 2, 64, 12, 3], P('item', None, 'seq'), may hold values from 0 to 63, as said below
- w_qkv: bfloat16 [2, 768, 2304], P(None, 'item'), may hold values from -0.3125 to 0.3125
- bias_query: bfloat16 [2, 768], P(None, 'item'), may hold values from -1.75 to 1.75
- bias_value: bfloat16 [2, 768], P(None, 'item'), may hold values from -0.1875 to 0.1875
- w_attn_out: bfloat16 [2, 768, 768], P(None, 'item'), may hold values from -1.75 to 1.75
- bias_attn_out: bfloat16 [2, 768], P(None, 'item'), may hold values from -0.625 to 0.625
- norm1_gain: bfloat16 [2, 768], P(None, 'item'), may hold values from 0.5 to 1.5
- norm1_shift: bfloat16 [2, 768], P(None, 'item'), may hold values from -0.625 to 0.625
- w_ffn_in: bfloat16 [2, 768, 3072], P(None, 'item'), may hold values from -0.21875 to 0.21875
- bias_ffn_in: bfloat16 [2, 3072], P(None, 'item'), may hold values from -0.625 to 0.625
- w_ffn_out: bfloat16 [2, 3072, 768], P(None, 'item'), may hold values from -0.15625 to 0.15625
- bias_ffn_out: bfloat16 [2, 768], P(None, 'item'), may hold values from -0.625 to 0.625
- norm2_gain: bfloat16 [2, 768], P(None, 'item'), may hold values from 0.5 to 1.5
- norm2_shift: bfloat16 [2, 768], P(None, 'item'), may hold values from -0.625 to 0.625
- cotangent: float32 [8, 4096, 768], P('item', 'seq'), may hold values from -6 to 6
Outputs:
- layer_output: float32 [8, 4096, 768], P('item', 'seq')
- input_grad: float32 [8, 4096, 768], P('item', 'seq')
- grad_w_qkv: float32 [2, 768, 2304], P(None, 'item')
- grad_bias_query: float32 [2, 768], P(None, 'item')
- grad_bias_value: float32 [2, 768], P(None, 'item')
- grad_w_attn_out: float32 [2, 768, 768], P(None, 'item')
- grad_bias_attn_out: float32 [2, 768], P(None, 'item')
- grad_norm1_gain: float32 [2, 768], P(None, 'item')
- grad_norm1_shift: float32 [2, 768], P(None, 'item')
- grad_w_ffn_in: float32 [2, 768, 3072], P(None, 'item')
- grad_bias_ffn_in: float32 [2, 3072], P(None, 'item')
- grad_w_ffn_out: float32 [2, 3072, 768], P(None, 'item')
- grad_bias_ffn_out: float32 [2, 768], P(None, 'item')
- grad_norm2_gain: float32 [2, 768], P(None, 'item')
- grad_norm2_shift: float32 [2, 768], P(None, 'item')
Inputs may be any that keep to these rules, and one draw needn't show every extreme that they name: `block_lists`: for one item, layer and head, of the random blocks listed by the 16 query blocks of one run of 16 consecutive blocks (runs aligned at multiples of 16), at most 12 lie in any one such run.
All inputs are finite; a program needn't handle non-finite values.
Results may differ from a plain program's by a relative error of at most 0.038.
The roundings to bfloat16 on the way count: a program that leaves them out, or rounds other values in their place, can miss the bound.
Values may be sent and summed in bfloat16 or wider, within the bound.
A program may use at most 768 MiB of HBM per device.

v0:
```python
from functools import partial

import jax
import jax.numpy as jnp
from jax import lax
from jax.sharding import PartitionSpec as P

D = 768
H = 12
HD = 64
BLK = 64
RAND = 3
LEN = 4096
LAYERS = 2


exact_mode = lax.Precision.HIGHEST
epsilon = 1e-05


def shortened(x):
    return jax.tree.map(lambda a: a.astype(jnp.bfloat16) if a.dtype == jnp.float32 else a, x)


def combined_all(part, axis, combine):
    gathered = jax.tree.map(lambda a: lax.all_gather(a, axis), part)

    def take(source):
        return jax.tree.map(lambda a: lax.dynamic_index_in_dim(a, source, 0, False), gathered)

    return lax.fori_loop(
        1, lax.axis_size(axis), lambda source, state: combine(state, take(source)), take(0)
    )


def with_halo(cells, sides, width):
    for axis, dim in sides:
        count = lax.axis_size(axis)
        head = lax.slice_in_dim(cells, 0, width, axis=dim)
        tail = lax.slice_in_dim(cells, cells.shape[dim] - width, cells.shape[dim], axis=dim)
        cells = jnp.concatenate(
            [
                lax.ppermute(tail, axis, [(i, (i + 1) % count) for i in range(count)]),
                cells,
                lax.ppermute(head, axis, [((i + 1) % count, i) for i in range(count)]),
            ],
            axis=dim,
        )
    return cells


def layer_norm(resid, gain, shift):
    centre = resid - jnp.mean(resid, -1, keepdims=True)
    spread = jnp.mean(centre * centre, -1, keepdims=True)
    return centre * lax.rsqrt(spread + epsilon) * gain + shift


def merge_parts(first_part, second_part):
    max_first, sum_first, num_first = first_part
    max_second, sum_second, num_second = second_part
    row_max = jnp.maximum(max_first, max_second)
    weight_first = jnp.exp(max_first - row_max)
    weight_second = jnp.exp(max_second - row_max)
    return (
        row_max,
        sum_first * weight_first + sum_second * weight_second,
        num_first * weight_first[..., None] + num_second * weight_second[..., None],
    )


def block_numbers(item_count, shared_ids, random_ids):
    local_blocks = shared_ids.shape[0]
    all_blocks = LEN // BLK
    base = (
        jnp.arange(item_count, dtype=jnp.int32)[:, None] * H
        + jnp.arange(H, dtype=jnp.int32)[None, :]
    ) * all_blocks
    shared_wide = jnp.broadcast_to(shared_ids[None, None], (item_count, H, local_blocks, 5))
    listed = jnp.concatenate(
        [shared_wide, random_ids.reshape(item_count, H, local_blocks, RAND)], 3
    )
    return base[:, :, None, None] + listed


def assemble(pairs_full, flat_ids):
    item_count, heads, local_blocks, listed = flat_ids.shape
    slabs = pairs_full.reshape(item_count * H * (LEN // BLK), BLK, 2 * HD)
    rows = jnp.take(slabs, flat_ids.reshape(-1), axis=0)
    return rows.reshape(item_count, H, local_blocks, listed * BLK, 2 * HD)


def local(
    hidden,
    block_lists,
    w_qkv,
    bias_query,
    bias_value,
    w_attn_out,
    bias_attn_out,
    norm1_gain,
    norm1_shift,
    w_ffn_in,
    bias_ffn_in,
    w_ffn_out,
    bias_ffn_out,
    norm2_gain,
    norm2_shift,
    cotangent,
):
    weight_shards = (
        w_qkv,
        bias_query,
        bias_value,
        w_attn_out,
        bias_attn_out,
        norm1_gain,
        norm1_shift,
        w_ffn_in,
        bias_ffn_in,
        w_ffn_out,
        bias_ffn_out,
        norm2_gain,
        norm2_shift,
    )
    seq_count = lax.axis_size("seq")
    seq_rank = lax.axis_index("seq")
    item_count = hidden.shape[0]
    tokens_here = hidden.shape[1]
    local_blocks = tokens_here // BLK
    all_blocks = LEN // BLK
    score_scale = HD ** (-0.5)
    block_ids = seq_rank * local_blocks + jnp.arange(local_blocks, dtype=jnp.int32)
    shared_ids = jnp.stack(
        [
            (block_ids - 1) % all_blocks,
            block_ids,
            (block_ids + 1) % all_blocks,
            jnp.zeros_like(block_ids),
            jnp.full_like(block_ids, all_blocks - 1),
        ],
        1,
    )
    row_regular = jnp.repeat((block_ids != 0) & (block_ids != all_blocks - 1), BLK)[None, :, None]
    is_first = seq_rank == 0
    is_last = seq_rank == seq_count - 1
    tail = tokens_here - BLK
    current = hidden
    saved_layers = []
    layer_weights = []
    for section_index in range(LAYERS):
        section_weights = lax.all_gather(
            shortened(tuple((shard_all[section_index] for shard_all in weight_shards))),
            "item",
            axis=0,
            tiled=True,
        )
        layer_weights.append(section_weights)
        (
            qkv_weight,
            query_bias,
            value_bias,
            out_weight,
            out_bias,
            gain_one,
            shift_one,
            inner_weight,
            inner_bias,
            outer_weight,
            outer_bias,
            gain_two,
            shift_two,
        ) = section_weights
        random_ids = jnp.transpose(block_lists[:, section_index], (0, 2, 1, 3)).reshape(
            item_count, H, local_blocks * RAND
        )
        flat_ids = block_numbers(item_count, shared_ids, random_ids)
        input_low = current.astype(jnp.bfloat16)
        projected = jnp.einsum(
            "itd,de->ite", input_low, qkv_weight, preferred_element_type=jnp.float32
        )
        projected = projected + jnp.concatenate(
            [query_bias, jnp.zeros_like(query_bias), value_bias]
        ).astype(jnp.float32)
        projected = projected.astype(jnp.bfloat16)
        queries = projected[..., :D]
        key_heads = projected[..., D : 2 * D].reshape(item_count, tokens_here, H, HD)
        value_heads = projected[..., 2 * D :].reshape(item_count, tokens_here, H, HD)
        pairs_local = jnp.concatenate([key_heads, value_heads], -1).transpose(0, 2, 1, 3)
        pairs_full = lax.all_gather(pairs_local, "seq", axis=2, tiled=True)
        rows_pairs = assemble(pairs_full, flat_ids)
        query_blocks = queries.reshape(item_count, local_blocks, BLK, H, HD)
        scores = (
            jnp.einsum(
                "inqhd,ihnkd->ihnqk",
                query_blocks,
                rows_pairs[..., :HD],
                preferred_element_type=jnp.float32,
            )
            * score_scale
        )
        row_max = jnp.max(scores, -1)
        exponent = jnp.exp(scores - row_max[..., None])
        row_sum = jnp.sum(exponent, -1)
        chances = exponent / row_sum[..., None]
        log_sum = row_max + jnp.log(row_sum)
        context = jnp.einsum(
            "ihnqk,ihnkd->inqhd",
            chances.astype(jnp.bfloat16),
            rows_pairs[..., HD:],
            preferred_element_type=jnp.float32,
        ).reshape(item_count, tokens_here, D)
        first_rows = jnp.where(is_first, queries[:, :BLK], jnp.zeros_like(queries[:, :BLK]))
        last_rows = jnp.where(is_last, queries[:, tail:], jnp.zeros_like(queries[:, tail:]))
        glob_queries = lax.psum(
            jnp.concatenate([first_rows, last_rows], 1).astype(jnp.float32).astype(jnp.bfloat16),
            "seq",
        )
        glob_heads = glob_queries.reshape(item_count, 2 * BLK, H, HD)
        glob_scores = (
            jnp.einsum(
                "iqhd,ihkd->ihqk",
                glob_heads,
                pairs_local[..., :HD],
                preferred_element_type=jnp.float32,
            )
            * score_scale
        )
        glob_max = jnp.max(glob_scores, -1)
        glob_exp = jnp.exp(glob_scores - glob_max[..., None])
        glob_sum = jnp.sum(glob_exp, -1)
        glob_num = jnp.einsum(
            "ihqk,ihkd->ihqd",
            glob_exp,
            pairs_local[..., HD:].astype(jnp.float32),
            precision=exact_mode,
        )
        glob_max, glob_sum, glob_num = combined_all(
            (glob_max, glob_sum, glob_num), "seq", merge_parts
        )
        glob_context = (
            (glob_num / glob_sum[..., None]).transpose(0, 2, 1, 3).reshape(item_count, 2 * BLK, D)
        )
        glob_lse = glob_max + jnp.log(glob_sum)
        first_ctx = jnp.where(is_first, glob_context[:, :BLK], context[:, :BLK])
        last_ctx = jnp.where(is_last, glob_context[:, BLK:], context[:, tail:])
        context = context.at[:, :BLK].set(first_ctx).at[:, tail:].set(last_ctx)
        context_low = context.astype(jnp.bfloat16)
        attn_out = jnp.einsum(
            "ite,ed->itd", context_low, out_weight, preferred_element_type=jnp.float32
        )
        resid_one = current + attn_out + out_bias.astype(jnp.float32)
        normed = layer_norm(resid_one, gain_one.astype(jnp.float32), shift_one.astype(jnp.float32))
        normed_low = normed.astype(jnp.bfloat16)
        pre_act = jnp.einsum(
            "itd,df->itf", normed_low, inner_weight, preferred_element_type=jnp.float32
        )
        pre_act = pre_act + inner_bias.astype(jnp.float32)
        activated = jax.nn.gelu(pre_act, approximate=True).astype(jnp.bfloat16)
        ffn_out = jnp.einsum(
            "itf,fd->itd", activated, outer_weight, preferred_element_type=jnp.float32
        )
        resid_two = normed + ffn_out + outer_bias.astype(jnp.float32)
        current = layer_norm(resid_two, gain_two.astype(jnp.float32), shift_two.astype(jnp.float32))
        saved_layers.append(
            (
                input_low,
                queries,
                pairs_local,
                pairs_full,
                random_ids,
                flat_ids,
                log_sum,
                glob_queries,
                glob_lse,
                context_low,
                resid_one,
                normed_low,
                pre_act,
                activated,
                resid_two,
            )
        )
    grad_state = cotangent
    collected = [None] * LAYERS
    item_index = jnp.arange(item_count, dtype=jnp.int32)[:, None, None]
    head_index = jnp.arange(H, dtype=jnp.int32)[None, :, None]
    for section_index in reversed(range(LAYERS)):
        (
            qkv_weight,
            query_bias,
            value_bias,
            out_weight,
            out_bias,
            gain_one,
            shift_one,
            inner_weight,
            inner_bias,
            outer_weight,
            outer_bias,
            gain_two,
            shift_two,
        ) = layer_weights[section_index]
        (
            input_low,
            queries,
            pairs_local,
            pairs_full,
            random_ids,
            flat_ids,
            log_sum,
            glob_queries,
            glob_lse,
            context_low,
            resid_one,
            normed_low,
            pre_act,
            activated,
            resid_two,
        ) = saved_layers[section_index]
        unused_two, pull_two = jax.vjp(
            layer_norm, resid_two, gain_two.astype(jnp.float32), shift_two.astype(jnp.float32)
        )
        grad_resid_two, grad_gain_two, grad_shift_two = pull_two(grad_state)
        grad_ffn = grad_resid_two.astype(jnp.bfloat16)
        grad_outer_weight = jnp.einsum(
            "itf,itd->fd", activated, grad_ffn, preferred_element_type=jnp.float32
        )
        grad_outer_bias = jnp.sum(grad_ffn.astype(jnp.float32), (0, 1))
        grad_act = jnp.einsum(
            "itd,fd->itf", grad_ffn, outer_weight, preferred_element_type=jnp.float32
        )
        unused_act, pull_gelu = jax.vjp(partial(jax.nn.gelu, approximate=True), pre_act)
        grad_pre = pull_gelu(grad_act)[0].astype(jnp.bfloat16)
        grad_inner_weight = jnp.einsum(
            "itd,itf->df", normed_low, grad_pre, preferred_element_type=jnp.float32
        )
        grad_inner_bias = jnp.sum(grad_pre.astype(jnp.float32), (0, 1))
        grad_normed = grad_resid_two + jnp.einsum(
            "itf,df->itd", grad_pre, inner_weight, preferred_element_type=jnp.float32
        )
        unused_one, pull_one = jax.vjp(
            layer_norm, resid_one, gain_one.astype(jnp.float32), shift_one.astype(jnp.float32)
        )
        grad_resid_one, grad_gain_one, grad_shift_one = pull_one(grad_normed)
        grad_attn = grad_resid_one.astype(jnp.bfloat16)
        grad_out_weight = jnp.einsum(
            "ite,itd->ed", context_low, grad_attn, preferred_element_type=jnp.float32
        )
        grad_out_bias = jnp.sum(grad_attn.astype(jnp.float32), (0, 1))
        grad_context = jnp.einsum(
            "itd,ed->ite", grad_attn, out_weight, preferred_element_type=jnp.float32
        ).astype(jnp.bfloat16)
        rows_pairs = assemble(pairs_full, flat_ids)
        query_blocks = queries.reshape(item_count, local_blocks, BLK, H, HD)
        scores = (
            jnp.einsum(
                "inqhd,ihnkd->ihnqk",
                query_blocks,
                rows_pairs[..., :HD],
                preferred_element_type=jnp.float32,
            )
            * score_scale
        )
        chances = jnp.exp(scores - log_sum[..., None])
        grad_regular = jnp.where(row_regular, grad_context, jnp.zeros_like(grad_context))
        grad_regular = grad_regular.reshape(item_count, local_blocks, BLK, H, HD)
        grad_prob = jnp.einsum(
            "inqhd,ihnkd->ihnqk",
            grad_regular,
            rows_pairs[..., HD:],
            preferred_element_type=jnp.float32,
        )
        row_delta = jnp.sum(chances * grad_prob, -1)
        grad_score = (chances * (grad_prob - row_delta[..., None])).astype(jnp.bfloat16)
        grad_queries = (
            jnp.einsum(
                "ihnqk,ihnkd->inqhd",
                grad_score,
                rows_pairs[..., :HD],
                preferred_element_type=jnp.float32,
            ).reshape(item_count, tokens_here, D)
            * score_scale
        )
        grad_key_rows = (
            jnp.einsum(
                "ihnqk,inqhd->ihnkd", grad_score, query_blocks, preferred_element_type=jnp.float32
            )
            * score_scale
        )
        grad_value_rows = jnp.einsum(
            "ihnqk,inqhd->ihnkd",
            chances.astype(jnp.bfloat16),
            grad_regular,
            preferred_element_type=jnp.float32,
        )
        grad_rows = jnp.concatenate([grad_key_rows, grad_value_rows], -1).reshape(
            item_count, H, local_blocks, 5 + RAND, BLK, 2 * HD
        )
        block_pad = ((0, 0), (0, 0), (0, 2), (0, 0), (0, 0))
        window_ext = (
            jnp.pad(grad_rows[:, :, :, 0], block_pad)
            + jnp.pad(grad_rows[:, :, :, 1], ((0, 0), (0, 0), (1, 1), (0, 0), (0, 0)))
            + jnp.pad(grad_rows[:, :, :, 2], ((0, 0), (0, 0), (2, 0), (0, 0), (0, 0)))
        )
        rims = jnp.stack([window_ext[:, :, 0], window_ext[:, :, local_blocks + 1]], 2)
        rim_halo = with_halo(rims.astype(jnp.bfloat16), (("seq", 2),), 1).astype(rims.dtype)
        nearby = window_ext[:, :, 1 : local_blocks + 1]
        nearby = nearby.at[:, :, 0].add(rim_halo[:, :, 0])
        nearby = nearby.at[:, :, local_blocks - 1].add(rim_halo[:, :, 3])
        glob_keys = lax.psum(
            jnp.stack(
                [jnp.sum(grad_rows[:, :, :, 3], 2), jnp.sum(grad_rows[:, :, :, 4], 2)], 2
            ).astype(jnp.bfloat16),
            "seq",
        ).astype(jnp.float32)
        nearby = nearby.at[:, :, 0].add(
            jnp.where(is_first, glob_keys[:, :, 0], jnp.zeros_like(glob_keys[:, :, 0]))
        )
        nearby = nearby.at[:, :, local_blocks - 1].add(
            jnp.where(is_last, glob_keys[:, :, 1], jnp.zeros_like(glob_keys[:, :, 1]))
        )
        entries = local_blocks * RAND
        capacity = (entries + seq_count - 1) // seq_count
        rand_rows = grad_rows[:, :, :, 5:].reshape(item_count, H, entries, BLK, 2 * HD)
        owner_ids = random_ids // local_blocks
        within_ids = random_ids % local_blocks
        owner_hot = (owner_ids[..., None] == jnp.arange(seq_count, dtype=jnp.int32)).astype(
            jnp.int32
        )
        earlier = jnp.cumsum(owner_hot, 2) - owner_hot
        slot_ids = jnp.sum(earlier * owner_hot, -1)
        positions = owner_ids * capacity + slot_ids
        send_rows = jnp.zeros((item_count, H, seq_count * capacity, BLK, 2 * HD), jnp.float32)
        send_rows = send_rows.at[item_index, head_index, positions].set(rand_rows)
        send_ids = jnp.full((item_count, H, seq_count * capacity), -1, jnp.int32)
        send_ids = send_ids.at[item_index, head_index, positions].set(within_ids)
        recv_rows, recv_ids = (
            lax.all_to_all(
                send_rows.astype(jnp.bfloat16), "seq", split_axis=2, concat_axis=2, tiled=True
            ).astype(send_rows.dtype),
            lax.all_to_all(send_ids, "seq", split_axis=2, concat_axis=2, tiled=True),
        )
        block_hot = (
            recv_ids[:, :, None, :] == jnp.arange(local_blocks, dtype=jnp.int32)[:, None]
        ).astype(jnp.float32)
        nearby = nearby + jnp.einsum(
            "ihlp,ihpkd->ihlkd", block_hot, recv_rows, precision=exact_mode
        )
        grad_pairs = nearby.reshape(item_count, H, tokens_here, 2 * HD)
        first_grads = jnp.where(
            is_first, grad_context[:, :BLK], jnp.zeros_like(grad_context[:, :BLK])
        )
        last_grads = jnp.where(
            is_last, grad_context[:, tail:], jnp.zeros_like(grad_context[:, tail:])
        )
        glob_grads = lax.psum(
            jnp.concatenate([first_grads, last_grads], 1).astype(jnp.float32).astype(jnp.bfloat16),
            "seq",
        )
        grad_heads = glob_grads.reshape(item_count, 2 * BLK, H, HD)
        glob_heads = glob_queries.reshape(item_count, 2 * BLK, H, HD)
        glob_scores = (
            jnp.einsum(
                "iqhd,ihkd->ihqk",
                glob_heads,
                pairs_local[..., :HD],
                preferred_element_type=jnp.float32,
            )
            * score_scale
        )
        glob_chances = jnp.exp(glob_scores - glob_lse[..., None])
        glob_grad_prob = jnp.einsum(
            "iqhd,ihkd->ihqk", grad_heads, pairs_local[..., HD:], preferred_element_type=jnp.float32
        )
        glob_delta = lax.psum(jnp.sum(glob_chances * glob_grad_prob, -1), "seq")
        glob_grad_score = (glob_chances * (glob_grad_prob - glob_delta[..., None])).astype(
            jnp.bfloat16
        )
        part_dquery = (
            jnp.einsum(
                "ihqk,ihkd->iqhd",
                glob_grad_score,
                pairs_local[..., :HD],
                preferred_element_type=jnp.float32,
            ).reshape(item_count, 2 * BLK, D)
            * score_scale
        )
        glob_dquery = lax.psum(part_dquery.astype(jnp.bfloat16), "seq").astype(jnp.float32)
        glob_dkey = (
            jnp.einsum(
                "ihqk,iqhd->ihkd", glob_grad_score, glob_heads, preferred_element_type=jnp.float32
            )
            * score_scale
        )
        glob_dvalue = jnp.einsum(
            "ihqk,iqhd->ihkd", glob_chances, grad_heads.astype(jnp.float32), precision=exact_mode
        )
        grad_pairs = grad_pairs + jnp.concatenate([glob_dkey, glob_dvalue], -1)
        grad_queries = grad_queries.at[:, :BLK].add(
            jnp.where(is_first, glob_dquery[:, :BLK], jnp.zeros_like(glob_dquery[:, :BLK]))
        )
        grad_queries = grad_queries.at[:, tail:].add(
            jnp.where(is_last, glob_dquery[:, BLK:], jnp.zeros_like(glob_dquery[:, BLK:]))
        )
        grad_keys = grad_pairs[..., :HD].transpose(0, 2, 1, 3).reshape(item_count, tokens_here, D)
        grad_values = grad_pairs[..., HD:].transpose(0, 2, 1, 3).reshape(item_count, tokens_here, D)
        grad_proj = jnp.concatenate([grad_queries, grad_keys, grad_values], -1).astype(jnp.bfloat16)
        grad_qkv_weight = jnp.einsum(
            "itd,ite->de", input_low, grad_proj, preferred_element_type=jnp.float32
        )
        grad_query_bias = jnp.sum(grad_proj[..., :D].astype(jnp.float32), (0, 1))
        grad_value_bias = jnp.sum(grad_proj[..., 2 * D :].astype(jnp.float32), (0, 1))
        grad_state = grad_resid_one + jnp.einsum(
            "ite,de->itd", grad_proj, qkv_weight, preferred_element_type=jnp.float32
        )
        grad_shares = (
            lax.psum_scatter(
                grad_qkv_weight.astype(jnp.bfloat16), "item", scatter_dimension=0, tiled=True
            ).astype(jnp.float32),
            lax.psum_scatter(
                grad_query_bias.astype(jnp.bfloat16), "item", scatter_dimension=0, tiled=True
            ).astype(jnp.float32),
            lax.psum_scatter(
                grad_value_bias.astype(jnp.bfloat16), "item", scatter_dimension=0, tiled=True
            ).astype(jnp.float32),
            lax.psum_scatter(
                grad_out_weight.astype(jnp.bfloat16), "item", scatter_dimension=0, tiled=True
            ).astype(jnp.float32),
            lax.psum_scatter(
                grad_out_bias.astype(jnp.bfloat16), "item", scatter_dimension=0, tiled=True
            ).astype(jnp.float32),
            lax.psum_scatter(
                grad_gain_one.astype(jnp.bfloat16), "item", scatter_dimension=0, tiled=True
            ).astype(jnp.float32),
            lax.psum_scatter(
                grad_shift_one.astype(jnp.bfloat16), "item", scatter_dimension=0, tiled=True
            ).astype(jnp.float32),
            lax.psum_scatter(
                grad_inner_weight.astype(jnp.bfloat16), "item", scatter_dimension=0, tiled=True
            ).astype(jnp.float32),
            lax.psum_scatter(
                grad_inner_bias.astype(jnp.bfloat16), "item", scatter_dimension=0, tiled=True
            ).astype(jnp.float32),
            lax.psum_scatter(
                grad_outer_weight.astype(jnp.bfloat16), "item", scatter_dimension=0, tiled=True
            ).astype(jnp.float32),
            lax.psum_scatter(
                grad_outer_bias.astype(jnp.bfloat16), "item", scatter_dimension=0, tiled=True
            ).astype(jnp.float32),
            lax.psum_scatter(
                grad_gain_two.astype(jnp.bfloat16), "item", scatter_dimension=0, tiled=True
            ).astype(jnp.float32),
            lax.psum_scatter(
                grad_shift_two.astype(jnp.bfloat16), "item", scatter_dimension=0, tiled=True
            ).astype(jnp.float32),
        )
        collected[section_index] = (
            lax.psum(grad_shares[0].astype(jnp.bfloat16), "seq").astype(jnp.float32),
            lax.psum(grad_shares[1].astype(jnp.bfloat16), "seq").astype(jnp.float32),
            lax.psum(grad_shares[2].astype(jnp.bfloat16), "seq").astype(jnp.float32),
            lax.psum(grad_shares[3].astype(jnp.bfloat16), "seq").astype(jnp.float32),
            lax.psum(grad_shares[4].astype(jnp.bfloat16), "seq").astype(jnp.float32),
            lax.psum(grad_shares[5].astype(jnp.bfloat16), "seq").astype(jnp.float32),
            lax.psum(grad_shares[6].astype(jnp.bfloat16), "seq").astype(jnp.float32),
            lax.psum(grad_shares[7].astype(jnp.bfloat16), "seq").astype(jnp.float32),
            lax.psum(grad_shares[8].astype(jnp.bfloat16), "seq").astype(jnp.float32),
            lax.psum(grad_shares[9].astype(jnp.bfloat16), "seq").astype(jnp.float32),
            lax.psum(grad_shares[10].astype(jnp.bfloat16), "seq").astype(jnp.float32),
            lax.psum(grad_shares[11].astype(jnp.bfloat16), "seq").astype(jnp.float32),
            lax.psum(grad_shares[12].astype(jnp.bfloat16), "seq").astype(jnp.float32),
        )
    weight_grads = tuple(
        (
            jnp.stack([collected[section_index][slot_index] for section_index in range(LAYERS)])
            for slot_index in range(13)
        )
    )
    return (current, grad_state) + weight_grads


def solution(mesh):
    placed = (
        P("item", "seq", None),
        P("item", None, "seq", None, None),
        P(None, "item", None),
        P(None, "item"),
        P(None, "item"),
        P(None, "item", None),
        P(None, "item"),
        P(None, "item"),
        P(None, "item"),
        P(None, "item", None),
        P(None, "item"),
        P(None, "item", None),
        P(None, "item"),
        P(None, "item"),
        P(None, "item"),
        P("item", "seq", None),
    )
    return jax.shard_map(
        local,
        mesh=mesh,
        in_specs=placed,
        out_specs=(
            P("item", "seq", None),
            P("item", "seq", None),
            P(None, "item", None),
            P(None, "item"),
            P(None, "item"),
            P(None, "item", None),
            P(None, "item"),
            P(None, "item"),
            P(None, "item"),
            P(None, "item", None),
            P(None, "item"),
            P(None, "item", None),
            P(None, "item"),
            P(None, "item"),
            P(None, "item"),
        ),
        check_vma=False,
    )
```

profile of v0, /device:TPU:0, one launch (start us, length us, event | category | flops | bytes accessed | tf_op | source)
XLA Modules:
  0.0 2927.6 jit_solution(11261773702888758552)
XLA Ops:
  20.9 32.2 %all-reduce.41 = (bf16[768]{0:T(1024)(128)(2,1)S(1)}, bf16[768]{0:T(1024)(128)(2,1)S(1)}, bf16[768]{0:T(1024)(128)(2,1)S(1)}, bf16[768]{0:T(1024)(128)(2,1)S(1)}...) all-reduce(bf16[768]{0:T(1024)(128)(2,1)S(1)} %dynamic-update-slice, ...), channel_id=9, replica_groups=mesh['seq'=4,'item'=8] {'item'}, use_global_device_ids=true, to_apply=%add.8 | all-reduce | flops 11520 | bytes 46080
  74.8 31.8 %all-reduce.54.cloned.1.call-done = bf16[128,12,64]{0,2,1:T(8,128)(2,1)} async-done(((bf16[128,12,64]{0,2,1:T(8,128)(2,1)}), bf16[128,12,64]{0,2,1:T(8,128)(2,1)}) %all-reduce.54.cloned.1.call-update) | async-done | bytes 196624 | tf_op jit(solution)/shard_map/psum | solution.py:214
  184.5 88.6 %all-gather.49.cloned.1.call-done = bf16[1,12,4096,128]{2,3,1,0:T(8,128)(2,1)} async-done(((bf16[1,12,1024,128]{2,3,1,0:T(8,128)(2,1)}), bf16[1,12,4096,128]{2,3,1,0:T(8,128)(2,1)}) %all-gather.49.cloned.1.call-update) | async-done | bytes 12582928 | tf_op jit(solution)/shard_map/all_gather | solution.py:189
  289.8 38.4 %gather_fusion = bf16[1536,64,128]{2,1,0:T(8,128)(2,1)} fusion(bf16[768,64,128]{2,1,0:T(8,128)(2,1)} %bitcast.642, s32[2048]{0:T(1024)S(1)} %pad_clamp_fusion.1), kind=kCustom, calls=%fused_computation.clone | custom fusion | bytes 50337792 | tf_op jit(solution)/shard_map/jit(_take)/gather | solution.py:88
  350.4 35.0 %slice_bitcast_fusion.1 = (bf16[12,16,512,64]{3,2,1,0:T(8,128)(2,1)}, bf16[1,12,16,512,64]{4,3,2,1,0:T(8,128)(2,1)}) fusion(bf16[1,12,16,512,128]{4,3,2,1,0:T(8,128)(2,1)} %bitcast.636), kind=kLoop, calls=%fused_computation.29 | loop fusion | bytes 50331648 | tf_op jit(solution)/shard_map/reshape.566
  523.0 31.5 %all-reduce.56.cloned.1.call-done = bf16[128,12,64]{0,2,1:T(8,128)(2,1)} async-done(((bf16[128,12,64]{0,2,1:T(8,128)(2,1)}), bf16[128,12,64]{0,2,1:T(8,128)(2,1)}) %all-reduce.56.cloned.1.call-update) | async-done | bytes 196624 | tf_op jit(solution)/shard_map/psum | solution.py:214
  570.6 30.2 %scatter_fusion = s32[12,48]{1,0:T(8,128)S(1)} fusion(s32[12,48]{1,0:T(8,128)S(1)} %broadcast.1343.clone, s32[576]{0:T(1024)S(1)} %reshape.2752, s32[576]{0:T(1024)S(1)} %reshape.2754), kind=kCustom, calls=%fused_computation.2 | custom fusion | bytes 11520 | tf_op jit(solution)/shard_map/scatter | solution.py:436
  607.2 30.2 %scatter_fusion.2 = s32[12,48]{1,0:T(8,128)S(1)} fusion(s32[12,48]{1,0:T(8,128)S(1)} %broadcast.1343.clone.1, s32[576]{0:T(1024)S(1)} %reshape.2772, s32[576]{0:T(1024)S(1)} %reshape.2774), kind=kCustom, calls=%fused_computation.4 | custom fusion | bytes 11520 | tf_op jit(solution)/shard_map/scatter | solution.py:436
  737.1 38.4 %gather_fusion.1 = bf16[1536,64,128]{2,1,0:T(8,128)(2,1)} fusion(bf16[768,64,128]{2,1,0:T(8,128)(2,1)} %bitcast.643, s32[2048]{0:T(1024)S(1)} %pad_clamp_fusion), kind=kCustom, calls=%fused_computation.1.clone | custom fusion | bytes 50337792 | tf_op jit(solution)/shard_map/jit(_take)/gather | solution.py:88
  797.8 33.8 %slice_bitcast_fusion = (bf16[12,16,512,64]{3,2,1,0:T(8,128)(2,1)}, bf16[1,12,16,512,64]{4,3,2,1,0:T(8,128)(2,1)}) fusion(bf16[1,12,16,512,128]{4,3,2,1,0:T(8,128)(2,1)} %bitcast.639), kind=kLoop, calls=%fused_computation.28 | loop fusion | bytes 50331648 | tf_op jit(solution)/shard_map/reshape.613
  995.0 28.1 multiply_reduce_fusion.1
  1042.2 36.4 %concatenate.268 = f32[1,12,16,8,64,64]{4,3,5,2,1,0:T(8,128)} reshape(f32[12,16,512,64]{2,3,1,0:T(8,128)} %fusion.24) | data formatting | bytes 50331648 | tf_op jit(solution)/shard_map/concatenate | solution.py:396
  1078.6 46.5 %copy.445 = f32[1,12,16,8,64,64]{5,2,4,1,3,0:T(8,128)} copy(f32[1,12,16,8,64,64]{4,3,5,2,1,0:T(8,128)} %concatenate.268) | data formatting | bytes 50331648 | tf_op jit(solution)/shard_map/concatenate | solution.py:396
  1163.1 36.4 %concatenate.267 = f32[1,12,16,8,64,64]{4,3,5,2,1,0:T(8,128)} reshape(f32[12,16,512,64]{2,3,1,0:T(8,128)} %broadcast_multiply_fusion.1) | data formatting | bytes 50331648 | tf_op jit(solution)/shard_map/concatenate | solution.py:396
  1199.5 46.9 %copy.444 = f32[1,12,16,8,64,64]{5,2,4,1,3,0:T(8,128)} copy(f32[1,12,16,8,64,64]{4,3,5,2,1,0:T(8,128)} %concatenate.267) | data formatting | bytes 50331648 | tf_op jit(solution)/shard_map/concatenate | solution.py:396
  1277.2 91.4 %scatter_fusion.1 = f32[12,48,64,128]{3,2,1,0:T(8,128)} fusion(f32[12,48,64,128]{3,2,1,0:T(8,128)} %broadcast.1345.clone, s32[576]{0:T(1024)S(1)} %copy-done.5, f32[576,64,128]{2,1,0:T(8,128)} %bitcast.652), kind=kCustom, calls=%fused_computation.3 | custom fusion | bytes 56627712 | tf_op jit(solution)/shard_map/scatter | solution.py:434
  1430.8 29.2 maximum_reduce_fusion.3
  1490.4 44.5 %all-reduce.58.cloned.1.call-done = bf16[128,12,64]{0,2,1:T(8,128)(2,1)} async-done(((bf16[128,12,64]{0,2,1:T(8,128)(2,1)}), bf16[128,12,64]{0,2,1:T(8,128)(2,1)}) %all-reduce.58.cloned.1.call-update) | async-done | bytes 196624 | tf_op jit(solution)/shard_map/psum | solution.py:456
  1727.4 28.3 multiply_reduce_fusion
  1774.8 36.4 %concatenate.282 = f32[1,12,16,8,64,64]{4,3,5,2,1,0:T(8,128)} reshape(f32[12,16,512,64]{2,3,1,0:T(8,128)} %fusion.22) | data formatting | bytes 50331648 | tf_op jit(solution)/shard_map/concatenate | solution.py:396
  1811.2 46.5 %copy.487 = f32[1,12,16,8,64,64]{5,2,4,1,3,0:T(8,128)} copy(f32[1,12,16,8,64,64]{4,3,5,2,1,0:T(8,128)} %concatenate.282) | data formatting | bytes 50331648 | tf_op jit(solution)/shard_map/concatenate | solution.py:396
  1895.7 36.4 %concatenate.281 = f32[1,12,16,8,64,64]{4,3,5,2,1,0:T(8,128)} reshape(f32[12,16,512,64]{2,3,1,0:T(8,128)} %broadcast_multiply_fusion) | data formatting | bytes 50331648 | tf_op jit(solution)/shard_map/concatenate | solution.py:396
  1932.2 46.7 %copy.486 = f32[1,12,16,8,64,64]{5,2,4,1,3,0:T(8,128)} copy(f32[1,12,16,8,64,64]{4,3,5,2,1,0:T(8,128)} %concatenate.281) | data formatting | bytes 50331648 | tf_op jit(solution)/shard_map/concatenate | solution.py:396
  1978.9 29.1 maximum_reduce_fusion.1
  2057.8 91.5 %scatter_fusion.3 = f32[12,48,64,128]{3,2,1,0:T(8,128)} fusion(f32[12,48,64,128]{3,2,1,0:T(8,128)} %broadcast.1345, s32[576]{0:T(1024)S(1)} %copy-done.3, f32[576,64,128]{2,1,0:T(8,128)} %bitcast.653), kind=kCustom, calls=%fused_computation.5 | custom fusion | bytes 56627712 | tf_op jit(solution)/shard_map/scatter | solution.py:434
  2186.2 96.9 %psum.259 = f32[12,128]{1,0:T(8,128)S(1)} all-reduce(f32[12,128]{1,0:T(8,128)S(1)} %get-tuple-element.932), channel_id=1, replica_groups=mesh['seq'=4,'item'=8] {'seq'}, use_global_device_ids=true, to_apply=%region_45.47 | all-reduce | flops 1536 | bytes 12288 | tf_op jit(solution)/shard_map/psum | solution.py:475
  2541.8 28.5 all-reduce.40
  2585.6 55.4 %reduce-scatter.19.cloned.1.call-done = bf16[96,3072]{1,0:T(8,128)(2,1)} async-done(((bf16[768,3072]{1,0:T(8,128)(2,1)}), bf16[96,3072]{1,0:T(8,128)(2,1)}) %reduce-scatter.19.cloned.1.call-update) | async-done | bytes 589840 | tf_op jit(solution)/shard_map/reduce_scatter | solution.py:538
  2641.0 55.5 %reduce-scatter.23.cloned.1.call-done = bf16[384,768]{1,0:T(8,128)(2,1)} async-done(((bf16[3072,768]{1,0:T(8,128)(2,1)}), bf16[384,768]{1,0:T(8,128)(2,1)}) %reduce-scatter.23.cloned.1.call-update) | async-done | bytes 589840 | tf_op jit(solution)/shard_map/reduce_scatter | solution.py:544
  2696.5 55.7 %reduce-scatter.17.cloned.1.call-done = bf16[96,3072]{1,0:T(8,128)(2,1)} async-done(((bf16[768,3072]{1,0:T(8,128)(2,1)}), bf16[96,3072]{1,0:T(8,128)(2,1)}) %reduce-scatter.17.cloned.1.call-update) | async-done | bytes 589840 | tf_op jit(solution)/shard_map/reduce_scatter | solution.py:538
  2752.1 55.5 %reduce-scatter.21.cloned.1.call-done = bf16[384,768]{1,0:T(8,128)(2,1)} async-done(((bf16[3072,768]{1,0:T(8,128)(2,1)}), bf16[384,768]{1,0:T(8,128)(2,1)}) %reduce-scatter.21.cloned.1.call-update) | async-done | bytes 589840 | tf_op jit(solution)/shard_map/reduce_scatter | solution.py:544
  2843.8 67.1 %all-reduce.62.cloned.1.call-done = (bf16[1,96,2304]{1,2,0:T(8,128)(2,1)}, bf16[1,96,2304]{1,2,0:T(8,128)(2,1)}, bf16[1,96,768]{2,1,0:T(8,128)(2,1)}, bf16[1,96,...) async-done(((bf16[1,96,2304]{1,2,0:T(8,128)(2,1)}, ...) | async-done | bytes 3538960 | tf_op jit(solution)/shard_map/psum | solution.py:558
  (895 shorter events, 1441.7 us)
Async XLA Ops:
  9.4 97.3 %all-reduce.54.cloned.1.call-start = ((), (), s32[]{:S(2)}) async-start(), calls=%async_computation.13 | async-start | bytes 393216 | tf_op jit(solution)/shard_map/psum | solution.py:214
  65.0 110.5 %all-gather.55.cloned.1.call-start = ((), (), s32[]{:S(2)}) async-start(), calls=%async_computation.25 | async-start | bytes 1966080 | tf_op jit(solution)/shard_map/all_gather | solution.py:26
  116.6 156.5 %all-gather.49.cloned.1.call-start = ((), (), s32[]{:S(2)}) async-start(), calls=%async_computation.12 | async-start | bytes 15728640 | tf_op jit(solution)/shard_map/all_gather | solution.py:189
  117.1 356.1 %all-gather.57.cloned.1.call-start = ((), (), s32[]{:S(2)}) async-start(), calls=%async_computation.26 | async-start | bytes 1327104 | tf_op jit(solution)/shard_map/all_gather | solution.py:151
  118.0 360.0 %all-gather.59.cloned.1.call-start = ((), (), s32[]{:S(2)}) async-start(), calls=%async_computation.27 | async-start | bytes 5308416 | tf_op jit(solution)/shard_map/all_gather | solution.py:151
  119.1 370.1 %all-gather.61.cloned.1.call-start = ((), (), s32[]{:S(2)}) async-start(), calls=%async_computation.28 | async-start | bytes 5308416 | tf_op jit(solution)/shard_map/all_gather | solution.py:151
  120.3 382.5 %all-gather.63.cloned.1.call-start = ((), (), s32[]{:S(2)}) async-start(), calls=%async_computation.29 | async-start | bytes 3981312 | tf_op jit(solution)/shard_map/all_gather | solution.py:151
  121.1 433.4 %all-reduce.56.cloned.1.call-start = ((), (), s32[]{:S(2)}) async-start(), calls=%async_computation.15 | async-start | bytes 393216 | tf_op jit(solution)/shard_map/psum | solution.py:214
  513.0 187.7 %all-gather.65.cloned.1.call-start = ((), (), s32[]{:S(2)}) async-start(), calls=%async_computation.30 | async-start | bytes 1966080 | tf_op jit(solution)/shard_map/all_gather | solution.py:26
  564.3 156.1 %all-gather.51.cloned.1.call-start = ((), (), s32[]{:S(2)}) async-start(), calls=%async_computation.14 | async-start | bytes 15728640 | tf_op jit(solution)/shard_map/all_gather | solution.py:189
  565.1 352.8 %all-gather.67.cloned.1.call-start = ((), (), s32[]{:S(2)}) async-start(), calls=%async_computation.31 | async-start | bytes 1327104 | tf_op jit(solution)/shard_map/all_gather | solution.py:151
  565.6 357.4 %all-gather.69.cloned.1.call-start = ((), (), s32[]{:S(2)}) async-start(), calls=%async_computation.32 | async-start | bytes 5308416 | tf_op jit(solution)/shard_map/all_gather | solution.py:151
  606.1 328.1 %all-gather.71.cloned.1.call-start = ((), (), s32[]{:S(2)}) async-start(), calls=%async_computation.33 | async-start | bytes 5308416 | tf_op jit(solution)/shard_map/all_gather | solution.py:151
  1389.5 251.9 %all-to-all-start.1 = ((bf16[1,12,48,64,128]{4,3,1,0,2:T(8,128)(2,1)}), bf16[1,12,48,64,128]{4,3,1,0,2:T(8,128)(2,1)}, u32[]{:S(2)}, u32[]{:S(2)}) async-start(bf16[1,12,48,64,128]{4,3,1,0,2:T(8,128)(2,1)} %copy.466), calls=%async_computation.1 | async-start | bytes 18874368 | tf_op jit(solution)/shard_map/all_to_all | solution.py:438
  1395.3 139.6 %all-reduce.58.cloned.1.call-start = ((), (), s32[]{:S(2)}) async-start(), calls=%async_computation.16 | async-start | bytes 393216 | tf_op jit(solution)/shard_map/psum | solution.py:456
  1430.7 176.8 %all-reduce.66.cloned.1.call-start = ((), (), s32[]{:S(2)}) async-start(), calls=%async_computation.38 | async-start | bytes 1179648 | tf_op jit(solution)/shard_map/psum | solution.py:488
  1483.5 77.7 %collective-permute-start.1 = (bf16[1,12,1,64,128]{4,2,3,1,0:T(2,128)(2,1)}, bf16[1,12,1,64,128]{4,2,3,1,0:T(2,128)(2,1)}, u32[]{:S(2)}, u32[]{:S(2)}) collective-permute-start(bf16[1,12,1,64,128]{4,2,3,1,0:T(2,128)(2,1)} %get-tuple-element.842), channel_id=1, source_target_pairs={{8,0},{16,8},{24,16},{0,24},{9,1},{17,9},{25,17},{1,25},{10,2},{18... | collective-permute-start | bytes 589832 | tf_op jit(solution)/shard_map/ppermute | solution.py:45
  1486.6 74.6 %collective-permute-start = (bf16[1,12,1,64,128]{4,2,3,1,0:T(2,128)(2,1)}, bf16[1,12,1,64,128]{4,2,3,1,0:T(2,128)(2,1)}, u32[]{:S(2)}, u32[]{:S(2)}) collective-permute-start(bf16[1,12,1,64,128]{4,2,3,1,0:T(2,128)(2,1)} %get-tuple-element.841), channel_id=1, source_target_pairs={{0,8},{8,16},{16,24},{24,0},{1,9},{9,17},{17,25},{25,1},{2,10},{10... | collective-permute-start | bytes 589832 | tf_op jit(solution)/shard_map/ppermute | solution.py:43
  1561.1 617.8 %all-reduce.60.cloned.1.call-start = ((), (), s32[]{:S(2)}) async-start(), calls=%async_computation.17 | async-start | bytes 393216 | tf_op jit(solution)/shard_map/psum | solution.py:456
  2035.9 318.9 %collective-permute-start.3 = (bf16[1,12,1,64,128]{4,2,3,1,0:T(2,128)(2,1)}, bf16[1,12,1,64,128]{4,2,3,1,0:T(2,128)(2,1)}, u32[]{:S(2)}, u32[]{:S(2)}) collective-permute-start(bf16[1,12,1,64,128]{4,2,3,1,0:T(2,128)(2,1)} %get-tuple-element.840), channel_id=1, source_target_pairs={{8,0},{16,8},{24,16},{0,24},{9,1},{17,9},{25,17},{1,25},{10,2},{18... | collective-permute-start | bytes 589832 | tf_op jit(solution)/shard_map/ppermute | solution.py:45
  2037.4 317.4 %collective-permute-start.2 = (bf16[1,12,1,64,128]{4,2,3,1,0:T(2,128)(2,1)}, bf16[1,12,1,64,128]{4,2,3,1,0:T(2,128)(2,1)}, u32[]{:S(2)}, u32[]{:S(2)}) collective-permute-start(bf16[1,12,1,64,128]{4,2,3,1,0:T(2,128)(2,1)} %get-tuple-element.839), channel_id=1, source_target_pairs={{0,8},{8,16},{16,24},{24,0},{1,9},{9,17},{17,25},{25,1},{2,10},{10... | collective-permute-start | bytes 589832 | tf_op jit(solution)/shard_map/ppermute | solution.py:43
  2170.2 260.7 %all-to-all-start.3 = ((bf16[1,12,48,64,128]{4,3,1,0,2:T(8,128)(2,1)}), bf16[1,12,48,64,128]{4,3,1,0,2:T(8,128)(2,1)}, u32[]{:S(2)}, u32[]{:S(2)}) async-start(bf16[1,12,48,64,128]{4,3,1,0,2:T(8,128)(2,1)} %copy.508), calls=%async_computation.3 | async-start | bytes 18874368 | tf_op jit(solution)/shard_map/all_to_all | solution.py:438
  2176.2 220.8 %all-reduce.64.cloned.1.call-start = ((), (), s32[]{:S(2)}) async-start(), calls=%async_computation.37 | async-start | bytes 1179648 | tf_op jit(solution)/shard_map/psum | solution.py:488
  2291.1 285.2 %reduce-scatter.27.cloned.1.call-start = ((), (), s32[]{:S(2)}) async-start(), calls=%async_computation.35 | async-start | bytes 3981312
  2300.7 277.6 %reduce-scatter.25.cloned.1.call-start = ((), (), s32[]{:S(2)}) async-start(), calls=%async_computation.34 | async-start | bytes 3981312
  2473.3 107.1 %reduce-scatter.15.cloned.1.call-start = ((), (), s32[]{:S(2)}) async-start(), calls=%async_computation.19 | async-start | bytes 1327104 | tf_op jit(solution)/shard_map/reduce_scatter | solution.py:526
  2477.8 107.7 %reduce-scatter.13.cloned.1.call-start = ((), (), s32[]{:S(2)}) async-start(), calls=%async_computation.18 | async-start | bytes 1327104 | tf_op jit(solution)/shard_map/reduce_scatter | solution.py:526
  2482.4 158.6 %reduce-scatter.19.cloned.1.call-start = ((), (), s32[]{:S(2)}) async-start(), calls=%async_computation.21 | async-start | bytes 5308416 | tf_op jit(solution)/shard_map/reduce_scatter | solution.py:538
  2492.3 204.2 %reduce-scatter.23.cloned.1.call-start = ((), (), s32[]{:S(2)}) async-start(), calls=%async_computation.23 | async-start | bytes 5308416 | tf_op jit(solution)/shard_map/reduce_scatter | solution.py:544
  2507.0 245.1 %reduce-scatter.17.cloned.1.call-start = ((), (), s32[]{:S(2)}) async-start(), calls=%async_computation.20 | async-start | bytes 5308416 | tf_op jit(solution)/shard_map/reduce_scatter | solution.py:538
  2518.8 288.9 %reduce-scatter.21.cloned.1.call-start = ((), (), s32[]{:S(2)}) async-start(), calls=%async_computation.22 | async-start | bytes 5308416 | tf_op jit(solution)/shard_map/reduce_scatter | solution.py:544
  2533.4 377.5 %all-reduce.62.cloned.1.call-start = ((), (), s32[]{:S(2)}) async-start(), calls=%async_computation.36 | async-start | bytes 7667712 | tf_op jit(solution)/shard_map/psum | solution.py:558
  (175 other events, 3157.4 us)
Sparse Core Ops, SparseCore 0:
  10.2 44.8 all-gather.52
  65.2 41.4 all-reduce.53
  116.7 30.9 all-gather.54
  150.1 122.9 all-gather.48
  274.7 22.6 all-gather.56
  299.5 51.4 all-gather.58
  353.4 50.5 all-gather.60
  405.6 40.3 all-gather.62
  513.1 41.3 all-reduce.55
  564.4 30.9 all-gather.64
  597.3 123.0 all-gather.50
  721.9 22.6 all-gather.66
  746.2 51.4 all-gather.68
  799.8 50.5 all-gather.70
  1430.8 104.0 all-reduce.57
  1561.3 46.1 all-reduce.65
  2030.4 42.8 all-reduce.59
  2291.2 46.4 all-reduce.63
  2340.0 43.8 reduce-scatter.26
  2473.4 44.4 reduce-scatter.24
  2520.2 31.3 reduce-scatter.14
  2554.5 31.0 reduce-scatter.12
  2587.9 53.0 reduce-scatter.18
  2643.1 53.3 reduce-scatter.22
  2698.8 53.3 reduce-scatter.16
  2754.3 53.3 reduce-scatter.20
  2812.0 98.8 all-reduce.61
where the time goes:
time: 2950 us; the launch traced here: 2930 us
  local copies, waits for them, and re-layouts  1210 us (41%)
  matrix products  523 us (18%)
  waiting for transfers between devices  511 us (17%)
  other arithmetic  394 us (13%)
  blocking collectives  242 us (8%)
    concatenate x8, local copies, waits for them, and re-layouts, local(): jnp.concatenate([grad_key_rows, grad_value_rows], -1)  332 us
    scatter x2, local copies, waits for them, and re-layouts, local(): send_rows = send_rows.at[item_index, head_index, positions].set(rand_rows)  183 us
    another operation x15, local copies, waits for them, and re-layouts  129 us
    unnamed x412, local copies, waits for them, and re-layouts  113 us
    reduce_scatter x2, waiting for transfers between devices, local(): lax.psum_scatter(grad_inner_weight.astype(jnp.bfloat16), 'item', scatter_...  111 us
    reduce_scatter x2, waiting for transfers between devices, local(): lax.psum_scatter(grad_outer_weight.astype(jnp.bfloat16), 'item', scatter_...  111 us
    psum x2, blocking collectives, local(): glob_delta = lax.psum(jnp.sum(glob_chances * glob_grad_prob, -1), 'seq')  106 us
    all_gather x2, waiting for transfers between devices, local(): pairs_full = lax.all_gather(pairs_local, 'seq', axis=2, tiled=True)  99.4 us
  transfers between devices with their start and end apart: 35, of which 13 were waited for; matrix products, arithmetic and copies ran while one was open for 42% of the time, Pallas kernels for 0%

commit v1 on v0

v1 whole, which is shorter than its diff:
```python
from functools import partial

import jax
import jax.numpy as jnp
from jax import lax
from jax.experimental import pallas as pl
from jax.experimental.pallas import tpu as pltpu
from jax.sharding import PartitionSpec as P

D = 768
H = 12
LAYERS = 2
epsilon = 1e-05

HD = 64
BLK = 64
RAND = 3
F32=jnp.float32; BF=jnp.bfloat16
LOG2E=1.4426950408889634
NT=(((1,),(1,)),((),()))
TN=(((0,),(0,)),((),()))
NN=(((1,),(0,)),((),()))
def dot(a,b,dn): return lax.dot_general(a,b,dn,preferred_element_type=F32)
KEYS=(5+RAND)*BLK
CH=512

def low(v): return jnp.concatenate([v,jnp.zeros_like(v)],1)
def high(v): return jnp.concatenate([jnp.zeros_like(v),v],1)
def diag(a,b):
    return jnp.concatenate([jnp.concatenate([a,jnp.zeros_like(b)],1),jnp.concatenate([jnp.zeros_like(a),b],1)],0)

def places(hp,h):
    base=hp*2*HD+h*HD
    return slice(h*2*HD,(h+1)*2*HD), slice(base,base+HD), slice(h*HD,(h+1)*HD)

def listed(x_ref,lists_ref,lanes,h,j):
    length=x_ref.shape[0]; nb=length//BLK
    row=pl.multiple_of(j*BLK,BLK); prev=pl.multiple_of(row-BLK,BLK)
    rows=[pl.multiple_of(lists_ref[(h*nb+j)*RAND+r]*BLK,BLK) for r in range(RAND)]
    parts=[x_ref[pl.ds(prev,3*BLK),lanes],x_ref[0:BLK,lanes],x_ref[length-BLK:length,lanes]]
    parts+=[x_ref[pl.ds(k,BLK),lanes] for k in rows]
    return jnp.concatenate(parts,0), row, prev, rows

def pair_of(x_ref,lists_ref,lanes,h,i):
    kva,rowa,preva,ra=listed(x_ref,lists_ref,lanes,h,1+2*i)
    kvb,rowb,prevb,rb=listed(x_ref,lists_ref,lanes,h,2+2*i)
    return jnp.concatenate([kva,kvb],1),(rowa,preva,ra),(rowb,prevb,rb)

def run_pairs(half,hp,first,second,third):
    for h in range(hp): first(0,h,0)
    def body(i,carry):
        for u in range(2):
            t=2*i+u
            for h in range(hp):
                first(jnp.minimum(t+1,half-1),h,1-u)
                second(h,u)
                third(t-1,h,1-u)
        return carry
    return body

def fwd_kernel(hp, lists_ref, x_ref, o_ref, s_ref, p_ref, g_ref):
    length=x_ref.shape[0]; nb=length//BLK
    c=LOG2E*HD**-0.5
    half=(nb-2)//2
    def stage_s(i,h,slot):
        lanes,qs,_=places(hp,h)
        kv,(rowa,_,_),(rowb,_,_)=pair_of(x_ref,lists_ref,lanes,h,i)
        w=diag(low(x_ref[pl.ds(rowa,BLK),qs]),low(x_ref[pl.ds(rowb,BLK),qs]))
        s_ref[slot,h]=dot(kv,w,NT)
    def stage_p(h,slot):
        s=s_ref[slot,h]
        m=jnp.max(s,0,keepdims=True)
        e=jnp.exp2(s*c-m*c)
        inv=1.0/jnp.sum(e,0,keepdims=True)
        p_ref[slot,h]=(e*inv).astype(BF)
    def stage_c(i,h,slot):
        lanes,_,ds_=places(hp,h)
        kv,(rowa,_,_),(rowb,_,_)=pair_of(x_ref,lists_ref,lanes,h,jnp.maximum(i,0))
        ctx=dot(p_ref[slot,h],kv,TN)
        o_ref[pl.ds(rowa,BLK),ds_]=ctx[:BLK,HD:2*HD].astype(BF)
        o_ref[pl.ds(rowb,BLK),ds_]=ctx[BLK:,3*HD:].astype(BF)
    p_ref[...]=jnp.zeros_like(p_ref)
    body=run_pairs(half,hp,stage_s,stage_p,stage_c)
    lax.fori_loop(0,(half+1)//2,body,0)
    for h in range(hp): stage_c(half-1,h,(half-1)%2)
    heads=range(hp)
    ws=[]
    for h in heads:
        _,qs,_=places(hp,h)
        ws.append(low(jnp.concatenate([x_ref[0:BLK,qs],x_ref[length-BLK:length,qs]],0)))
    def chunk(i): return pl.ds(pl.multiple_of(i*CH,CH),CH)
    def one(i,ms):
        out=[]
        for h in heads:
            s=dot(x_ref[chunk(i),places(hp,h)[0]],ws[h],NT)
            g_ref[h,chunk(i),:]=s
            out.append(jnp.maximum(ms[h],jnp.max(s,0,keepdims=True)))
        return tuple(out)
    ms=lax.fori_loop(0,length//CH,one,tuple(jnp.full((1,2*BLK),-jnp.inf,F32) for h in heads),unroll=2)
    def two(i,ls):
        out=[]
        for h in heads:
            e=jnp.exp2(g_ref[h,chunk(i),:]*c-ms[h]*c)
            g_ref[h,chunk(i),:]=e
            out.append(ls[h]+jnp.sum(e,0,keepdims=True))
        return tuple(out)
    ls=lax.fori_loop(0,length//CH,two,tuple(jnp.zeros((1,2*BLK),F32) for h in heads))
    invs=[1.0/l for l in ls]
    acc_ref=s_ref
    for h in heads: s_ref[0,h]=jnp.zeros((KEYS,2*BLK),F32)
    def three(i,carry):
        for h in heads:
            p=g_ref[h,chunk(i),:]*invs[h]
            hi=p.astype(BF); lo=(p-hi.astype(F32)).astype(BF)
            s_ref[0,h,0:4*BLK,:]+=dot(jnp.concatenate([hi,lo],1),x_ref[chunk(i),places(hp,h)[0]],TN)
        return carry
    lax.fori_loop(0,length//CH,three,0,unroll=2)
    for h in heads:
        ds_=places(hp,h)[2]
        ctx=(s_ref[0,h,0:2*BLK,:]+s_ref[0,h,2*BLK:4*BLK,:])[:,HD:].astype(BF)
        o_ref[0:BLK,ds_]=ctx[:BLK]
        o_ref[length-BLK:length,ds_]=ctx[BLK:]

def attn_fwd(lists,x):
    length=x.shape[0]; hp=x.shape[1]//(3*HD)
    return pl.pallas_call(lambda *a: fwd_kernel(hp,*a),
        out_shape=jax.ShapeDtypeStruct((length,hp*HD),BF),
        in_specs=[pl.BlockSpec(memory_space=pltpu.SMEM),pl.BlockSpec(memory_space=pltpu.VMEM)],
        out_specs=pl.BlockSpec(memory_space=pltpu.VMEM),
        scratch_shapes=[pltpu.VMEM((2,hp,KEYS,2*BLK),F32),pltpu.VMEM((2,hp,KEYS,2*BLK),BF),pltpu.VMEM((hp,length,2*BLK),F32)],
        compiler_params=pltpu.CompilerParams(vmem_limit_bytes=48<<20),
        name="attn_fwd")(lists.reshape(-1),x)

def bwd_kernel(hp, lists_ref, x_ref, d_ref, o_ref, win_ref, rnd_ref, s_ref, p_ref, g_ref):
    length=x_ref.shape[0]; nb=length//BLK
    scale=HD**-0.5; c=LOG2E*scale
    half=(nb-2)//2
    win_ref[...]=jnp.zeros_like(win_ref)
    rnd_ref[...]=jnp.zeros_like(rnd_ref)
    def weights(rowa,rowb,qs,ds_):
        return jnp.concatenate([diag(low(x_ref[pl.ds(rowa,BLK),qs]),low(x_ref[pl.ds(rowb,BLK),qs])),
                                diag(high(d_ref[pl.ds(rowa,BLK),ds_]),high(d_ref[pl.ds(rowb,BLK),ds_]))],0)
    def stage_s(i,h,slot):
        lanes,qs,ds_=places(hp,h)
        kv,(rowa,_,_),(rowb,_,_)=pair_of(x_ref,lists_ref,lanes,h,i)
        s_ref[slot,h]=dot(kv,weights(rowa,rowb,qs,ds_),NT)
    def stage_p(h,slot):
        s=s_ref[slot,h,:,:2*BLK]; g=s_ref[slot,h,:,2*BLK:]
        m=jnp.max(s,0,keepdims=True)
        e=jnp.exp2(s*c-m*c)
        inv=1.0/jnp.sum(e,0,keepdims=True)
        delta=jnp.sum(e*g,0,keepdims=True)*inv
        p=e*inv
        p_ref[slot,h,:,:2*BLK]=(p*(g-delta)).astype(BF)
        p_ref[slot,h,:,2*BLK:]=p.astype(BF)
    def stage_c(i,h,slot):
        lanes,qs,ds_=places(hp,h)
        kv,(rowa,preva,ra),(rowb,prevb,rb)=pair_of(x_ref,lists_ref,lanes,h,jnp.maximum(i,0))
        dq=dot(p_ref[slot,h,:,:2*BLK],kv,TN)*scale
        o_ref[pl.ds(rowa,BLK),qs]=dq[:BLK,:HD].astype(BF)
        o_ref[pl.ds(rowb,BLK),qs]=dq[BLK:,2*HD:3*HD].astype(BF)
        dkv=dot(p_ref[slot,h],weights(rowa,rowb,qs,ds_),NN)
        for prev,rows,col in ((preva,ra,0),(prevb,rb,2*HD)):
            part=dkv[:,col:col+2*HD]
            win_ref[h,pl.ds(prev,3*BLK),:]+=part[:3*BLK]
            win_ref[h,length:length+2*BLK,:]+=part[3*BLK:5*BLK]
            for r in range(RAND):
                rnd_ref[h,pl.ds(rows[r],BLK),:]+=part[(5+r)*BLK:(6+r)*BLK]
    p_ref[...]=jnp.zeros_like(p_ref)
    body=run_pairs(half,hp,stage_s,stage_p,stage_c)
    lax.fori_loop(0,half//2,body,0)
    if half%2:
        for h in range(hp):
            stage_p(h,0); stage_c(half-2,h,1)
        for h in range(hp): stage_c(half-1,h,0)
    else:
        for h in range(hp): stage_c(half-1,h,1)
    lane_scale=jnp.where(lax.broadcasted_iota(jnp.int32,(1,2*HD),1)<HD,scale,1.0).astype(F32)
    heads=range(hp)
    ws=[];threes=[]
    for h in heads:
        _,qs,ds_=places(hp,h)
        q=low(jnp.concatenate([x_ref[0:BLK,qs],x_ref[length-BLK:length,qs]],0))
        d=high(jnp.concatenate([d_ref[0:BLK,ds_],d_ref[length-BLK:length,ds_]],0))
        ws.append(jnp.concatenate([q,d],0)); threes.append(jnp.concatenate([q,d,d],0))
    def chunk(i): return pl.ds(pl.multiple_of(i*CH,CH),CH)
    for h in heads:
        win_ref[h,0:BLK,:]+=win_ref[h,length:length+BLK,:]
        win_ref[h,length-BLK:length,:]+=win_ref[h,length+BLK:length+2*BLK,:]
    for h in heads:
        lanes,qs,ds_=places(hp,h)
        def one(i,m):
            s=dot(x_ref[chunk(i),lanes],ws[h],NT)
            g_ref[chunk(i),:]=s
            return jnp.maximum(m,jnp.max(s[:,:2*BLK],0,keepdims=True))
        m=lax.fori_loop(0,length//CH,one,jnp.full((1,2*BLK),-jnp.inf,F32),unroll=4)
        def two(i,st):
            l,eg=st
            e=jnp.exp2(g_ref[chunk(i),:2*BLK]*c-m*c)
            g_ref[chunk(i),:2*BLK]=e
            return l+jnp.sum(e,0,keepdims=True), eg+jnp.sum(e*g_ref[chunk(i),2*BLK:],0,keepdims=True)
        l,eg=lax.fori_loop(0,length//CH,two,(jnp.zeros((1,2*BLK),F32),)*2,unroll=2)
        inv=1.0/l; delta=eg*inv
        def three(i,dq):
            p=g_ref[chunk(i),:2*BLK]*inv
            ds=(p*(g_ref[chunk(i),2*BLK:]-delta)).astype(BF)
            hi=p.astype(BF); lo=(p-hi.astype(F32)).astype(BF)
            dkv=dot(jnp.concatenate([ds,hi,lo],1),threes[h],NN)
            tot=win_ref[h,chunk(i),:]+rnd_ref[h,chunk(i),:]+dkv
            o_ref[chunk(i),lanes]=(tot*lane_scale).astype(BF)
            return dq+dot(ds,x_ref[chunk(i),lanes],TN)
        dq=lax.fori_loop(0,length//CH,three,jnp.zeros((2*BLK,2*HD),F32),unroll=4)
        dq=(dq[:,:HD]*scale).astype(BF)
        o_ref[0:BLK,qs]=dq[:BLK]
        o_ref[length-BLK:length,qs]=dq[BLK:]

def attn_bwd(lists,x,d):
    length=x.shape[0]; hp=x.shape[1]//(3*HD)
    return pl.pallas_call(lambda *a: bwd_kernel(hp,*a),
        out_shape=jax.ShapeDtypeStruct(x.shape,BF),
        in_specs=[pl.BlockSpec(memory_space=pltpu.SMEM),pl.BlockSpec(memory_space=pltpu.VMEM),pl.BlockSpec(memory_space=pltpu.VMEM)],
        out_specs=pl.BlockSpec(memory_space=pltpu.VMEM),
        scratch_shapes=[pltpu.VMEM((hp,length+2*BLK,2*HD),F32),pltpu.VMEM((hp,length,2*HD),F32),pltpu.VMEM((2,hp,KEYS,4*BLK),F32),pltpu.VMEM((2,hp,KEYS,4*BLK),BF),pltpu.VMEM((length,4*BLK),F32)],
        compiler_params=pltpu.CompilerParams(vmem_limit_bytes=56<<20),
        name="attn_bwd")(lists.reshape(-1),x,d)


def layer_norm(resid, gain, shift):
    centre = resid - jnp.mean(resid, -1, keepdims=True)
    spread = jnp.mean(centre * centre, -1, keepdims=True)
    return centre * lax.rsqrt(spread + epsilon) * gain + shift


def to_groups(w, groups, hp):
    lead = w.shape[:-1]
    w = w.reshape(lead + (3, H, HD))
    w = jnp.pad(w, [(0, 0)] * (len(lead) + 1) + [(0, groups * hp - H), (0, 0)])
    w = w.reshape(lead + (3, groups, hp, HD))
    q, k, v = (w[..., n, :, :, :] for n in range(3))
    kv = jnp.stack([k, v], -2).reshape(lead + (groups, hp * 2 * HD))
    return jnp.concatenate([kv, q.reshape(lead + (groups, hp * HD))], -1).reshape(
        lead + (groups * hp * 3 * HD,)
    )


def from_groups(w, groups, hp):
    lead = w.shape[:-1]
    w = w.reshape(lead + (groups, hp * 3 * HD))
    kv = w[..., : hp * 2 * HD].reshape(lead + (groups, hp, 2, HD))
    q = w[..., hp * 2 * HD :].reshape(lead + (groups * hp, HD))
    k = kv[..., 0, :].reshape(lead + (groups * hp, HD))
    v = kv[..., 1, :].reshape(lead + (groups * hp, HD))
    return jnp.concatenate(
        [p[..., :H, :].reshape(lead + (H * HD,)) for p in (q, k, v)], -1
    )


def exchange(x):
    return lax.all_to_all(x, "seq", split_axis=0, concat_axis=0, tiled=True)


def mm(spec, a, b):
    return jnp.einsum(spec, a, b, preferred_element_type=jnp.float32)


def local(
    hidden,
    block_lists,
    w_qkv,
    bias_query,
    bias_value,
    w_attn_out,
    bias_attn_out,
    norm1_gain,
    norm1_shift,
    w_ffn_in,
    bias_ffn_in,
    w_ffn_out,
    bias_ffn_out,
    norm2_gain,
    norm2_shift,
    cotangent,
):
    groups = lax.axis_size("seq")
    hp = -(-H // groups)
    wide = groups * hp * HD
    tokens = hidden.shape[1]
    blocks_here = tokens // BLK
    ids = jnp.pad(block_lists[0], ((0, 0), (0, 0), (0, groups * hp - H), (0, 0)))
    ids = ids.reshape(LAYERS, blocks_here, groups, hp * RAND).transpose(2, 0, 1, 3)
    ids = exchange(ids.reshape(groups, -1)).reshape(groups, LAYERS, blocks_here, hp, RAND)
    ids = ids.transpose(1, 3, 0, 2, 4).reshape(LAYERS, -1)

    small = (bias_query, bias_value, bias_attn_out, norm1_gain, norm1_shift, bias_ffn_in, bias_ffn_out, norm2_gain, norm2_shift)
    sizes = [s.shape[1] for s in small]
    packed = lax.all_gather(jnp.concatenate(small, 1), "item", axis=0)
    rows = packed.shape[0]
    vectors = []
    for layer in range(LAYERS):
        at, out = 0, []
        for size in sizes:
            out.append(packed[:, layer, at : at + size].reshape(rows * size).astype(jnp.float32))
            at += size
        vectors.append(out)
    shards = (to_groups(w_qkv, groups, hp), w_attn_out, w_ffn_in, w_ffn_out)
    weights = [
        tuple(lax.all_gather(s[layer], "item", axis=0, tiled=True) for s in shards)
        for layer in range(LAYERS)
    ]
    current = hidden[0]
    saved = []
    for layer in range(LAYERS):
        qkv_weight, out_weight, inner_weight, outer_weight = weights[layer]
        query_bias, value_bias, out_bias, gain_one, shift_one, inner_bias, outer_bias, gain_two, shift_two = vectors[layer]
        bias = to_groups(jnp.concatenate([query_bias, jnp.zeros_like(query_bias), value_bias]), groups, hp)
        input_low = current.astype(BF)
        qkv_split = qkv_weight.reshape(D, groups, hp * 3 * HD)
        out_split = jnp.pad(out_weight, ((0, wide - D), (0, 0))).reshape(groups, hp * HD, D)
        proj = mm("td,dne->nte", input_low, qkv_split) + bias.reshape(groups, 1, hp * 3 * HD)
        x = exchange(proj.astype(BF)).reshape(groups * tokens, hp * 3 * HD)
        ctx = attn_fwd(ids[layer], x)
        context = exchange(ctx.reshape(groups, tokens, hp * HD))
        attn_out = mm("nte,ned->td", context, out_split)
        resid_one = current + attn_out + out_bias
        normed = layer_norm(resid_one, gain_one, shift_one)
        normed_low = normed.astype(BF)
        pre_act = mm("td,df->tf", normed_low, inner_weight) + inner_bias
        activated = jax.nn.gelu(pre_act, approximate=True).astype(BF)
        resid_two = normed + mm("tf,fd->td", activated, outer_weight) + outer_bias
        current = layer_norm(resid_two, gain_two, shift_two)
        saved.append((input_low, qkv_split, out_split, x, context, resid_one, normed_low, pre_act, activated, resid_two))
    grad_state = cotangent[0]
    collected = [None] * LAYERS
    for layer in reversed(range(LAYERS)):
        qkv_weight, out_weight, inner_weight, outer_weight = weights[layer]
        query_bias, value_bias, out_bias, gain_one, shift_one, inner_bias, outer_bias, gain_two, shift_two = vectors[layer]
        input_low, qkv_split, out_split, x, context, resid_one, normed_low, pre_act, activated, resid_two = saved[layer]
        unused, pull_two = jax.vjp(layer_norm, resid_two, gain_two, shift_two)
        grad_resid_two, grad_gain_two, grad_shift_two = pull_two(grad_state)
        grad_ffn = grad_resid_two.astype(BF)
        grad_act = mm("td,fd->tf", grad_ffn, outer_weight)
        unused, pull_gelu = jax.vjp(partial(jax.nn.gelu, approximate=True), pre_act)
        grad_pre = pull_gelu(grad_act)[0].astype(BF)
        grad_normed = grad_resid_two + mm("tf,df->td", grad_pre, inner_weight)
        unused, pull_one = jax.vjp(layer_norm, resid_one, gain_one, shift_one)
        grad_resid_one, grad_gain_one, grad_shift_one = pull_one(grad_normed)
        grad_attn = grad_resid_one.astype(BF)
        grad_context = mm("td,ned->nte", grad_attn, out_split).astype(BF)
        dctx = exchange(grad_context).reshape(groups * tokens, hp * HD)
        dx = attn_bwd(ids[layer], x, dctx)
        dproj = exchange(dx.reshape(groups, tokens, hp * 3 * HD))
        grad_outer_weight = mm("tf,td->fd", activated, grad_ffn)
        grad_inner_weight = mm("td,tf->df", normed_low, grad_pre)
        grad_out_weight = mm("nte,td->ned", context, grad_attn).reshape(wide, D)[:D]
        grad_qkv_weight = mm("td,nte->dne", input_low, dproj).reshape(D, -1)
        grad_state = grad_resid_one + mm("nte,dne->td", dproj, qkv_split)
        total = lambda g: jnp.sum(g.astype(jnp.float32), tuple(range(g.ndim - 1)))
        dbias = from_groups(jnp.sum(dproj.astype(jnp.float32), 1).reshape(-1), groups, hp)
        flat = (dbias[:D], dbias[2 * D :], total(grad_attn), grad_gain_one, grad_shift_one, total(grad_pre), total(grad_ffn), grad_gain_two, grad_shift_two)
        big = tuple(
            lax.psum(lax.psum_scatter(g.astype(BF), "item", scatter_dimension=0, tiled=True), "seq").astype(jnp.float32)
            for g in (grad_qkv_weight, grad_out_weight, grad_inner_weight, grad_outer_weight)
        )
        collected[layer] = (from_groups(big[0], groups, hp),) + big[1:], flat
    parts = [
        jnp.concatenate([g.reshape(rows, -1) for g in collected[layer][1]], 1) for layer in range(LAYERS)
    ]
    part = jnp.stack(parts, 1)
    part = part.reshape(rows, -1).astype(BF)
    mine = lax.psum(lax.psum_scatter(part, "item", scatter_dimension=0, tiled=True), "seq")
    mine = mine.astype(jnp.float32).reshape(LAYERS, -1)
    at, vecs = 0, []
    for size in sizes:
        vecs.append(mine[:, at : at + size])
        at += size
    gq, go, gi, gf = (jnp.stack([collected[layer][0][n] for layer in range(LAYERS)]) for n in range(4))
    return (
        current[None],
        grad_state[None],
        gq,
        vecs[0],
        vecs[1],
        go,
        vecs[2],
        vecs[3],
        vecs[4],
        gi,
        vecs[5],
        gf,
        vecs[6],
        vecs[7],
        vecs[8],
    )


def solution(mesh):
    placed = (
        P("item", "seq", None),
        P("item", None, "seq", None, None),
        P(None, "item", None),
        P(None, "item"),
        P(None, "item"),
        P(None, "item", None),
        P(None, "item"),
        P(None, "item"),
        P(None, "item"),
        P(None, "item", None),
        P(None, "item"),
        P(None, "item", None),
        P(None, "item"),
        P(None, "item"),
        P(None, "item"),
        P("item", "seq", None),
    )
    return jax.shard_map(
        local,
        mesh=mesh,
        in_specs=placed,
        out_specs=(
            P("item", "seq", None),
            P("item", "seq", None),
            P(None, "item", None),
            P(None, "item"),
            P(None, "item"),
            P(None, "item", None),
            P(None, "item"),
            P(None, "item"),
            P(None, "item"),
            P(None, "item", None),
            P(None, "item"),
            P(None, "item", None),
            P(None, "item"),
            P(None, "item"),
            P(None, "item"),
        ),
        check_vma=False,
    )
```

time: 2950 us -> 1220 us (0.41)
  local copies, waits for them, and re-layouts: 1210 us -> 110 us
  other arithmetic: 394 us -> 25.1 us
  matrix products: 523 us -> 207 us
  Pallas kernels: 0 us -> 144 us
  blocking collectives: 242 us -> 200 us
  waiting for transfers between devices: 511 us -> 481 us
    concatenate x21 -> x3, local copies, waits for them, and re-layouts: 345 us -> 0.3 us  [the longest x2 0.2 us: local(): jnp.concatenate([g.reshape(rows, -1) for g in collected[layer][1]], 1)]
    dot_general x50 -> x24, matrix products: 523 us -> 207 us  [mm(): return jnp.einsum(spec, a, b, preferred_element_type=jnp.float32)]
    scatter x10 -> x0, local copies, waits for them, and re-layouts: 256 us -> none  [the longest x2 183 us: local(): send_rows = send_rows.at[item_index, head_index, positions].set(rand_rows)]
    all_to_all x0 -> x4, blocking collectives: none -> 150 us  [exchange(): return lax.all_to_all(x, 'seq', split_axis=0, concat_axis=0, tiled=True)]
    pallas_call x0 -> x4, Pallas kernels: none -> 144 us  [the longest x2 91.7 us: attn_bwd(): pl.pallas_call(lambda *a: bwd_kernel(hp, *a), out_shape=jax.ShapeDtypeStr...]
    psum x7 -> x1, waiting for transfers between devices: 179 us -> 38.5 us  [local(): lax.psum(lax.psum_scatter(g.astype(BF), 'item', scatter_dimension=0, tile...]
    another operation x38 -> x7, local copies, waits for them, and re-layouts: 133 us -> 0.44 us  [the longest x4 0.34 us: local(): g.reshape(rows, -1)]
    all_to_all x4 -> x5, waiting for transfers between devices: 0.01 us -> 132 us  [exchange(): return lax.all_to_all(x, 'seq', split_axis=0, concat_axis=0, tiled=True)]
  transfers between devices with their start and end apart: 35 -> 22, of which waited for: 13 -> 13; matrix products, arithmetic and copies ran while one was open for 42% -> 20% of each run, Pallas kernels for 0% -> 8%
where the time goes in v1:
time: 1220 us; the launch traced here: 1210 us
  waiting for transfers between devices  481 us (39%)
  matrix products  207 us (17%)
  blocking collectives  200 us (16%)
  Pallas kernels  144 us (12%)
  local copies, waits for them, and re-layouts  110 us (9%)
  starting transfers between devices  25.9 us (2%)
  other arithmetic  25.1 us (2%)
  between operations  15.7 us (1%)
    reduce_scatter x6, waiting for transfers between devices, local(): lax.psum_scatter(g.astype(BF), 'item', scatter_dimension=0, tiled=True)  269 us
    dot_general x24, matrix products, mm(): return jnp.einsum(spec, a, b, preferred_element_type=jnp.float32)  207 us
    all_to_all x4, blocking collectives, exchange(): return lax.all_to_all(x, 'seq', split_axis=0, concat_axis=0, tiled=True)  150 us
    all_to_all x5, waiting for transfers between devices, exchange(): return lax.all_to_all(x, 'seq', split_axis=0, concat_axis=0, tiled=True)  132 us
    pallas_call x2, Pallas kernels, attn_bwd(): pl.pallas_call(lambda *a: bwd_kernel(hp, *a), out_shape=jax.ShapeDtypeStr...  91.7 us
    pallas_call x2, Pallas kernels, attn_fwd(): pl.pallas_call(lambda *a: fwd_kernel(hp, *a), out_shape=jax.ShapeDtypeStr...  52.6 us
    unnamed x190, local copies, waits for them, and re-layouts  42 us
    all_gather x8, waiting for transfers between devices, local(): lax.all_gather(s[layer], 'item', axis=0, tiled=True)  39 us
  transfers between devices with their start and end apart: 22, of which 13 were waited for; matrix products, arithmetic and copies ran while one was open for 20% of the time, Pallas kernels for 8%

profile of v1, /device:TPU:0, one launch (start us, length us, event | category | flops | bytes accessed | tf_op | source)
XLA Modules:
  0.0 1208.6 jit_solution(12022578367299244743)
XLA Ops:
  23.4 14.4 %all-gather.7 = bf16[8,2,1152]{2,1,0:T(2,128)(2,1)S(1)} all-gather(bf16[1,2,1152]{2,1,0:T(2,128)(2,1)S(1)} %bitcast.252), channel_id=2, replica_groups=mesh['seq'=4,'item'=8] {'item'}, dimensions={0}, use_global_device_ids=true | all-gather | bytes 41472 | tf_op jit(solution)/shard_map/all_gather | solution.py:296
  39.4 15.8 %all-gather.17.cloned.1.call-done = bf16[768,2304]{1,0:T(8,128)(2,1)} async-done(((bf16[96,2304]{1,0:T(8,128)(2,1)}), bf16[768,2304]{1,0:T(8,128)(2,1)}) %all-gather.17.cloned.1.call-update) | async-done | bytes 3538960 | tf_op jit(solution)/shard_map/all_gather | solution.py:307
  74.2 53.1 %all-to-all-done.1 = bf16[4,1024,576]{1,2,0:T(8,128)(2,1)} async-done(((bf16[4,1024,576]{1,2,0:T(8,128)(2,1)}), bf16[4,1024,576]{1,2,0:T(8,128)(2,1)}, u32[]{:S(2)}, u32[]{:S(2)}) %all-to-all-start.1) | async-done | bytes 4718624 | tf_op jit(solution)/shard_map/all_to_all | solution.py:259
  135.1 26.1 %attn_fwd.2 = bf16[4096,192]{1,0:T(8,128)(2,1)S(1)} custom-call(s32[576]{0:T(1024)S(1)} %squeeze.40.a_0_, bf16[4096,576]{1,0:T(8,128)(2,1)} %bitcast.207), custom_call_target="tpu_custom_call" | custom-call | tf_op jit(solution)/shard_map/attn_fwd/pallas_call | solution.py:126
  192.2 11.3 fusion.30
  203.5 23.1 %all-gather.25.cloned.1.call-done = bf16[1,3072,768]{2,1,0:T(8,128)(2,1)} async-done(((bf16[1,384,768]{2,1,0:T(8,128)(2,1)}), bf16[1,3072,768]{2,1,0:T(8,128)(2,1)}) %all-gather.25.cloned.1.call-update) | async-done | bytes 4718608 | tf_op jit(solution)/shard_map/all_gather | solution.py:307
  226.6 11.5 fusion.114
  251.1 53.5 %all-to-all-done.3 = bf16[4,1024,576]{1,2,0:T(8,128)(2,1)} async-done(((bf16[4,1024,576]{1,2,0:T(8,128)(2,1)}), bf16[4,1024,576]{1,2,0:T(8,128)(2,1)}, u32[]{:S(2)}, u32[]{:S(2)}) %all-to-all-start.3) | async-done | bytes 4718624 | tf_op jit(solution)/shard_map/all_to_all | solution.py:259
  312.3 26.5 %attn_fwd.3 = bf16[4096,192]{1,0:T(8,128)(2,1)S(1)} custom-call(s32[576]{0:T(1024)S(1)} %squeeze.45.a_0_, bf16[4096,576]{1,0:T(8,128)(2,1)} %bitcast.209), custom_call_target="tpu_custom_call" | custom-call | tf_op jit(solution)/shard_map/attn_fwd/pallas_call | solution.py:126
  348.5 16.4 %all-to-all-done.4 = bf16[4,1024,192]{1,2,0:T(8,128)(2,1)} async-done(((bf16[4,1024,192]{1,2,0:T(8,128)(2,1)}), bf16[4,1024,192]{1,2,0:T(8,128)(2,1)}, u32[]{:S(2)}, u32[]{:S(2)}) %all-to-all-start.4) | async-done | bytes 1572896 | tf_op jit(solution)/shard_map/all_to_all | solution.py:259
  370.0 11.2 fusion.22
  381.3 11.8 fusion.116
  400.3 17.9 %fusion.98 = (bf16[3072]{0:T(1024)(128)(2,1)}, bf16[1024,3072]{1,0:T(8,128)(2,1)}) fusion(f32[1024,3072]{1,0:T(8,128)} %fusion.22, f32[3072]{0:T(1024)S(1)} %bitcast.257, bf16[1024,768]{0,1:T(8,128)(2,1)S(1)} %get-tuple-element.117, bf16[1,3072,768]{2,1,0:T(8,128)(2,1)S(1)} %bitcast.260), kind=kOutput, calls=%fused_computation.176 | convolution fusion | flops 4901041152 | bytes 25184256 | tf_op jit(solution)/shard_map/td,fd->tf/dot_general | solution.py:263
  431.8 21.6 %all_to_all.50 = bf16[4,1024,192]{1,2,0:T(8,128)(2,1)S(1)} all-to-all(bf16[4,1024,192]{1,2,0:T(8,128)(2,1)S(1)} %fusion.64), channel_id=1, replica_groups=mesh['seq'=4,'item'=8] {'seq'}, dimensions={0} | all-to-all | bytes 3145728 | tf_op jit(solution)/shard_map/all_to_all | solution.py:259
  455.9 45.8 %attn_bwd.2 = bf16[4096,576]{1,0:T(8,128)(2,1)} custom-call(s32[576]{0:T(1024)} %copy-done.1, bf16[4096,576]{1,0:T(8,128)(2,1)} %bitcast.210, bf16[4096,192]{1,0:T(8,128)(2,1)} %bitcast.213), custom_call_target="tpu_custom_call" | custom-call | tf_op jit(solution)/shard_map/attn_bwd/pallas_call | solution.py:219
  509.6 56.0 %all_to_all.51 = bf16[4,1024,576]{1,2,0:T(8,128)(2,1)S(1)} all-to-all(bf16[4,1024,576]{1,2,0:T(8,128)(2,1)} %copy.149), channel_id=1, replica_groups=mesh['seq'=4,'item'=8] {'seq'}, dimensions={0} | all-to-all | bytes 9437184 | tf_op jit(solution)/shard_map/all_to_all | solution.py:259
  584.5 16.9 %fusion.94 = (bf16[3072]{0:T(1024)(128)(2,1)S(1)}, bf16[1024,3072]{1,0:T(8,128)(2,1)S(1)}) fusion(f32[1024,3072]{1,0:T(8,128)} %fusion.30, f32[3072]{0:T(1024)S(1)} %bitcast.254, bf16[1024,768]{0,1:T(8,128)(2,1)S(1)} %get-tuple-element.111, bf16[1,3072,768]{2,1,0:T(8,128)(2,1)} %all-gather.25.cloned.1.call-done), kind=kOutput, calls=%fused_computation.173 | convolution fusion | flops 4901041152 | bytes 25184256 | tf_op jit(solution)/shard_map/td,fd->tf/dot_general | solution.py:263
  615.8 19.4 %all_to_all.52 = bf16[4,1024,192]{1,2,0:T(8,128)(2,1)} all-to-all(bf16[4,1024,192]{1,2,0:T(8,128)(2,1)S(1)} %fusion.67), channel_id=1, replica_groups=mesh['seq'=4,'item'=8] {'seq'}, dimensions={0} | all-to-all | bytes 3145728 | tf_op jit(solution)/shard_map/all_to_all | solution.py:259
  638.9 45.8 %attn_bwd.3 = bf16[4096,576]{1,0:T(8,128)(2,1)} custom-call(s32[576]{0:T(1024)} %copy-done, bf16[4096,576]{1,0:T(8,128)(2,1)} %bitcast.208, bf16[4096,192]{1,0:T(8,128)(2,1)} %bitcast.214), custom_call_target="tpu_custom_call" | custom-call | tf_op jit(solution)/shard_map/attn_bwd/pallas_call | solution.py:219
  692.5 52.5 %all_to_all.53 = bf16[4,1024,576]{1,2,0:T(8,128)(2,1)S(1)} all-to-all(bf16[4,1024,576]{1,2,0:T(8,128)(2,1)} %copy.154), channel_id=1, replica_groups=mesh['seq'=4,'item'=8] {'seq'}, dimensions={0} | all-to-all | bytes 9437184 | tf_op jit(solution)/shard_map/all_to_all | solution.py:259
  765.2 9.8 convolution_convert_fusion.2
  775.8 13.5 %convolution_convert_fusion = bf16[3072,768]{1,0:T(8,128)(2,1)} fusion(bf16[1024,768]{0,1:T(8,128)(2,1)} %copy-done.24, f32[1024,3072]{1,0:T(8,128)} %fusion.22, f32[3072]{0:T(1024)S(1)} %bitcast.258), kind=kOutput, calls=%fused_computation.22 | convolution fusion | flops 4865654784 | bytes 18886656 | tf_op jit(solution)/shard_map/tf,td->fd/dot_general | solution.py:263
  801.2 13.0 %convolution_convert_fusion.1 = bf16[3072,768]{1,0:T(8,128)(2,1)} fusion(bf16[1024,768]{0,1:T(8,128)(2,1)S(1)} %copy-done.26, f32[1024,3072]{1,0:T(8,128)} %fusion.30, f32[3072]{0:T(1024)S(1)} %bitcast.255), kind=kOutput, calls=%fused_computation.23 | convolution fusion | flops 4865654784 | bytes 18886656 | tf_op jit(solution)/shard_map/tf,td->fd/dot_general | solution.py:263
  818.6 13.2 %reduce-scatter.15.cloned.1.call-done = bf16[96,768]{1,0:T(8,128)(2,1)} async-done(((bf16[768,768]{1,0:T(8,128)(2,1)}), bf16[96,768]{1,0:T(8,128)(2,1)}) %reduce-scatter.15.cloned.1.call-update) | async-done | bytes 147472 | tf_op jit(solution)/shard_map/reduce_scatter | solution.py:361
  831.7 33.8 %reduce-scatter.13.cloned.1.call-done = bf16[96,768]{1,0:T(8,128)(2,1)} async-done(((bf16[768,768]{1,0:T(8,128)(2,1)}), bf16[96,768]{1,0:T(8,128)(2,1)}) %reduce-scatter.13.cloned.1.call-update) | async-done | bytes 147472 | tf_op jit(solution)/shard_map/reduce_scatter | solution.py:361
  865.5 55.5 %reduce-scatter.19.cloned.1.call-done = bf16[96,3072]{1,0:T(8,128)(2,1)} async-done(((bf16[768,3072]{1,0:T(8,128)(2,1)}), bf16[96,3072]{1,0:T(8,128)(2,1)}) %reduce-scatter.19.cloned.1.call-update) | async-done | bytes 589840 | tf_op jit(solution)/shard_map/reduce_scatter | solution.py:361
  921.0 55.5 %reduce-scatter.23.cloned.1.call-done = bf16[384,768]{1,0:T(8,128)(2,1)} async-done(((bf16[3072,768]{1,0:T(8,128)(2,1)}), bf16[384,768]{1,0:T(8,128)(2,1)}) %reduce-scatter.23.cloned.1.call-update) | async-done | bytes 589840 | tf_op jit(solution)/shard_map/reduce_scatter | solution.py:361
  976.5 55.5 %reduce-scatter.17.cloned.1.call-done = bf16[96,3072]{1,0:T(8,128)(2,1)} async-done(((bf16[768,3072]{1,0:T(8,128)(2,1)}), bf16[96,3072]{1,0:T(8,128)(2,1)}) %reduce-scatter.17.cloned.1.call-update) | async-done | bytes 589840 | tf_op jit(solution)/shard_map/reduce_scatter | solution.py:361
  1032.0 55.5 %reduce-scatter.21.cloned.1.call-done = bf16[384,768]{1,0:T(8,128)(2,1)} async-done(((bf16[3072,768]{1,0:T(8,128)(2,1)}), bf16[384,768]{1,0:T(8,128)(2,1)}) %reduce-scatter.21.cloned.1.call-update) | async-done | bytes 589840 | tf_op jit(solution)/shard_map/reduce_scatter | solution.py:361
  1114.0 26.3 %all-reduce.2 = bf16[8,2304]{1,0:T(8,128)(2,1)S(1)} all-reduce(bf16[8,2304]{1,0:T(8,128)(2,1)S(1)} %bitcast.246), channel_id=11, replica_groups=mesh['seq'=4,'item'=8] {'item'}, use_global_device_ids=true, to_apply=%region_36.37.clone | all-reduce | flops 18432 | bytes 73728
  1141.0 10.2 psum.65
  1152.5 38.5 %all-reduce.6.cloned.1.call-done = (bf16[96,4,576]{0,2,1:T(8,128)(2,1)}, bf16[96,4,576]{0,2,1:T(8,128)(2,1)}, bf16[1,96,768]{2,1,0:T(8,128)(2,1)}, bf16[1,96,768...) async-done(((bf16[96,4,576]{0,2,1:T(8,128)(2,1)}, ...) | async-done | bytes 3538960 | tf_op jit(solution)/shard_map/psum | solution.py:361
  (385 shorter events, 261.9 us)
Async XLA Ops:
  7.2 48.0 %all-gather.17.cloned.1.call-start = ((), (), s32[]{:S(2)}) async-start(), calls=%async_computation.17 | async-start | bytes 3981312 | tf_op jit(solution)/shard_map/all_gather | solution.py:307
  10.5 161.8 %all-gather.19.cloned.1.call-start = ((), (), s32[]{:S(2)}) async-start(), calls=%async_computation.18 | async-start | bytes 3981312 | tf_op jit(solution)/shard_map/all_gather | solution.py:307
  11.6 166.5 %all-gather.21.cloned.1.call-start = ((), (), s32[]{:S(2)}) async-start(), calls=%async_computation.25 | async-start | bytes 1327104 | tf_op jit(solution)/shard_map/all_gather | solution.py:307
  13.5 178.6 %all-gather.23.cloned.1.call-start = ((), (), s32[]{:S(2)}) async-start(), calls=%async_computation.26 | async-start | bytes 5308416 | tf_op jit(solution)/shard_map/all_gather | solution.py:307
  14.7 211.9 %all-gather.25.cloned.1.call-start = ((), (), s32[]{:S(2)}) async-start(), calls=%async_computation.27 | async-start | bytes 5308416 | tf_op jit(solution)/shard_map/all_gather | solution.py:307
  15.9 332.7 %all-gather.27.cloned.1.call-start = ((), (), s32[]{:S(2)}) async-start(), calls=%async_computation.28 | async-start | bytes 1327104 | tf_op jit(solution)/shard_map/all_gather | solution.py:307
  16.5 353.5 %all-gather.29.cloned.1.call-start = ((), (), s32[]{:S(2)}) async-start(), calls=%async_computation.29 | async-start | bytes 5308416 | tf_op jit(solution)/shard_map/all_gather | solution.py:307
  18.0 50.5 %all-to-all-start = ((s32[4,1,288]{2,1,0:T(1,128)}), s32[4,1,288]{2,1,0:T(1,128)S(1)}, u32[]{:S(2)}, u32[]{:S(2)}) async-start(s32[4,1,288]{2,1,0:T(1,128)} %all_to_all.40), calls=%async_computation | async-start | bytes 12288 | tf_op jit(solution)/shard_map/all_to_all | solution.py:259
  68.6 58.7 %all-to-all-start.1 = ((bf16[4,1024,576]{1,2,0:T(8,128)(2,1)}), bf16[4,1024,576]{1,2,0:T(8,128)(2,1)}, u32[]{:S(2)}, u32[]{:S(2)}) async-start(bf16[4,1024,576]{1,2,0:T(8,128)(2,1)} %fusion.14), calls=%async_computation.1 | async-start | bytes 9437184 | tf_op jit(solution)/shard_map/all_to_all | solution.py:259
  74.1 60.9 %copy-start = (s32[576]{0:T(1024)}, s32[576]{0:T(1024)S(1)}, u32[]{:S(2)}) copy-start(s32[576]{0:T(1024)S(1)} %squeeze.40.a_0_) | copy-start | bytes 6916
  163.5 23.9 %all-to-all-start.2 = ((bf16[4,1024,192]{1,2,0:T(8,128)(2,1)}), bf16[4,1024,192]{1,2,0:T(8,128)(2,1)}, u32[]{:S(2)}, u32[]{:S(2)}) async-start(bf16[4,1024,192]{1,2,0:T(8,128)(2,1)} %copy.136), calls=%async_computation.2 | async-start | bytes 3145728 | tf_op jit(solution)/shard_map/all_to_all | solution.py:259
  168.1 213.2 %all-gather.31.cloned.1.call-start = ((), (), s32[]{:S(2)}) async-start(), calls=%async_computation.30 | async-start | bytes 5308416 | tf_op jit(solution)/shard_map/all_gather | solution.py:307
  172.1 192.8 %copy-start.66 = (f32[768]{0:T(1024)}, f32[768]{0:T(1024)S(1)}, u32[]{:S(2)}) copy-start(f32[768]{0:T(1024)S(1)} %reshape.545) | copy-start | bytes 9220
  172.2 192.7 %copy-start.52 = (f32[768]{0:T(1024)}, f32[768]{0:T(1024)S(1)}, u32[]{:S(2)}) copy-start(f32[768]{0:T(1024)S(1)} %reshape.544) | copy-start | bytes 9220
  172.3 228.0 %copy-start.60 = (f32[8,1,384]{2,1,0:T(1,128)}, f32[8,1,384]{2,1,0:T(1,128)S(1)}, u32[]{:S(2)}) copy-start(f32[8,1,384]{2,1,0:T(1,128)S(1)} %get-tuple-element.148) | copy-start | bytes 36868
  238.2 126.7 %copy-start.45 = (f32[1024]{0:T(1024)}, f32[1024]{0:T(1024)S(1)}, u32[]{:S(2)}) copy-start(f32[1024]{0:T(1024)S(1)} %broadcast_multiply_fusion.2) | copy-start | bytes 12292
  238.6 126.3 %copy-start.54 = (f32[1024]{0:T(1024)}, f32[1024]{0:T(1024)S(1)}, u32[]{:S(2)}) copy-start(f32[1024]{0:T(1024)S(1)} %fusion.84) | copy-start | bytes 12292
  245.7 58.8 %all-to-all-start.3 = ((bf16[4,1024,576]{1,2,0:T(8,128)(2,1)}), bf16[4,1024,576]{1,2,0:T(8,128)(2,1)}, u32[]{:S(2)}, u32[]{:S(2)}) async-start(bf16[4,1024,576]{1,2,0:T(8,128)(2,1)} %fusion.15), calls=%async_computation.3 | async-start | bytes 9437184 | tf_op jit(solution)/shard_map/all_to_all | solution.py:259
  251.1 61.3 %copy-start.1 = (s32[576]{0:T(1024)}, s32[576]{0:T(1024)S(1)}, u32[]{:S(2)}) copy-start(s32[576]{0:T(1024)S(1)} %squeeze.45.a_0_) | copy-start | bytes 6916
  341.1 23.8 %all-to-all-start.4 = ((bf16[4,1024,192]{1,2,0:T(8,128)(2,1)}), bf16[4,1024,192]{1,2,0:T(8,128)(2,1)}, u32[]{:S(2)}, u32[]{:S(2)}) async-start(bf16[4,1024,192]{1,2,0:T(8,128)(2,1)} %copy.143), calls=%async_computation.4 | async-start | bytes 3145728 | tf_op jit(solution)/shard_map/all_to_all | solution.py:259
  345.7 468.6 %reduce-scatter.27.cloned.1.call-start = ((), (), s32[]{:S(2)}) async-start(), calls=%async_computation.32 | async-start | bytes 3981312
  369.6 57.8 %copy-start.4 = (f32[1024,768]{0,1:T(8,128)}, f32[1024,768]{0,1:T(8,128)S(1)}, u32[]{:S(2)}) copy-start(f32[1024,768]{0,1:T(8,128)S(1)} %get-tuple-element.163) | copy-start | bytes 9437188
  501.7 63.9 %copy-start.20 = (bf16[768,2304]{0,1:T(8,128)(2,1)S(1)}, bf16[768,2304]{0,1:T(8,128)(2,1)}, u32[]{:S(2)}) copy-start(bf16[768,2304]{0,1:T(8,128)(2,1)} %copy.139) | copy-start | bytes 10616836
  583.8 232.7 %reduce-scatter.25.cloned.1.call-start = ((), (), s32[]{:S(2)}) async-start(), calls=%async_computation.31 | async-start | bytes 3981312
  756.2 75.6 %reduce-scatter.15.cloned.1.call-start = ((), (), s32[]{:S(2)}) async-start(), calls=%async_computation.20 | async-start | bytes 1327104 | tf_op jit(solution)/shard_map/reduce_scatter | solution.py:361
  760.6 104.9 %reduce-scatter.13.cloned.1.call-start = ((), (), s32[]{:S(2)}) async-start(), calls=%async_computation.19 | async-start | bytes 1327104 | tf_op jit(solution)/shard_map/reduce_scatter | solution.py:361
  765.2 155.9 %reduce-scatter.19.cloned.1.call-start = ((), (), s32[]{:S(2)}) async-start(), calls=%async_computation.22 | async-start | bytes 5308416 | tf_op jit(solution)/shard_map/reduce_scatter | solution.py:361
  775.1 201.4 %reduce-scatter.23.cloned.1.call-start = ((), (), s32[]{:S(2)}) async-start(), calls=%async_computation.24 | async-start | bytes 5308416 | tf_op jit(solution)/shard_map/reduce_scatter | solution.py:361
  789.3 242.7 %reduce-scatter.17.cloned.1.call-start = ((), (), s32[]{:S(2)}) async-start(), calls=%async_computation.21 | async-start | bytes 5308416 | tf_op jit(solution)/shard_map/reduce_scatter | solution.py:361
  799.8 287.7 %reduce-scatter.21.cloned.1.call-start = ((), (), s32[]{:S(2)}) async-start(), calls=%async_computation.23 | async-start | bytes 5308416 | tf_op jit(solution)/shard_map/reduce_scatter | solution.py:361
  814.2 273.4 %copy-start.9 = (f32[1,1024,768]{2,1,0:T(8,128)S(1)}, f32[1,1024,768]{2,1,0:T(8,128)}, u32[]{:S(2)}) copy-start(f32[1,1024,768]{2,1,0:T(8,128)} %param.31) | copy-start | bytes 9437188
  814.2 376.8 %all-reduce.6.cloned.1.call-start = ((), (), s32[]{:S(2)}) async-start(), calls=%async_computation.33 | async-start | bytes 7667712 | tf_op jit(solution)/shard_map/psum | solution.py:361
  (79 other events, 1108.4 us)
Sparse Core Ops, SparseCore 0:
  10.7 44.5 all-gather.16
  56.9 40.3 all-gather.18
  98.9 21.5 all-gather.20
  122.6 51.3 all-gather.22
  176.0 50.5 all-gather.24
  228.1 21.4 all-gather.26
  251.8 51.4 all-gather.28
  305.5 50.5 all-gather.30
  583.9 41.0 reduce-scatter.26
  756.3 41.2 reduce-scatter.24
  800.5 31.1 reduce-scatter.14
  834.5 31.0 reduce-scatter.12
  867.8 53.1 reduce-scatter.18
  923.2 53.2 reduce-scatter.22
  978.7 53.3 reduce-scatter.16
  1034.2 53.3 reduce-scatter.20
  1092.5 98.5 all-reduce.5

commit v2 on v1

--- a/solution.py
+++ b/solution.py
@@ -129,6 +129,7 @@
         out_specs=pl.BlockSpec(memory_space=pltpu.VMEM),
         scratch_shapes=[pltpu.VMEM((2,hp,KEYS,2*BLK),F32),pltpu.VMEM((2,hp,KEYS,2*BLK),BF),pltpu.VMEM((hp,length,2*BLK),F32)],
         compiler_params=pltpu.CompilerParams(vmem_limit_bytes=48<<20),
+        cost_estimate=pl.CostEstimate(flops=26*10**9,bytes_accessed=6*10**6,transcendentals=6*10**6),
         name="attn_fwd")(lists.reshape(-1),x)
 
 def bwd_kernel(hp, lists_ref, x_ref, d_ref, o_ref, win_ref, rnd_ref, s_ref, p_ref, g_ref):
@@ -222,6 +223,7 @@
         out_specs=pl.BlockSpec(memory_space=pltpu.VMEM),
         scratch_shapes=[pltpu.VMEM((hp,length+2*BLK,2*HD),F32),pltpu.VMEM((hp,length,2*HD),F32),pltpu.VMEM((2,hp,KEYS,4*BLK),F32),pltpu.VMEM((2,hp,KEYS,4*BLK),BF),pltpu.VMEM((length,4*BLK),F32)],
         compiler_params=pltpu.CompilerParams(vmem_limit_bytes=56<<20),
+        cost_estimate=pl.CostEstimate(flops=46*10**9,bytes_accessed=12*10**6,transcendentals=6*10**6),
         name="attn_bwd")(lists.reshape(-1),x,d)
 
 
@@ -308,6 +310,12 @@
         for layer in range(LAYERS)
     ]
     current = hidden[0]
+    seq_rank = lax.axis_index("seq")
+    item_rank = lax.axis_index("item")
+    cols = hp * 3 * HD
+    hidden_all = exchange(jnp.broadcast_to(current.astype(BF)[None], (groups, tokens, D))).reshape(groups * tokens, D)
+    own_shard = lax.dynamic_index_in_dim(shards[0][0].reshape(-1, groups, cols), seq_rank, 1, False)
+    own_weight = lax.all_gather(own_shard, "item", axis=0, tiled=True)
     saved = []
     for layer in range(LAYERS):
         qkv_weight, out_weight, inner_weight, outer_weight = weights[layer]
@@ -316,8 +324,12 @@
         input_low = current.astype(BF)
         qkv_split = qkv_weight.reshape(D, groups, hp * 3 * HD)
         out_split = jnp.pad(out_weight, ((0, wide - D), (0, 0))).reshape(groups, hp * HD, D)
-        proj = mm("td,dne->nte", input_low, qkv_split) + bias.reshape(groups, 1, hp * 3 * HD)
-        x = exchange(proj.astype(BF)).reshape(groups * tokens, hp * 3 * HD)
+        if layer == 0:
+            own_bias = lax.dynamic_index_in_dim(bias.reshape(groups, cols), seq_rank, 0, True)
+            x = (mm("td,de->te", hidden_all, own_weight) + own_bias).astype(BF)
+        else:
+            proj = mm("td,dne->nte", input_low, qkv_split) + bias.reshape(groups, 1, cols)
+            x = exchange(proj.astype(BF)).reshape(groups * tokens, cols)
         ctx = attn_fwd(ids[layer], x)
         context = exchange(ctx.reshape(groups, tokens, hp * HD))
         attn_out = mm("nte,ned->td", context, out_split)
@@ -331,6 +343,38 @@
         saved.append((input_low, qkv_split, out_split, x, context, resid_one, normed_low, pre_act, activated, resid_two))
     grad_state = cotangent[0]
     collected = [None] * LAYERS
+    flats = [None] * LAYERS
+    previous = None
+
+    def scattered(g):
+        return lax.psum_scatter(g, "item", scatter_dimension=0, tiled=True)
+
+    def seq_total(shares):
+        flat = jnp.concatenate([p.reshape(-1, D) for p in shares])
+        flat = jnp.pad(flat, ((0, -flat.shape[0] % (8 * groups)), (0, 0)))
+        parts = exchange(flat.reshape(groups, -1, D))
+        own = jnp.sum(parts.astype(jnp.float32), 0).astype(BF)
+        whole = exchange(jnp.broadcast_to(own[None], (groups,) + own.shape)).reshape(-1, D).astype(jnp.float32)
+        at, out = 0, []
+        for p in shares:
+            n = p.size // D
+            out.append(whole[at : at + n].reshape(p.shape))
+            at += n
+        return out
+
+    def with_rows(grad, vectors):
+        width = grad.shape[1]
+        part = jnp.concatenate([v.reshape(rows, -1) for v in vectors], 1)
+        part = jnp.pad(part, ((0, 0), (0, 8 * width - part.shape[1]))).reshape(rows, 8, width)
+        return jnp.concatenate([grad.reshape(rows, -1, width), part.astype(BF)], 1).reshape(-1, width)
+
+    def split_rows(share, counts):
+        flat, at, out = share[-8:].reshape(-1), 0, []
+        for n in counts:
+            out.append(flat[at : at + n])
+            at += n
+        return share[:-8], out
+
     for layer in reversed(range(LAYERS)):
         qkv_weight, out_weight, inner_weight, outer_weight = weights[layer]
         query_bias, value_bias, out_bias, gain_one, shift_one, inner_bias, outer_bias, gain_two, shift_two = vectors[layer]
@@ -347,33 +391,51 @@
         grad_attn = grad_resid_one.astype(BF)
         grad_context = mm("td,ned->nte", grad_attn, out_split).astype(BF)
         dctx = exchange(grad_context).reshape(groups * tokens, hp * HD)
+        grad_outer_weight = mm("tf,td->fd", activated, grad_ffn).astype(BF)
+        grad_inner_weight = mm("td,tf->df", normed_low, grad_pre).astype(BF)
+        grad_out_weight = mm("nte,td->ned", context, grad_attn).reshape(wide, D)[:D].astype(BF)
+        total = lambda g: jnp.sum(g.astype(jnp.float32), tuple(range(g.ndim - 1)))
+        early = (total(grad_attn), grad_gain_one, grad_shift_one, total(grad_pre), total(grad_ffn), grad_gain_two, grad_shift_two)
+        counts = [v.size // rows for v in early]
+        grad_out_weight = with_rows(grad_out_weight, early)
+        dctx, grad_outer_weight, grad_inner_weight, grad_out_weight = lax.optimization_barrier((dctx, grad_outer_weight, grad_inner_weight, grad_out_weight))
+        ffn_shares = (scattered(grad_inner_weight), scattered(grad_outer_weight), scattered(grad_out_weight))
+        if previous is None:
+            dctx, early_weight = lax.optimization_barrier((dctx, weights[0][0]))
+            saved[0] = (saved[0][0], early_weight.reshape(D, groups, cols)) + saved[0][2:]
+        else:
+            dctx, previous = lax.optimization_barrier((dctx, previous))
+            qkv, inner, outer, attn = seq_total(previous)
+            qkv, late_one = split_rows(qkv, [D // rows] * 2)
+            attn, early_one = split_rows(attn, counts)
+            collected[layer + 1] = (from_groups(qkv, groups, hp), attn, inner, outer)
+            flats[layer + 1] = late_one + early_one
         dx = attn_bwd(ids[layer], x, dctx)
-        dproj = exchange(dx.reshape(groups, tokens, hp * 3 * HD))
-        grad_outer_weight = mm("tf,td->fd", activated, grad_ffn)
-        grad_inner_weight = mm("td,tf->df", normed_low, grad_pre)
-        grad_out_weight = mm("nte,td->ned", context, grad_attn).reshape(wide, D)[:D]
-        grad_qkv_weight = mm("td,nte->dne", input_low, dproj).reshape(D, -1)
+        if layer == 0:
+            dx, collected[1], flats[1] = lax.optimization_barrier((dx, collected[1], flats[1]))
+            own_grad = mm("td,te->de", hidden_all, dx).reshape(rows, -1, cols)
+            own_sum = jnp.broadcast_to(total(dx)[None, None], (rows, 8, cols))
+            packed_grad = jnp.concatenate([own_grad, own_sum], 1).astype(BF)
+            dproj = exchange(dx.reshape(groups, tokens, cols))
+            packed_grad, ffn_shares = lax.optimization_barrier((packed_grad, ffn_shares))
+            share = scattered(packed_grad.reshape(-1, cols))
+            inner, outer, attn = seq_total(ffn_shares)
+            share = exchange(jnp.broadcast_to(share[None], (groups,) + share.shape)).astype(jnp.float32)
+            gq0 = from_groups(share[:, :-8].transpose(1, 0, 2).reshape(-1, groups * cols), groups, hp)
+            db = from_groups(share[:, -8].reshape(-1), groups, hp)
+            attn, flats[0] = split_rows(attn, counts)
+            collected[0] = (gq0, attn, inner, outer)
+            late = [lax.dynamic_slice_in_dim(db, part * D + item_rank * (D // rows), D // rows) for part in (0, 2)]
+        else:
+            dproj = exchange(dx.reshape(groups, tokens, cols))
+            grad_qkv_weight = mm("td,nte->dne", input_low, dproj).reshape(D, -1).astype(BF)
+            dbias = from_groups(jnp.sum(dproj.astype(jnp.float32), 1).reshape(-1), groups, hp)
+            previous = (scattered(with_rows(grad_qkv_weight, (dbias[:D], dbias[2 * D :]))),) + ffn_shares
         grad_state = grad_resid_one + mm("nte,dne->td", dproj, qkv_split)
-        total = lambda g: jnp.sum(g.astype(jnp.float32), tuple(range(g.ndim - 1)))
-        dbias = from_groups(jnp.sum(dproj.astype(jnp.float32), 1).reshape(-1), groups, hp)
-        flat = (dbias[:D], dbias[2 * D :], total(grad_attn), grad_gain_one, grad_shift_one, total(grad_pre), total(grad_ffn), grad_gain_two, grad_shift_two)
-        big = tuple(
-            lax.psum(lax.psum_scatter(g.astype(BF), "item", scatter_dimension=0, tiled=True), "seq").astype(jnp.float32)
-            for g in (grad_qkv_weight, grad_out_weight, grad_inner_weight, grad_outer_weight)
-        )
-        collected[layer] = (from_groups(big[0], groups, hp),) + big[1:], flat
-    parts = [
-        jnp.concatenate([g.reshape(rows, -1) for g in collected[layer][1]], 1) for layer in range(LAYERS)
-    ]
-    part = jnp.stack(parts, 1)
-    part = part.reshape(rows, -1).astype(BF)
-    mine = lax.psum(lax.psum_scatter(part, "item", scatter_dimension=0, tiled=True), "seq")
-    mine = mine.astype(jnp.float32).reshape(LAYERS, -1)
-    at, vecs = 0, []
-    for size in sizes:
-        vecs.append(mine[:, at : at + size])
-        at += size
-    gq, go, gi, gf = (jnp.stack([collected[layer][0][n] for layer in range(LAYERS)]) for n in range(4))
+    first, second = flats
+    vecs = [jnp.stack([late[n], second[n]]) for n in range(2)]
+    vecs += [jnp.stack([first[n], second[n + 2]]) for n in range(7)]
+    gq, go, gi, gf = (jnp.stack([collected[layer][n] for layer in range(LAYERS)]) for n in range(4))
     return (
         current[None],
         grad_state[None],

time: 1220 us -> 951 us (0.78)
  waiting for transfers between devices: 481 us -> 261 us
  blocking collectives: 200 us -> 62 us
  starting transfers between devices: 25.9 us -> 62.2 us
  local copies, waits for them, and re-layouts: 110 us -> 133 us
  other arithmetic: 25.1 us -> 47.1 us
    reduce_scatter x6 -> x7, waiting for transfers between devices: 269 us -> 37.7 us  [scattered(): return lax.psum_scatter(g, 'item', scatter_dimension=0, tiled=True)]
    all_to_all x4 -> x1, blocking collectives: 150 us -> 24.8 us  [exchange(): return lax.all_to_all(x, 'seq', split_axis=0, concat_axis=0, tiled=True)]
    all_to_all x5 -> x13, waiting for transfers between devices: 132 us -> 218 us  [exchange(): return lax.all_to_all(x, 'seq', split_axis=0, concat_axis=0, tiled=True)]
    psum x1 -> x0, waiting for transfers between devices: 38.5 us -> none  [local(): lax.psum(lax.psum_scatter(g.astype(BF), 'item', scatter_dimension=0, tile...]
    all_gather x8, waiting for transfers between devices: 39 us -> 0.8 us  [local(): lax.all_gather(s[layer], 'item', axis=0, tiled=True)]
    all_to_all x5 -> x13, starting transfers between devices: 24.5 us -> 61.1 us  [exchange(): return lax.all_to_all(x, 'seq', split_axis=0, concat_axis=0, tiled=True)]
    unnamed x1 -> x0, blocking collectives: 26.3 us -> none
    all_gather x0 -> x1, blocking collectives: none -> 23 us  [local(): own_weight = lax.all_gather(own_shard, 'item', axis=0, tiled=True)]
  transfers between devices with their start and end apart: 22 -> 29, of which waited for: 13 -> 11; matrix products, arithmetic and copies ran while one was open for 20% -> 38% of each run, Pallas kernels for 8% -> 15%
where the time goes in v2:
time: 951 us; the launch traced here: 941 us
  waiting for transfers between devices  261 us (27%)
  matrix products  215 us (23%)
  Pallas kernels  145 us (15%)
  local copies, waits for them, and re-layouts  133 us (14%)
  starting transfers between devices  62.2 us (7%)
  blocking collectives  62 us (7%)
  other arithmetic  47.1 us (5%)
  between operations  15.7 us (2%)
    all_to_all x13, waiting for transfers between devices, exchange(): return lax.all_to_all(x, 'seq', split_axis=0, concat_axis=0, tiled=True)  218 us
    dot_general x24, matrix products, mm(): return jnp.einsum(spec, a, b, preferred_element_type=jnp.float32)  215 us
    pallas_call x2, Pallas kernels, attn_bwd(): pl.pallas_call(lambda *a: bwd_kernel(hp, *a), out_shape=jax.ShapeDtypeStr...  92.3 us
    all_to_all x13, starting transfers between devices, exchange(): return lax.all_to_all(x, 'seq', split_axis=0, concat_axis=0, tiled=True)  61.1 us
    pallas_call x2, Pallas kernels, attn_fwd(): pl.pallas_call(lambda *a: fwd_kernel(hp, *a), out_shape=jax.ShapeDtypeStr...  52.4 us
    reduce_scatter x7, waiting for transfers between devices, scattered(): return lax.psum_scatter(g, 'item', scatter_dimension=0, tiled=True)  37.7 us
    unnamed x149, local copies, waits for them, and re-layouts  29.2 us
    all_to_all x1, blocking collectives, exchange(): return lax.all_to_all(x, 'seq', split_axis=0, concat_axis=0, tiled=True)  24.8 us
  transfers between devices with their start and end apart: 29, of which 11 were waited for; matrix products, arithmetic and copies ran while one was open for 38% of the time, Pallas kernels for 15%

profile of v2, /device:TPU:0, one launch (start us, length us, event | category | flops | bytes accessed | tf_op | source)
XLA Modules:
  0.0 940.8 jit_solution(6799098361349287666)
XLA Ops:
  40.2 14.3 %all-gather.8 = bf16[8,2,1152]{2,1,0:T(2,128)(2,1)S(1)} all-gather(bf16[1,2,1152]{2,1,0:T(2,128)(2,1)S(1)} %bitcast.291), channel_id=3, replica_groups=mesh['seq'=4,'item'=8] {'item'}, dimensions={0}, use_global_device_ids=true | all-gather | bytes 41472 | tf_op jit(solution)/shard_map/all_gather | solution.py:298
  56.0 23.0 %all-gather = bf16[1,768,1,576]{3,1,2,0:T(8,128)(2,1)S(1)} all-gather(bf16[1,96,1,576]{3,1,2,0:T(8,128)(2,1)S(1)} %copy.225), channel_id=2, replica_groups=mesh['seq'=4,'item'=8] {'item'}, dimensions={1}, use_global_device_ids=true | all-gather | bytes 995328 | tf_op jit(solution)/shard_map/all_gather | solution.py:318
  79.6 29.0 %all-to-all-done.1 = bf16[4,1024,768]{2,1,0:T(8,128)(2,1)} async-done(((bf16[4,1024,768]{2,1,0:T(8,128)(2,1)}), bf16[4,1024,768]{2,1,0:T(8,128)(2,1)}, u32[]{:S(2)}, u32[]{:S(2)}) %all-to-all-start.1) | async-done | bytes 6291488 | tf_op jit(solution)/shard_map/all_to_all | solution.py:261
  108.5 8.7 fusion.14.a_1_
  117.2 26.1 %attn_fwd.2 = bf16[4096,192]{1,0:T(8,128)(2,1)S(1)} custom-call(s32[576]{0:T(1024)S(1)} %squeeze.44.a_0_, bf16[4096,576]{1,0:T(8,128)(2,1)} %fusion.14.a_1_), custom_call_target="tpu_custom_call" | custom-call | flops 25999998976 | bytes 6000000 | tf_op jit(solution)/shard_map/attn_fwd/pallas_call | solution.py:126
  154.5 14.4 %all-to-all-done.2 = bf16[4,1024,192]{1,2,0:T(8,128)(2,1)} async-done(((bf16[4,1024,192]{1,2,0:T(8,128)(2,1)}), bf16[4,1024,192]{1,2,0:T(8,128)(2,1)}, u32[]{:S(2)}, u32[]{:S(2)}) %all-to-all-start.2) | async-done | bytes 1572896 | tf_op jit(solution)/shard_map/all_to_all | solution.py:261
  180.1 10.7 %fusion.30 = f32[1024,3072]{1,0:T(8,128)} fusion(bf16[1,768,3072]{2,1,0:T(8,128)(2,1)} %all-gather.24.cloned.1.call-done, f32[1024,768]{0,1:T(8,128)S(1)} %get-tuple-element.261, f32[768]{0:T(1024)S(1)} %reshape.601, f32[768]{0:T(1024)S(1)} %reshape.600, f32[1024]{0:T(1024)S(1)} %fusion.89, f32[1024]{0:T(1024)S(1)} %broadcast_multiply_fusion.3), kind=kOutput, calls=%fused_computation.46 | convolution fusion | flops 4835770368 | bytes 20461568 | tf_op jit(solution)/shard_map/td,df->tf/dot_general | solution.py:265
  191.6 11.5 %fusion.123 = (f32[1024]{0:T(1024)S(1)}, f32[1024,768]{0,1:T(8,128)S(1)}) fusion(f32[768]{0:T(1024)S(1)} %reshape.603, bf16[1,3072,768]{2,1,0:T(8,128)(2,1)} %all-gather.26.cloned.1.call-done, f32[1024,3072]{1,0:T(8,128)} %fusion.30, f32[3072]{0:T(1024)S(1)} %bitcast.292, f32[768]{0:T(1024)S(1)} %reshape.601, f32[768]{0:T(1024)S(1)} %reshape.600, ...), kind=kOutput, calls=%fused_computation.239 | convolution fusion | flops 4868799488 | bytes 23626752 | tf_op jit(solution)/shard_map/tf,fd->td/dot_general | solution.py:265
  216.1 53.5 %all-to-all-done.3 = bf16[4,1024,576]{1,2,0:T(8,128)(2,1)} async-done(((bf16[4,1024,576]{1,2,0:T(8,128)(2,1)}), bf16[4,1024,576]{1,2,0:T(8,128)(2,1)}, u32[]{:S(2)}, u32[]{:S(2)}) %all-to-all-start.3) | async-done | bytes 4718624 | tf_op jit(solution)/shard_map/all_to_all | solution.py:261
  277.3 26.3 %attn_fwd.3 = bf16[4096,192]{1,0:T(8,128)(2,1)S(1)} custom-call(s32[576]{0:T(1024)S(1)} %squeeze.49.a_0_, bf16[4096,576]{1,0:T(8,128)(2,1)} %bitcast.250), custom_call_target="tpu_custom_call" | custom-call | flops 25999998976 | bytes 6000000 | tf_op jit(solution)/shard_map/attn_fwd/pallas_call | solution.py:126
  315.8 14.1 %all-to-all-done.4 = bf16[4,1024,192]{1,2,0:T(8,128)(2,1)} async-done(((bf16[4,1024,192]{1,2,0:T(8,128)(2,1)}), bf16[4,1024,192]{1,2,0:T(8,128)(2,1)}, u32[]{:S(2)}, u32[]{:S(2)}) %all-to-all-start.4) | async-done | bytes 1572896 | tf_op jit(solution)/shard_map/all_to_all | solution.py:261
  334.9 10.6 %fusion.22 = f32[1024,3072]{1,0:T(8,128)} fusion(bf16[1,768,3072]{2,1,0:T(8,128)(2,1)} %all-gather.30.cloned.1.call-done, f32[1024,768]{0,1:T(8,128)S(1)} %get-tuple-element.265, f32[768]{0:T(1024)S(1)} %reshape.608, f32[768]{0:T(1024)S(1)} %reshape.607, f32[1024]{0:T(1024)S(1)} %fusion.91, f32[1024]{0:T(1024)S(1)} %broadcast_multiply_fusion.1), kind=kOutput, calls=%fused_computation.38 | convolution fusion | flops 4835770368 | bytes 20461568 | tf_op jit(solution)/shard_map/td,df->tf/dot_general | solution.py:265
  345.5 11.9 %fusion.125 = (f32[1024]{0:T(1024)S(1)}, f32[1024,768]{0,1:T(8,128)S(1)}) fusion(f32[768]{0:T(1024)S(1)} %reshape.610, bf16[1,3072,768]{2,1,0:T(8,128)(2,1)} %all-gather.32.cloned.1.call-done, f32[1024,3072]{1,0:T(8,128)} %fusion.22, f32[3072]{0:T(1024)S(1)} %bitcast.295, f32[768]{0:T(1024)S(1)} %reshape.608, f32[768]{0:T(1024)S(1)} %reshape.607, ...), kind=kOutput, calls=%fused_computation.241 | convolution fusion | flops 4868799488 | bytes 23626752 | tf_op jit(solution)/shard_map/tf,fd->td/dot_general | solution.py:265
  363.6 17.1 %fusion.107 = (bf16[3072]{0:T(1024)(128)(2,1)S(1)}, bf16[1024,3072]{1,0:T(8,128)(2,1)}) fusion(f32[1024,3072]{1,0:T(8,128)} %fusion.22, f32[3072]{0:T(1024)S(1)} %bitcast.296, bf16[1024,768]{0,1:T(8,128)(2,1)S(1)} %get-tuple-element.211, bf16[1,3072,768]{2,1,0:T(8,128)(2,1)S(1)} %bitcast.307), kind=kOutput, calls=%fused_computation.224 | convolution fusion | flops 4901041152 | bytes 25184256 | tf_op jit(solution)/shard_map/td,fd->tf/dot_general | solution.py:265
  380.8 8.5 multiply_reduce_fusion.4
  405.3 13.0 %convolution_convert_fusion.3 = bf16[3072,768]{1,0:T(8,128)(2,1)} fusion(bf16[1024,768]{0,1:T(8,128)(2,1)S(1)} %copy-done.24, f32[1024,3072]{1,0:T(8,128)} %fusion.22, f32[3072]{0:T(1024)S(1)} %bitcast.297), kind=kOutput, calls=%fused_computation.26 | convolution fusion | flops 4865654784 | bytes 18886656 | tf_op jit(solution)/shard_map/tf,td->fd/dot_general | solution.py:265
  418.3 9.8 %convolution_convert_fusion.2 = bf16[768,3072]{1,0:T(8,128)(2,1)} fusion(bf16[1024,3072]{1,0:T(8,128)(2,1)} %get-tuple-element.213, f32[1024,768]{0,1:T(8,128)S(1)} %get-tuple-element.265, f32[768]{0:T(1024)S(1)} %reshape.608, f32[768]{0:T(1024)S(1)} %reshape.607, f32[1024]{0:T(1024)S(1)} %fusion.91, f32[1024]{0:T(1024)S(1)} %broadcast_multiply_fusion.1), kind=kOutput, calls=%fused_computation.25 | convolution fusion | flops 4838129664 | bytes 14170112 | tf_op jit(solution)/shard_map/td,tf->df/dot_general | solution.py:265
  432.4 46.0 %attn_bwd.2 = bf16[4096,576]{1,0:T(8,128)(2,1)} custom-call(s32[576]{0:T(1024)} %copy-done.1, bf16[4096,576]{1,0:T(8,128)(2,1)} %bitcast.251, bf16[4096,192]{1,0:T(8,128)(2,1)} %bitcast.272), custom_call_target="tpu_custom_call" | custom-call | flops 46000001024 | bytes 12000000 | tf_op jit(solution)/shard_map/attn_bwd/pallas_call | solution.py:220
  492.0 52.0 %all-to-all-done.6 = bf16[4,1024,576]{1,2,0:T(8,128)(2,1)} async-done(((bf16[4,1024,576]{1,2,0:T(8,128)(2,1)}), bf16[4,1024,576]{1,2,0:T(8,128)(2,1)}, u32[]{:S(2)}, u32[]{:S(2)}) %all-to-all-start.6) | async-done | bytes 4718624 | tf_op jit(solution)/shard_map/all_to_all | solution.py:261
  548.3 8.7 convolution_convert_fusion.4
  557.0 8.9 reshape.638
  571.3 11.3 %multiply_reduce_fusion = (bf16[768]{0:T(1024)(128)(2,1)}, f32[1024]{0:T(1024)S(1)}, bf16[768]{0:T(1024)(128)(2,1)}, f32[1024,768]{0,1:T(8,128)S(1)}) fusion(f32[1024,768]{0,1:T(8,128)} %copy-done.12, f32[1024]{0:T(1024)S(1)} %copy-done.46, f32[1024]{0:T(1024)S(1)} %copy-done.37, f32[768]{0:T(1024)S(1)} %copy-done.44, ...), kind=kOutput, calls=%fused_computation.59 | convolution fusion | flops 3631740416 | bytes 17717248 | tf_op jit(solution)/shard_map/nte,dne->td/dot_general | solution.py:265
  589.3 17.2 %fusion.101 = (bf16[3072]{0:T(1024)(128)(2,1)S(1)}, bf16[1024,3072]{1,0:T(8,128)(2,1)S(1)}) fusion(f32[1024,3072]{1,0:T(8,128)} %fusion.30, f32[3072]{0:T(1024)S(1)} %bitcast.293, bf16[1024,768]{0,1:T(8,128)(2,1)} %get-tuple-element.201, bf16[1,3072,768]{2,1,0:T(8,128)(2,1)} %all-gather.26.cloned.1.call-done), kind=kOutput, calls=%fused_computation.219 | convolution fusion | flops 4901041152 | bytes 25184256 | tf_op jit(solution)/shard_map/td,fd->tf/dot_general | solution.py:265
  606.5 9.8 %multiply_reduce_fusion.1 = (bf16[768]{0:T(1024)(128)(2,1)S(1)}, f32[1024]{0:T(1024)S(1)}, bf16[768]{0:T(1024)(128)(2,1)S(1)}, f32[1024,768]{0,1:T(8,128)S(1)}) fusion(f32[1024,768]{0,1:T(8,128)S(1)} %copy-done.3, f32[1024]{0:T(1024)S(1)} %copy-done.33, f32[1024]{0:T(1024)S(1)} %copy-done.29, f32[768]{0:T(1024)S(1)} %copy-done.31, ...), kind=kOutput, calls=%fused_computation.60 | convolution fusion | flops 4839699456 | bytes 20469760 | tf_op jit(solution)/shard_map/tf,df->td/dot_general | solution.py:265
  633.0 13.1 %convolution_convert_fusion.1 = bf16[3072,768]{1,0:T(8,128)(2,1)} fusion(bf16[1024,768]{0,1:T(8,128)(2,1)S(1)} %copy-done.22, f32[1024,3072]{1,0:T(8,128)} %fusion.30, f32[3072]{0:T(1024)S(1)} %bitcast.294), kind=kOutput, calls=%fused_computation.24 | convolution fusion | flops 4865654784 | bytes 18886656 | tf_op jit(solution)/shard_map/tf,td->fd/dot_general | solution.py:265
  646.1 9.7 %convolution_convert_fusion = bf16[768,3072]{1,0:T(8,128)(2,1)} fusion(bf16[1024,3072]{1,0:T(8,128)(2,1)} %copy-done.64, f32[1024,768]{0,1:T(8,128)S(1)} %copy-done.3, f32[768]{0:T(1024)S(1)} %copy-done.35, f32[768]{0:T(1024)S(1)} %copy-done.31, f32[1024]{0:T(1024)S(1)} %copy-done.33, f32[1024]{0:T(1024)S(1)} %copy-done.29), kind=kOutput, calls=%fused_computation.23 | convolution fusion | flops 4838129664 | bytes 14170112 | tf_op jit(solution)/shard_map/td,tf->df/dot_general | solution.py:265
  664.9 24.8 %all_to_all.75 = bf16[4,296,768]{2,1,0:T(8,128)(2,1)S(1)} all-to-all(bf16[4,296,768]{2,1,0:T(8,128)(2,1)S(1)} %bitcast.249), channel_id=1, replica_groups=mesh['seq'=4,'item'=8] {'seq'}, dimensions={0} | all-to-all | bytes 3637248 | tf_op jit(solution)/shard_map/all_to_all | solution.py:261
  695.5 46.4 %attn_bwd.3 = bf16[4096,576]{1,0:T(8,128)(2,1)} custom-call(s32[576]{0:T(1024)} %copy-done, bf16[4096,576]{1,0:T(8,128)(2,1)} %fusion.14.a_1_, bf16[4096,192]{1,0:T(8,128)(2,1)} %bitcast.271), custom_call_target="tpu_custom_call" | custom-call | flops 46000001024 | bytes 12000000 | tf_op jit(solution)/shard_map/attn_bwd/pallas_call | solution.py:220
  764.8 37.6 %reduce-scatter.21.cloned.1.call-done = bf16[384,768]{1,0:T(8,128)(2,1)} async-done(((bf16[3072,768]{1,0:T(8,128)(2,1)}), bf16[384,768]{1,0:T(8,128)(2,1)}) %reduce-scatter.21.cloned.1.call-update) | async-done | bytes 589840 | tf_op jit(solution)/shard_map/reduce_scatter | solution.py:350
  811.1 14.7 %all-to-all-done.12 = bf16[4,224,768]{2,1,0:T(8,128)(2,1)} async-done(((bf16[4,224,768]{2,1,0:T(8,128)(2,1)}), bf16[4,224,768]{2,1,0:T(8,128)(2,1)}, u32[]{:S(2)}, u32[]{:S(2)}) %all-to-all-start.12) | async-done | bytes 1376288 | tf_op jit(solution)/shard_map/all_to_all | solution.py:261
  885.5 35.9 %all-to-all-done.10 = bf16[4,1024,576]{1,2,0:T(8,128)(2,1)} async-done(((bf16[4,1024,576]{1,2,0:T(8,128)(2,1)}), bf16[4,1024,576]{1,2,0:T(8,128)(2,1)}, u32[]{:S(2)}, u32[]{:S(2)}) %all-to-all-start.10) | async-done | bytes 4718624 | tf_op jit(solution)/shard_map/all_to_all | solution.py:261
  921.5 9.0 fusion.32
  (418 shorter events, 277.8 us)
Async XLA Ops:
  7.2 147.4 %all-gather.22.cloned.1.call-start = ((), (), s32[]{:S(2)}) async-start(), calls=%async_computation.31 | async-start | bytes 1327104 | tf_op jit(solution)/shard_map/all_gather | solution.py:309
  9.0 164.8 %all-gather.18.cloned.1.call-start = ((), (), s32[]{:S(2)}) async-start(), calls=%async_computation.22 | async-start | bytes 3981312 | tf_op jit(solution)/shard_map/all_gather | solution.py:309
  13.2 167.0 %all-gather.24.cloned.1.call-start = ((), (), s32[]{:S(2)}) async-start(), calls=%async_computation.32 | async-start | bytes 5308416 | tf_op jit(solution)/shard_map/all_gather | solution.py:309
  15.7 175.8 %all-gather.26.cloned.1.call-start = ((), (), s32[]{:S(2)}) async-start(), calls=%async_computation.33 | async-start | bytes 5308416 | tf_op jit(solution)/shard_map/all_gather | solution.py:309
  18.1 297.7 %all-gather.28.cloned.1.call-start = ((), (), s32[]{:S(2)}) async-start(), calls=%async_computation.34 | async-start | bytes 1327104 | tf_op jit(solution)/shard_map/all_gather | solution.py:309
  19.5 9.8 %all-to-all-start = ((s32[4,1,288]{2,1,0:T(1,128)}), s32[4,1,288]{2,1,0:T(1,128)S(1)}, u32[]{:S(2)}, u32[]{:S(2)}) async-start(s32[4,1,288]{2,1,0:T(1,128)} %all_to_all.60), calls=%async_computation | async-start | bytes 12288 | tf_op jit(solution)/shard_map/all_to_all | solution.py:261
  34.0 74.6 %all-to-all-start.1 = ((bf16[4,1024,768]{2,1,0:T(8,128)(2,1)}), bf16[4,1024,768]{2,1,0:T(8,128)(2,1)}, u32[]{:S(2)}, u32[]{:S(2)}) async-start(bf16[4,1024,768]{2,1,0:T(8,128)(2,1)} %broadcast_in_dim.33), calls=%async_computation.1 | async-start | bytes 12582912 | tf_op jit(solution)/shard_map/all_to_all | solution.py:261
  39.4 295.5 %all-gather.30.cloned.1.call-start = ((), (), s32[]{:S(2)}) async-start(), calls=%async_computation.35 | async-start | bytes 5308416 | tf_op jit(solution)/shard_map/all_gather | solution.py:309
  145.6 23.4 %all-to-all-start.2 = ((bf16[4,1024,192]{1,2,0:T(8,128)(2,1)}), bf16[4,1024,192]{1,2,0:T(8,128)(2,1)}, u32[]{:S(2)}, u32[]{:S(2)}) async-start(bf16[4,1024,192]{1,2,0:T(8,128)(2,1)} %copy.229), calls=%async_computation.2 | async-start | bytes 3145728 | tf_op jit(solution)/shard_map/all_to_all | solution.py:261
  150.3 195.2 %all-gather.32.cloned.1.call-start = ((), (), s32[]{:S(2)}) async-start(), calls=%async_computation.36 | async-start | bytes 5308416 | tf_op jit(solution)/shard_map/all_gather | solution.py:309
  154.3 175.5 %copy-start.49 = (f32[768]{0:T(1024)}, f32[768]{0:T(1024)S(1)}, u32[]{:S(2)}) copy-start(f32[768]{0:T(1024)S(1)} %reshape.605) | copy-start | bytes 9220
  154.4 175.4 %copy-start.43 = (f32[768]{0:T(1024)}, f32[768]{0:T(1024)S(1)}, u32[]{:S(2)}) copy-start(f32[768]{0:T(1024)S(1)} %reshape.604) | copy-start | bytes 9220
  203.1 126.7 %copy-start.36 = (f32[1024]{0:T(1024)}, f32[1024]{0:T(1024)S(1)}, u32[]{:S(2)}) copy-start(f32[1024]{0:T(1024)S(1)} %broadcast_multiply_fusion.2) | copy-start | bytes 12292
  210.6 58.9 %all-to-all-start.3 = ((bf16[4,1024,576]{1,2,0:T(8,128)(2,1)}), bf16[4,1024,576]{1,2,0:T(8,128)(2,1)}, u32[]{:S(2)}, u32[]{:S(2)}) async-start(bf16[4,1024,576]{1,2,0:T(8,128)(2,1)} %fusion.15), calls=%async_computation.3 | async-start | bytes 9437184 | tf_op jit(solution)/shard_map/all_to_all | solution.py:261
  305.9 24.0 %all-to-all-start.4 = ((bf16[4,1024,192]{1,2,0:T(8,128)(2,1)}), bf16[4,1024,192]{1,2,0:T(8,128)(2,1)}, u32[]{:S(2)}, u32[]{:S(2)}) async-start(bf16[4,1024,192]{1,2,0:T(8,128)(2,1)} %copy.236), calls=%async_computation.4 | async-start | bytes 3145728 | tf_op jit(solution)/shard_map/all_to_all | solution.py:261
  310.5 122.0 %all-gather.20.cloned.1.call-start = ((), (), s32[]{:S(2)}) async-start(), calls=%async_computation.23 | async-start | bytes 3981312 | tf_op jit(solution)/shard_map/all_gather | solution.py:309
  395.8 32.3 %all-to-all-start.5 = ((bf16[4,1024,192]{1,2,0:T(8,128)(2,1)}), bf16[4,1024,192]{1,2,0:T(8,128)(2,1)}, u32[]{:S(2)}, u32[]{:S(2)}) async-start(bf16[4,1024,192]{1,2,0:T(8,128)(2,1)} %fusion.63), calls=%async_computation.5 | async-start | bytes 3145728 | tf_op jit(solution)/shard_map/all_to_all | solution.py:261
  400.1 260.6 %reduce-scatter.17.cloned.1.call-start = ((), (), s32[]{:S(2)}) async-start(), calls=%async_computation.27 | async-start | bytes 1437696 | tf_op jit(solution)/shard_map/reduce_scatter | solution.py:350
  431.8 228.9 %reduce-scatter.13.cloned.1.call-start = ((), (), s32[]{:S(2)}) async-start(), calls=%async_computation.25 | async-start | bytes 5308416 | tf_op jit(solution)/shard_map/reduce_scatter | solution.py:350
  486.1 57.9 %all-to-all-start.6 = ((bf16[4,1024,576]{1,2,0:T(8,128)(2,1)}), bf16[4,1024,576]{1,2,0:T(8,128)(2,1)}, u32[]{:S(2)}, u32[]{:S(2)}) async-start(bf16[4,1024,576]{1,2,0:T(8,128)(2,1)} %copy.244), calls=%async_computation.6 | async-start | bytes 9437184 | tf_op jit(solution)/shard_map/all_to_all | solution.py:261
  491.2 169.6 %reduce-scatter.15.cloned.1.call-start = ((), (), s32[]{:S(2)}) async-start(), calls=%async_computation.26 | async-start | bytes 5308416 | tf_op jit(solution)/shard_map/reduce_scatter | solution.py:350
  491.9 168.9 %reduce-scatter.11.cloned.1.call-start = ((), (), s32[]{:S(2)}) async-start(), calls=%async_computation.24 | async-start | bytes 4313088 | tf_op jit(solution)/shard_map/reduce_scatter | solution.py:350
  623.0 32.8 %all-to-all-start.7 = ((bf16[4,1024,192]{1,2,0:T(8,128)(2,1)}), bf16[4,1024,192]{1,2,0:T(8,128)(2,1)}, u32[]{:S(2)}, u32[]{:S(2)}) async-start(bf16[4,1024,192]{1,2,0:T(8,128)(2,1)} %fusion.66), calls=%async_computation.7 | async-start | bytes 3145728 | tf_op jit(solution)/shard_map/all_to_all | solution.py:261
  627.5 137.4 %reduce-scatter.23.cloned.1.call-start = ((), (), s32[]{:S(2)}) async-start(), calls=%async_computation.30 | async-start | bytes 1437696 | tf_op jit(solution)/shard_map/reduce_scatter | solution.py:350
  659.5 105.3 %reduce-scatter.19.cloned.1.call-start = ((), (), s32[]{:S(2)}) async-start(), calls=%async_computation.28 | async-start | bytes 5308416 | tf_op jit(solution)/shard_map/reduce_scatter | solution.py:350
  660.1 142.3 %reduce-scatter.21.cloned.1.call-start = ((), (), s32[]{:S(2)}) async-start(), calls=%async_computation.29 | async-start | bytes 5308416 | tf_op jit(solution)/shard_map/reduce_scatter | solution.py:350
  691.5 50.4 %all-to-all-start.9 = ((bf16[4,296,768]{2,1,0:T(8,128)(2,1)}), bf16[4,296,768]{2,1,0:T(8,128)(2,1)S(1)}, u32[]{:S(2)}, u32[]{:S(2)}) async-start(bf16[4,296,768]{2,1,0:T(8,128)(2,1)} %broadcast_in_dim.43), calls=%async_computation.13 | async-start | bytes 3637248 | tf_op jit(solution)/shard_map/all_to_all | solution.py:261
  806.2 19.7 %all-to-all-start.12 = ((bf16[4,224,768]{2,1,0:T(8,128)(2,1)}), bf16[4,224,768]{2,1,0:T(8,128)(2,1)}, u32[]{:S(2)}, u32[]{:S(2)}) async-start(bf16[4,224,768]{2,1,0:T(8,128)(2,1)} %bitcast.75), calls=%async_computation.19 | async-start | bytes 2752512 | tf_op jit(solution)/shard_map/all_to_all | solution.py:261
  810.6 38.4 %reduce-scatter.25.cloned.1.call-start = ((), (), s32[]{:S(2)}) async-start(), calls=%async_computation.37 | async-start | bytes 1198080
  828.7 21.0 %all-to-all-start.13 = ((bf16[4,224,768]{2,1,0:T(8,128)(2,1)}), bf16[4,224,768]{2,1,0:T(8,128)(2,1)}, u32[]{:S(2)}, u32[]{:S(2)}) async-start(bf16[4,224,768]{2,1,0:T(8,128)(2,1)} %broadcast_in_dim.47), calls=%async_computation.20 | async-start | bytes 2752512 | tf_op jit(solution)/shard_map/all_to_all | solution.py:261
  851.5 12.3 %all-to-all-start.11 = ((bf16[4,104,576]{2,1,0:T(8,128)(2,1)}), bf16[4,104,576]{2,1,0:T(8,128)(2,1)}, u32[]{:S(2)}, u32[]{:S(2)}) async-start(bf16[4,104,576]{2,1,0:T(8,128)(2,1)} %broadcast_in_dim.46), calls=%async_computation.18 | async-start | bytes 1064960 | tf_op jit(solution)/shard_map/all_to_all | solution.py:261
  863.7 57.8 %all-to-all-start.10 = ((bf16[4,1024,576]{1,2,0:T(8,128)(2,1)}), bf16[4,1024,576]{1,2,0:T(8,128)(2,1)}, u32[]{:S(2)}, u32[]{:S(2)}) async-start(bf16[4,1024,576]{1,2,0:T(8,128)(2,1)} %copy.254), calls=%async_computation.14 | async-start | bytes 9437184 | tf_op jit(solution)/shard_map/all_to_all | solution.py:261
  (69 other events, 1107.4 us)
Sparse Core Ops, SparseCore 0:
  9.7 25.3 all-gather.21
  36.7 49.3 all-gather.17
  88.3 50.5 all-gather.23
  141.0 50.5 all-gather.25
  193.0 21.4 all-gather.27
  216.6 51.4 all-gather.29
  270.3 50.5 all-gather.31
  322.5 40.3 all-gather.19
  431.9 32.9 reduce-scatter.16
  467.1 53.0 reduce-scatter.12
  522.5 53.3 reduce-scatter.14
  588.7 44.5 reduce-scatter.10
  659.7 31.9 reduce-scatter.22
  693.8 53.0 reduce-scatter.18
  749.1 53.3 reduce-scatter.20
  814.0 32.5 reduce-scatter.24

commit v3 on v1

v3 whole, which is shorter than its diff:
```python
from functools import partial

import jax
import jax.numpy as jnp
from jax import lax
from jax.experimental import pallas as pl
from jax.experimental.pallas import tpu as pltpu
from jax.sharding import PartitionSpec as P

D = 768
H = 12
HD = 64
BLK = 64
RAND = 3
LAYERS = 2
LISTED = 5 + RAND
KEYS = LISTED * BLK
WIDE = 2 * HD
F32 = jnp.float32
BF = jnp.bfloat16
LOG2E = 1.4426950408889634
epsilon = 1e-05
NT = (((1,), (1,)), ((), ()))
TN = (((0,), (0,)), ((), ()))
NN = (((1,), (0,)), ((), ()))
VMEM = pltpu.VMEM


def dot(a, b, dims):
    return lax.dot_general(a, b, dims, preferred_element_type=F32)


class Plan:
    def __init__(self, groups, tokens, half=128):
        self.groups = groups
        self.tokens = tokens
        self.hp = -(-H // groups)
        self.pairs = self.hp // 2
        self.odd = self.hp % 2
        self.half = min(half, tokens // 2)
        self.chunks = tokens // 2 // self.half
        self.per = self.half // BLK
        self.rows = 2 * self.half
        self.xp = 2 * self.hp + 2 * self.pairs + self.odd
        self.cp = 2 * self.pairs + self.odd
        self.blocks = groups * tokens // BLK
        self.own = (2 * self.hp + self.hp) * HD
        self.cols = groups * self.own
        self.ctx = groups * self.hp * HD

    def x_shape(self):
        return (self.groups, self.chunks, self.xp, self.per, BLK, WIDE)

    def c_shape(self):
        return (self.groups, self.chunks, self.cp, self.per, BLK, WIDE)


def low(v):
    return jnp.concatenate([v, jnp.zeros_like(v)], 1)


def high(v):
    return jnp.concatenate([jnp.zeros_like(v), v], 1)


def diag(a, b):
    return jnp.concatenate(
        [jnp.concatenate([a, jnp.zeros_like(b)], 1), jnp.concatenate([jnp.zeros_like(a), b], 1)], 0
    )


def spots(plan, h, i):
    per = plan.per
    xb = (i // per) * (plan.xp * per) + i % per
    cb = (i // per) * (plan.cp * per) + i % per
    if h < 2 * plan.pairs:
        lanes = slice((h % 2) * HD, (h % 2 + 1) * HD)
        x0 = xb + (2 * plan.hp + 2 * (h // 2)) * per
        c0 = cb + 2 * (h // 2) * per
        return ((x0, lanes), (x0 + per, lanes)), ((c0, lanes), (c0 + per, lanes))
    x0 = xb + (2 * plan.hp + 2 * plan.pairs) * per
    c0 = cb + 2 * plan.pairs * per
    first, second = slice(0, HD), slice(HD, WIDE)
    return ((x0, first), (x0, second)), ((c0, first), (c0, second))


def listed(plan, x_ref, lists_ref, h, i):
    sides, places = [], []
    for side in range(2):
        at = ((h * (plan.blocks // 2) + i) * 2 + side) * LISTED
        ids = [lists_ref[at + n] for n in range(LISTED)]
        sides.append(jnp.concatenate([x_ref[n] for n in ids], 0))
        places.append(ids)
    return jnp.concatenate(sides, 1), places


def run_pairs(count, hp, first, second, third):
    for h in range(hp):
        first(0, h, 0)

    def body(i, carry):
        for u in range(2):
            t = 2 * i + u
            for h in range(hp):
                first(jnp.minimum(t + 1, count - 1), h, 1 - u)
                second(h, u)
                third(jnp.maximum(t - 1, 0), h, 1 - u)
        return carry

    lax.fori_loop(0, count // 2, body, 0)
    for h in range(hp):
        third(count - 1, h, 1)


def keys_of(plan, x_ref, h, n):
    per = plan.per
    at = (n * plan.xp + 2 * h) * per
    return pl.ds(at, 2 * per)


def attn_fwd_kernel(plan, lists_ref, x_ref, o_ref, s_ref, p_ref, g_ref, a_ref):
    c = LOG2E * HD**-0.5
    hp, count = plan.hp, plan.blocks // 2
    heads = range(hp)

    def stage_s(i, h, slot):
        kv, _ = listed(plan, x_ref, lists_ref, h, i)
        ((xa, la), (xb, lb)), _ = spots(plan, h, i)
        s_ref[slot, h] = dot(kv, diag(low(x_ref[xa, :, la]), low(x_ref[xb, :, lb])), NT)

    def stage_p(h, slot):
        s = s_ref[slot, h]
        m = jnp.max(s, 0, keepdims=True)
        e = jnp.exp2(s * c - m * c)
        inv = 1.0 / jnp.sum(e, 0, keepdims=True)
        p_ref[slot, h] = (e * inv).astype(BF)

    def stage_c(i, h, slot):
        kv, _ = listed(plan, x_ref, lists_ref, h, i)
        _, ((ca, la), (cb, lb)) = spots(plan, h, i)
        ctx = dot(p_ref[slot, h], kv, TN)
        o_ref[ca, :, la] = ctx[:BLK, HD:WIDE].astype(BF)
        o_ref[cb, :, lb] = ctx[BLK:, WIDE + HD :].astype(BF)

    p_ref[...] = jnp.zeros_like(p_ref)
    run_pairs(count, hp, stage_s, stage_p, stage_c)
    size = plan.rows
    steps = plan.groups * plan.chunks
    ws, outs = [], []
    for h in heads:
        ((xa, la), _), (c_first, _) = spots(plan, h, 0)
        (_, (xb, lb)), (_, c_last) = spots(plan, h, count - 1)
        ws.append(low(jnp.concatenate([x_ref[xa, :, la], x_ref[xb, :, lb]], 0)))
        outs.append((c_first, c_last))

    def chunk(n):
        return pl.ds(pl.multiple_of(n * size, size), size)

    def keys(h, n):
        return x_ref[keys_of(plan, x_ref, h, n)].reshape(size, WIDE)

    def one(n, ms):
        out = []
        for h in heads:
            s = dot(keys(h, n), ws[h], NT)
            g_ref[h, chunk(n), :] = s
            out.append(jnp.maximum(ms[h], jnp.max(s, 0, keepdims=True)))
        return tuple(out)

    ms = lax.fori_loop(
        0, steps, one, tuple(jnp.full((1, 2 * BLK), -jnp.inf, F32) for h in heads), unroll=2
    )

    def two(n, ls):
        out = []
        for h in heads:
            e = jnp.exp2(g_ref[h, chunk(n), :] * c - ms[h] * c)
            g_ref[h, chunk(n), :] = e
            out.append(ls[h] + jnp.sum(e, 0, keepdims=True))
        return tuple(out)

    ls = lax.fori_loop(0, steps, two, tuple(jnp.zeros((1, 2 * BLK), F32) for h in heads), unroll=2)
    invs = [1.0 / l for l in ls]
    a_ref[...] = jnp.zeros_like(a_ref)

    def three(n, carry):
        for h in heads:
            p = g_ref[h, chunk(n), :] * invs[h]
            hi = p.astype(BF)
            lo = (p - hi.astype(F32)).astype(BF)
            a_ref[h] += dot(jnp.concatenate([hi, lo], 1), keys(h, n), TN)
        return carry

    lax.fori_loop(0, steps, three, 0, unroll=2)
    for h in heads:
        ctx = (a_ref[h, : 2 * BLK, :] + a_ref[h, 2 * BLK :, :])[:, HD:].astype(BF)
        (ca, la), (cb, lb) = outs[h]
        o_ref[ca, :, la] = ctx[:BLK]
        o_ref[cb, :, lb] = ctx[BLK:]


def attn_fwd(plan, lists, x):
    flat = x.reshape(-1, BLK, WIDE)
    blocks = plan.groups * plan.chunks * plan.cp * plan.per
    keys = plan.blocks * BLK
    return pl.pallas_call(
        partial(attn_fwd_kernel, plan),
        out_shape=jax.ShapeDtypeStruct((blocks, BLK, WIDE), BF),
        in_specs=[pl.BlockSpec(memory_space=pltpu.SMEM), pl.BlockSpec(memory_space=VMEM)],
        out_specs=pl.BlockSpec(memory_space=VMEM),
        scratch_shapes=[
            VMEM((2, plan.hp, KEYS, 2 * BLK), F32),
            VMEM((2, plan.hp, KEYS, 2 * BLK), BF),
            VMEM((plan.hp, keys, 2 * BLK), F32),
            VMEM((plan.hp, 4 * BLK, WIDE), F32),
        ],
        compiler_params=pltpu.CompilerParams(vmem_limit_bytes=48 << 20),
        cost_estimate=pl.CostEstimate(flops=26 * 10**9, bytes_accessed=6 * 10**6, transcendentals=6 * 10**6),
        name="attn_fwd",
    )(lists, flat).reshape(plan.c_shape())


def attn_bwd_kernel(plan, lists_ref, x_ref, d_ref, o_ref, acc_ref, s_ref, p_ref, g_ref):
    scale = HD**-0.5
    c = LOG2E * scale
    hp, count = plan.hp, plan.blocks // 2
    heads = range(hp)
    acc_ref[...] = jnp.zeros_like(acc_ref)

    def weights(i, h):
        ((xa, xla), (xb, xlb)), ((ca, cla), (cb, clb)) = spots(plan, h, i)
        da, db = d_ref[ca, :, cla], d_ref[cb, :, clb]
        da = jnp.where(i == 0, jnp.zeros_like(da), da)
        db = jnp.where(i == count - 1, jnp.zeros_like(db), db)
        return jnp.concatenate(
            [diag(low(x_ref[xa, :, xla]), low(x_ref[xb, :, xlb])), diag(high(da), high(db))], 0
        )

    def stage_s(i, h, slot):
        kv, _ = listed(plan, x_ref, lists_ref, h, i)
        s_ref[slot, h] = dot(kv, weights(i, h), NT)

    def stage_p(h, slot):
        s = s_ref[slot, h, :, : 2 * BLK]
        g = s_ref[slot, h, :, 2 * BLK :]
        m = jnp.max(s, 0, keepdims=True)
        e = jnp.exp2(s * c - m * c)
        inv = 1.0 / jnp.sum(e, 0, keepdims=True)
        delta = jnp.sum(e * g, 0, keepdims=True) * inv
        p = e * inv
        p_ref[slot, h, :, : 2 * BLK] = (p * (g - delta)).astype(BF)
        p_ref[slot, h, :, 2 * BLK :] = p.astype(BF)

    def stage_c(i, h, slot):
        kv, places = listed(plan, x_ref, lists_ref, h, i)
        ((xa, la), (xb, lb)), _ = spots(plan, h, i)
        dq = dot(p_ref[slot, h, :, : 2 * BLK], kv, TN) * scale
        o_ref[xa, :, la] = dq[:BLK, :HD].astype(BF)
        o_ref[xb, :, lb] = dq[BLK:, WIDE : WIDE + HD].astype(BF)
        dkv = dot(p_ref[slot, h], weights(i, h), NN)
        for side in range(2):
            part = dkv[:, side * WIDE : (side + 1) * WIDE]
            for n in range(LISTED):
                acc_ref[places[side][n]] += part[n * BLK : (n + 1) * BLK]

    p_ref[...] = jnp.zeros_like(p_ref)
    run_pairs(count, hp, stage_s, stage_p, stage_c)
    lane_scale = jnp.where(
        lax.broadcasted_iota(jnp.int32, (1, WIDE), 1) < HD, scale, 1.0
    ).astype(F32)
    size = plan.rows
    steps = plan.groups * plan.chunks

    def chunk(n):
        return pl.ds(pl.multiple_of(n * size, size), size)

    for h in heads:
        ((xa, xla), _), ((ca, cla), _) = spots(plan, h, 0)
        (_, (xb, xlb)), (_, (cb, clb)) = spots(plan, h, count - 1)
        q = low(jnp.concatenate([x_ref[xa, :, xla], x_ref[xb, :, xlb]], 0))
        d = high(jnp.concatenate([d_ref[ca, :, cla], d_ref[cb, :, clb]], 0))
        w = jnp.concatenate([q, d], 0)
        three_w = jnp.concatenate([q, d, d], 0)

        def keys(n):
            return x_ref[keys_of(plan, x_ref, h, n)].reshape(size, WIDE)

        def one(n, m):
            s = dot(keys(n), w, NT)
            g_ref[chunk(n), :] = s
            return jnp.maximum(m, jnp.max(s[:, : 2 * BLK], 0, keepdims=True))

        m = lax.fori_loop(0, steps, one, jnp.full((1, 2 * BLK), -jnp.inf, F32), unroll=4)

        def two(n, state):
            l, eg = state
            e = jnp.exp2(g_ref[chunk(n), : 2 * BLK] * c - m * c)
            g_ref[chunk(n), : 2 * BLK] = e
            return (
                l + jnp.sum(e, 0, keepdims=True),
                eg + jnp.sum(e * g_ref[chunk(n), 2 * BLK :], 0, keepdims=True),
            )

        l, eg = lax.fori_loop(0, steps, two, (jnp.zeros((1, 2 * BLK), F32),) * 2, unroll=4)
        inv = 1.0 / l
        delta = eg * inv

        def three(n, dq):
            p = g_ref[chunk(n), : 2 * BLK] * inv
            ds = (p * (g_ref[chunk(n), 2 * BLK :] - delta)).astype(BF)
            hi = p.astype(BF)
            lo = (p - hi.astype(F32)).astype(BF)
            dkv = dot(jnp.concatenate([ds, hi, lo], 1), three_w, NN)
            where = keys_of(plan, x_ref, h, n)
            total = acc_ref[where].reshape(size, WIDE) + dkv
            o_ref[where] = (total * lane_scale).astype(BF).reshape(2 * plan.per, BLK, WIDE)
            return dq + dot(ds, keys(n), TN)

        dq = lax.fori_loop(0, steps, three, jnp.zeros((2 * BLK, WIDE), F32), unroll=4)
        dq = (dq[:, :HD] * scale).astype(BF)
        o_ref[xa, :, xla] = dq[:BLK]
        o_ref[xb, :, xlb] = dq[BLK:]


def attn_bwd(plan, lists, x, d):
    flat = x.reshape(-1, BLK, WIDE)
    keys = plan.blocks * BLK
    return pl.pallas_call(
        partial(attn_bwd_kernel, plan),
        out_shape=jax.ShapeDtypeStruct(flat.shape, BF),
        in_specs=[pl.BlockSpec(memory_space=pltpu.SMEM)] + [pl.BlockSpec(memory_space=VMEM)] * 2,
        out_specs=pl.BlockSpec(memory_space=VMEM),
        scratch_shapes=[
            VMEM(flat.shape, F32),
            VMEM((2, plan.hp, KEYS, 4 * BLK), F32),
            VMEM((2, plan.hp, KEYS, 4 * BLK), BF),
            VMEM((keys, 4 * BLK), F32),
        ],
        compiler_params=pltpu.CompilerParams(vmem_limit_bytes=56 << 20),
        cost_estimate=pl.CostEstimate(flops=46 * 10**9, bytes_accessed=12 * 10**6, transcendentals=6 * 10**6),
        name="attn_bwd",
    )(lists, flat, d.reshape(-1, BLK, WIDE)).reshape(plan.x_shape())


def mean(v):
    return jnp.sum(v, -1, keepdims=True) * (1.0 / v.shape[-1])


def normalise(resid):
    centre = resid - mean(resid)
    inv = lax.rsqrt(mean(centre * centre) + epsilon)
    return centre * inv, inv


def norm_back(unit, inv, gain, grad):
    g = grad * gain
    return inv * (g - mean(g) - unit * mean(g * unit))


def gelu_parts(u):
    k = 0.7978845608028654
    sq = u * u
    t = jnp.tanh(k * (u + 0.044715 * (u * sq)))
    half = 0.5 * (1.0 + t)
    return half * u, half + 0.5 * u * (1.0 - t * t) * (k + (3 * 0.044715 * k) * sq)


def rows_of(ref):
    return ref[...].reshape(-1, ref.shape[-1])


def pick_context(plan, pieces):
    half = plan.half
    tiles = []
    for g in range(plan.groups):
        for p in range(plan.pairs):
            tiles.append(pieces[g, 2 * p : 2 * p + 2].reshape(plan.rows, WIDE))
        if plan.odd:
            both = pieces[g, 2 * plan.pairs].reshape(half, WIDE)
            tiles.append(jnp.concatenate([both[:, :HD], both[:, HD:]], 0))
    return jnp.concatenate(tiles, 1)[:, :D]


def put_context(plan, value, ref):
    half, per = plan.half, plan.per
    if plan.ctx > D:
        value = jnp.concatenate([value, jnp.zeros((value.shape[0], plan.ctx - D), value.dtype)], 1)
    for g in range(plan.groups):
        at = g * plan.hp * HD
        for p in range(plan.pairs):
            ref[g, 2 * p : 2 * p + 2] = value[:, at : at + WIDE].reshape(2, per, BLK, WIDE)
            at += WIDE
        if plan.odd:
            one = value[:, at : at + HD]
            ref[g, 2 * plan.pairs] = jnp.concatenate([one[:half], one[half:]], 1).reshape(per, BLK, WIDE)


def put_heads(plan, value, ref):
    half, per, hp = plan.half, plan.per, plan.hp
    pairs_at = plan.groups * hp * WIDE
    single_at = pairs_at + plan.groups * plan.pairs * WIDE
    for g in range(plan.groups):
        for h in range(hp):
            at = (g * hp + h) * WIDE
            ref[g, 2 * h : 2 * h + 2] = value[:, at : at + WIDE].reshape(2, per, BLK, WIDE)
        for p in range(plan.pairs):
            at = pairs_at + (g * plan.pairs + p) * WIDE
            ref[g, 2 * hp + 2 * p : 2 * hp + 2 * p + 2] = value[:, at : at + WIDE].reshape(2, per, BLK, WIDE)
        if plan.odd:
            at = single_at + g * HD
            one = value[:, at : at + HD]
            ref[g, plan.xp - 1] = jnp.concatenate([one[:half], one[half:]], 1).reshape(per, BLK, WIDE)


def pick_heads(plan, pieces):
    half, hp = plan.half, plan.hp
    kv, pairs, singles = [], [], []
    for g in range(pieces.shape[0]):
        for h in range(hp):
            kv.append(pieces[g, 2 * h : 2 * h + 2].reshape(plan.rows, WIDE))
        for p in range(plan.pairs):
            pairs.append(pieces[g, 2 * hp + 2 * p : 2 * hp + 2 * p + 2].reshape(plan.rows, WIDE))
        if plan.odd:
            both = pieces[g, plan.xp - 1].reshape(half, WIDE)
            singles.append(jnp.concatenate([both[:, :HD], both[:, HD:]], 0))
    return jnp.concatenate(kv + pairs + singles, 1)


def whole(shape):
    return pl.BlockSpec(shape, lambda *i: (0,) * len(shape), pipeline_mode=pl.Buffered(1))


def own_kernel(plan, a_ref, w_ref, b_ref, o_ref):
    a = a_ref[...].reshape(plan.rows, D)
    y = (dot(a, rows_of(w_ref), NN) + b_ref[...]).astype(BF)
    one = Plan.__new__(Plan)
    one.__dict__.update(plan.__dict__)
    one.groups = 1
    put_heads(one, y, o_ref.at[:, 0])


def own_heads(plan, hidden_all, weight, bias):
    a = hidden_all.reshape(plan.groups, 2, plan.chunks, plan.half, D)
    return pl.pallas_call(
        partial(own_kernel, plan),
        out_shape=jax.ShapeDtypeStruct(plan.x_shape(), BF),
        grid=(plan.groups, plan.chunks),
        in_specs=[
            pl.BlockSpec((1, 2, 1, plan.half, D), lambda g, c: (g, 0, c, 0, 0)),
            whole(weight.shape),
            whole(bias.shape),
        ],
        out_specs=pl.BlockSpec((1, 1) + plan.x_shape()[2:], lambda g, c: (g, c, 0, 0, 0, 0)),
        compiler_params=pltpu.CompilerParams(vmem_limit_bytes=48 << 20),
        cost_estimate=pl.CostEstimate(flops=7 * 10**9, bytes_accessed=12 * 10**6, transcendentals=0),
        name="own_heads",
    )(a, weight, bias)


def own_grad_kernel(plan, item, steps, a_ref, d_ref, o_ref, acc_ref, sum_ref):
    n = pl.program_id(0) * plan.chunks + pl.program_id(1)

    @pl.when(n == 0)
    def _():
        acc_ref[...] = jnp.zeros_like(acc_ref)
        sum_ref[...] = jnp.zeros_like(sum_ref)

    d = pick_heads(plan, d_ref[:, 0])
    acc_ref[...] += dot(a_ref[...].reshape(plan.rows, D), d, TN)
    sum_ref[...] += jnp.sum(d.astype(F32).reshape(-1, 8, d.shape[1]), 0)

    @pl.when(n == steps - 1)
    def _():
        share = D // item
        total = jnp.broadcast_to(jnp.sum(sum_ref[...], 0, keepdims=True), (16, sum_ref.shape[1])).astype(BF)
        for r in range(item):
            o_ref[r, :share] = acc_ref[r * share : (r + 1) * share].astype(BF)
            o_ref[r, share:] = total


def own_grad(plan, item, hidden_all, dx):
    a = hidden_all.reshape(plan.groups, 2, plan.chunks, plan.half, D)
    return pl.pallas_call(
        partial(own_grad_kernel, plan, item, plan.groups * plan.chunks),
        out_shape=jax.ShapeDtypeStruct((item, D // item + 16, plan.own), BF),
        grid=(plan.groups, plan.chunks),
        in_specs=[
            pl.BlockSpec((1, 2, 1, plan.half, D), lambda g, c: (g, 0, c, 0, 0)),
            pl.BlockSpec((1, 1) + plan.x_shape()[2:], lambda g, c: (g, c, 0, 0, 0, 0)),
        ],
        out_specs=whole((item, D // item + 16, plan.own)),
        scratch_shapes=[VMEM((D, plan.own), F32), VMEM((8, plan.own), F32)],
        compiler_params=pltpu.CompilerParams(vmem_limit_bytes=48 << 20),
        cost_estimate=pl.CostEstimate(flops=7 * 10**9, bytes_accessed=12 * 10**6, transcendentals=0),
        name="own_grad",
    )(a, dx)


def halves(plan, width):
    return pl.BlockSpec((2, plan.half, width), lambda c: (0, c, 0))


def cut(plan, v):
    return v.reshape(2, plan.tokens // 2, v.shape[-1])


def read(ref):
    return ref[...].reshape(-1, ref.shape[-1])


def write(ref, value):
    ref[...] = value.reshape(ref.shape).astype(ref.dtype)


class Packed:
    def __init__(self, ref, ff):
        self.ref = ref
        self.item = ref.shape[0]
        self.share = D // self.item
        self.parts = ff // D

    def rows(self, first):
        return self.ref[:, first : first + self.share].reshape(D, D)

    def out(self):
        return self.rows(0)

    def ffn_in(self, n):
        return self.rows(self.share * (1 + n))

    def ffn_out(self, n):
        ranks = self.item // self.parts
        first = self.share * (1 + self.parts)
        return self.ref[n * ranks : (n + 1) * ranks, first : first + self.share * self.parts].reshape(D, D)

    def columns(self, n):
        return self.rows(self.share * (1 + 2 * self.parts + n))


def wide_parts(w):
    return jnp.concatenate([w[:, n : n + D] for n in range(0, w.shape[1], D)])


OUT_BIAS, GAIN1, SHIFT1, FFN_BIAS, GAIN2, SHIFT2 = range(6)


def first_half(plan, ctx, h, w, vec_ref):
    r1 = h + dot(ctx, w.out(), NN) + vec_ref[OUT_BIAS : OUT_BIAS + 1]
    unit1, inv1 = normalise(r1)
    y1 = unit1 * vec_ref[GAIN1 : GAIN1 + 1] + vec_ref[SHIFT1 : SHIFT1 + 1]
    return r1, unit1, inv1, y1, y1.astype(BF)


def part_of(n):
    return slice(n * D, (n + 1) * D)


def put(ref, n, value):
    ref[:, :, part_of(n)] = value.reshape(ref.shape[:2] + (D,)).astype(ref.dtype)


def get(ref, n):
    return ref[:, :, part_of(n)].reshape(-1, D)


def fwd_kernel(plan, ff, c_ref, h_ref, w_ref, vec_ref, inner_ref, bias_ref,
               x_ref, next_ref, next_low_ref, r1_ref, r2_ref, u_ref, y_ref, ctx_ref):
    w = Packed(w_ref, ff)
    ctx = pick_context(plan, c_ref[:, 0])
    write(ctx_ref, ctx)
    r1, _, _, y1, y1_low = first_half(plan, ctx, read(h_ref), w, vec_ref)
    write(r1_ref, r1)
    write(y_ref, y1_low)
    r2 = y1 + vec_ref[FFN_BIAS : FFN_BIAS + 1]
    for n in range(w.parts):
        u = dot(y1_low, w.ffn_in(n), NN) + inner_ref[:, part_of(n)]
        put(u_ref, n, u)
        r2 = r2 + dot(gelu_parts(u)[0].astype(BF), w.ffn_out(n), NN)
    write(r2_ref, r2)
    unit2, _ = normalise(r2)
    nxt = unit2 * vec_ref[GAIN2 : GAIN2 + 1] + vec_ref[SHIFT2 : SHIFT2 + 1]
    low_ = nxt.astype(BF)
    write(next_ref, nxt)
    write(next_low_ref, low_)
    y = [
        (dot(low_, w.columns(n), NN) + bias_ref[:, part_of(n)]).astype(BF) for n in range(plan.cols // D)
    ]
    put_heads(plan, jnp.concatenate(y, 1), x_ref.at[:, 0])


def piece_spec(shape):
    return pl.BlockSpec((shape[0], 1) + shape[2:], lambda c: (0, c, 0, 0, 0, 0))


def layer_fwd(plan, ctx, h, packed, vec, inner, bias):
    t = (2, plan.tokens // 2)
    ff = inner.shape[-1]
    shapes = [(D, F32), (D, BF), (D, F32), (D, F32), (ff, F32), (D, BF), (D, BF)]
    return pl.pallas_call(
        partial(fwd_kernel, plan, ff),
        out_shape=[jax.ShapeDtypeStruct(plan.x_shape(), BF)] + [jax.ShapeDtypeStruct(t + (n,), d) for n, d in shapes],
        grid=(plan.chunks,),
        in_specs=[piece_spec(plan.c_shape()), halves(plan, D)]
        + [whole(w.shape) for w in (packed, vec, inner, bias)],
        out_specs=[piece_spec(plan.x_shape())] + [halves(plan, n) for n, _ in shapes],
        compiler_params=pltpu.CompilerParams(vmem_limit_bytes=60 << 20),
        cost_estimate=pl.CostEstimate(flops=30 * 10**9, bytes_accessed=50 * 10**6, transcendentals=3 * 10**6),
        name="layer_fwd",
    )(ctx, cut(plan, h), packed, vec, inner, bias)


SUM_DO, D_GAIN1, D_SHIFT1, SUM_DF, D_GAIN2, D_SHIFT2 = range(6)


def add_sums(ref, at, value):
    ref[at] += jnp.sum(value.reshape(-1, 8, value.shape[-1]), 0)


def back_chunk(plan, gy, unit1, inv1, unit2, inv2, gate, w, vec_ref, sums_ref, inner_sum_ref, du_ref):
    @pl.when(pl.program_id(0) == 0)
    def _():
        sums_ref[...] = jnp.zeros_like(sums_ref)
        inner_sum_ref[...] = jnp.zeros_like(inner_sum_ref)

    dr2 = norm_back(unit2, inv2, vec_ref[GAIN2 : GAIN2 + 1], gy)
    df = dr2.astype(BF)
    dy1 = dr2
    for n in range(w.parts):
        du = (dot(df, w.ffn_out(n), NT) * gate(n)).astype(BF)
        put(du_ref, n, du)
        dy1 = dy1 + dot(du, w.ffn_in(n), NT)
        inner_sum_ref[:, part_of(n)] += jnp.sum(du.astype(F32).reshape(-1, 8, D), 0)
    dr1 = norm_back(unit1, inv1, vec_ref[GAIN1 : GAIN1 + 1], dy1)
    do = dr1.astype(BF)
    dc = dot(do, w.out(), NT).astype(BF)
    add_sums(sums_ref, SUM_DO, do.astype(F32))
    add_sums(sums_ref, D_GAIN1, dy1 * unit1)
    add_sums(sums_ref, D_SHIFT1, dy1)
    add_sums(sums_ref, SUM_DF, df.astype(F32))
    add_sums(sums_ref, D_GAIN2, gy * unit2)
    add_sums(sums_ref, D_SHIFT2, gy)
    return df, dr1, do, dc


def mid_kernel(plan, ff, c_ref, h_ref, gy_ref, w_ref, vec_ref, inner_ref,
               d_ref, out_ref, dr1_ref, gz_ref, du_ref, df_ref, do_ref, y_ref, ctx_ref, sums_ref, inner_sum_ref, gate_ref):
    w = Packed(w_ref, ff)
    ctx = pick_context(plan, c_ref[:, 0])
    write(ctx_ref, ctx)
    _, unit1, inv1, y1, y1_low = first_half(plan, ctx, read(h_ref), w, vec_ref)
    write(y_ref, y1_low)
    r2 = y1 + vec_ref[FFN_BIAS : FFN_BIAS + 1]
    for n in range(w.parts):
        u = dot(y1_low, w.ffn_in(n), NN) + inner_ref[:, part_of(n)]
        gz, gate_ref[n] = gelu_parts(u)
        gz = gz.astype(BF)
        put(gz_ref, n, gz)
        r2 = r2 + dot(gz, w.ffn_out(n), NN)
    unit2, inv2 = normalise(r2)
    write(out_ref, unit2 * vec_ref[GAIN2 : GAIN2 + 1] + vec_ref[SHIFT2 : SHIFT2 + 1])
    df, dr1, do, dc = back_chunk(plan, read(gy_ref), unit1, inv1, unit2, inv2, lambda n: gate_ref[n],
                                 w, vec_ref, sums_ref, inner_sum_ref, du_ref)
    put_context(plan, dc, d_ref.at[:, 0])
    write(dr1_ref, dr1)
    write(df_ref, df)
    write(do_ref, do)


def sum_specs(ff):
    return (
        [jax.ShapeDtypeStruct((6, 8, D), F32), jax.ShapeDtypeStruct((8, ff), F32)],
        [pl.BlockSpec((6, 8, D), lambda c: (0, 0, 0)), pl.BlockSpec((8, ff), lambda c: (0, 0))],
    )


def layer_mid(plan, ctx, h, gy, packed, vec, inner):
    t = (2, plan.tokens // 2)
    ff = inner.shape[-1]
    shapes = [(D, F32), (D, F32), (ff, BF), (ff, BF), (D, BF), (D, BF), (D, BF), (D, BF)]
    sums, sums_at = sum_specs(ff)
    return pl.pallas_call(
        partial(mid_kernel, plan, ff),
        out_shape=[jax.ShapeDtypeStruct(plan.c_shape(), BF)] + [jax.ShapeDtypeStruct(t + (n,), d) for n, d in shapes] + sums,
        grid=(plan.chunks,),
        in_specs=[piece_spec(plan.c_shape()), halves(plan, D), halves(plan, D)]
        + [whole(w.shape) for w in (packed, vec, inner)],
        out_specs=[piece_spec(plan.c_shape())] + [halves(plan, n) for n, _ in shapes] + sums_at,
        scratch_shapes=[VMEM((ff // D, plan.rows, D), F32)],
        compiler_params=pltpu.CompilerParams(vmem_limit_bytes=60 << 20),
        cost_estimate=pl.CostEstimate(flops=45 * 10**9, bytes_accessed=50 * 10**6, transcendentals=3 * 10**6),
        name="layer_mid",
    )(ctx, cut(plan, h), cut(plan, gy), packed, vec, inner)


def bwd_kernel(plan, ff, dx_ref, up_ref, r1_ref, r2_ref, u_ref, w_ref, vec_ref,
               d_ref, dr1_ref, gz_ref, du_ref, df_ref, do_ref, dqkv_ref, sums_ref, inner_sum_ref, qkv_sum_ref):
    w = Packed(w_ref, ff)
    dqkv = pick_heads(plan, dx_ref[:, 0])
    write(dqkv_ref, dqkv)
    gy = read(up_ref)
    for n in range(plan.cols // D):
        gy = gy + dot(dqkv[:, part_of(n)], w.columns(n), NT)

    @pl.when(pl.program_id(0) == 0)
    def _():
        qkv_sum_ref[...] = jnp.zeros_like(qkv_sum_ref)

    qkv_sum_ref[...] += jnp.sum(dqkv.astype(F32).reshape(-1, 8, dqkv.shape[-1]), 0)
    unit1, inv1 = normalise(read(r1_ref))
    unit2, inv2 = normalise(read(r2_ref))

    def gate(n):
        gz, value = gelu_parts(get(u_ref, n))
        put(gz_ref, n, gz)
        return value

    df, dr1, do, dc = back_chunk(plan, gy, unit1, inv1, unit2, inv2, gate, w, vec_ref, sums_ref, inner_sum_ref, du_ref)
    put_context(plan, dc, d_ref.at[:, 0])
    write(dr1_ref, dr1)
    write(df_ref, df)
    write(do_ref, do)


def layer_bwd(plan, dx, up, r1, r2, u, packed, vec):
    t = (2, plan.tokens // 2)
    ff = u.shape[-1]
    shapes = [(D, F32), (ff, BF), (ff, BF), (D, BF), (D, BF), (plan.cols, BF)]
    sums, sums_at = sum_specs(ff)
    sums = sums + [jax.ShapeDtypeStruct((8, plan.cols), F32)]
    sums_at = sums_at + [pl.BlockSpec((8, plan.cols), lambda c: (0, 0))]
    return pl.pallas_call(
        partial(bwd_kernel, plan, ff),
        out_shape=[jax.ShapeDtypeStruct(plan.c_shape(), BF)] + [jax.ShapeDtypeStruct(t + (n,), d) for n, d in shapes] + sums,
        grid=(plan.chunks,),
        in_specs=[piece_spec(plan.x_shape()), halves(plan, D), halves(plan, D), halves(plan, D), halves(plan, ff)]
        + [whole(w.shape) for w in (packed, vec)],
        out_specs=[piece_spec(plan.c_shape())] + [halves(plan, n) for n, _ in shapes] + sums_at,
        compiler_params=pltpu.CompilerParams(vmem_limit_bytes=60 << 20),
        cost_estimate=pl.CostEstimate(flops=40 * 10**9, bytes_accessed=50 * 10**6, transcendentals=3 * 10**6),
        name="layer_bwd",
    )(dx, up, r1, r2, u, packed, vec)


def dense_grad_kernel(item, gz_ref, df_ref, y_ref, du_ref, ctx_ref, do_ref, vec_ref, fo_ref, rest_ref):
    n = pl.program_id(0)
    parts = pl.num_programs(0)
    share = D // item
    ranks = item // parts
    fo_ref[...] = dot(gz_ref[...], df_ref[...], TN).astype(BF).reshape(fo_ref.shape)
    first = pl.multiple_of(n * share, 16)
    rest_ref[:, pl.ds(first, share)] = dot(y_ref[...], du_ref[...], TN).astype(BF).reshape(item, share, D)

    @pl.when(n == parts - 1)
    def _():
        at = parts * share
        rest_ref[:, at : at + share] = dot(ctx_ref[...], do_ref[...], TN).astype(BF).reshape(item, share, D)
        rest_ref[:, at + share :] = vec_ref[...]


def dense_grads(item, gz, df, y, du, ctx, do, vecs):
    tokens, ff = gz.shape
    parts = ff // D
    share = D // item
    rest = parts * share + share + vecs.shape[1]
    column = pl.BlockSpec((tokens, D), lambda n: (0, n))
    return pl.pallas_call(
        partial(dense_grad_kernel, item),
        out_shape=[jax.ShapeDtypeStruct((item, ff // item, D), BF), jax.ShapeDtypeStruct((item, rest, D), BF)],
        grid=(parts,),
        in_specs=[column, whole(df.shape), whole(y.shape), column, whole(ctx.shape), whole(do.shape), whole(vecs.shape)],
        out_specs=[pl.BlockSpec((item // parts, ff // item, D), lambda n: (n, 0, 0)), whole((item, rest, D))],
        compiler_params=pltpu.CompilerParams(vmem_limit_bytes=56 << 20),
        cost_estimate=pl.CostEstimate(flops=14 * 10**9, bytes_accessed=30 * 10**6, transcendentals=0),
        name="dense_grads",
    )(gz, df, y, du, ctx, do, vecs)


def column_grad_kernel(item, a_ref, d_ref, vec_ref, o_ref):
    n = pl.program_id(0)
    share = D // item
    first = pl.multiple_of(n * share, 16)
    o_ref[:, pl.ds(first, share)] = dot(a_ref[...], d_ref[...], TN).astype(BF).reshape(item, share, D)

    @pl.when(n == pl.num_programs(0) - 1)
    def _():
        o_ref[:, o_ref.shape[1] - vec_ref.shape[1] :] = vec_ref[...]


def column_grads(item, a, d, vecs):
    tokens = a.shape[0]
    parts = d.shape[1] // D
    out = (item, parts * (D // item) + vecs.shape[1], D)
    return pl.pallas_call(
        partial(column_grad_kernel, item),
        out_shape=jax.ShapeDtypeStruct(out, BF),
        grid=(parts,),
        in_specs=[whole(a.shape), pl.BlockSpec((tokens, D), lambda n: (0, n)), whole(vecs.shape)],
        out_specs=whole(out),
        compiler_params=pltpu.CompilerParams(vmem_limit_bytes=48 << 20),
        cost_estimate=pl.CostEstimate(flops=6 * 10**9, bytes_accessed=10 * 10**6, transcendentals=0),
        name="column_grads",
    )(a, d, vecs)


def tail_kernel(plan, dx_ref, up_ref, w_ref, o_ref):
    dqkv = pick_heads(plan, dx_ref[:, 0])
    share = D // w_ref.shape[0]
    out = read(up_ref)
    for n in range(plan.cols // D):
        out = out + dot(dqkv[:, part_of(n)], w_ref[:, n * share : (n + 1) * share].reshape(D, D), NT)
    write(o_ref, out)


def layer_tail(plan, dx, up, w_qkv):
    return pl.pallas_call(
        partial(tail_kernel, plan),
        out_shape=jax.ShapeDtypeStruct(up.shape, F32),
        grid=(plan.chunks,),
        in_specs=[piece_spec(plan.x_shape()), halves(plan, D), whole(w_qkv.shape)],
        out_specs=halves(plan, D),
        compiler_params=pltpu.CompilerParams(vmem_limit_bytes=48 << 20),
        cost_estimate=pl.CostEstimate(flops=8 * 10**9, bytes_accessed=12 * 10**6, transcendentals=0),
        name="layer_tail",
    )(dx, up, w_qkv)


def column_parts(plan, w):
    lead = w.shape[:-1]
    g, hp = plan.groups, plan.hp
    w = w.reshape(lead + (3, H, HD))
    w = jnp.pad(w, [(0, 0)] * (len(lead) + 1) + [(0, g * hp - H), (0, 0)])
    q, k, v = (w[..., n, :, :] for n in range(3))
    kv = jnp.stack([k, v], -2).reshape(lead + (g, hp * WIDE))
    q = q.reshape(lead + (g, hp, HD))
    pairs = q[..., : 2 * plan.pairs, :].reshape(lead + (g, plan.pairs * WIDE))
    last = q[..., 2 * plan.pairs :, :].reshape(lead + (g, plan.odd * HD))
    return kv, pairs, last


def all_columns(plan, w):
    lead = w.shape[:-1]
    return jnp.concatenate([p.reshape(lead + (-1,)) for p in column_parts(plan, w)], -1)


def own_columns(plan, w, rank):
    axis = w.ndim - 1
    return jnp.concatenate(
        [lax.dynamic_index_in_dim(p, rank, axis, False) for p in column_parts(plan, w)], -1
    )


def natural(plan, kv, pairs, last):
    lead = kv.shape[:-2]
    g, hp = plan.groups, plan.hp
    kv = kv.reshape(lead + (g * hp, 2, HD))
    q = jnp.concatenate(
        [pairs.reshape(lead + (g, 2 * plan.pairs, HD)), last.reshape(lead + (g, plan.odd, HD))], -2
    ).reshape(lead + (g * hp, HD))
    return jnp.concatenate(
        [p[..., :H, :].reshape(lead + (H * HD,)) for p in (q, kv[..., 0, :], kv[..., 1, :])], -1
    )


def from_all(plan, w):
    lead = w.shape[:-1]
    a = plan.groups * plan.hp * WIDE
    b = a + plan.groups * plan.pairs * WIDE
    return natural(plan, *(p.reshape(lead + (plan.groups, -1)) for p in (w[..., :a], w[..., a:b], w[..., b:])))


def from_own(plan, w):
    a = plan.hp * WIDE
    b = a + plan.pairs * WIDE
    w = jnp.moveaxis(w, 0, -2)
    return natural(plan, w[..., :a], w[..., a:b], w[..., b:])


def exchange(x):
    y = x.reshape((x.shape[0], -1, x.shape[-1]))
    return lax.all_to_all(y, "seq", split_axis=0, concat_axis=0, tiled=True).reshape(x.shape)


def tie(*args):
    return lax.optimization_barrier(args)


def key_table(plan, random_ids):
    n = plan.blocks
    here = n // plan.groups
    j = jnp.arange(n, dtype=jnp.int32)
    shared = jnp.stack(
        [jnp.maximum(j - 1, 0), j, jnp.minimum(j + 1, n - 1), jnp.zeros_like(j), jnp.full_like(j, n - 1)], 1
    )
    ids = jnp.concatenate([jnp.broadcast_to(shared[None], (plan.hp, n, 5)), random_ids], 2)
    inside = ids % here
    r = inside % (here // 2)
    head = jnp.arange(plan.hp, dtype=jnp.int32)[:, None, None]
    piece = 2 * head + inside // (here // 2)
    place = (((ids // here) * plan.chunks + r // plan.per) * plan.xp + piece) * plan.per + r % plan.per
    place = place.reshape(plan.hp, plan.groups, 2, here // 2, LISTED).transpose(0, 1, 3, 2, 4)
    return place.reshape(-1)


def local(
    hidden,
    block_lists,
    w_qkv,
    bias_query,
    bias_value,
    w_attn_out,
    bias_attn_out,
    norm1_gain,
    norm1_shift,
    w_ffn_in,
    bias_ffn_in,
    w_ffn_out,
    bias_ffn_out,
    norm2_gain,
    norm2_shift,
    cotangent,
):
    groups = lax.axis_size("seq")
    item = lax.axis_size("item")
    seq_rank = lax.axis_index("seq")
    item_rank = lax.axis_index("item")
    tokens = hidden.shape[1]
    plan = Plan(groups, tokens)
    here = tokens // BLK
    share = D // item
    hidden_low = hidden[0].astype(BF)
    hidden_all = exchange(jnp.broadcast_to(hidden_low[None], (groups, tokens, D)))
    hidden_all, block_lists = tie(hidden_all, block_lists)

    ids = jnp.pad(block_lists[0], ((0, 0), (0, 0), (0, groups * plan.hp - H), (0, 0)))
    ids = ids.reshape(LAYERS, here, groups, plan.hp * RAND).transpose(2, 0, 1, 3)
    ids = exchange(ids.reshape(groups, 1, -1)).reshape(groups, LAYERS, here, plan.hp, RAND)
    ids = ids.transpose(1, 3, 0, 2, 4).reshape(LAYERS, plan.hp, plan.blocks, RAND)
    tables = [key_table(plan, ids[layer]) for layer in range(LAYERS)]

    small = (bias_query, bias_value, bias_attn_out, norm1_gain, norm1_shift, bias_ffn_in, bias_ffn_out, norm2_gain, norm2_shift)
    packed = lax.all_gather(jnp.concatenate(small, 1), "item", axis=0).astype(F32)
    vectors = []
    for layer in range(LAYERS):
        at, out = 0, []
        for s in small:
            out.append(packed[:, layer, at : at + s.shape[1]].reshape(-1))
            at += s.shape[1]
        vectors.append(out)
    stacked = [jnp.stack(v[2:5] + v[6:9] + [v[2]] * 2) for v in vectors]
    inner = [v[5][None] for v in vectors]
    qkv_bias = [jnp.concatenate([v[0], jnp.zeros_like(v[0]), v[1]])[None] for v in vectors]

    own_weight = lax.all_gather(own_columns(plan, w_qkv[0], seq_rank), "item", axis=0)
    own_bias = own_columns(plan, qkv_bias[0], seq_rank)
    columns = wide_parts(all_columns(plan, w_qkv[0])), wide_parts(all_columns(plan, w_qkv[1]))

    def dense(layer):
        return [w_attn_out[layer], wide_parts(w_ffn_in[layer]), w_ffn_out[layer]]

    packed0 = lax.all_gather(jnp.concatenate(dense(0) + [columns[1]]), "item", axis=0)
    packed1 = lax.all_gather(jnp.concatenate(dense(1)), "item", axis=0)
    columns0 = lax.all_gather(columns[0], "item", axis=0)

    x0 = own_heads(plan, hidden_all, own_weight, own_bias)
    ctx0 = exchange(attn_fwd(plan, tables[0], x0))
    x1, h1, h1_low, r1, r2, u, y0, ctx0 = layer_fwd(
        plan, ctx0, hidden[0], packed0, stacked[0], inner[0], all_columns(plan, qkv_bias[1])
    )
    x1 = exchange(x1)
    ctx1 = exchange(attn_fwd(plan, tables[1], x1))
    d1, output, up1, gz1, du1, df1, do1, y1, ctx1, sums1, inner1 = layer_mid(
        plan, ctx1, h1, cotangent[0], packed1, stacked[1], inner[1]
    )

    def flat(a):
        return a.reshape(tokens, -1)

    def scattered(g):
        return lax.psum_scatter(g, "item", scatter_dimension=0, tiled=False)

    def rows_for(vecs):
        part = jnp.concatenate([v.reshape(item, -1) for v in vecs], 1)
        return jnp.pad(part, ((0, 0), (0, 16 * D - part.shape[1]))).reshape(item, 16, D).astype(BF)

    def split_rows(part, counts):
        values, at, out = part.reshape(-1), 0, []
        for n in counts:
            out.append(values[at : at + n])
            at += n
        return out

    def grads(gz, du, df, do, y, ctx, sums, inner_sum):
        sums = jnp.sum(sums, 1)
        vecs = (sums[SUM_DO], sums[D_GAIN1], sums[D_SHIFT1], jnp.sum(inner_sum, 0), sums[SUM_DF], sums[D_GAIN2], sums[D_SHIFT2])
        return dense_grads(item, flat(gz), flat(df), flat(y), flat(du), flat(ctx), flat(do), rows_for(vecs))

    def seq_parts(shares):
        rows = jnp.concatenate(shares)
        rows = jnp.pad(rows, ((0, -rows.shape[0] % (16 * groups)), (0, 0)))
        return jnp.sum(exchange(rows.reshape(groups, -1, D)).astype(F32), 0).astype(BF)

    def seq_gather(part):
        return exchange(jnp.broadcast_to(part[None], (groups,) + part.shape))

    def taken(full, shares):
        rows, at, out = full.reshape(-1, D), 0, []
        for p in shares:
            out.append(rows[at : at + p.shape[0]].astype(F32))
            at += p.shape[0]
        return out

    def unpart(rows):
        return jnp.concatenate([rows[n : n + share] for n in range(0, rows.shape[0], share)], 1)

    parts = w_ffn_in.shape[2] // D
    counts = [share] * 3 + [w_ffn_in.shape[2] // item] + [share] * 3
    dc1 = exchange(d1)
    fo1, rest1 = grads(gz1, du1, df1, do1, y1, ctx1, sums1, inner1)
    dc1, fo1, rest1 = tie(dc1, fo1, rest1)
    fo1, rest1 = scattered(fo1), scattered(rest1)
    dc1, columns0 = tie(dc1, columns0)
    dx1 = attn_bwd(plan, tables[1], x1, dc1)
    dx1 = exchange(dx1)
    dx1, fo1 = tie(dx1, fo1)
    d0, up0, gz0, du0, df0, do0, dqkv1, sums0, inner0, qkv_sum1 = layer_bwd(
        plan, dx1, up1, r1, r2, u, packed0, stacked[0]
    )
    d0, rest1 = tie(d0, rest1)
    dc0 = exchange(d0)
    bias1 = from_all(plan, jnp.sum(qkv_sum1, 0))
    qkv1 = column_grads(item, flat(h1_low), flat(dqkv1), rows_for((bias1[:D], bias1[2 * D :])))
    fo0, rest0 = grads(gz0, du0, df0, do0, y0, ctx0, sums0, inner0)
    dc0, qkv1, fo0, rest0 = tie(dc0, qkv1, fo0, rest0)
    qkv1, fo0, rest0 = scattered(qkv1), scattered(fo0), scattered(rest0)
    part1 = seq_parts([fo1, rest1])
    dx0 = attn_bwd(plan, tables[0], x0, dc0)
    dx0, qkv1, part1 = tie(dx0, qkv1, part1)
    own0 = own_grad(plan, item, hidden_all, dx0)
    dx0 = exchange(dx0)
    own0, dx0 = tie(own0, dx0)
    own0 = lax.all_to_all(own0, "item", split_axis=0, concat_axis=0, tiled=True)
    input_grad = layer_tail(plan, dx0, up0, columns0)
    input_grad, own0, fo0 = tie(input_grad, own0, fo0)
    own0 = seq_gather(jnp.sum(own0.astype(F32), 0).astype(BF)).astype(F32)
    part0 = seq_parts([qkv1, fo0])
    early, own0 = tie(jnp.concatenate([part1, part0]), own0)
    full = seq_gather(early)
    full, rest0 = tie(full, rest0)
    late = seq_gather(seq_parts([rest0]))
    outer_1, rest_1 = taken(full[:, : part1.shape[0]], [fo1, rest1])
    qkv_1, outer_0 = taken(full[:, part1.shape[0] :], [qkv1, fo0])
    (rest_0,) = taken(late, [rest0])
    qkv_0 = from_own(plan, own0[:, :-16])
    bias0 = from_own(plan, own0[:, -16])
    late0 = [lax.dynamic_slice_in_dim(bias0, part * D + item_rank * share, share) for part in (0, 2)]
    late1 = split_rows(qkv_1[-16:], [share] * 2)
    qkv_1 = from_all(plan, unpart(qkv_1[:-16]))
    inner_1, attn_1, early1 = unpart(rest_1[: parts * share]), rest_1[parts * share : -16], split_rows(rest_1[-16:], counts)
    inner_0, attn_0, early0 = unpart(rest_0[: parts * share]), rest_0[parts * share : -16], split_rows(rest_0[-16:], counts)
    vecs = [jnp.stack(pair) for pair in zip(late0 + early0, late1 + early1)]
    return (
        output.reshape(hidden.shape),
        input_grad.reshape(hidden.shape),
        jnp.stack([qkv_0, qkv_1]),
        vecs[0],
        vecs[1],
        jnp.stack([attn_0, attn_1]),
        vecs[2],
        vecs[3],
        vecs[4],
        jnp.stack([inner_0, inner_1]),
        vecs[5],
        jnp.stack([outer_0, outer_1]),
        vecs[6],
        vecs[7],
        vecs[8],
    )


def solution(mesh):
    placed = (
        P("item", "seq", None),
        P("item", None, "seq", None, None),
        P(None, "item", None),
        P(None, "item"),
        P(None, "item"),
        P(None, "item", None),
        P(None, "item"),
        P(None, "item"),
        P(None, "item"),
        P(None, "item", None),
        P(None, "item"),
        P(None, "item", None),
        P(None, "item"),
        P(None, "item"),
        P(None, "item"),
        P("item", "seq", None),
    )
    return jax.shard_map(
        local,
        mesh=mesh,
        in_specs=placed,
        out_specs=(
            P("item", "seq", None),
            P("item", "seq", None),
            P(None, "item", None),
            P(None, "item"),
            P(None, "item"),
            P(None, "item", None),
            P(None, "item"),
            P(None, "item"),
            P(None, "item"),
            P(None, "item", None),
            P(None, "item"),
            P(None, "item", None),
            P(None, "item"),
            P(None, "item"),
            P(None, "item"),
        ),
        check_vma=False,
    )
```

time: 1220 us -> 872 us (0.71)
  waiting for transfers between devices: 481 us -> 239 us
  matrix products: 207 us -> 0 us
  Pallas kernels: 144 us -> 345 us
  blocking collectives: 200 us -> 122 us
  local copies, waits for them, and re-layouts: 110 us -> 56.4 us
  starting transfers between devices: 25.9 us -> 57.5 us
    reduce_scatter x6 -> x5, waiting for transfers between devices: 269 us -> 0.01 us  [scattered(): return lax.psum_scatter(g, 'item', scatter_dimension=0, tiled=False)]
    dot_general x24 -> x0, matrix products: 207 us -> none  [mm(): return jnp.einsum(spec, a, b, preferred_element_type=jnp.float32)]
    pallas_call x4 -> x13, Pallas kernels: 144 us -> 345 us  [the longest x2 100 us: attn_bwd(): pl.pallas_call(partial(attn_bwd_kernel, plan), out_shape=jax.ShapeDtypeSt...]
    all_to_all x5 -> x14, waiting for transfers between devices: 132 us -> 237 us  [the longest x13 198 us: exchange(): lax.all_to_all(y, 'seq', split_axis=0, concat_axis=0, tiled=True)]
    all_to_all x4 -> x2, blocking collectives: 150 us -> 78.7 us  [exchange(): lax.all_to_all(y, 'seq', split_axis=0, concat_axis=0, tiled=True)]
    all_gather x8 -> x3, waiting for transfers between devices: 39 us -> 0.02 us  [the longest x1 0.02 us: local(): columns0 = lax.all_gather(columns[0], 'item', axis=0)]
    psum x1 -> x0, waiting for transfers between devices: 38.5 us -> none  [local(): lax.psum(lax.psum_scatter(g.astype(BF), 'item', scatter_dimension=0, tile...]
    all_to_all x5 -> x14, starting transfers between devices: 24.5 us -> 56.7 us  [the longest x13 52.4 us: exchange(): lax.all_to_all(y, 'seq', split_axis=0, concat_axis=0, tiled=True)]
  transfers between devices with their start and end apart: 22 -> 22, of which waited for: 13 -> 11; matrix products, arithmetic and copies ran while one was open for 20% -> 5% of each run, Pallas kernels for 8% -> 40%
where the time goes in v3:
time: 872 us; the launch traced here: 862 us
  Pallas kernels  345 us (40%)
  waiting for transfers between devices  239 us (27%)
  blocking collectives  122 us (14%)
  starting transfers between devices  57.5 us (7%)
  local copies, waits for them, and re-layouts  56.4 us (6%)
  other arithmetic  25.7 us (3%)
  between operations  15.7 us (2%)
    all_to_all x13, waiting for transfers between devices, exchange(): lax.all_to_all(y, 'seq', split_axis=0, concat_axis=0, tiled=True)  198 us
    pallas_call x2, Pallas kernels, attn_bwd(): pl.pallas_call(partial(attn_bwd_kernel, plan), out_shape=jax.ShapeDtypeSt...  100 us
    all_to_all x2, blocking collectives, exchange(): lax.all_to_all(y, 'seq', split_axis=0, concat_axis=0, tiled=True)  78.7 us
    pallas_call x2, Pallas kernels, attn_fwd(): pl.pallas_call(partial(attn_fwd_kernel, plan), out_shape=jax.ShapeDtypeSt...  57.6 us
    all_to_all x13, starting transfers between devices, exchange(): lax.all_to_all(y, 'seq', split_axis=0, concat_axis=0, tiled=True)  52.4 us
    pallas_call x1, Pallas kernels, layer_mid(): pl.pallas_call(partial(mid_kernel, plan, ff), out_shape=[jax.ShapeDtypeSt...  41.4 us
    all_to_all x1, waiting for transfers between devices, local(): own0 = lax.all_to_all(own0, 'item', split_axis=0, concat_axis=0, tiled=True)  39.1 us
    pallas_call x2, Pallas kernels, dense_grads(): pl.pallas_call(partial(dense_grad_kernel, item), out_shape=[jax.ShapeDtyp...  37.5 us
  transfers between devices with their start and end apart: 22, of which 11 were waited for; matrix products, arithmetic and copies ran while one was open for 5% of the time, Pallas kernels for 40%

profile of v3, /device:TPU:0, one launch (start us, length us, event | category | flops | bytes accessed | tf_op | source)
XLA Modules:
  0.0 861.6 jit_solution(6325906848777497153)
XLA Ops:
  22.8 5.2 all-to-all-start
  29.8 18.8 %all-gather.5 = bf16[8,2,1152]{2,1,0:T(2,128)(2,1)S(1)} all-gather(bf16[1,2,1152]{2,1,0:T(2,128)(2,1)S(1)} %bitcast.266), channel_id=3, replica_groups=mesh['seq'=4,'item'=8] {'item'}, dimensions={0}, use_global_device_ids=true | all-gather | bytes 41472 | tf_op jit(solution)/shard_map/all_gather | solution.py:941
  50.4 25.0 %all-gather = bf16[768,576]{1,0:T(8,128)(2,1)S(1)} all-gather(bf16[96,576]{1,0:T(8,128)(2,1)S(1)} %pad_maximum_fusion.10), channel_id=2, replica_groups=mesh['seq'=4,'item'=8] {'item'}, dimensions={0}, use_global_device_ids=true | all-gather | bytes 995328 | tf_op jit(solution)/shard_map/all_gather | solution.py:953
  75.4 24.0 %all-to-all-done = bf16[4,1024,768]{2,1,0:T(8,128)(2,1)} async-done(((bf16[4,1024,768]{2,1,0:T(8,128)(2,1)}), bf16[4,1024,768]{2,1,0:T(8,128)(2,1)}, u32[]{:S(2)}, u32[]{:S(2)}) %all-to-all-start) | async-done | bytes 6291488 | tf_op jit(solution)/shard_map/all_to_all | solution.py:880
  103.5 13.3 %own_heads.1 = bf16[4,4,9,2,64,128]{5,4,3,2,1,0:T(8,128)(2,1)S(1)} custom-call(bf16[4,2,4,128,768]{4,3,2,1,0:T(8,128)(2,1)} %bitcast.8.a_ref, bf16[8,96,576]{2,1,0:T(8,128)(2,1)S(1)} %bitcast.201, f32[1,576]{1,0:T(1,128)S(1)} %pad_maximum_fusion.18.b_ref), custom_call_target="tpu_custom_call" | custom-call | flops 7000000000 | bytes 12000000 | tf_op jit(solution)/shard_map/own_heads/pallas_call | solution.py:444
  121.9 28.8 %attn_fwd.2 = bf16[96,64,128]{2,1,0:T(8,128)(2,1)} custom-call(s32[1536]{0:T(1024)S(1)} %reshape.308.lists_ref, bf16[288,64,128]{2,1,0:T(8,128)(2,1)} %bitcast.203), custom_call_target="tpu_custom_call" | custom-call | flops 25999998976 | bytes 6000000 | tf_op jit(solution)/shard_map/attn_fwd/pallas_call | solution.py:206
  150.8 4.4 all-to-all-start.2
  157.9 15.7 %all-to-all-done.2 = bf16[4,1536,128]{2,1,0:T(8,128)(2,1)S(1)} async-done(((bf16[4,1536,128]{2,1,0:T(8,128)(2,1)}), bf16[4,1536,128]{2,1,0:T(8,128)(2,1)S(1)}, u32[]{:S(2)}, u32[]{:S(2)}) %all-to-all-start.2) | async-done | bytes 1572896 | tf_op jit(solution)/shard_map/all_to_all | solution.py:880
  174.7 29.4 %layer_fwd.1 = (bf16[4,4,9,2,64,128]{5,4,3,2,1,0:T(8,128)(2,1)}, f32[2,512,768]{2,1,0:T(8,128)}, bf16[2,512,768]{2,1,0:T(8,128)(2,1)}, f32[2,512,768]{2,1,0:T(8,...) custom-call(bf16[4,4,3,2,64,128]{5,4,3,2,1,0:T(8,128)(2,1)} %bitcast, ...), custom_call_target="tpu_custom_call" | custom-call | flops 30000001024 | bytes 50000000 | tf_op jit(solution)/shard_map/layer_fwd/pallas_call | solution.py:599
  204.1 5.0 all-to-all-start.3
  209.3 52.4 %all-to-all-done.3 = bf16[4,4608,128]{2,1,0:T(8,128)(2,1)} async-done(((bf16[4,4608,128]{2,1,0:T(8,128)(2,1)}), bf16[4,4608,128]{2,1,0:T(8,128)(2,1)}, u32[]{:S(2)}, u32[]{:S(2)}) %all-to-all-start.3) | async-done | bytes 4718624 | tf_op jit(solution)/shard_map/all_to_all | solution.py:880
  261.7 28.8 %attn_fwd.3 = bf16[96,64,128]{2,1,0:T(8,128)(2,1)} custom-call(s32[1536]{0:T(1024)S(1)} %reshape.307.lists_ref, bf16[288,64,128]{2,1,0:T(8,128)(2,1)} %bitcast.45.x_ref), custom_call_target="tpu_custom_call" | custom-call | flops 25999998976 | bytes 6000000 | tf_op jit(solution)/shard_map/attn_fwd/pallas_call | solution.py:206
  297.1 15.6 %all-to-all-done.4 = bf16[4,1536,128]{2,1,0:T(8,128)(2,1)S(1)} async-done(((bf16[4,1536,128]{2,1,0:T(8,128)(2,1)}), bf16[4,1536,128]{2,1,0:T(8,128)(2,1)S(1)}, u32[]{:S(2)}, u32[]{:S(2)}) %all-to-all-start.4) | async-done | bytes 1572896 | tf_op jit(solution)/shard_map/all_to_all | solution.py:880
  313.9 41.4 %layer_mid.1 = (bf16[4,4,3,2,64,128]{5,4,3,2,1,0:T(8,128)(2,1)}, f32[2,512,768]{2,1,0:T(8,128)}, f32[2,512,768]{2,1,0:T(8,128)}, bf16[2,512,3072]{2,1,0:T(8,128)...) custom-call(bf16[4,4,3,2,64,128]{5,4,3,2,1,0:T(8,128)(2,1)} %bitcast, ...), custom_call_target="tpu_custom_call" | custom-call | flops 44999999488 | bytes 50000000 | tf_op jit(solution)/shard_map/layer_mid/pallas_call | solution.py:681
  362.3 18.7 %dense_grads.2 = (bf16[8,384,768]{2,1,0:T(8,128)(2,1)}, bf16[8,496,768]{2,1,0:T(8,128)(2,1)}) custom-call(bf16[1024,3072]{1,0:T(8,128)(2,1)} %bitcast.276, bf16[1024,768]{1,0:T(8,128)(2,1)} %bitcast.285, bf16[1024,768]{1,0:T(8,128)(2,1)} %bitcast.287, bf16[1024,3072]{1,0:T(8,128)(2,1)} %bitcast.277, bf16[1024,768]{1,0:T(8,128)(2,1)} %bitcast.288, ...), custom_call_target="tpu_custom_call" | custom-call | flops 14000000000 | bytes 30000000 | tf_op jit(solution)/shard_map/dense_grads/pallas_call | solution.py:766
  382.7 50.0 %attn_bwd.2 = bf16[288,64,128]{2,1,0:T(8,128)(2,1)} custom-call(s32[1536]{0:T(1024)} %copy-done.3, bf16[288,64,128]{2,1,0:T(8,128)(2,1)} %bitcast.45.x_ref, bf16[96,64,128]{2,1,0:T(8,128)(2,1)} %bitcast.226), custom_call_target="tpu_custom_call" | custom-call | flops 46000001024 | bytes 12000000 | tf_op jit(solution)/shard_map/attn_bwd/pallas_call | solution.py:328
  432.8 59.0 %all_to_all.80 = bf16[4,4608,128]{2,1,0:T(8,128)(2,1)} all-to-all(bf16[4,4608,128]{2,1,0:T(8,128)(2,1)} %bitcast.211), channel_id=1, replica_groups=mesh['seq'=4,'item'=8] {'seq'}, dimensions={0} | all-to-all | bytes 9437184 | tf_op jit(solution)/shard_map/all_to_all | solution.py:880
  491.8 36.9 %layer_bwd.1 = (bf16[4,4,3,2,64,128]{5,4,3,2,1,0:T(8,128)(2,1)}, f32[2,512,768]{2,1,0:T(8,128)}, bf16[2,512,3072]{2,1,0:T(8,128)(2,1)}, bf16[2,512,3072]{2,1,0:T...) custom-call(bf16[4,4,9,2,64,128]{5,4,3,2,1,0:T(8,128)(2,1)} %bitcast, ...), custom_call_target="tpu_custom_call" | custom-call | flops 40000000000 | bytes 50000000 | tf_op jit(solution)/shard_map/layer_bwd/pallas_call | solution.py:731
  533.7 5.8 column_grads.1
  544.9 18.8 %dense_grads.3 = (bf16[8,384,768]{2,1,0:T(8,128)(2,1)}, bf16[8,496,768]{2,1,0:T(8,128)(2,1)}) custom-call(bf16[1024,3072]{1,0:T(8,128)(2,1)} %bitcast.274, bf16[1024,768]{1,0:T(8,128)(2,1)} %bitcast.283, bf16[1024,768]{1,0:T(8,128)(2,1)} %bitcast.281, bf16[1024,3072]{1,0:T(8,128)(2,1)} %bitcast.275, bf16[1024,768]{1,0:T(8,128)(2,1)} %bitcast.282, ...), custom_call_target="tpu_custom_call" | custom-call | flops 14000000000 | bytes 30000000 | tf_op jit(solution)/shard_map/dense_grads/pallas_call | solution.py:766
  566.3 19.7 %all_to_all.81 = bf16[4,224,768]{2,1,0:T(8,128)(2,1)S(1)} all-to-all(bf16[4,224,768]{2,1,0:T(8,128)(2,1)S(1)} %bitcast.206), channel_id=1, replica_groups=mesh['seq'=4,'item'=8] {'seq'}, dimensions={0} | all-to-all | bytes 2752512 | tf_op jit(solution)/shard_map/all_to_all | solution.py:880
  586.3 50.2 %attn_bwd.3 = bf16[288,64,128]{2,1,0:T(8,128)(2,1)} custom-call(s32[1536]{0:T(1024)} %copy-done.2, bf16[288,64,128]{2,1,0:T(8,128)(2,1)} %bitcast.204, bf16[96,64,128]{2,1,0:T(8,128)(2,1)} %bitcast.225), custom_call_target="tpu_custom_call" | custom-call | flops 46000001024 | bytes 12000000 | tf_op jit(solution)/shard_map/attn_bwd/pallas_call | solution.py:328
  636.5 5.0 all-to-all-start.9
  643.9 14.5 %own_grad.1 = bf16[8,112,576]{2,1,0:T(8,128)(2,1)} custom-call(bf16[4,2,4,128,768]{4,3,2,1,0:T(8,128)(2,1)} %bitcast.8.a_ref, bf16[4,4,9,2,64,128]{5,4,3,2,1,0:T(8,128)(2,1)S(1)} %bitcast.200), custom_call_target="tpu_custom_call" | custom-call | flops 7000000000 | bytes 12000000 | tf_op jit(solution)/shard_map/own_grad/pallas_call | solution.py:483
  658.4 32.9 %all-to-all-done.9 = bf16[4,4608,128]{2,1,0:T(8,128)(2,1)} async-done(((bf16[4,4608,128]{2,1,0:T(8,128)(2,1)}), bf16[4,4608,128]{2,1,0:T(8,128)(2,1)}, u32[]{:S(2)}, u32[]{:S(2)}) %all-to-all-start.9) | async-done | bytes 4718624 | tf_op jit(solution)/shard_map/all_to_all | solution.py:880
  695.6 8.5 layer_tail.1
  704.0 39.1 %all-to-all-done.10 = bf16[8,112,576]{2,1,0:T(8,128)(2,1)} async-done(((bf16[8,112,576]{2,1,0:T(8,128)(2,1)}), bf16[8,112,576]{2,1,0:T(8,128)(2,1)}, u32[]{:S(2)}, u32[]{:S(2)}) %all-to-all-start.10) | async-done | bytes 1032224 | tf_op jit(solution)/shard_map/all_to_all | solution.py:1041
  750.1 7.6 all-to-all-done.12
  761.7 12.9 %all-to-all-done.11 = bf16[4,176,768]{2,1,0:T(8,128)(2,1)S(1)} async-done(((bf16[4,176,768]{2,1,0:T(8,128)(2,1)}), bf16[4,176,768]{2,1,0:T(8,128)(2,1)S(1)}, u32[]{:S(2)}, u32[]{:S(2)}) %all-to-all-start.11) | async-done | bytes 1081376 | tf_op jit(solution)/shard_map/all_to_all | solution.py:880
  777.2 4.5 all-to-all-start.13
  784.3 25.7 %all-to-all-done.13 = bf16[4,400,768]{2,1,0:T(8,128)(2,1)} async-done(((bf16[4,400,768]{2,1,0:T(8,128)(2,1)}), bf16[4,400,768]{2,1,0:T(8,128)(2,1)}, u32[]{:S(2)}, u32[]{:S(2)}) %all-to-all-start.13) | async-done | bytes 2457632 | tf_op jit(solution)/shard_map/all_to_all | solution.py:880
  837.4 9.6 %all-to-all-done.15 = bf16[4,128,768]{2,1,0:T(8,128)(2,1)S(1)} async-done(((bf16[4,128,768]{2,1,0:T(8,128)(2,1)}), bf16[4,128,768]{2,1,0:T(8,128)(2,1)S(1)}, u32[]{:S(2)}, u32[]{:S(2)}) %all-to-all-start.15) | async-done | bytes 786464 | tf_op jit(solution)/shard_map/all_to_all | solution.py:880
  (350 shorter events, 118.7 us)
Async XLA Ops:
  7.2 166.4 %all-gather.10.cloned.1.call-start = ((), (), s32[]{:S(2)}) async-start(), calls=%async_computation.26 | async-start | bytes 15925248 | tf_op jit(solution)/shard_map/all_gather | solution.py:960
  14.3 5.4 copy-start.10
  22.8 76.6 %all-to-all-start = ((bf16[4,1024,768]{2,1,0:T(8,128)(2,1)}), bf16[4,1024,768]{2,1,0:T(8,128)(2,1)}, u32[]{:S(2)}, u32[]{:S(2)}) async-start(bf16[4,1024,768]{2,1,0:T(8,128)(2,1)} %broadcast_in_dim.14), calls=%async_computation | async-start | bytes 12582912 | tf_op jit(solution)/shard_map/all_to_all | solution.py:880
  28.1 269.0 %all-gather.12.cloned.1.call-start = ((), (), s32[]{:S(2)}) async-start(), calls=%async_computation.27 | async-start | bytes 11943936 | tf_op jit(solution)/shard_map/all_gather | solution.py:961
  49.7 49.7 %copy-start.27 = (s32[1,2,16,12,3]{2,1,4,3,0:T(2,128)S(1)}, s32[1,2,16,12,3]{2,1,4,3,0:T(2,128)}, u32[]{:S(2)}) copy-start(s32[1,2,16,12,3]{2,1,4,3,0:T(2,128)} %param.17) | copy-start | bytes 13828
  100.3 18.6 %all-to-all-start.1 = ((s32[4,1,288]{2,1,0:T(1,128)}), s32[4,1,288]{2,1,0:T(1,128)S(1)}, u32[]{:S(2)}, u32[]{:S(2)}) async-start(s32[4,1,288]{2,1,0:T(1,128)} %reshape.371), calls=%async_computation.1 | async-start | bytes 12288 | tf_op jit(solution)/shard_map/all_to_all | solution.py:880
  121.9 28.8 %copy-start.2 = (s32[1536]{0:T(1024)}, s32[1536]{0:T(1024)S(1)}, u32[]{:S(2)}) copy-start(s32[1536]{0:T(1024)S(1)} %reshape.308.lists_ref) | copy-start | bytes 18436
  150.8 22.8 %all-to-all-start.2 = ((bf16[4,1536,128]{2,1,0:T(8,128)(2,1)}), bf16[4,1536,128]{2,1,0:T(8,128)(2,1)S(1)}, u32[]{:S(2)}, u32[]{:S(2)}) async-start(bf16[4,1536,128]{2,1,0:T(8,128)(2,1)} %bitcast.26), calls=%async_computation.2 | async-start | bytes 3145728 | tf_op jit(solution)/shard_map/all_to_all | solution.py:880
  204.1 57.6 %all-to-all-start.3 = ((bf16[4,4608,128]{2,1,0:T(8,128)(2,1)}), bf16[4,4608,128]{2,1,0:T(8,128)(2,1)}, u32[]{:S(2)}, u32[]{:S(2)}) async-start(bf16[4,4608,128]{2,1,0:T(8,128)(2,1)} %bitcast.210), calls=%async_computation.3 | async-start | bytes 9437184 | tf_op jit(solution)/shard_map/all_to_all | solution.py:880
  209.3 81.2 %copy-start.3 = (s32[1536]{0:T(1024)}, s32[1536]{0:T(1024)S(1)}, u32[]{:S(2)}) copy-start(s32[1536]{0:T(1024)S(1)} %reshape.307.lists_ref) | copy-start | bytes 18436
  290.5 22.2 %all-to-all-start.4 = ((bf16[4,1536,128]{2,1,0:T(8,128)(2,1)}), bf16[4,1536,128]{2,1,0:T(8,128)(2,1)S(1)}, u32[]{:S(2)}, u32[]{:S(2)}) async-start(bf16[4,1536,128]{2,1,0:T(8,128)(2,1)} %bitcast.46), calls=%async_computation.4 | async-start | bytes 3145728 | tf_op jit(solution)/shard_map/all_to_all | solution.py:880
  294.1 88.3 %all-gather.14.cloned.1.call-start = ((), (), s32[]{:S(2)}) async-start(), calls=%async_computation.28 | async-start | bytes 3981312 | tf_op jit(solution)/shard_map/all_gather | solution.py:962
  358.6 22.4 %all-to-all-start.5 = ((bf16[4,1536,128]{2,1,0:T(8,128)(2,1)}), bf16[4,1536,128]{2,1,0:T(8,128)(2,1)S(1)}, u32[]{:S(2)}, u32[]{:S(2)}) async-start(bf16[4,1536,128]{2,1,0:T(8,128)(2,1)} %bitcast.223), calls=%async_computation.5 | async-start | bytes 3145728 | tf_op jit(solution)/shard_map/all_to_all | solution.py:880
  362.2 129.6 %reduce-scatter.6.cloned.1.call-start = ((), (), s32[]{:S(2)}) async-start(), calls=%async_computation.21 | async-start | bytes 5308416 | tf_op jit(solution)/shard_map/reduce_scatter | solution.py:979
  382.2 159.2 %reduce-scatter.8.cloned.1.call-start = ((), (), s32[]{:S(2)}) async-start(), calls=%async_computation.22 | async-start | bytes 6856704 | tf_op jit(solution)/shard_map/reduce_scatter | solution.py:979
  528.7 5.0 copy-start.5
  541.3 22.4 %all-to-all-start.7 = ((bf16[4,1536,128]{2,1,0:T(8,128)(2,1)}), bf16[4,1536,128]{2,1,0:T(8,128)(2,1)S(1)}, u32[]{:S(2)}, u32[]{:S(2)}) async-start(bf16[4,1536,128]{2,1,0:T(8,128)(2,1)} %bitcast.72), calls=%async_computation.9 | async-start | bytes 3145728 | tf_op jit(solution)/shard_map/all_to_all | solution.py:880
  544.9 91.6 %reduce-scatter.10.cloned.1.call-start = ((), (), s32[]{:S(2)}) async-start(), calls=%async_computation.23 | async-start | bytes 4202496 | tf_op jit(solution)/shard_map/reduce_scatter | solution.py:979
  564.9 139.1 %reduce-scatter.12.cloned.1.call-start = ((), (), s32[]{:S(2)}) async-start(), calls=%async_computation.24 | async-start | bytes 5308416 | tf_op jit(solution)/shard_map/reduce_scatter | solution.py:979
  565.6 218.6 %reduce-scatter.14.cloned.1.call-start = ((), (), s32[]{:S(2)}) async-start(), calls=%async_computation.25 | async-start | bytes 6856704 | tf_op jit(solution)/shard_map/reduce_scatter | solution.py:979
  636.5 54.8 %all-to-all-start.9 = ((bf16[4,4608,128]{2,1,0:T(8,128)(2,1)}), bf16[4,4608,128]{2,1,0:T(8,128)(2,1)}, u32[]{:S(2)}, u32[]{:S(2)}) async-start(bf16[4,4608,128]{2,1,0:T(8,128)(2,1)} %bitcast.199), calls=%async_computation.12 | async-start | bytes 9437184 | tf_op jit(solution)/shard_map/all_to_all | solution.py:880
  643.9 51.6 %copy-start.6 = (f32[2,512,768]{2,1,0:T(8,128)S(1)}, f32[2,512,768]{2,1,0:T(8,128)}, u32[]{:S(2)}) copy-start(f32[2,512,768]{2,1,0:T(8,128)} %get-tuple-element.121.up_ref) | copy-start | bytes 9437188
  691.3 51.9 %all-to-all-start.10 = ((bf16[8,112,576]{2,1,0:T(8,128)(2,1)}), bf16[8,112,576]{2,1,0:T(8,128)(2,1)}, u32[]{:S(2)}, u32[]{:S(2)}) async-start(bf16[8,112,576]{2,1,0:T(8,128)(2,1)} %own_grad.1), calls=%async_computation.13 | async-start | bytes 2293760 | tf_op jit(solution)/shard_map/all_to_all | solution.py:1041
  743.2 5.9 copy-start.23
  743.2 5.9 copy-start.24
  745.6 12.2 %all-to-all-start.12 = ((bf16[4,112,576]{2,1,0:T(8,128)(2,1)}), bf16[4,112,576]{2,1,0:T(8,128)(2,1)S(1)}, u32[]{:S(2)}, u32[]{:S(2)}) async-start(bf16[4,112,576]{2,1,0:T(8,128)(2,1)} %broadcast_in_dim.15), calls=%async_computation.16 | async-start | bytes 1146880 | tf_op jit(solution)/shard_map/all_to_all | solution.py:880
  757.7 16.8 %all-to-all-start.11 = ((bf16[4,176,768]{2,1,0:T(8,128)(2,1)}), bf16[4,176,768]{2,1,0:T(8,128)(2,1)S(1)}, u32[]{:S(2)}, u32[]{:S(2)}) async-start(bf16[4,176,768]{2,1,0:T(8,128)(2,1)} %bitcast.90), calls=%async_computation.15 | async-start | bytes 2162688 | tf_op jit(solution)/shard_map/all_to_all | solution.py:880
  777.2 32.8 %all-to-all-start.13 = ((bf16[4,400,768]{2,1,0:T(8,128)(2,1)}), bf16[4,400,768]{2,1,0:T(8,128)(2,1)}, u32[]{:S(2)}, u32[]{:S(2)}) async-start(bf16[4,400,768]{2,1,0:T(8,128)(2,1)} %broadcast_in_dim.16), calls=%async_computation.17 | async-start | bytes 4915200 | tf_op jit(solution)/shard_map/all_to_all | solution.py:880
  818.0 3.9 slice-start.1
  818.0 14.1 %all-to-all-start.14 = ((bf16[4,128,768]{2,1,0:T(8,128)(2,1)}), bf16[4,128,768]{2,1,0:T(8,128)(2,1)S(1)}, u32[]{:S(2)}, u32[]{:S(2)}) async-start(bf16[4,128,768]{2,1,0:T(8,128)(2,1)} %bitcast.115), calls=%async_computation.19 | async-start | bytes 1572864 | tf_op jit(solution)/shard_map/all_to_all | solution.py:880
  833.2 13.8 %all-to-all-start.15 = ((bf16[4,128,768]{2,1,0:T(8,128)(2,1)}), bf16[4,128,768]{2,1,0:T(8,128)(2,1)S(1)}, u32[]{:S(2)}, u32[]{:S(2)}) async-start(bf16[4,128,768]{2,1,0:T(8,128)(2,1)} %broadcast_in_dim.17), calls=%async_computation.20 | async-start | bytes 1572864 | tf_op jit(solution)/shard_map/all_to_all | solution.py:880
  850.1 3.4 copy-start.18
  (35 other events, 42.0 us)
Sparse Core Ops, SparseCore 0:
  19.8 140.4 all-gather.9
  162.5 98.6 all-gather.11
  297.1 43.2 all-gather.13
  381.2 56.6 reduce-scatter.5
  440.0 66.2 reduce-scatter.7
  563.9 47.3 reduce-scatter.9
  613.7 53.2 reduce-scatter.11
  669.4 84.7 reduce-scatter.13

commit v4 on v3

--- a/solution.py
+++ b/solution.py
@@ -693,19 +693,13 @@
 
 
 def bwd_kernel(plan, ff, dx_ref, up_ref, r1_ref, r2_ref, u_ref, w_ref, vec_ref,
-               d_ref, dr1_ref, gz_ref, du_ref, df_ref, do_ref, dqkv_ref, sums_ref, inner_sum_ref, qkv_sum_ref):
+               d_ref, dr1_ref, gz_ref, du_ref, df_ref, do_ref, sums_ref, inner_sum_ref):
     w = Packed(w_ref, ff)
     dqkv = pick_heads(plan, dx_ref[:, 0])
-    write(dqkv_ref, dqkv)
     gy = read(up_ref)
     for n in range(plan.cols // D):
         gy = gy + dot(dqkv[:, part_of(n)], w.columns(n), NT)
 
-    @pl.when(pl.program_id(0) == 0)
-    def _():
-        qkv_sum_ref[...] = jnp.zeros_like(qkv_sum_ref)
-
-    qkv_sum_ref[...] += jnp.sum(dqkv.astype(F32).reshape(-1, 8, dqkv.shape[-1]), 0)
     unit1, inv1 = normalise(read(r1_ref))
     unit2, inv2 = normalise(read(r2_ref))
 
@@ -724,10 +718,8 @@
 def layer_bwd(plan, dx, up, r1, r2, u, packed, vec):
     t = (2, plan.tokens // 2)
     ff = u.shape[-1]
-    shapes = [(D, F32), (ff, BF), (ff, BF), (D, BF), (D, BF), (plan.cols, BF)]
+    shapes = [(D, F32), (ff, BF), (ff, BF), (D, BF), (D, BF)]
     sums, sums_at = sum_specs(ff)
-    sums = sums + [jax.ShapeDtypeStruct((8, plan.cols), F32)]
-    sums_at = sums_at + [pl.BlockSpec((8, plan.cols), lambda c: (0, 0))]
     return pl.pallas_call(
         partial(bwd_kernel, plan, ff),
         out_shape=[jax.ShapeDtypeStruct(plan.c_shape(), BF)] + [jax.ShapeDtypeStruct(t + (n,), d) for n, d in shapes] + sums,
@@ -775,33 +767,6 @@
     )(gz, df, y, du, ctx, do, vecs)
 
 
-def column_grad_kernel(item, a_ref, d_ref, vec_ref, o_ref):
-    n = pl.program_id(0)
-    share = D // item
-    first = pl.multiple_of(n * share, 16)
-    o_ref[:, pl.ds(first, share)] = dot(a_ref[...], d_ref[...], TN).astype(BF).reshape(item, share, D)
-
-    @pl.when(n == pl.num_programs(0) - 1)
-    def _():
-        o_ref[:, o_ref.shape[1] - vec_ref.shape[1] :] = vec_ref[...]
-
-
-def column_grads(item, a, d, vecs):
-    tokens = a.shape[0]
-    parts = d.shape[1] // D
-    out = (item, parts * (D // item) + vecs.shape[1], D)
-    return pl.pallas_call(
-        partial(column_grad_kernel, item),
-        out_shape=jax.ShapeDtypeStruct(out, BF),
-        grid=(parts,),
-        in_specs=[whole(a.shape), pl.BlockSpec((tokens, D), lambda n: (0, n)), whole(vecs.shape)],
-        out_specs=whole(out),
-        compiler_params=pltpu.CompilerParams(vmem_limit_bytes=48 << 20),
-        cost_estimate=pl.CostEstimate(flops=6 * 10**9, bytes_accessed=10 * 10**6, transcendentals=0),
-        name="column_grads",
-    )(a, d, vecs)
-
-
 def tail_kernel(plan, dx_ref, up_ref, w_ref, o_ref):
     dqkv = pick_heads(plan, dx_ref[:, 0])
     share = D // w_ref.shape[0]
@@ -824,6 +789,52 @@
     )(dx, up, w_qkv)
 
 
+def finish_kernel(plan, share, counts, *refs):
+    fulls, owns, outs = refs[:LAYERS], refs[LAYERS], refs[LAYERS + 1 :]
+    qkv_ref, bias_ref, attn_ref, inner_ref, outer_ref = outs[:5]
+    small = outs[5:]
+    outer = outer_ref.shape[1]
+    parts = inner_ref.shape[2] // D
+    each = owns.shape[1] // LAYERS
+    for layer in range(LAYERS):
+        flat = fulls[layer][...].reshape(-1, D)
+        outer_ref[layer] = flat[:outer].astype(F32)
+        at = outer
+        for n in range(parts):
+            inner_ref[layer, :, part_of(n)] = flat[at : at + share].astype(F32)
+            at += share
+        attn_ref[layer] = flat[at : at + share].astype(F32)
+        at += share
+        vecs = flat[at : at + 16].astype(F32)
+        at = 0
+        for ref, n in zip(small, counts):
+            ref[layer : layer + 1, :] = vecs[at // D : at // D + 1, at % D : at % D + n]
+            at += n
+        pieces = {}
+        for g in range(plan.groups):
+            rows = owns[g, layer * each : (layer + 1) * each].astype(F32)
+            for i in range(plan.hp):
+                head = g * plan.hp + i
+                pieces["k", head] = rows[:, i * WIDE : i * WIDE + HD]
+                pieces["v", head] = rows[:, i * WIDE + HD : (i + 1) * WIDE]
+                pieces["q", head] = rows[:, (2 * plan.hp + i) * HD : (2 * plan.hp + i + 1) * HD]
+        value = jnp.concatenate([pieces[kind, head] for kind in "qkv" for head in range(H)], 1)
+        qkv_ref[layer] = value[:share]
+        bias_ref[layer : layer + 1, :] = value[share : share + 1]
+
+
+def finish(plan, share, ff, item, counts, fulls, owns):
+    out = [(share, 3 * D), (3 * D,), (share, D), (share, ff), (ff // item, D)] + [(n,) for n in counts]
+    return pl.pallas_call(
+        partial(finish_kernel, plan, share, counts),
+        out_shape=[jax.ShapeDtypeStruct((LAYERS,) + s, F32) for s in out],
+        in_specs=[pl.BlockSpec(memory_space=VMEM)] * (LAYERS + 1),
+        out_specs=[pl.BlockSpec(memory_space=VMEM)] * len(out),
+        compiler_params=pltpu.CompilerParams(vmem_limit_bytes=48 << 20),
+        name="finish",
+    )(*fulls, owns)
+
+
 def column_parts(plan, w):
     lead = w.shape[:-1]
     g, hp = plan.groups, plan.hp
@@ -847,32 +858,6 @@
     return jnp.concatenate(
         [lax.dynamic_index_in_dim(p, rank, axis, False) for p in column_parts(plan, w)], -1
     )
-
-
-def natural(plan, kv, pairs, last):
-    lead = kv.shape[:-2]
-    g, hp = plan.groups, plan.hp
-    kv = kv.reshape(lead + (g * hp, 2, HD))
-    q = jnp.concatenate(
-        [pairs.reshape(lead + (g, 2 * plan.pairs, HD)), last.reshape(lead + (g, plan.odd, HD))], -2
-    ).reshape(lead + (g * hp, HD))
-    return jnp.concatenate(
-        [p[..., :H, :].reshape(lead + (H * HD,)) for p in (q, kv[..., 0, :], kv[..., 1, :])], -1
-    )
-
-
-def from_all(plan, w):
-    lead = w.shape[:-1]
-    a = plan.groups * plan.hp * WIDE
-    b = a + plan.groups * plan.pairs * WIDE
-    return natural(plan, *(p.reshape(lead + (plan.groups, -1)) for p in (w[..., :a], w[..., a:b], w[..., b:])))
-
-
-def from_own(plan, w):
-    a = plan.hp * WIDE
-    b = a + plan.pairs * WIDE
-    w = jnp.moveaxis(w, 0, -2)
-    return natural(plan, w[..., :a], w[..., a:b], w[..., b:])
 
 
 def exchange(x):
@@ -968,6 +953,7 @@
     )
     x1 = exchange(x1)
     ctx1 = exchange(attn_fwd(plan, tables[1], x1))
+    h1_all = lax.all_gather(h1_low.reshape(tokens, D), "seq", axis=0)
     d1, output, up1, gz1, du1, df1, do1, y1, ctx1, sums1, inner1 = layer_mid(
         plan, ctx1, h1, cotangent[0], packed1, stacked[1], inner[1]
     )
@@ -981,99 +967,73 @@
     def rows_for(vecs):
         part = jnp.concatenate([v.reshape(item, -1) for v in vecs], 1)
         return jnp.pad(part, ((0, 0), (0, 16 * D - part.shape[1]))).reshape(item, 16, D).astype(BF)
-
-    def split_rows(part, counts):
-        values, at, out = part.reshape(-1), 0, []
-        for n in counts:
-            out.append(values[at : at + n])
-            at += n
-        return out
 
     def grads(gz, du, df, do, y, ctx, sums, inner_sum):
         sums = jnp.sum(sums, 1)
         vecs = (sums[SUM_DO], sums[D_GAIN1], sums[D_SHIFT1], jnp.sum(inner_sum, 0), sums[SUM_DF], sums[D_GAIN2], sums[D_SHIFT2])
         return dense_grads(item, flat(gz), flat(df), flat(y), flat(du), flat(ctx), flat(do), rows_for(vecs))
 
-    def seq_parts(shares):
+    def seq_send(shares):
         rows = jnp.concatenate(shares)
         rows = jnp.pad(rows, ((0, -rows.shape[0] % (16 * groups)), (0, 0)))
-        return jnp.sum(exchange(rows.reshape(groups, -1, D)).astype(F32), 0).astype(BF)
+        return exchange(rows.reshape(groups, -1, D))
+
+    def seq_sum(sent):
+        return jnp.sum(sent.astype(F32), 0).astype(BF)
 
     def seq_gather(part):
         return exchange(jnp.broadcast_to(part[None], (groups,) + part.shape))
 
-    def taken(full, shares):
-        rows, at, out = full.reshape(-1, D), 0, []
-        for p in shares:
-            out.append(rows[at : at + p.shape[0]].astype(F32))
-            at += p.shape[0]
-        return out
-
-    def unpart(rows):
-        return jnp.concatenate([rows[n : n + share] for n in range(0, rows.shape[0], share)], 1)
-
-    parts = w_ffn_in.shape[2] // D
     counts = [share] * 3 + [w_ffn_in.shape[2] // item] + [share] * 3
     dc1 = exchange(d1)
     fo1, rest1 = grads(gz1, du1, df1, do1, y1, ctx1, sums1, inner1)
     dc1, fo1, rest1 = tie(dc1, fo1, rest1)
     fo1, rest1 = scattered(fo1), scattered(rest1)
-    dc1, columns0 = tie(dc1, columns0)
+    dc1, columns0, h1_all = tie(dc1, columns0, h1_all)
     dx1 = attn_bwd(plan, tables[1], x1, dc1)
+    own1 = own_grad(plan, item, h1_all, dx1)
     dx1 = exchange(dx1)
+    dx1, own1 = tie(dx1, own1)
+    own1 = scattered(own1)
     dx1, fo1 = tie(dx1, fo1)
-    d0, up0, gz0, du0, df0, do0, dqkv1, sums0, inner0, qkv_sum1 = layer_bwd(
-        plan, dx1, up1, r1, r2, u, packed0, stacked[0]
-    )
+    d0, up0, gz0, du0, df0, do0, sums0, inner0 = layer_bwd(plan, dx1, up1, r1, r2, u, packed0, stacked[0])
     d0, rest1 = tie(d0, rest1)
     dc0 = exchange(d0)
-    bias1 = from_all(plan, jnp.sum(qkv_sum1, 0))
-    qkv1 = column_grads(item, flat(h1_low), flat(dqkv1), rows_for((bias1[:D], bias1[2 * D :])))
     fo0, rest0 = grads(gz0, du0, df0, do0, y0, ctx0, sums0, inner0)
-    dc0, qkv1, fo0, rest0 = tie(dc0, qkv1, fo0, rest0)
-    qkv1, fo0, rest0 = scattered(qkv1), scattered(fo0), scattered(rest0)
-    part1 = seq_parts([fo1, rest1])
+    dc0, fo0, rest0, own1 = tie(dc0, fo0, rest0, own1)
+    fo0, rest0 = scattered(fo0), scattered(rest0)
+    sent1 = seq_send([fo1, rest1])
     dx0 = attn_bwd(plan, tables[0], x0, dc0)
-    dx0, qkv1, part1 = tie(dx0, qkv1, part1)
+    dx0, sent1 = tie(dx0, sent1)
     own0 = own_grad(plan, item, hidden_all, dx0)
     dx0 = exchange(dx0)
-    own0, dx0 = tie(own0, dx0)
-    own0 = lax.all_to_all(own0, "item", split_axis=0, concat_axis=0, tiled=True)
+    dx0, own0, part1 = tie(dx0, own0, seq_sum(sent1))
+    own0 = scattered(own0)
+    full1 = seq_gather(part1)
     input_grad = layer_tail(plan, dx0, up0, columns0)
-    input_grad, own0, fo0 = tie(input_grad, own0, fo0)
-    own0 = seq_gather(jnp.sum(own0.astype(F32), 0).astype(BF)).astype(F32)
-    part0 = seq_parts([qkv1, fo0])
-    early, own0 = tie(jnp.concatenate([part1, part0]), own0)
-    full = seq_gather(early)
-    full, rest0 = tie(full, rest0)
-    late = seq_gather(seq_parts([rest0]))
-    outer_1, rest_1 = taken(full[:, : part1.shape[0]], [fo1, rest1])
-    qkv_1, outer_0 = taken(full[:, part1.shape[0] :], [qkv1, fo0])
-    (rest_0,) = taken(late, [rest0])
-    qkv_0 = from_own(plan, own0[:, :-16])
-    bias0 = from_own(plan, own0[:, -16])
-    late0 = [lax.dynamic_slice_in_dim(bias0, part * D + item_rank * share, share) for part in (0, 2)]
-    late1 = split_rows(qkv_1[-16:], [share] * 2)
-    qkv_1 = from_all(plan, unpart(qkv_1[:-16]))
-    inner_1, attn_1, early1 = unpart(rest_1[: parts * share]), rest_1[parts * share : -16], split_rows(rest_1[-16:], counts)
-    inner_0, attn_0, early0 = unpart(rest_0[: parts * share]), rest_0[parts * share : -16], split_rows(rest_0[-16:], counts)
-    vecs = [jnp.stack(pair) for pair in zip(late0 + early0, late1 + early1)]
+    full0 = seq_gather(seq_sum(seq_send([fo0, rest0])))
+    owns = seq_gather(jnp.concatenate([own0, own1]))
+    qkv, bias, attn, inner_grad, outer, *small_grads = finish(
+        plan, share, w_ffn_in.shape[2], item, counts, (full0, full1), owns
+    )
+    bias_q, bias_v = (lax.dynamic_slice_in_dim(bias, part * D + item_rank * share, share, 1) for part in (0, 2))
+    out_bias, gain1, shift1, inner_bias, ffn_bias, gain2, shift2 = small_grads
     return (
         output.reshape(hidden.shape),
         input_grad.reshape(hidden.shape),
-        jnp.stack([qkv_0, qkv_1]),
-        vecs[0],
-        vecs[1],
-        jnp.stack([attn_0, attn_1]),
-        vecs[2],
-        vecs[3],
-        vecs[4],
-        jnp.stack([inner_0, inner_1]),
-        vecs[5],
-        jnp.stack([outer_0, outer_1]),
-        vecs[6],
-        vecs[7],
-        vecs[8],
+        qkv,
+        bias_q,
+        bias_v,
+        attn,
+        out_bias,
+        gain1,
+        shift1,
+        inner_grad,
+        inner_bias,
+        outer,
+        ffn_bias,
+        gain2,
+        shift2,
     )
 
 

time: 872 us -> 782 us (0.90)
  blocking collectives: 122 us -> 43.2 us
  other arithmetic: 25.7 us -> 14.1 us
  local copies, waits for them, and re-layouts: 56.4 us -> 45.7 us
  Pallas kernels: 345 us -> 354 us
    all_to_all x2 -> x0, blocking collectives: 78.7 us -> none  [exchange(): lax.all_to_all(y, 'seq', split_axis=0, concat_axis=0, tiled=True)]
    all_to_all x1 -> x0, waiting for transfers between devices: 39.1 us -> none  [local(): own0 = lax.all_to_all(own0, 'item', split_axis=0, concat_axis=0, tiled=True)]
    reduce_scatter x5 -> x6, waiting for transfers between devices: 0.01 us -> 24.4 us  [scattered(): return lax.psum_scatter(g, 'item', scatter_dimension=0, tiled=False)]
    all_to_all x13 -> x14, waiting for transfers between devices: 198 us -> 213 us  [exchange(): lax.all_to_all(y, 'seq', split_axis=0, concat_axis=0, tiled=True)]
    pallas_call x1 -> x2, Pallas kernels: 14.5 us -> 28.6 us  [own_grad(): pl.pallas_call(partial(own_grad_kernel, plan, item, plan.groups * plan.ch...]
    another operation x17 -> x0, other arithmetic: 12.1 us -> none  [the longest x9 5.14 us: local(): vecs = [jnp.stack(pair) for pair in zip(late0 + early0, late1 + early1)]]
    all_to_all x13 -> x14, starting transfers between devices: 52.4 us -> 57.1 us  [exchange(): lax.all_to_all(y, 'seq', split_axis=0, concat_axis=0, tiled=True)]
    unnamed x99 -> x79, local copies, waits for them, and re-layouts: 23 us -> 25.2 us
  transfers between devices with their start and end apart: 22 -> 24, of which waited for: 11 -> 12; matrix products, arithmetic and copies ran while one was open for 5% -> 4% of each run, Pallas kernels for 40% -> 46%
where the time goes in v4:
time: 782 us; the launch traced here: 771 us
  Pallas kernels  354 us (45%)
  waiting for transfers between devices  240 us (31%)
  starting transfers between devices  57.8 us (7%)
  local copies, waits for them, and re-layouts  45.7 us (6%)
  blocking collectives  43.2 us (6%)
  between operations  15.3 us (2%)
  other arithmetic  14.1 us (2%)
    all_to_all x14, waiting for transfers between devices, exchange(): lax.all_to_all(y, 'seq', split_axis=0, concat_axis=0, tiled=True)  213 us
    pallas_call x2, Pallas kernels, attn_bwd(): pl.pallas_call(partial(attn_bwd_kernel, plan), out_shape=jax.ShapeDtypeSt...  100 us
    pallas_call x2, Pallas kernels, attn_fwd(): pl.pallas_call(partial(attn_fwd_kernel, plan), out_shape=jax.ShapeDtypeSt...  57.6 us
    all_to_all x14, starting transfers between devices, exchange(): lax.all_to_all(y, 'seq', split_axis=0, concat_axis=0, tiled=True)  57.1 us
    pallas_call x1, Pallas kernels, layer_mid(): pl.pallas_call(partial(mid_kernel, plan, ff), out_shape=[jax.ShapeDtypeSt...  41.3 us
    pallas_call x2, Pallas kernels, dense_grads(): pl.pallas_call(partial(dense_grad_kernel, item), out_shape=[jax.ShapeDtyp...  37.6 us
    pallas_call x1, Pallas kernels, layer_bwd(): pl.pallas_call(partial(bwd_kernel, plan, ff), out_shape=[jax.ShapeDtypeSt...  34.5 us
    pallas_call x1, Pallas kernels, layer_fwd(): pl.pallas_call(partial(fwd_kernel, plan, ff), out_shape=[jax.ShapeDtypeSt...  29.4 us
  transfers between devices with their start and end apart: 24, of which 12 were waited for; matrix products, arithmetic and copies ran while one was open for 4% of the time, Pallas kernels for 46%

profile of v4, /device:TPU:0, one launch (start us, length us, event | category | flops | bytes accessed | tf_op | source)
XLA Modules:
  0.0 770.8 jit_solution(3446826010105950605)
XLA Ops:
  23.1 5.4 all-to-all-start
  29.4 18.1 %all-gather.5 = bf16[8,2,1152]{2,1,0:T(2,128)(2,1)S(1)} all-gather(bf16[1,2,1152]{2,1,0:T(2,128)(2,1)S(1)} %bitcast.175), channel_id=3, replica_groups=mesh['seq'=4,'item'=8] {'item'}, dimensions={0}, use_global_device_ids=true | all-gather | bytes 41472 | tf_op jit(solution)/shard_map/all_gather | solution.py:926
  49.3 25.1 %all-gather = bf16[768,576]{1,0:T(8,128)(2,1)S(1)} all-gather(bf16[96,576]{1,0:T(8,128)(2,1)S(1)} %pad_maximum_fusion.4), channel_id=2, replica_groups=mesh['seq'=4,'item'=8] {'item'}, dimensions={0}, use_global_device_ids=true | all-gather | bytes 995328 | tf_op jit(solution)/shard_map/all_gather | solution.py:938
  74.4 25.4 %all-to-all-done = bf16[4,1024,768]{2,1,0:T(8,128)(2,1)} async-done(((bf16[4,1024,768]{2,1,0:T(8,128)(2,1)}), bf16[4,1024,768]{2,1,0:T(8,128)(2,1)}, u32[]{:S(2)}, u32[]{:S(2)}) %all-to-all-start) | async-done | bytes 6291488 | tf_op jit(solution)/shard_map/all_to_all | solution.py:865
  103.9 13.3 %own_heads.1 = bf16[4,4,9,2,64,128]{5,4,3,2,1,0:T(8,128)(2,1)S(1)} custom-call(bf16[4,2,4,128,768]{4,3,2,1,0:T(8,128)(2,1)} %bitcast.8.a_ref, bf16[8,96,576]{2,1,0:T(8,128)(2,1)S(1)} %bitcast.129, f32[1,576]{1,0:T(1,128)S(1)} %pad_maximum_fusion.9.b_ref), custom_call_target="tpu_custom_call" | custom-call | flops 7000000000 | bytes 12000000 | tf_op jit(solution)/shard_map/own_heads/pallas_call | solution.py:444
  122.5 28.9 %attn_fwd.2 = bf16[96,64,128]{2,1,0:T(8,128)(2,1)} custom-call(s32[1536]{0:T(1024)S(1)} %reshape.243.lists_ref, bf16[288,64,128]{2,1,0:T(8,128)(2,1)} %bitcast.130), custom_call_target="tpu_custom_call" | custom-call | flops 25999998976 | bytes 6000000 | tf_op jit(solution)/shard_map/attn_fwd/pallas_call | solution.py:206
  159.8 14.2 %all-to-all-done.2 = bf16[4,1536,128]{2,1,0:T(8,128)(2,1)S(1)} async-done(((bf16[4,1536,128]{2,1,0:T(8,128)(2,1)}), bf16[4,1536,128]{2,1,0:T(8,128)(2,1)S(1)}, u32[]{:S(2)}, u32[]{:S(2)}) %all-to-all-start.2) | async-done | bytes 1572896 | tf_op jit(solution)/shard_map/all_to_all | solution.py:865
  175.1 29.4 %layer_fwd.1 = (bf16[4,4,9,2,64,128]{5,4,3,2,1,0:T(8,128)(2,1)}, f32[2,512,768]{2,1,0:T(8,128)}, bf16[2,512,768]{2,1,0:T(8,128)(2,1)}, f32[2,512,768]{2,1,0:T(8,...) custom-call(bf16[4,4,3,2,64,128]{5,4,3,2,1,0:T(8,128)(2,1)} %bitcast, ...), custom_call_target="tpu_custom_call" | custom-call | flops 30000001024 | bytes 50000000 | tf_op jit(solution)/shard_map/layer_fwd/pallas_call | solution.py:599
  204.5 5.0 all-to-all-start.3
  210.2 51.8 %all-to-all-done.3 = bf16[4,4608,128]{2,1,0:T(8,128)(2,1)} async-done(((bf16[4,4608,128]{2,1,0:T(8,128)(2,1)}), bf16[4,4608,128]{2,1,0:T(8,128)(2,1)}, u32[]{:S(2)}, u32[]{:S(2)}) %all-to-all-start.3) | async-done | bytes 4718624 | tf_op jit(solution)/shard_map/all_to_all | solution.py:865
  262.1 28.8 %attn_fwd.3 = bf16[96,64,128]{2,1,0:T(8,128)(2,1)} custom-call(s32[1536]{0:T(1024)S(1)} %reshape.242.lists_ref, bf16[288,64,128]{2,1,0:T(8,128)(2,1)} %bitcast.45.x_ref), custom_call_target="tpu_custom_call" | custom-call | flops 25999998976 | bytes 6000000 | tf_op jit(solution)/shard_map/attn_fwd/pallas_call | solution.py:206
  295.9 17.5 %all-to-all-done.4 = bf16[4,1536,128]{2,1,0:T(8,128)(2,1)S(1)} async-done(((bf16[4,1536,128]{2,1,0:T(8,128)(2,1)}), bf16[4,1536,128]{2,1,0:T(8,128)(2,1)S(1)}, u32[]{:S(2)}, u32[]{:S(2)}) %all-to-all-start.4) | async-done | bytes 1572896 | tf_op jit(solution)/shard_map/all_to_all | solution.py:865
  314.6 41.3 %layer_mid.1 = (bf16[4,4,3,2,64,128]{5,4,3,2,1,0:T(8,128)(2,1)}, f32[2,512,768]{2,1,0:T(8,128)}, f32[2,512,768]{2,1,0:T(8,128)}, bf16[2,512,3072]{2,1,0:T(8,128)...) custom-call(bf16[4,4,3,2,64,128]{5,4,3,2,1,0:T(8,128)(2,1)} %bitcast, ...), custom_call_target="tpu_custom_call" | custom-call | flops 44999999488 | bytes 50000000 | tf_op jit(solution)/shard_map/layer_mid/pallas_call | solution.py:681
  362.9 18.8 %dense_grads.2 = (bf16[8,384,768]{2,1,0:T(8,128)(2,1)}, bf16[8,496,768]{2,1,0:T(8,128)(2,1)}) custom-call(bf16[1024,3072]{1,0:T(8,128)(2,1)} %bitcast.186, bf16[1024,768]{1,0:T(8,128)(2,1)} %bitcast.194, bf16[1024,768]{1,0:T(8,128)(2,1)} %bitcast.196, bf16[1024,3072]{1,0:T(8,128)(2,1)} %bitcast.187, bf16[1024,768]{1,0:T(8,128)(2,1)} %bitcast.197, ...), custom_call_target="tpu_custom_call" | custom-call | flops 14000000000 | bytes 30000000 | tf_op jit(solution)/shard_map/dense_grads/pallas_call | solution.py:758
  381.7 8.4 %all-to-all-done.5 = bf16[4,1536,128]{2,1,0:T(8,128)(2,1)S(1)} async-done(((bf16[4,1536,128]{2,1,0:T(8,128)(2,1)}), bf16[4,1536,128]{2,1,0:T(8,128)(2,1)S(1)}, u32[]{:S(2)}, u32[]{:S(2)}) %all-to-all-start.5) | async-done | bytes 1572896 | tf_op jit(solution)/shard_map/all_to_all | solution.py:865
  391.9 50.1 %attn_bwd.2 = bf16[288,64,128]{2,1,0:T(8,128)(2,1)} custom-call(s32[1536]{0:T(1024)} %copy-done.5, bf16[288,64,128]{2,1,0:T(8,128)(2,1)} %bitcast.45.x_ref, bf16[96,64,128]{2,1,0:T(8,128)(2,1)} %bitcast.144), custom_call_target="tpu_custom_call" | custom-call | flops 46000001024 | bytes 12000000 | tf_op jit(solution)/shard_map/attn_bwd/pallas_call | solution.py:328
  442.0 5.0 all-to-all-start.6
  449.4 14.3 %own_grad.2 = bf16[8,112,576]{2,1,0:T(8,128)(2,1)} custom-call(bf16[4,2,4,128,768]{4,3,2,1,0:T(8,128)(2,1)} %bitcast.181, bf16[4,4,9,2,64,128]{5,4,3,2,1,0:T(8,128)(2,1)S(1)} %bitcast.128), custom_call_target="tpu_custom_call" | custom-call | flops 7000000000 | bytes 12000000 | tf_op jit(solution)/shard_map/own_grad/pallas_call | solution.py:483
  463.7 36.4 %all-to-all-done.6 = bf16[4,4608,128]{2,1,0:T(8,128)(2,1)} async-done(((bf16[4,4608,128]{2,1,0:T(8,128)(2,1)}), bf16[4,4608,128]{2,1,0:T(8,128)(2,1)}, u32[]{:S(2)}, u32[]{:S(2)}) %all-to-all-start.6) | async-done | bytes 4718624 | tf_op jit(solution)/shard_map/all_to_all | solution.py:865
  500.1 34.5 %layer_bwd.1 = (bf16[4,4,3,2,64,128]{5,4,3,2,1,0:T(8,128)(2,1)}, f32[2,512,768]{2,1,0:T(8,128)}, bf16[2,512,3072]{2,1,0:T(8,128)(2,1)}, bf16[2,512,3072]{2,1,0:T...) custom-call(bf16[4,4,9,2,64,128]{5,4,3,2,1,0:T(8,128)(2,1)} %bitcast, ...), custom_call_target="tpu_custom_call" | custom-call | flops 40000000000 | bytes 50000000 | tf_op jit(solution)/shard_map/layer_bwd/pallas_call | solution.py:723
  541.6 18.9 %dense_grads.3 = (bf16[8,384,768]{2,1,0:T(8,128)(2,1)}, bf16[8,496,768]{2,1,0:T(8,128)(2,1)}) custom-call(bf16[1024,3072]{1,0:T(8,128)(2,1)} %bitcast.184, bf16[1024,768]{1,0:T(8,128)(2,1)} %bitcast.192, bf16[1024,768]{1,0:T(8,128)(2,1)} %bitcast.190, bf16[1024,3072]{1,0:T(8,128)(2,1)} %bitcast.185, bf16[1024,768]{1,0:T(8,128)(2,1)} %bitcast.191, ...), custom_call_target="tpu_custom_call" | custom-call | flops 14000000000 | bytes 30000000 | tf_op jit(solution)/shard_map/dense_grads/pallas_call | solution.py:758
  564.1 4.3 all-to-all-start.8
  568.4 50.1 %attn_bwd.3 = bf16[288,64,128]{2,1,0:T(8,128)(2,1)} custom-call(s32[1536]{0:T(1024)} %copy-done.4, bf16[288,64,128]{2,1,0:T(8,128)(2,1)} %bitcast.131, bf16[96,64,128]{2,1,0:T(8,128)(2,1)} %bitcast.143), custom_call_target="tpu_custom_call" | custom-call | flops 46000001024 | bytes 12000000 | tf_op jit(solution)/shard_map/attn_bwd/pallas_call | solution.py:328
  618.5 5.0 all-to-all-start.9
  626.3 14.3 %own_grad.3 = bf16[8,112,576]{2,1,0:T(8,128)(2,1)} custom-call(bf16[4,2,4,128,768]{4,3,2,1,0:T(8,128)(2,1)} %bitcast.8.a_ref, bf16[4,4,9,2,64,128]{5,4,3,2,1,0:T(8,128)(2,1)S(1)} %bitcast.126), custom_call_target="tpu_custom_call" | custom-call | flops 7000000000 | bytes 12000000 | tf_op jit(solution)/shard_map/own_grad/pallas_call | solution.py:483
  640.6 35.2 %all-to-all-done.9 = bf16[4,4608,128]{2,1,0:T(8,128)(2,1)} async-done(((bf16[4,4608,128]{2,1,0:T(8,128)(2,1)}), bf16[4,4608,128]{2,1,0:T(8,128)(2,1)}, u32[]{:S(2)}, u32[]{:S(2)}) %all-to-all-start.9) | async-done | bytes 4718624 | tf_op jit(solution)/shard_map/all_to_all | solution.py:865
  680.6 5.3 reduce-scatter.15.cloned.1.call-done
  688.4 8.8 %all-to-all-done.12.refs_1_ = bf16[4,224,768]{2,1,0:T(8,128)(2,1)S(1)} async-done(((bf16[4,224,768]{2,1,0:T(8,128)(2,1)}), bf16[4,224,768]{2,1,0:T(8,128)(2,1)S(1)}, u32[]{:S(2)}, u32[]{:S(2)}) %all-to-all-start.12) | async-done | bytes 1376288 | tf_op jit(solution)/shard_map/all_to_all | solution.py:865
  700.7 19.1 %reduce-scatter.17.cloned.1.call-done = bf16[1,112,576]{2,1,0:T(8,128)(2,1)} async-done(((bf16[8,112,576]{2,1,0:T(8,128)(2,1)}), bf16[1,112,576]{2,1,0:T(8,128)(2,1)}) %reduce-scatter.17.cloned.1.call-update) | async-done | bytes 129040 | tf_op jit(solution)/shard_map/reduce_scatter | solution.py:965
  727.4 9.9 %all-to-all-done.13.refs_2_ = bf16[4,224,576]{2,1,0:T(8,128)(2,1)S(1)} async-done(((bf16[4,224,576]{2,1,0:T(8,128)(2,1)}), bf16[4,224,576]{2,1,0:T(8,128)(2,1)S(1)}, u32[]{:S(2)}, u32[]{:S(2)}) %all-to-all-start.13) | async-done | bytes 1032224 | tf_op jit(solution)/shard_map/all_to_all | solution.py:865
  744.2 8.3 %layer_tail.1 = f32[2,512,768]{2,1,0:T(8,128)} custom-call(bf16[4,4,9,2,64,128]{5,4,3,2,1,0:T(8,128)(2,1)} %bitcast.88.dx_ref, f32[2,512,768]{2,1,0:T(8,128)S(1)} %copy-done.7, bf16[8,288,768]{2,1,0:T(8,128)(2,1)} %bitcast.182), custom_call_target="tpu_custom_call" | custom-call | flops 8000000000 | bytes 12000000 | tf_op jit(solution)/shard_map/layer_tail/pallas_call | solution.py:780
  752.6 5.7 all-to-all-done.11.refs_0_
  (246 shorter events, 98.9 us)
Async XLA Ops:
  7.2 2.5 copy-start.16
  7.2 166.7 %all-gather.13.cloned.1.call-start = ((), (), s32[]{:S(2)}) async-start(), calls=%async_computation.27 | async-start | bytes 15925248 | tf_op jit(solution)/shard_map/all_gather | solution.py:945
  18.6 277.3 %all-gather.15.cloned.1.call-start = ((), (), s32[]{:S(2)}) async-start(), calls=%async_computation.28 | async-start | bytes 11943936 | tf_op jit(solution)/shard_map/all_gather | solution.py:946
  23.1 5.5 copy-start.10
  23.1 76.8 %all-to-all-start = ((bf16[4,1024,768]{2,1,0:T(8,128)(2,1)}), bf16[4,1024,768]{2,1,0:T(8,128)(2,1)}, u32[]{:S(2)}, u32[]{:S(2)}) async-start(bf16[4,1024,768]{2,1,0:T(8,128)(2,1)} %broadcast_in_dim.14), calls=%async_computation | async-start | bytes 12582912 | tf_op jit(solution)/shard_map/all_to_all | solution.py:865
  48.6 51.3 %copy-start.22 = (s32[1,2,16,12,3]{2,1,4,3,0:T(2,128)S(1)}, s32[1,2,16,12,3]{2,1,4,3,0:T(2,128)}, u32[]{:S(2)}) copy-start(s32[1,2,16,12,3]{2,1,4,3,0:T(2,128)} %param.17) | copy-start | bytes 13828
  100.7 18.8 %all-to-all-start.1 = ((s32[4,1,288]{2,1,0:T(1,128)}), s32[4,1,288]{2,1,0:T(1,128)S(1)}, u32[]{:S(2)}, u32[]{:S(2)}) async-start(s32[4,1,288]{2,1,0:T(1,128)} %reshape.293), calls=%async_computation.1 | async-start | bytes 12288 | tf_op jit(solution)/shard_map/all_to_all | solution.py:865
  122.5 28.9 %copy-start.4 = (s32[1536]{0:T(1024)}, s32[1536]{0:T(1024)S(1)}, u32[]{:S(2)}) copy-start(s32[1536]{0:T(1024)S(1)} %reshape.243.lists_ref) | copy-start | bytes 18436
  151.4 22.5 %all-to-all-start.2 = ((bf16[4,1536,128]{2,1,0:T(8,128)(2,1)}), bf16[4,1536,128]{2,1,0:T(8,128)(2,1)S(1)}, u32[]{:S(2)}, u32[]{:S(2)}) async-start(bf16[4,1536,128]{2,1,0:T(8,128)(2,1)} %bitcast.26), calls=%async_computation.2 | async-start | bytes 3145728 | tf_op jit(solution)/shard_map/all_to_all | solution.py:865
  155.4 236.5 %all-gather.17.cloned.1.call-start = ((), (), s32[]{:S(2)}) async-start(), calls=%async_computation.29 | async-start | bytes 3981312 | tf_op jit(solution)/shard_map/all_gather | solution.py:947
  204.5 57.6 %all-to-all-start.3 = ((bf16[4,4608,128]{2,1,0:T(8,128)(2,1)}), bf16[4,4608,128]{2,1,0:T(8,128)(2,1)}, u32[]{:S(2)}, u32[]{:S(2)}) async-start(bf16[4,4608,128]{2,1,0:T(8,128)(2,1)} %bitcast.133), calls=%async_computation.3 | async-start | bytes 9437184 | tf_op jit(solution)/shard_map/all_to_all | solution.py:865
  209.5 182.4 %all-gather.11.cloned.1.call-start = ((), (), s32[]{:S(2)}) async-start(), calls=%async_computation.20 | async-start | bytes 7864320 | tf_op jit(solution)/shard_map/all_gather | solution.py:956
  210.2 80.6 %copy-start.5 = (s32[1536]{0:T(1024)}, s32[1536]{0:T(1024)S(1)}, u32[]{:S(2)}) copy-start(s32[1536]{0:T(1024)S(1)} %reshape.242.lists_ref) | copy-start | bytes 18436
  290.8 22.6 %all-to-all-start.4 = ((bf16[4,1536,128]{2,1,0:T(8,128)(2,1)}), bf16[4,1536,128]{2,1,0:T(8,128)(2,1)S(1)}, u32[]{:S(2)}, u32[]{:S(2)}) async-start(bf16[4,1536,128]{2,1,0:T(8,128)(2,1)} %bitcast.46), calls=%async_computation.4 | async-start | bytes 3145728 | tf_op jit(solution)/shard_map/all_to_all | solution.py:865
  359.3 30.9 %all-to-all-start.5 = ((bf16[4,1536,128]{2,1,0:T(8,128)(2,1)}), bf16[4,1536,128]{2,1,0:T(8,128)(2,1)S(1)}, u32[]{:S(2)}, u32[]{:S(2)}) async-start(bf16[4,1536,128]{2,1,0:T(8,128)(2,1)} %bitcast.142), calls=%async_computation.5 | async-start | bytes 3145728 | tf_op jit(solution)/shard_map/all_to_all | solution.py:865
  362.8 137.3 %reduce-scatter.7.cloned.1.call-start = ((), (), s32[]{:S(2)}) async-start(), calls=%async_computation.21 | async-start | bytes 5308416 | tf_op jit(solution)/shard_map/reduce_scatter | solution.py:965
  391.3 146.7 %reduce-scatter.9.cloned.1.call-start = ((), (), s32[]{:S(2)}) async-start(), calls=%async_computation.22 | async-start | bytes 6856704 | tf_op jit(solution)/shard_map/reduce_scatter | solution.py:965
  442.0 58.1 %all-to-all-start.6 = ((bf16[4,4608,128]{2,1,0:T(8,128)(2,1)}), bf16[4,4608,128]{2,1,0:T(8,128)(2,1)}, u32[]{:S(2)}, u32[]{:S(2)}) async-start(bf16[4,4608,128]{2,1,0:T(8,128)(2,1)} %bitcast.127), calls=%async_computation.6 | async-start | bytes 9437184 | tf_op jit(solution)/shard_map/all_to_all | solution.py:865
  447.0 113.5 %reduce-scatter.11.cloned.1.call-start = ((), (), s32[]{:S(2)}) async-start(), calls=%async_computation.23 | async-start | bytes 1290240 | tf_op jit(solution)/shard_map/reduce_scatter | solution.py:965
  447.1 2.4 copy-start.1
  538.0 22.5 %all-to-all-start.7 = ((bf16[4,1536,128]{2,1,0:T(8,128)(2,1)}), bf16[4,1536,128]{2,1,0:T(8,128)(2,1)S(1)}, u32[]{:S(2)}, u32[]{:S(2)}) async-start(bf16[4,1536,128]{2,1,0:T(8,128)(2,1)} %bitcast.141), calls=%async_computation.9 | async-start | bytes 3145728 | tf_op jit(solution)/shard_map/all_to_all | solution.py:865
  541.6 139.0 %reduce-scatter.13.cloned.1.call-start = ((), (), s32[]{:S(2)}) async-start(), calls=%async_computation.24 | async-start | bytes 5308416 | tf_op jit(solution)/shard_map/reduce_scatter | solution.py:965
  561.7 124.2 %reduce-scatter.15.cloned.1.call-start = ((), (), s32[]{:S(2)}) async-start(), calls=%async_computation.25 | async-start | bytes 6856704 | tf_op jit(solution)/shard_map/reduce_scatter | solution.py:965
  564.1 54.4 %all-to-all-start.8 = ((bf16[4,224,768]{2,1,0:T(8,128)(2,1)}), bf16[4,224,768]{2,1,0:T(8,128)(2,1)S(1)}, u32[]{:S(2)}, u32[]{:S(2)}) async-start(bf16[4,224,768]{2,1,0:T(8,128)(2,1)} %bitcast.86), calls=%async_computation.11 | async-start | bytes 2752512 | tf_op jit(solution)/shard_map/all_to_all | solution.py:865
  618.5 57.4 %all-to-all-start.9 = ((bf16[4,4608,128]{2,1,0:T(8,128)(2,1)}), bf16[4,4608,128]{2,1,0:T(8,128)(2,1)}, u32[]{:S(2)}, u32[]{:S(2)}) async-start(bf16[4,4608,128]{2,1,0:T(8,128)(2,1)} %bitcast.125), calls=%async_computation.12 | async-start | bytes 9437184 | tf_op jit(solution)/shard_map/all_to_all | solution.py:865
  623.5 96.3 %reduce-scatter.17.cloned.1.call-start = ((), (), s32[]{:S(2)}) async-start(), calls=%async_computation.26 | async-start | bytes 1290240 | tf_op jit(solution)/shard_map/reduce_scatter | solution.py:965
  623.9 2.5 copy-start
  677.0 20.1 %all-to-all-start.12 = ((bf16[4,224,768]{2,1,0:T(8,128)(2,1)}), bf16[4,224,768]{2,1,0:T(8,128)(2,1)S(1)}, u32[]{:S(2)}, u32[]{:S(2)}) async-start(bf16[4,224,768]{2,1,0:T(8,128)(2,1)} %broadcast_in_dim.16), calls=%async_computation.17 | async-start | bytes 2752512 | tf_op jit(solution)/shard_map/all_to_all | solution.py:865
  688.4 31.5 %copy-start.21 = (bf16[1,112,576]{2,1,0:T(8,128)(2,1)S(1)}, bf16[1,112,576]{2,1,0:T(8,128)(2,1)}, u32[]{:S(2)}) copy-start(bf16[1,112,576]{2,1,0:T(8,128)(2,1)} %reduce-scatter.11.cloned.1.call-done) | copy-start | bytes 387076
  697.2 23.6 %all-to-all-start.10 = ((bf16[4,224,768]{2,1,0:T(8,128)(2,1)}), bf16[4,224,768]{2,1,0:T(8,128)(2,1)S(1)}, u32[]{:S(2)}, u32[]{:S(2)}) async-start(bf16[4,224,768]{2,1,0:T(8,128)(2,1)} %bitcast.132), calls=%async_computation.15 | async-start | bytes 2752512 | tf_op jit(solution)/shard_map/all_to_all | solution.py:865
  722.2 15.1 %all-to-all-start.13 = ((bf16[4,224,576]{2,1,0:T(8,128)(2,1)}), bf16[4,224,576]{2,1,0:T(8,128)(2,1)S(1)}, u32[]{:S(2)}, u32[]{:S(2)}) async-start(bf16[4,224,576]{2,1,0:T(8,128)(2,1)} %broadcast_in_dim.17), calls=%async_computation.19 | async-start | bytes 2293760 | tf_op jit(solution)/shard_map/all_to_all | solution.py:865
  738.8 19.5 %all-to-all-start.11 = ((bf16[4,224,768]{2,1,0:T(8,128)(2,1)}), bf16[4,224,768]{2,1,0:T(8,128)(2,1)S(1)}, u32[]{:S(2)}, u32[]{:S(2)}) async-start(bf16[4,224,768]{2,1,0:T(8,128)(2,1)} %broadcast_in_dim.15), calls=%async_computation.16 | async-start | bytes 2752512 | tf_op jit(solution)/shard_map/all_to_all | solution.py:865
  (24 other events, 26.9 us)
Sparse Core Ops, SparseCore 0:
  18.7 140.4 all-gather.12
  161.5 98.6 all-gather.14
  262.3 39.8 all-gather.16
  304.5 85.5 all-gather.10
  392.3 54.0 reduce-scatter.6
  448.6 66.2 reduce-scatter.8
  517.3 31.0 reduce-scatter.10
  560.7 56.4 reduce-scatter.12
  619.6 66.2 reduce-scatter.14
  688.6 31.1 reduce-scatter.16

commit v5 on v4

--- a/solution.py
+++ b/solution.py
@@ -430,31 +430,151 @@
     return pl.BlockSpec(shape, lambda *i: (0,) * len(shape), pipeline_mode=pl.Buffered(1))
 
 
-def own_kernel(plan, a_ref, w_ref, b_ref, o_ref):
-    a = a_ref[...].reshape(plan.rows, D)
-    y = (dot(a, rows_of(w_ref), NN) + b_ref[...]).astype(BF)
+MESH = pl.DeviceIdType.MESH
+SMALL = 32
+
+
+def start_kernel(plan, item, hid_ref, shard_ref, small_ref, ids_ref, all_ref, x_ref, small_all_ref, ids_all_ref,
+                 hall, wall, xall, h_send, h_recv, i_send, i_recv, w_send, w_recv, v_send, v_recv, local_sem):
+    groups = plan.groups
+    me = lax.axis_index("seq")
+    rank = lax.axis_index("item")
+    seq_peers = [lax.rem(me + k, groups) for k in range(1, groups)]
+    item_peers = [lax.rem(rank + k, item) for k in range(1, item)]
+    barrier = pltpu.get_barrier_semaphore()
+    for p in seq_peers:
+        pl.semaphore_signal(barrier, inc=1, device_id=(p, rank), device_id_type=MESH)
+    for p in item_peers:
+        pl.semaphore_signal(barrier, inc=1, device_id=(me, p), device_id_type=MESH)
+    pl.semaphore_wait(barrier, len(seq_peers) + len(item_peers))
+
+    def remote(src, dst, send, recv, seq, it):
+        copy = pltpu.make_async_remote_copy(
+            src_ref=src, dst_ref=dst, send_sem=send, recv_sem=recv, device_id=(seq, it), device_id_type=MESH
+        )
+        copy.start()
+        return copy
+
+    if groups == 4:
+        xn = me + 1 - 2 * lax.rem(me, 2)
+        yn = lax.rem(me + 2, 4)
+        dn = lax.rem(xn + 2, 4)
+        order = [xn, yn, dn]
+
+        def to(n, half):
+            return remote(hid_ref.at[half], hall.at[me, half], h_send.at[n, half], h_recv.at[n, half], (xn, yn)[n], rank)
+
+        sent = {(0, 0): to(0, 0), (1, 1): to(1, 1)}
+        sent[0, 1] = to(0, 1)
+        sent[1, 0] = to(1, 0)
+    else:
+        order = [lax.rem(me + groups - k, groups) for k in range(1, groups)]
+        sent = {}
+        for k, p in enumerate(seq_peers):
+            for half in range(2):
+                sent[k, half] = remote(hid_ref.at[half], hall.at[me, half], h_send.at[k, half], h_recv.at[k, half], p, rank)
+    shards = [remote(shard_ref, wall.at[rank], w_send.at[k], w_recv.at[k], me, p) for k, p in enumerate(item_peers)]
+    smalls = [remote(small_ref, small_all_ref.at[rank], v_send.at[k], v_recv.at[k], me, p) for k, p in enumerate(item_peers)]
+    lists = [remote(ids_ref.at[p], ids_all_ref.at[me], i_send.at[k], i_recv.at[k], p, rank) for k, p in enumerate(seq_peers)]
+    mine = [
+        pltpu.make_async_copy(hid_ref, all_ref.at[me], local_sem.at[0]),
+        pltpu.make_async_copy(hid_ref, hall.at[me], local_sem.at[1]),
+    ]
+    for copy in mine:
+        copy.start()
+    wall[rank] = shard_ref[...]
+    small_all_ref[rank] = small_ref[...]
+    ids_all_ref[me] = ids_ref[me]
+    for copy in shards:
+        copy.wait()
+    mine[1].wait()
+    share = D // item
     one = Plan.__new__(Plan)
     one.__dict__.update(plan.__dict__)
     one.groups = 1
-    put_heads(one, y, o_ref.at[:, 0])
-
-
-def own_heads(plan, hidden_all, weight, bias):
-    a = hidden_all.reshape(plan.groups, 2, plan.chunks, plan.half, D)
+    out = []
+
+    def project(source, n):
+        weight = wall[:, :share].reshape(D, plan.own)
+        bias = jnp.sum(wall[:, share : share + 1].astype(F32), 0)
+
+        def chunk(c, carry):
+            rows = pl.ds(pl.multiple_of(c * plan.half, plan.half), plan.half)
+            a = jnp.concatenate([hall[source, 0, rows], hall[source, 1, rows]], 0)
+            put_heads(one, (dot(a, weight, NN) + bias).astype(BF), xall.at[pl.ds(source, 1), c])
+            return carry
+
+        lax.fori_loop(0, plan.chunks, chunk, 0)
+        copy = pltpu.make_async_copy(xall.at[source], x_ref.at[source], local_sem.at[2 + n])
+        copy.start()
+        out.append(copy)
+
+    if groups == 4:
+        sent[0, 0].wait_recv()
+        forward = [remote(hall.at[xn, 0], hall.at[xn, 0], h_send.at[2, 0], h_recv.at[2, 0], yn, rank)]
+        sent[1, 1].wait_recv()
+        forward.append(remote(hall.at[yn, 1], hall.at[yn, 1], h_send.at[2, 1], h_recv.at[2, 1], xn, rank))
+        project(me, 0)
+        sent[0, 1].wait_recv()
+        project(xn, 1)
+        sent[1, 0].wait_recv()
+        project(yn, 2)
+        for copy in forward:
+            copy.wait_recv()
+        project(dn, 3)
+        ends = list(sent.values()) + forward
+    else:
+        project(me, 0)
+        for k in range(groups - 1):
+            for half in range(2):
+                sent[k, half].wait_recv()
+            project(order[k], k + 1)
+        ends = list(sent.values())
+    for k, source in enumerate(order):
+        copy = pltpu.make_async_copy(hall.at[source], all_ref.at[source], local_sem.at[2 + groups + k])
+        copy.start()
+        out.append(copy)
+    for copy in ends:
+        copy.wait_send()
+    for copy in smalls + lists:
+        copy.wait()
+    mine[0].wait()
+    for copy in out:
+        copy.wait()
+
+
+def start(plan, item, hidden_low, shard, small, ids):
+    g = plan.groups
+    dma = pltpu.SemaphoreType.DMA
+    hid = hidden_low.reshape(2, plan.tokens // 2, D)
     return pl.pallas_call(
-        partial(own_kernel, plan),
-        out_shape=jax.ShapeDtypeStruct(plan.x_shape(), BF),
-        grid=(plan.groups, plan.chunks),
-        in_specs=[
-            pl.BlockSpec((1, 2, 1, plan.half, D), lambda g, c: (g, 0, c, 0, 0)),
-            whole(weight.shape),
-            whole(bias.shape),
+        partial(start_kernel, plan, item),
+        out_shape=[
+            jax.ShapeDtypeStruct((g,) + hid.shape, BF),
+            jax.ShapeDtypeStruct(plan.x_shape(), BF),
+            jax.ShapeDtypeStruct((item,) + small.shape, BF),
+            jax.ShapeDtypeStruct(ids.shape, jnp.int32),
         ],
-        out_specs=pl.BlockSpec((1, 1) + plan.x_shape()[2:], lambda g, c: (g, c, 0, 0, 0, 0)),
-        compiler_params=pltpu.CompilerParams(vmem_limit_bytes=48 << 20),
-        cost_estimate=pl.CostEstimate(flops=7 * 10**9, bytes_accessed=12 * 10**6, transcendentals=0),
-        name="own_heads",
-    )(a, weight, bias)
+        in_specs=[pl.BlockSpec(memory_space=VMEM)] * 4,
+        out_specs=[pl.BlockSpec(memory_space=pl.ANY)] * 2 + [pl.BlockSpec(memory_space=VMEM)] * 2,
+        scratch_shapes=[
+            VMEM((g,) + hid.shape, BF),
+            VMEM((item,) + shard.shape, BF),
+            VMEM(plan.x_shape(), BF),
+            dma((g - 1, 2)),
+            dma((g - 1, 2)),
+            dma((g - 1,)),
+            dma((g - 1,)),
+            dma((item - 1,)),
+            dma((item - 1,)),
+            dma((item - 1,)),
+            dma((item - 1,)),
+            dma((2 + 2 * g,)),
+        ],
+        compiler_params=pltpu.CompilerParams(collective_id=1, has_side_effects=True, vmem_limit_bytes=40 << 20),
+        cost_estimate=pl.CostEstimate(flops=55 * 10**9, bytes_accessed=12 * 10**6, transcendentals=0),
+        name="start",
+    )(hid, shard, small, ids)
 
 
 def own_grad_kernel(plan, item, steps, a_ref, d_ref, o_ref, acc_ref, sum_ref):
@@ -473,22 +593,24 @@
     def _():
         share = D // item
         total = jnp.broadcast_to(jnp.sum(sum_ref[...], 0, keepdims=True), (16, sum_ref.shape[1])).astype(BF)
+        own = sum_ref.shape[1]
         for r in range(item):
-            o_ref[r, :share] = acc_ref[r * share : (r + 1) * share].astype(BF)
-            o_ref[r, share:] = total
+            o_ref[r, :share, :own] = acc_ref[r * share : (r + 1) * share].astype(BF)
+            o_ref[r, share:, :own] = total
+            o_ref[r, :, own:] = jnp.zeros((share + 16, o_ref.shape[2] - own), BF)
 
 
 def own_grad(plan, item, hidden_all, dx):
     a = hidden_all.reshape(plan.groups, 2, plan.chunks, plan.half, D)
     return pl.pallas_call(
         partial(own_grad_kernel, plan, item, plan.groups * plan.chunks),
-        out_shape=jax.ShapeDtypeStruct((item, D // item + 16, plan.own), BF),
+        out_shape=jax.ShapeDtypeStruct((item, D // item + 16, D), BF),
         grid=(plan.groups, plan.chunks),
         in_specs=[
             pl.BlockSpec((1, 2, 1, plan.half, D), lambda g, c: (g, 0, c, 0, 0)),
             pl.BlockSpec((1, 1) + plan.x_shape()[2:], lambda g, c: (g, c, 0, 0, 0, 0)),
         ],
-        out_specs=whole((item, D // item + 16, plan.own)),
+        out_specs=whole((item, D // item + 16, D)),
         scratch_shapes=[VMEM((D, plan.own), F32), VMEM((8, plan.own), F32)],
         compiler_params=pltpu.CompilerParams(vmem_limit_bytes=48 << 20),
         cost_estimate=pl.CostEstimate(flops=7 * 10**9, bytes_accessed=12 * 10**6, transcendentals=0),
@@ -533,8 +655,10 @@
         first = self.share * (1 + self.parts)
         return self.ref[n * ranks : (n + 1) * ranks, first : first + self.share * self.parts].reshape(D, D)
 
-    def columns(self, n):
-        return self.rows(self.share * (1 + 2 * self.parts + n))
+
+def column_part(ref, n):
+    share = D // ref.shape[0]
+    return ref[:, n * share : (n + 1) * share].reshape(D, D)
 
 
 def wide_parts(w):
@@ -563,10 +687,67 @@
     return ref[:, :, part_of(n)].reshape(-1, D)
 
 
-def fwd_kernel(plan, ff, c_ref, h_ref, w_ref, vec_ref, inner_ref, bias_ref,
-               x_ref, next_ref, next_low_ref, r1_ref, r2_ref, u_ref, y_ref, ctx_ref):
+class Swap:
+    def __init__(self, plan, src, buf, send, recv, own):
+        self.plan, self.src, self.buf, self.send, self.recv, self.own = plan, src, buf, send, recv, own
+        self.me = lax.axis_index("seq")
+        self.rank = lax.axis_index("item")
+
+    def copy(self, c, k):
+        peer = lax.rem(self.me + k, self.plan.groups)
+        return pltpu.make_async_remote_copy(
+            src_ref=self.src.at[peer, c],
+            dst_ref=self.buf.at[self.me, c],
+            send_sem=self.send.at[c, k - 1],
+            recv_sem=self.recv.at[c, k - 1],
+            device_id=(peer, self.rank),
+            device_id_type=MESH,
+        )
+
+    def local(self):
+        return pltpu.make_async_copy(self.src.at[self.me], self.buf.at[self.me], self.own.at[0])
+
+    def step(self):
+        c, groups = pl.program_id(0), self.plan.groups
+
+        @pl.when(c == 0)
+        def _():
+            barrier = pltpu.get_barrier_semaphore()
+            for k in range(1, groups):
+                peer = lax.rem(self.me + k, groups)
+                pl.semaphore_signal(barrier, inc=1, device_id=(peer, self.rank), device_id_type=MESH)
+            pl.semaphore_wait(barrier, groups - 1)
+            self.local().start()
+            for n in range(self.plan.chunks):
+                for k in range(1, groups):
+                    self.copy(n, k).start()
+            self.local().wait()
+
+        for k in range(1, groups):
+            self.copy(c, k).wait_recv()
+        return self.buf[:, c]
+
+    def end(self):
+        c = pl.program_id(0)
+        for k in range(1, self.plan.groups):
+            self.copy(c, k).wait_send()
+
+    @staticmethod
+    def scratch(plan, shape):
+        sems = (plan.chunks, plan.groups - 1)
+        dma = pltpu.SemaphoreType.DMA
+        return [VMEM(shape, BF), dma(sems), dma(sems), dma((1,))]
+
+
+def swap_params(number):
+    return pltpu.CompilerParams(collective_id=number, has_side_effects=True, vmem_limit_bytes=60 << 20)
+
+
+def fwd_kernel(plan, ff, c_ref, h_ref, w_ref, vec_ref, inner_ref,
+               next_ref, next_low_ref, r1_ref, r2_ref, u_ref, y_ref, ctx_ref, *swapping):
+    swap = Swap(plan, c_ref, *swapping)
     w = Packed(w_ref, ff)
-    ctx = pick_context(plan, c_ref[:, 0])
+    ctx = pick_context(plan, swap.step())
     write(ctx_ref, ctx)
     r1, _, _, y1, y1_low = first_half(plan, ctx, read(h_ref), w, vec_ref)
     write(r1_ref, r1)
@@ -582,8 +763,13 @@
     low_ = nxt.astype(BF)
     write(next_ref, nxt)
     write(next_low_ref, low_)
+    swap.end()
+
+
+def project_kernel(plan, a_ref, w_ref, bias_ref, x_ref):
+    a = read(a_ref)
     y = [
-        (dot(low_, w.columns(n), NN) + bias_ref[:, part_of(n)]).astype(BF) for n in range(plan.cols // D)
+        (dot(a, column_part(w_ref, n), NN) + bias_ref[:, part_of(n)]).astype(BF) for n in range(plan.cols // D)
     ]
     put_heads(plan, jnp.concatenate(y, 1), x_ref.at[:, 0])
 
@@ -592,21 +778,34 @@
     return pl.BlockSpec((shape[0], 1) + shape[2:], lambda c: (0, c, 0, 0, 0, 0))
 
 
-def layer_fwd(plan, ctx, h, packed, vec, inner, bias):
+def layer_fwd(plan, ctx, h, packed, vec, inner):
     t = (2, plan.tokens // 2)
     ff = inner.shape[-1]
     shapes = [(D, F32), (D, BF), (D, F32), (D, F32), (ff, F32), (D, BF), (D, BF)]
     return pl.pallas_call(
         partial(fwd_kernel, plan, ff),
-        out_shape=[jax.ShapeDtypeStruct(plan.x_shape(), BF)] + [jax.ShapeDtypeStruct(t + (n,), d) for n, d in shapes],
+        out_shape=[jax.ShapeDtypeStruct(t + (n,), d) for n, d in shapes],
         grid=(plan.chunks,),
-        in_specs=[piece_spec(plan.c_shape()), halves(plan, D)]
-        + [whole(w.shape) for w in (packed, vec, inner, bias)],
-        out_specs=[piece_spec(plan.x_shape())] + [halves(plan, n) for n, _ in shapes],
-        compiler_params=pltpu.CompilerParams(vmem_limit_bytes=60 << 20),
-        cost_estimate=pl.CostEstimate(flops=30 * 10**9, bytes_accessed=50 * 10**6, transcendentals=3 * 10**6),
+        in_specs=[pl.BlockSpec(memory_space=pl.ANY), halves(plan, D)] + [whole(w.shape) for w in (packed, vec, inner)],
+        out_specs=[halves(plan, n) for n, _ in shapes],
+        scratch_shapes=Swap.scratch(plan, plan.c_shape()),
+        compiler_params=swap_params(2),
+        cost_estimate=pl.CostEstimate(flops=24 * 10**9, bytes_accessed=50 * 10**6, transcendentals=3 * 10**6),
         name="layer_fwd",
-    )(ctx, cut(plan, h), packed, vec, inner, bias)
+    )(ctx, cut(plan, h), packed, vec, inner)
+
+
+def project(plan, a, columns, bias):
+    return pl.pallas_call(
+        partial(project_kernel, plan),
+        out_shape=jax.ShapeDtypeStruct(plan.x_shape(), BF),
+        grid=(plan.chunks,),
+        in_specs=[halves(plan, D), whole(columns.shape), whole(bias.shape)],
+        out_specs=piece_spec(plan.x_shape()),
+        compiler_params=pltpu.CompilerParams(vmem_limit_bytes=48 << 20),
+        cost_estimate=pl.CostEstimate(flops=8 * 10**9, bytes_accessed=10 * 10**6, transcendentals=0),
+        name="project",
+    )(a, columns, bias)
 
 
 SUM_DO, D_GAIN1, D_SHIFT1, SUM_DF, D_GAIN2, D_SHIFT2 = range(6)
@@ -643,9 +842,10 @@
 
 
 def mid_kernel(plan, ff, c_ref, h_ref, gy_ref, w_ref, vec_ref, inner_ref,
-               d_ref, out_ref, dr1_ref, gz_ref, du_ref, df_ref, do_ref, y_ref, ctx_ref, sums_ref, inner_sum_ref, gate_ref):
+               d_ref, out_ref, dr1_ref, gz_ref, du_ref, df_ref, do_ref, y_ref, ctx_ref, sums_ref, inner_sum_ref, gate_ref, *swapping):
+    swap = Swap(plan, c_ref, *swapping)
     w = Packed(w_ref, ff)
-    ctx = pick_context(plan, c_ref[:, 0])
+    ctx = pick_context(plan, swap.step())
     write(ctx_ref, ctx)
     _, unit1, inv1, y1, y1_low = first_half(plan, ctx, read(h_ref), w, vec_ref)
     write(y_ref, y1_low)
@@ -664,6 +864,7 @@
     write(dr1_ref, dr1)
     write(df_ref, df)
     write(do_ref, do)
+    swap.end()
 
 
 def sum_specs(ff):
@@ -682,23 +883,31 @@
         partial(mid_kernel, plan, ff),
         out_shape=[jax.ShapeDtypeStruct(plan.c_shape(), BF)] + [jax.ShapeDtypeStruct(t + (n,), d) for n, d in shapes] + sums,
         grid=(plan.chunks,),
-        in_specs=[piece_spec(plan.c_shape()), halves(plan, D), halves(plan, D)]
+        in_specs=[pl.BlockSpec(memory_space=pl.ANY), halves(plan, D), halves(plan, D)]
         + [whole(w.shape) for w in (packed, vec, inner)],
         out_specs=[piece_spec(plan.c_shape())] + [halves(plan, n) for n, _ in shapes] + sums_at,
-        scratch_shapes=[VMEM((ff // D, plan.rows, D), F32)],
-        compiler_params=pltpu.CompilerParams(vmem_limit_bytes=60 << 20),
+        scratch_shapes=[VMEM((ff // D, plan.rows, D), F32)] + Swap.scratch(plan, plan.c_shape()),
+        compiler_params=swap_params(3),
         cost_estimate=pl.CostEstimate(flops=45 * 10**9, bytes_accessed=50 * 10**6, transcendentals=3 * 10**6),
         name="layer_mid",
     )(ctx, cut(plan, h), cut(plan, gy), packed, vec, inner)
 
 
-def bwd_kernel(plan, ff, dx_ref, up_ref, r1_ref, r2_ref, u_ref, w_ref, vec_ref,
-               d_ref, dr1_ref, gz_ref, du_ref, df_ref, do_ref, sums_ref, inner_sum_ref):
+def bwd_kernel(plan, ff, dx_ref, up_ref, r1_ref, r2_ref, u_ref, w_ref, cols_ref, vec_ref,
+               d_ref, dr1_ref, gz_ref, du_ref, df_ref, do_ref, dqkv_ref, sums_ref, inner_sum_ref, qkv_sum_ref, *swapping):
+    swap = Swap(plan, dx_ref, *swapping)
     w = Packed(w_ref, ff)
-    dqkv = pick_heads(plan, dx_ref[:, 0])
+    dqkv = pick_heads(plan, swap.step())
+    write(dqkv_ref, dqkv)
+
+    @pl.when(pl.program_id(0) == 0)
+    def _():
+        qkv_sum_ref[...] = jnp.zeros_like(qkv_sum_ref)
+
+    qkv_sum_ref[...] += jnp.sum(dqkv.astype(F32).reshape(-1, 8, dqkv.shape[-1]), 0)
     gy = read(up_ref)
     for n in range(plan.cols // D):
-        gy = gy + dot(dqkv[:, part_of(n)], w.columns(n), NT)
+        gy = gy + dot(dqkv[:, part_of(n)], column_part(cols_ref, n), NT)
 
     unit1, inv1 = normalise(read(r1_ref))
     unit2, inv2 = normalise(read(r2_ref))
@@ -713,24 +922,28 @@
     write(dr1_ref, dr1)
     write(df_ref, df)
     write(do_ref, do)
-
-
-def layer_bwd(plan, dx, up, r1, r2, u, packed, vec):
+    swap.end()
+
+
+def layer_bwd(plan, dx, up, r1, r2, u, packed, columns, vec):
     t = (2, plan.tokens // 2)
     ff = u.shape[-1]
-    shapes = [(D, F32), (ff, BF), (ff, BF), (D, BF), (D, BF)]
+    shapes = [(D, F32), (ff, BF), (ff, BF), (D, BF), (D, BF), (plan.cols, BF)]
     sums, sums_at = sum_specs(ff)
+    sums = sums + [jax.ShapeDtypeStruct((8, plan.cols), F32)]
+    sums_at = sums_at + [pl.BlockSpec((8, plan.cols), lambda c: (0, 0))]
     return pl.pallas_call(
         partial(bwd_kernel, plan, ff),
         out_shape=[jax.ShapeDtypeStruct(plan.c_shape(), BF)] + [jax.ShapeDtypeStruct(t + (n,), d) for n, d in shapes] + sums,
         grid=(plan.chunks,),
-        in_specs=[piece_spec(plan.x_shape()), halves(plan, D), halves(plan, D), halves(plan, D), halves(plan, ff)]
-        + [whole(w.shape) for w in (packed, vec)],
+        in_specs=[pl.BlockSpec(memory_space=pl.ANY), halves(plan, D), halves(plan, D), halves(plan, D), halves(plan, ff)]
+        + [whole(w.shape) for w in (packed, columns, vec)],
         out_specs=[piece_spec(plan.c_shape())] + [halves(plan, n) for n, _ in shapes] + sums_at,
-        compiler_params=pltpu.CompilerParams(vmem_limit_bytes=60 << 20),
+        scratch_shapes=Swap.scratch(plan, plan.x_shape()),
+        compiler_params=swap_params(4),
         cost_estimate=pl.CostEstimate(flops=40 * 10**9, bytes_accessed=50 * 10**6, transcendentals=3 * 10**6),
         name="layer_bwd",
-    )(dx, up, r1, r2, u, packed, vec)
+    )(dx, up, r1, r2, u, packed, columns, vec)
 
 
 def dense_grad_kernel(item, gz_ref, df_ref, y_ref, du_ref, ctx_ref, do_ref, vec_ref, fo_ref, rest_ref):
@@ -738,7 +951,15 @@
     parts = pl.num_programs(0)
     share = D // item
     ranks = item // parts
-    fo_ref[...] = dot(gz_ref[...], df_ref[...], TN).astype(BF).reshape(fo_ref.shape)
+    fo = dot(gz_ref[...], df_ref[...], TN).astype(BF)
+    if len(fo_ref.shape) == 3:
+        fo_ref[...] = fo.reshape(fo_ref.shape)
+    else:
+        count, here, rows = fo_ref.shape[:3]
+        for r in range(here):
+            for g in range(count):
+                first = (r * count + g) * rows
+                fo_ref[g, r] = fo[first : first + rows]
     first = pl.multiple_of(n * share, 16)
     rest_ref[:, pl.ds(first, share)] = dot(y_ref[...], du_ref[...], TN).astype(BF).reshape(item, share, D)
 
@@ -749,30 +970,60 @@
         rest_ref[:, at + share :] = vec_ref[...]
 
 
-def dense_grads(item, gz, df, y, du, ctx, do, vecs):
+def dense_grads(item, gz, df, y, du, ctx, do, vecs, cut_for=0):
     tokens, ff = gz.shape
     parts = ff // D
     share = D // item
     rest = parts * share + share + vecs.shape[1]
     column = pl.BlockSpec((tokens, D), lambda n: (0, n))
+    fo_shape, fo_spec = (item, ff // item, D), pl.BlockSpec((item // parts, ff // item, D), lambda n: (n, 0, 0))
+    if cut_for:
+        fo_shape = (cut_for, item, ff // item // cut_for, D)
+        fo_spec = pl.BlockSpec((cut_for, item // parts) + fo_shape[2:], lambda n: (0, n, 0, 0))
     return pl.pallas_call(
         partial(dense_grad_kernel, item),
-        out_shape=[jax.ShapeDtypeStruct((item, ff // item, D), BF), jax.ShapeDtypeStruct((item, rest, D), BF)],
+        out_shape=[jax.ShapeDtypeStruct(fo_shape, BF), jax.ShapeDtypeStruct((item, rest, D), BF)],
         grid=(parts,),
         in_specs=[column, whole(df.shape), whole(y.shape), column, whole(ctx.shape), whole(do.shape), whole(vecs.shape)],
-        out_specs=[pl.BlockSpec((item // parts, ff // item, D), lambda n: (n, 0, 0)), whole((item, rest, D))],
+        out_specs=[fo_spec, whole((item, rest, D))],
         compiler_params=pltpu.CompilerParams(vmem_limit_bytes=56 << 20),
         cost_estimate=pl.CostEstimate(flops=14 * 10**9, bytes_accessed=30 * 10**6, transcendentals=0),
         name="dense_grads",
     )(gz, df, y, du, ctx, do, vecs)
 
 
+def column_grad_kernel(item, a_ref, d_ref, vec_ref, o_ref):
+    n = pl.program_id(0)
+    share = D // item
+    first = pl.multiple_of(n * share, 16)
+    o_ref[:, pl.ds(first, share)] = dot(a_ref[...], d_ref[...], TN).astype(BF).reshape(item, share, D)
+
+    @pl.when(n == pl.num_programs(0) - 1)
+    def _():
+        o_ref[:, o_ref.shape[1] - vec_ref.shape[1] :] = vec_ref[...]
+
+
+def column_grads(item, a, d, vecs):
+    tokens = a.shape[0]
+    parts = d.shape[1] // D
+    out = (item, parts * (D // item) + vecs.shape[1], D)
+    return pl.pallas_call(
+        partial(column_grad_kernel, item),
+        out_shape=jax.ShapeDtypeStruct(out, BF),
+        grid=(parts,),
+        in_specs=[whole(a.shape), pl.BlockSpec((tokens, D), lambda n: (0, n)), whole(vecs.shape)],
+        out_specs=whole(out),
+        compiler_params=pltpu.CompilerParams(vmem_limit_bytes=48 << 20),
+        cost_estimate=pl.CostEstimate(flops=6 * 10**9, bytes_accessed=10 * 10**6, transcendentals=0),
+        name="column_grads",
+    )(a, d, vecs)
+
+
 def tail_kernel(plan, dx_ref, up_ref, w_ref, o_ref):
     dqkv = pick_heads(plan, dx_ref[:, 0])
-    share = D // w_ref.shape[0]
     out = read(up_ref)
     for n in range(plan.cols // D):
-        out = out + dot(dqkv[:, part_of(n)], w_ref[:, n * share : (n + 1) * share].reshape(D, D), NT)
+        out = out + dot(dqkv[:, part_of(n)], column_part(w_ref, n), NT)
     write(o_ref, out)
 
 
@@ -789,50 +1040,81 @@
     )(dx, up, w_qkv)
 
 
-def finish_kernel(plan, share, counts, *refs):
-    fulls, owns, outs = refs[:LAYERS], refs[LAYERS], refs[LAYERS + 1 :]
-    qkv_ref, bias_ref, attn_ref, inner_ref, outer_ref = outs[:5]
-    small = outs[5:]
+def finish_kernel(plan, share, counts, seq_first, full_ref, owns_ref, *outs):
+    qkv_ref, bias0_ref, biasq_ref, biasv_ref, attn_ref, inner_ref, outer_ref = outs[:7]
+    small = outs[7:]
     outer = outer_ref.shape[1]
     parts = inner_ref.shape[2] // D
-    each = owns.shape[1] // LAYERS
-    for layer in range(LAYERS):
-        flat = fulls[layer][...].reshape(-1, D)
-        outer_ref[layer] = flat[:outer].astype(F32)
-        at = outer
+    hp, pairs, groups = plan.hp, plan.pairs, plan.groups
+
+    def rest(layer, flat, at):
         for n in range(parts):
             inner_ref[layer, :, part_of(n)] = flat[at : at + share].astype(F32)
             at += share
         attn_ref[layer] = flat[at : at + share].astype(F32)
         at += share
         vecs = flat[at : at + 16].astype(F32)
-        at = 0
+        first = 0
         for ref, n in zip(small, counts):
-            ref[layer : layer + 1, :] = vecs[at // D : at // D + 1, at % D : at % D + n]
-            at += n
-        pieces = {}
-        for g in range(plan.groups):
-            rows = owns[g, layer * each : (layer + 1) * each].astype(F32)
-            for i in range(plan.hp):
-                head = g * plan.hp + i
-                pieces["k", head] = rows[:, i * WIDE : i * WIDE + HD]
-                pieces["v", head] = rows[:, i * WIDE + HD : (i + 1) * WIDE]
-                pieces["q", head] = rows[:, (2 * plan.hp + i) * HD : (2 * plan.hp + i + 1) * HD]
-        value = jnp.concatenate([pieces[kind, head] for kind in "qkv" for head in range(H)], 1)
-        qkv_ref[layer] = value[:share]
-        bias_ref[layer : layer + 1, :] = value[share : share + 1]
-
-
-def finish(plan, share, ff, item, counts, fulls, owns):
-    out = [(share, 3 * D), (3 * D,), (share, D), (share, ff), (ff // item, D)] + [(n,) for n in counts]
+            ref[layer : layer + 1, :] = vecs[first // D : first // D + 1, first % D : first % D + n]
+            first += n
+        return at + 16
+
+    def in_order(pieces):
+        return jnp.concatenate([pieces[kind, head] for kind in "qkv" for head in range(H)], 1)
+
+    zero = full_ref[...].reshape(-1, D)
+    outer_ref[1] = zero[:outer].astype(F32)
+    zero = zero[rest(1, zero, outer) :]
+    columns = plan.cols // D
+    values = jnp.concatenate([zero[n * share : (n + 1) * share] for n in range(columns)], 1).astype(F32)
+    at = columns * share
+    vec = zero[at : at + 16].astype(F32)
+    biasq_ref[...] = vec[:1, :share]
+    biasv_ref[...] = vec[:1, share : 2 * share]
+    pieces = {}
+    for head in range(H):
+        g, i = head // hp, head % hp
+        pieces["k", head] = values[:, head * WIDE : head * WIDE + HD]
+        pieces["v", head] = values[:, head * WIDE + HD : (head + 1) * WIDE]
+        first = groups * hp * WIDE
+        if i < 2 * pairs:
+            first += (g * pairs + i // 2) * WIDE + (i % 2) * HD
+        else:
+            first += groups * pairs * WIDE + g * HD
+        pieces["q", head] = values[:, first : first + HD]
+    qkv_ref[1] = in_order(pieces)
+    at = rest(0, zero, at + 16)
+    own_at = 0
+    if seq_first:
+        own_at = outer // groups
+        for g in range(groups):
+            outer_ref[0, g * own_at : (g + 1) * own_at] = owns_ref[g, :own_at].astype(F32)
+    else:
+        outer_ref[0] = zero[at : at + outer].astype(F32)
+    pieces = {}
+    for head in range(H):
+        g, i = head // hp, head % hp
+        rows = owns_ref[g, own_at : own_at + share + 16].astype(F32)
+        pieces["k", head] = rows[:, i * WIDE : i * WIDE + HD]
+        pieces["v", head] = rows[:, i * WIDE + HD : (i + 1) * WIDE]
+        pieces["q", head] = rows[:, (2 * hp + i) * HD : (2 * hp + i + 1) * HD]
+    value = in_order(pieces)
+    qkv_ref[0] = value[:share]
+    bias0_ref[...] = value[share : share + 1]
+
+
+def finish(plan, share, ff, item, counts, seq_first, full, owns):
+    out = [(LAYERS, share, 3 * D), (1, 3 * D), (1, share), (1, share), (LAYERS, share, D), (LAYERS, share, ff), (LAYERS, ff // item, D)]
+    out += [(LAYERS, n) for n in counts]
     return pl.pallas_call(
-        partial(finish_kernel, plan, share, counts),
-        out_shape=[jax.ShapeDtypeStruct((LAYERS,) + s, F32) for s in out],
-        in_specs=[pl.BlockSpec(memory_space=VMEM)] * (LAYERS + 1),
+        partial(finish_kernel, plan, share, counts, seq_first),
+        out_shape=[jax.ShapeDtypeStruct(s, F32) for s in out],
+        in_specs=[pl.BlockSpec(memory_space=VMEM)] * 2,
         out_specs=[pl.BlockSpec(memory_space=VMEM)] * len(out),
         compiler_params=pltpu.CompilerParams(vmem_limit_bytes=48 << 20),
         name="finish",
-    )(*fulls, owns)
+    )(full, owns)
 
 
 def column_parts(plan, w):
@@ -858,6 +1140,25 @@
     return jnp.concatenate(
         [lax.dynamic_index_in_dim(p, rank, axis, False) for p in column_parts(plan, w)], -1
     )
+
+
+def natural(plan, kv, pairs, last):
+    lead = kv.shape[:-2]
+    g, hp = plan.groups, plan.hp
+    kv = kv.reshape(lead + (g * hp, 2, HD))
+    q = jnp.concatenate(
+        [pairs.reshape(lead + (g, 2 * plan.pairs, HD)), last.reshape(lead + (g, plan.odd, HD))], -2
+    ).reshape(lead + (g * hp, HD))
+    return jnp.concatenate(
+        [p[..., :H, :].reshape(lead + (H * HD,)) for p in (q, kv[..., 0, :], kv[..., 1, :])], -1
+    )
+
+
+def from_all(plan, w):
+    lead = w.shape[:-1]
+    a = plan.groups * plan.hp * WIDE
+    b = a + plan.groups * plan.pairs * WIDE
+    return natural(plan, *(p.reshape(lead + (plan.groups, -1)) for p in (w[..., :a], w[..., a:b], w[..., b:])))
 
 
 def exchange(x):
@@ -912,18 +1213,27 @@
     plan = Plan(groups, tokens)
     here = tokens // BLK
     share = D // item
-    hidden_low = hidden[0].astype(BF)
-    hidden_all = exchange(jnp.broadcast_to(hidden_low[None], (groups, tokens, D)))
-    hidden_all, block_lists = tie(hidden_all, block_lists)
-
     ids = jnp.pad(block_lists[0], ((0, 0), (0, 0), (0, groups * plan.hp - H), (0, 0)))
-    ids = ids.reshape(LAYERS, here, groups, plan.hp * RAND).transpose(2, 0, 1, 3)
-    ids = exchange(ids.reshape(groups, 1, -1)).reshape(groups, LAYERS, here, plan.hp, RAND)
+    ids = ids.reshape(LAYERS, here, groups, plan.hp * RAND).transpose(2, 0, 1, 3).reshape(groups, -1)
+    used = ids.shape[1]
+    ids = jnp.pad(ids, ((0, 0), (0, -used % 1024))).reshape(groups, -1, 128)
+    small = (bias_query, bias_value, bias_attn_out, norm1_gain, norm1_shift, bias_ffn_in, bias_ffn_out, norm2_gain, norm2_shift)
+    flat_small = jnp.concatenate(small, 1).reshape(-1)
+    own_bias = lax.dynamic_update_slice(jnp.zeros((3 * D,), BF), bias_query[0], (item_rank * share,))
+    own_bias = lax.dynamic_update_slice(own_bias, bias_value[0], (2 * D + item_rank * share,))
+    shard = jnp.concatenate([w_qkv[0], own_bias[None], jnp.zeros((15, 3 * D), BF)])
+    hidden_all, x0, small_all, ids = start(
+        plan,
+        item,
+        hidden[0].astype(BF),
+        own_columns(plan, shard, seq_rank),
+        jnp.pad(flat_small, (0, SMALL * 128 - flat_small.shape[0])).reshape(SMALL, 128),
+        ids,
+    )
+    ids = ids.reshape(groups, -1)[:, :used].reshape(groups, LAYERS, here, plan.hp, RAND)
     ids = ids.transpose(1, 3, 0, 2, 4).reshape(LAYERS, plan.hp, plan.blocks, RAND)
     tables = [key_table(plan, ids[layer]) for layer in range(LAYERS)]
-
-    small = (bias_query, bias_value, bias_attn_out, norm1_gain, norm1_shift, bias_ffn_in, bias_ffn_out, norm2_gain, norm2_shift)
-    packed = lax.all_gather(jnp.concatenate(small, 1), "item", axis=0).astype(F32)
+    packed = small_all.reshape(item, -1)[:, : flat_small.shape[0]].reshape(item, LAYERS, -1).astype(F32)
     vectors = []
     for layer in range(LAYERS):
         at, out = 0, []
@@ -935,25 +1245,20 @@
     inner = [v[5][None] for v in vectors]
     qkv_bias = [jnp.concatenate([v[0], jnp.zeros_like(v[0]), v[1]])[None] for v in vectors]
 
-    own_weight = lax.all_gather(own_columns(plan, w_qkv[0], seq_rank), "item", axis=0)
-    own_bias = own_columns(plan, qkv_bias[0], seq_rank)
     columns = wide_parts(all_columns(plan, w_qkv[0])), wide_parts(all_columns(plan, w_qkv[1]))
 
     def dense(layer):
         return [w_attn_out[layer], wide_parts(w_ffn_in[layer]), w_ffn_out[layer]]
 
-    packed0 = lax.all_gather(jnp.concatenate(dense(0) + [columns[1]]), "item", axis=0)
+    packed0 = lax.all_gather(jnp.concatenate(dense(0)), "item", axis=0)
+    columns1 = lax.all_gather(columns[1], "item", axis=0)
     packed1 = lax.all_gather(jnp.concatenate(dense(1)), "item", axis=0)
     columns0 = lax.all_gather(columns[0], "item", axis=0)
 
-    x0 = own_heads(plan, hidden_all, own_weight, own_bias)
-    ctx0 = exchange(attn_fwd(plan, tables[0], x0))
-    x1, h1, h1_low, r1, r2, u, y0, ctx0 = layer_fwd(
-        plan, ctx0, hidden[0], packed0, stacked[0], inner[0], all_columns(plan, qkv_bias[1])
-    )
-    x1 = exchange(x1)
-    ctx1 = exchange(attn_fwd(plan, tables[1], x1))
-    h1_all = lax.all_gather(h1_low.reshape(tokens, D), "seq", axis=0)
+    ctx0 = attn_fwd(plan, tables[0], x0)
+    h1, h1_low, r1, r2, u, y0, ctx0 = layer_fwd(plan, ctx0, hidden[0], packed0, stacked[0], inner[0])
+    x1 = exchange(project(plan, h1_low, columns1, all_columns(plan, qkv_bias[1])))
+    ctx1 = attn_fwd(plan, tables[1], x1)
     d1, output, up1, gz1, du1, df1, do1, y1, ctx1, sums1, inner1 = layer_mid(
         plan, ctx1, h1, cotangent[0], packed1, stacked[1], inner[1]
     )
@@ -968,10 +1273,10 @@
         part = jnp.concatenate([v.reshape(item, -1) for v in vecs], 1)
         return jnp.pad(part, ((0, 0), (0, 16 * D - part.shape[1]))).reshape(item, 16, D).astype(BF)
 
-    def grads(gz, du, df, do, y, ctx, sums, inner_sum):
+    def grads(gz, du, df, do, y, ctx, sums, inner_sum, cut_for=0):
         sums = jnp.sum(sums, 1)
         vecs = (sums[SUM_DO], sums[D_GAIN1], sums[D_SHIFT1], jnp.sum(inner_sum, 0), sums[SUM_DF], sums[D_GAIN2], sums[D_SHIFT2])
-        return dense_grads(item, flat(gz), flat(df), flat(y), flat(du), flat(ctx), flat(do), rows_for(vecs))
+        return dense_grads(item, flat(gz), flat(df), flat(y), flat(du), flat(ctx), flat(do), rows_for(vecs), cut_for)
 
     def seq_send(shares):
         rows = jnp.concatenate(shares)
@@ -989,34 +1294,37 @@
     fo1, rest1 = grads(gz1, du1, df1, do1, y1, ctx1, sums1, inner1)
     dc1, fo1, rest1 = tie(dc1, fo1, rest1)
     fo1, rest1 = scattered(fo1), scattered(rest1)
-    dc1, columns0, h1_all = tie(dc1, columns0, h1_all)
     dx1 = attn_bwd(plan, tables[1], x1, dc1)
-    own1 = own_grad(plan, item, h1_all, dx1)
-    dx1 = exchange(dx1)
-    dx1, own1 = tie(dx1, own1)
-    own1 = scattered(own1)
-    dx1, fo1 = tie(dx1, fo1)
-    d0, up0, gz0, du0, df0, do0, sums0, inner0 = layer_bwd(plan, dx1, up1, r1, r2, u, packed0, stacked[0])
-    d0, rest1 = tie(d0, rest1)
+    dx1, columns0 = tie(dx1, columns0)
+    d0, up0, gz0, du0, df0, do0, dqkv1, sums0, inner0, qkv_sum1 = layer_bwd(
+        plan, dx1, up1, r1, r2, u, packed0, columns1, stacked[0]
+    )
+    d0, fo1 = tie(d0, fo1)
     dc0 = exchange(d0)
-    fo0, rest0 = grads(gz0, du0, df0, do0, y0, ctx0, sums0, inner0)
-    dc0, fo0, rest0, own1 = tie(dc0, fo0, rest0, own1)
-    fo0, rest0 = scattered(fo0), scattered(rest0)
-    sent1 = seq_send([fo1, rest1])
+    bias1 = from_all(plan, jnp.sum(qkv_sum1, 0))
+    qkv1 = column_grads(item, flat(h1_low), flat(dqkv1), rows_for((bias1[:D], bias1[2 * D :])))
+    seq_first = (w_ffn_out.shape[1] // groups) % 16 == 0
+    fo0, rest0 = grads(gz0, du0, df0, do0, y0, ctx0, sums0, inner0, groups if seq_first else 0)
+    dc0, qkv1, fo0, rest0, rest1 = tie(dc0, qkv1, fo0, rest0, rest1)
+    qkv1, rest0 = scattered(qkv1), scattered(rest0)
+    fo0 = exchange(fo0) if seq_first else scattered(fo0)
     dx0 = attn_bwd(plan, tables[0], x0, dc0)
-    dx0, sent1 = tie(dx0, sent1)
+    dx0, fo0, qkv1 = tie(dx0, fo0, qkv1)
     own0 = own_grad(plan, item, hidden_all, dx0)
     dx0 = exchange(dx0)
-    dx0, own0, part1 = tie(dx0, own0, seq_sum(sent1))
+    if seq_first:
+        own0 = jnp.concatenate([seq_sum(fo0), own0], 1)
+    dx0, own0 = tie(dx0, own0)
     own0 = scattered(own0)
-    full1 = seq_gather(part1)
+    sent = seq_send([fo1, rest1, qkv1, rest0] + ([] if seq_first else [fo0]))
     input_grad = layer_tail(plan, dx0, up0, columns0)
-    full0 = seq_gather(seq_sum(seq_send([fo0, rest0])))
-    owns = seq_gather(jnp.concatenate([own0, own1]))
-    qkv, bias, attn, inner_grad, outer, *small_grads = finish(
-        plan, share, w_ffn_in.shape[2], item, counts, (full0, full1), owns
+    full = seq_gather(seq_sum(sent))
+    owns = seq_gather(own0)
+    qkv, bias0, biasq1, biasv1, attn, inner_grad, outer, *small_grads = finish(
+        plan, share, w_ffn_in.shape[2], item, counts, seq_first, full, owns
     )
-    bias_q, bias_v = (lax.dynamic_slice_in_dim(bias, part * D + item_rank * share, share, 1) for part in (0, 2))
+    biasq0, biasv0 = (lax.dynamic_slice_in_dim(bias0, part * D + item_rank * share, share, 1) for part in (0, 2))
+    bias_q, bias_v = jnp.concatenate([biasq0, biasq1]), jnp.concatenate([biasv0, biasv1])
     out_bias, gain1, shift1, inner_bias, ffn_bias, gain2, shift2 = small_grads
     return (
         output.reshape(hidden.shape),

time: 782 us -> 753 us (0.963)
  Pallas kernels: 354 us -> 452 us
  waiting for transfers between devices: 240 us -> 149 us
  starting transfers between devices: 57.8 us -> 30.7 us
  blocking collectives: 43.2 us -> 33.5 us
    all_to_all x14 -> x7, waiting for transfers between devices: 213 us -> 119 us  [exchange(): lax.all_to_all(y, 'seq', split_axis=0, concat_axis=0, tiled=True)]
    pallas_call x2 -> x4, Pallas kernels: 16.6 us -> 82.3 us  [the longest x1 65.8 us: start(): pl.pallas_call(partial(start_kernel, plan, item), out_shape=[jax.ShapeDty...]
    all_gather x2 -> x0, blocking collectives: 43.2 us -> none  [the longest x1 25.1 us: local(): lax.all_gather(own_columns(plan, w_qkv[0], seq_rank), 'item', axis=0)]
    pallas_call x1, Pallas kernels: 34.5 us -> 71.1 us  [layer_bwd(): pl.pallas_call(partial(bwd_kernel, plan, ff), out_shape=[jax.ShapeDtypeSt...]
    all_to_all x0 -> x1, blocking collectives: none -> 33.5 us  [exchange(): lax.all_to_all(y, 'seq', split_axis=0, concat_axis=0, tiled=True)]
    all_to_all x14 -> x7, starting transfers between devices: 57.1 us -> 30.4 us  [exchange(): lax.all_to_all(y, 'seq', split_axis=0, concat_axis=0, tiled=True)]
    reduce_scatter x6 -> x5, waiting for transfers between devices: 24.4 us -> 0.05 us  [scattered(): return lax.psum_scatter(g, 'item', scatter_dimension=0, tiled=False)]
    all_gather x2, waiting for transfers between devices: 0.02 us -> 22.8 us  [the longest x1 13.6 us: local(): packed0 = lax.all_gather(jnp.concatenate(dense(0)), 'item', axis=0)]
  transfers between devices with their start and end apart: 24 -> 16, of which waited for: 12 -> 9; matrix products, arithmetic and copies ran while one was open for 4% -> 5% of each run, Pallas kernels for 46% -> 60%
where the time goes in v5:
time: 753 us; the launch traced here: 742 us
  Pallas kernels  452 us (60%)
  waiting for transfers between devices  149 us (20%)
  local copies, waits for them, and re-layouts  43.3 us (6%)
  blocking collectives  33.5 us (4%)
  starting transfers between devices  30.7 us (4%)
  other arithmetic  18.2 us (2%)
  between operations  15.2 us (2%)
    all_to_all x7, waiting for transfers between devices, exchange(): lax.all_to_all(y, 'seq', split_axis=0, concat_axis=0, tiled=True)  119 us
    pallas_call x2, Pallas kernels, attn_bwd(): pl.pallas_call(partial(attn_bwd_kernel, plan), out_shape=jax.ShapeDtypeSt...  100 us
    pallas_call x1, Pallas kernels, layer_bwd(): pl.pallas_call(partial(bwd_kernel, plan, ff), out_shape=[jax.ShapeDtypeSt...  71.1 us
    pallas_call x1, Pallas kernels, start(): pl.pallas_call(partial(start_kernel, plan, item), out_shape=[jax.ShapeDty...  65.8 us
    pallas_call x2, Pallas kernels, attn_fwd(): pl.pallas_call(partial(attn_fwd_kernel, plan), out_shape=jax.ShapeDtypeSt...  55.8 us
    pallas_call x1, Pallas kernels, layer_mid(): pl.pallas_call(partial(mid_kernel, plan, ff), out_shape=[jax.ShapeDtypeSt...  50.6 us
    pallas_call x2, Pallas kernels, dense_grads(): pl.pallas_call(partial(dense_grad_kernel, item), out_shape=[jax.ShapeDtyp...  37.5 us
    all_to_all x1, blocking collectives, exchange(): lax.all_to_all(y, 'seq', split_axis=0, concat_axis=0, tiled=True)  33.5 us
  transfers between devices with their start and end apart: 16, of which 9 were waited for; matrix products, arithmetic and copies ran while one was open for 5% of the time, Pallas kernels for 60%

profile of v5, /device:TPU:0, one launch (start us, length us, event | category | flops | bytes accessed | tf_op | source)
XLA Modules:
  0.0 742.1 jit_solution(3838686425597755270)
XLA Ops:
  21.1 65.8 %start.1 = (bf16[4,2,512,768]{3,2,1,0:T(8,128)(2,1)S(1)}, bf16[4,4,9,2,64,128]{5,4,3,2,1,0:T(8,128)(2,1)S(1)}, bf16[8,32,128]{2,1,0:T(8,128)(2,1)S(1)}, s32[4,8,128]{2,1,0:T(8,128)S(1)}) custom-call(bf16[2,512,768]{2,1,0:T(8,128)(2,1)S(1)} %convert_element_type.32.hid_ref, bf16[112,576]{1,0:T(8,128)(2,1)S(1)} %pad_maximum_fusion.4.shard_ref, ...), custom_call_target="tpu_custom_call" | custom-call | flops 54999998464 | bytes 12000000 | tf_op jit(solution)/shard_map/start/pallas_call | solution.py:550
  86.9 2.6 copy-done.5
  97.4 27.9 %attn_fwd.2 = bf16[96,64,128]{2,1,0:T(8,128)(2,1)S(1)} custom-call(s32[1536]{0:T(1024)S(1)} %reshape.297.lists_ref, bf16[288,64,128]{2,1,0:T(8,128)(2,1)} %bitcast.178), custom_call_target="tpu_custom_call" | custom-call | flops 25999998976 | bytes 6000000 | tf_op jit(solution)/shard_map/attn_fwd/pallas_call | solution.py:206
  126.4 13.6 %all-gather.9.cloned.1.call-done = bf16[6912,768]{1,0:T(8,128)(2,1)} async-done(((bf16[864,768]{1,0:T(8,128)(2,1)}), bf16[6912,768]{1,0:T(8,128)(2,1)}) %all-gather.9.cloned.1.call-update) | async-done | bytes 10616848 | tf_op jit(solution)/shard_map/all_gather | solution.py:1253
  140.0 32.9 %layer_fwd.1 = (f32[2,512,768]{2,1,0:T(8,128)}, bf16[2,512,768]{2,1,0:T(8,128)(2,1)}, f32[2,512,768]{2,1,0:T(8,128)}, f32[2,512,768]{2,1,0:T(8,128)}, f32[2,512,...) custom-call(bf16[4,4,3,2,64,128]{5,4,3,2,1,0:T(8,128)(2,1)} %bitcast.182, ...), custom_call_target="tpu_custom_call" | custom-call | flops 24000000000 | bytes 50000000 | tf_op jit(solution)/shard_map/layer_fwd/pallas_call | solution.py:785
  172.9 9.2 %all-gather.11.cloned.1.call-done = bf16[2304,768]{1,0:T(8,128)(2,1)} async-done(((bf16[288,768]{1,0:T(8,128)(2,1)}), bf16[2304,768]{1,0:T(8,128)(2,1)}) %all-gather.11.cloned.1.call-update) | async-done | bytes 3538960 | tf_op jit(solution)/shard_map/all_gather | solution.py:1254
  185.6 5.8 project.1
  191.4 5.0 all-to-all-start
  200.0 50.2 %all-to-all-done = bf16[4,4608,128]{2,1,0:T(8,128)(2,1)} async-done(((bf16[4,4608,128]{2,1,0:T(8,128)(2,1)}), bf16[4,4608,128]{2,1,0:T(8,128)(2,1)}, u32[]{:S(2)}, u32[]{:S(2)}) %all-to-all-start) | async-done | bytes 4718624 | tf_op jit(solution)/shard_map/all_to_all | solution.py:1166
  250.2 27.9 %attn_fwd.3 = bf16[96,64,128]{2,1,0:T(8,128)(2,1)S(1)} custom-call(s32[1536]{0:T(1024)S(1)} %reshape.296.lists_ref, bf16[288,64,128]{2,1,0:T(8,128)(2,1)} %bitcast.38.x_ref), custom_call_target="tpu_custom_call" | custom-call | flops 25999998976 | bytes 6000000 | tf_op jit(solution)/shard_map/attn_fwd/pallas_call | solution.py:206
  279.2 4.6 all-gather.13.cloned.1.call-done
  283.8 50.6 %layer_mid.1 = (bf16[4,4,3,2,64,128]{5,4,3,2,1,0:T(8,128)(2,1)}, f32[2,512,768]{2,1,0:T(8,128)}, f32[2,512,768]{2,1,0:T(8,128)}, bf16[2,512,3072]{2,1,0:T(8,128)...) custom-call(bf16[4,4,3,2,64,128]{5,4,3,2,1,0:T(8,128)(2,1)} %bitcast, ...), custom_call_target="tpu_custom_call" | custom-call | flops 44999999488 | bytes 50000000 | tf_op jit(solution)/shard_map/layer_mid/pallas_call | solution.py:882
  335.3 3.7 all-to-all-start.1
  340.6 18.7 %dense_grads.2 = (bf16[8,384,768]{2,1,0:T(8,128)(2,1)}, bf16[8,496,768]{2,1,0:T(8,128)(2,1)}) custom-call(bf16[1024,3072]{1,0:T(8,128)(2,1)} %bitcast.244, bf16[1024,768]{1,0:T(8,128)(2,1)} %bitcast.253, bf16[1024,768]{1,0:T(8,128)(2,1)} %bitcast.255, bf16[1024,3072]{1,0:T(8,128)(2,1)} %bitcast.245, bf16[1024,768]{1,0:T(8,128)(2,1)} %bitcast.256, ...), custom_call_target="tpu_custom_call" | custom-call | flops 14000000000 | bytes 30000000 | tf_op jit(solution)/shard_map/dense_grads/pallas_call | solution.py:983
  361.0 50.2 %attn_bwd.2 = bf16[288,64,128]{2,1,0:T(8,128)(2,1)} custom-call(s32[1536]{0:T(1024)} %copy-done.3, bf16[288,64,128]{2,1,0:T(8,128)(2,1)} %bitcast.38.x_ref, bf16[96,64,128]{2,1,0:T(8,128)(2,1)} %bitcast.192), custom_call_target="tpu_custom_call" | custom-call | flops 46000001024 | bytes 12000000 | tf_op jit(solution)/shard_map/attn_bwd/pallas_call | solution.py:328
  411.1 71.1 %layer_bwd.1 = (bf16[4,4,3,2,64,128]{5,4,3,2,1,0:T(8,128)(2,1)}, f32[2,512,768]{2,1,0:T(8,128)}, bf16[2,512,3072]{2,1,0:T(8,128)(2,1)}, bf16[2,512,3072]{2,1,0:T...) custom-call(bf16[4,4,9,2,64,128]{5,4,3,2,1,0:T(8,128)(2,1)} %bitcast, ...), custom_call_target="tpu_custom_call" | custom-call | flops 40000000000 | bytes 50000000 | tf_op jit(solution)/shard_map/layer_bwd/pallas_call | solution.py:935
  487.2 6.0 column_grads.1
  495.0 3.6 all-to-all-start.2
  498.7 18.8 %dense_grads.3 = (bf16[4,8,96,768]{3,2,1,0:T(8,128)(2,1)}, bf16[8,496,768]{2,1,0:T(8,128)(2,1)}) custom-call(bf16[1024,3072]{1,0:T(8,128)(2,1)} %bitcast.242, bf16[1024,768]{1,0:T(8,128)(2,1)} %bitcast.251, bf16[1024,768]{1,0:T(8,128)(2,1)} %bitcast.249, bf16[1024,3072]{1,0:T(8,128)(2,1)} %bitcast.243, bf16[1024,768]{1,0:T(8,128)(2,1)} %bitcast.250, ...), custom_call_target="tpu_custom_call" | custom-call | flops 14000000000 | bytes 30000000 | tf_op jit(solution)/shard_map/dense_grads/pallas_call | solution.py:983
  520.1 5.1 all-to-all-start.3
  525.2 50.1 %attn_bwd.3 = bf16[288,64,128]{2,1,0:T(8,128)(2,1)} custom-call(s32[1536]{0:T(1024)} %copy-done.2, bf16[288,64,128]{2,1,0:T(8,128)(2,1)} %bitcast.179, bf16[96,64,128]{2,1,0:T(8,128)(2,1)} %bitcast.194), custom_call_target="tpu_custom_call" | custom-call | flops 46000001024 | bytes 12000000 | tf_op jit(solution)/shard_map/attn_bwd/pallas_call | solution.py:328
  577.8 5.0 all-to-all-start.4
  582.8 3.3 reduce_sum.74
  588.5 13.6 %own_grad.1 = bf16[8,112,768]{2,1,0:T(8,128)(2,1)S(1)} custom-call(bf16[4,2,4,128,768]{4,3,2,1,0:T(8,128)(2,1)} %bitcast.177, bf16[4,4,9,2,64,128]{5,4,3,2,1,0:T(8,128)(2,1)S(1)} %bitcast.170), custom_call_target="tpu_custom_call" | custom-call | flops 7000000000 | bytes 12000000 | tf_op jit(solution)/shard_map/own_grad/pallas_call | solution.py:605
  603.7 31.5 %all-to-all-done.4 = bf16[4,4608,128]{2,1,0:T(8,128)(2,1)} async-done(((bf16[4,4608,128]{2,1,0:T(8,128)(2,1)}), bf16[4,4608,128]{2,1,0:T(8,128)(2,1)}, u32[]{:S(2)}, u32[]{:S(2)}) %all-to-all-start.4) | async-done | bytes 4718624 | tf_op jit(solution)/shard_map/all_to_all | solution.py:1166
  636.6 33.5 %all_to_all.40 = bf16[4,432,768]{2,1,0:T(8,128)(2,1)S(1)} all-to-all(bf16[4,432,768]{2,1,0:T(8,128)(2,1)S(1)} %bitcast.183), channel_id=1, replica_groups=mesh['seq'=4,'item'=8] {'seq'}, dimensions={0} | all-to-all | bytes 5308416 | tf_op jit(solution)/shard_map/all_to_all | solution.py:1166
  672.6 3.7 all-to-all-start.6
  676.3 29.2 %all-to-all-done.6.full_ref = bf16[4,432,768]{2,1,0:T(8,128)(2,1)S(1)} async-done(((bf16[4,432,768]{2,1,0:T(8,128)(2,1)}), bf16[4,432,768]{2,1,0:T(8,128)(2,1)S(1)}, u32[]{:S(2)}, u32[]{:S(2)}) %all-to-all-start.6) | async-done | bytes 2654240 | tf_op jit(solution)/shard_map/all_to_all | solution.py:1166
  707.6 4.3 all-to-all-start.7
  713.8 8.3 %layer_tail.1 = f32[2,512,768]{2,1,0:T(8,128)} custom-call(bf16[4,4,9,2,64,128]{5,4,3,2,1,0:T(8,128)(2,1)} %bitcast.81.dx_ref, f32[2,512,768]{2,1,0:T(8,128)S(1)} %copy-done.11, bf16[8,288,768]{2,1,0:T(8,128)(2,1)} %bitcast.240), custom_call_target="tpu_custom_call" | custom-call | flops 8000000000 | bytes 12000000 | tf_op jit(solution)/shard_map/layer_tail/pallas_call | solution.py:1031
  722.2 5.4 all-to-all-done.7.owns_ref
  727.5 4.7 finish.1
  (248 shorter events, 61.1 us)
Async XLA Ops:
  7.2 132.8 %all-gather.9.cloned.1.call-start = ((), (), s32[]{:S(2)}) async-start(), calls=%async_computation.18 | async-start | bytes 11943936 | tf_op jit(solution)/shard_map/all_gather | solution.py:1253
  10.0 2.7 copy-start.13
  11.0 171.1 %all-gather.11.cloned.1.call-start = ((), (), s32[]{:S(2)}) async-start(), calls=%async_computation.19 | async-start | bytes 3981312 | tf_op jit(solution)/shard_map/all_gather | solution.py:1254
  13.2 2.0 copy-start.25
  14.2 269.5 %all-gather.13.cloned.1.call-start = ((), (), s32[]{:S(2)}) async-start(), calls=%async_computation.20 | async-start | bytes 11943936 | tf_op jit(solution)/shard_map/all_gather | solution.py:1255
  86.9 2.7 copy-start.5
  89.5 2.2 copy-start.6
  96.7 28.6 %copy-start.2 = (s32[1536]{0:T(1024)}, s32[1536]{0:T(1024)S(1)}, u32[]{:S(2)}) copy-start(s32[1536]{0:T(1024)S(1)} %reshape.297.lists_ref) | copy-start | bytes 18436
  182.2 2.0 copy-start.4
  191.4 58.8 %all-to-all-start = ((bf16[4,4608,128]{2,1,0:T(8,128)(2,1)}), bf16[4,4608,128]{2,1,0:T(8,128)(2,1)}, u32[]{:S(2)}, u32[]{:S(2)}) async-start(bf16[4,4608,128]{2,1,0:T(8,128)(2,1)} %bitcast.186), calls=%async_computation | async-start | bytes 9437184 | tf_op jit(solution)/shard_map/all_to_all | solution.py:1166
  196.5 214.7 %all-gather.15.cloned.1.call-start = ((), (), s32[]{:S(2)}) async-start(), calls=%async_computation.21 | async-start | bytes 3981312 | tf_op jit(solution)/shard_map/all_gather | solution.py:1256
  199.4 78.7 %copy-start.3 = (s32[1536]{0:T(1024)}, s32[1536]{0:T(1024)S(1)}, u32[]{:S(2)}) copy-start(s32[1536]{0:T(1024)S(1)} %reshape.296.lists_ref) | copy-start | bytes 18436
  335.3 3.8 copy-start.22
  335.3 23.9 %all-to-all-start.1 = ((bf16[4,1536,128]{2,1,0:T(8,128)(2,1)}), bf16[4,1536,128]{2,1,0:T(8,128)(2,1)S(1)}, u32[]{:S(2)}, u32[]{:S(2)}) async-start(bf16[4,1536,128]{2,1,0:T(8,128)(2,1)} %bitcast.193), calls=%async_computation.1 | async-start | bytes 3145728 | tf_op jit(solution)/shard_map/all_to_all | solution.py:1166
  339.1 156.0 %reduce-scatter.6.cloned.1.call-start = ((), (), s32[]{:S(2)}) async-start(), calls=%async_computation.13 | async-start | bytes 5308416 | tf_op jit(solution)/shard_map/reduce_scatter | solution.py:1270
  360.4 157.8 %reduce-scatter.8.cloned.1.call-start = ((), (), s32[]{:S(2)}) async-start(), calls=%async_computation.14 | async-start | bytes 6856704 | tf_op jit(solution)/shard_map/reduce_scatter | solution.py:1270
  482.2 5.0 copy-start.8
  493.2 1.8 copy-start.1
  495.0 23.2 %all-to-all-start.2 = ((bf16[4,1536,128]{2,1,0:T(8,128)(2,1)}), bf16[4,1536,128]{2,1,0:T(8,128)(2,1)S(1)}, u32[]{:S(2)}, u32[]{:S(2)}) async-start(bf16[4,1536,128]{2,1,0:T(8,128)(2,1)} %bitcast.64), calls=%async_computation.3 | async-start | bytes 3145728 | tf_op jit(solution)/shard_map/all_to_all | solution.py:1166
  498.6 79.1 %reduce-scatter.10.cloned.1.call-start = ((), (), s32[]{:S(2)}) async-start(), calls=%async_computation.15 | async-start | bytes 4202496 | tf_op jit(solution)/shard_map/reduce_scatter | solution.py:1270
  519.3 115.9 %reduce-scatter.12.cloned.1.call-start = ((), (), s32[]{:S(2)}) async-start(), calls=%async_computation.16 | async-start | bytes 6856704 | tf_op jit(solution)/shard_map/reduce_scatter | solution.py:1270
  520.1 57.7 %all-to-all-start.3 = ((bf16[4,768,768]{2,1,0:T(8,128)(2,1)}), bf16[4,768,768]{2,1,0:T(8,128)(2,1)}, u32[]{:S(2)}, u32[]{:S(2)}) async-start(bf16[4,768,768]{2,1,0:T(8,128)(2,1)} %bitcast.187), calls=%async_computation.5 | async-start | bytes 9437184 | tf_op jit(solution)/shard_map/all_to_all | solution.py:1166
  577.8 57.4 %all-to-all-start.4 = ((bf16[4,4608,128]{2,1,0:T(8,128)(2,1)}), bf16[4,4608,128]{2,1,0:T(8,128)(2,1)}, u32[]{:S(2)}, u32[]{:S(2)}) async-start(bf16[4,4608,128]{2,1,0:T(8,128)(2,1)} %bitcast.169), calls=%async_computation.7 | async-start | bytes 9437184 | tf_op jit(solution)/shard_map/all_to_all | solution.py:1166
  582.7 93.5 %reduce-scatter.14.cloned.1.call-start = ((), (), s32[]{:S(2)}) async-start(), calls=%async_computation.17 | async-start | bytes 2875392 | tf_op jit(solution)/shard_map/reduce_scatter | solution.py:1270
  586.1 2.4 copy-start
  603.7 31.5 %copy-start.18 = (bf16[1,496,768]{2,1,0:T(8,128)(2,1)S(1)}, bf16[1,496,768]{2,1,0:T(8,128)(2,1)}, u32[]{:S(2)}) copy-start(bf16[1,496,768]{2,1,0:T(8,128)(2,1)} %reduce-scatter.8.cloned.1.call-done) | copy-start | bytes 2285572
  603.7 31.5 %copy-start.19 = (bf16[1,384,768]{2,1,0:T(8,128)(2,1)S(1)}, bf16[1,384,768]{2,1,0:T(8,128)(2,1)}, u32[]{:S(2)}) copy-start(bf16[1,384,768]{2,1,0:T(8,128)(2,1)} %reduce-scatter.6.cloned.1.call-done) | copy-start | bytes 1769476
  603.7 31.5 %copy-start.20 = (bf16[1,304,768]{2,1,0:T(8,128)(2,1)S(1)}, bf16[1,304,768]{2,1,0:T(8,128)(2,1)}, u32[]{:S(2)}) copy-start(bf16[1,304,768]{2,1,0:T(8,128)(2,1)} %reduce-scatter.10.cloned.1.call-done) | copy-start | bytes 1400836
  672.6 32.9 %all-to-all-start.6 = ((bf16[4,432,768]{2,1,0:T(8,128)(2,1)}), bf16[4,432,768]{2,1,0:T(8,128)(2,1)S(1)}, u32[]{:S(2)}, u32[]{:S(2)}) async-start(bf16[4,432,768]{2,1,0:T(8,128)(2,1)} %broadcast_in_dim.18), calls=%async_computation.10 | async-start | bytes 5308416 | tf_op jit(solution)/shard_map/all_to_all | solution.py:1166
  707.6 19.9 %all-to-all-start.7 = ((bf16[4,208,768]{2,1,0:T(8,128)(2,1)}), bf16[4,208,768]{2,1,0:T(8,128)(2,1)}, u32[]{:S(2)}, u32[]{:S(2)}) async-start(bf16[4,208,768]{2,1,0:T(8,128)(2,1)} %broadcast_in_dim.20), calls=%async_computation.12 | async-start | bytes 2555904 | tf_op jit(solution)/shard_map/all_to_all | solution.py:1166
  711.9 1.9 copy-start.11
  727.5 6.0 copy-start.12
  (17 other events, 17.5 us)
Sparse Core Ops, SparseCore 0:
  11.2 128.8 all-gather.8
  142.2 39.8 all-gather.10
  184.4 99.3 all-gather.12
  285.8 39.8 all-gather.14
  359.4 53.8 reduce-scatter.5
  415.4 66.2 reduce-scatter.7
  518.4 43.8 reduce-scatter.9
  564.7 66.2 reduce-scatter.11
  635.3 34.5 reduce-scatter.13

commit v6 on v5

--- a/solution.py
+++ b/solution.py
@@ -220,7 +220,7 @@
     )(lists, flat).reshape(plan.c_shape())
 
 
-def attn_bwd_kernel(plan, lists_ref, x_ref, d_ref, o_ref, acc_ref, s_ref, p_ref, g_ref):
+def attn_bwd_kernel(plan, lists_ref, x_ref, d_ref, o_ref, acc_ref, s_ref, p_ref, g_ref, q_ref):
     scale = HD**-0.5
     c = LOG2E * scale
     hp, count = plan.hp, plan.blocks // 2
@@ -274,50 +274,65 @@
     def chunk(n):
         return pl.ds(pl.multiple_of(n * size, size), size)
 
+    ws, threes, ends = [], [], []
     for h in heads:
         ((xa, xla), _), ((ca, cla), _) = spots(plan, h, 0)
         (_, (xb, xlb)), (_, (cb, clb)) = spots(plan, h, count - 1)
         q = low(jnp.concatenate([x_ref[xa, :, xla], x_ref[xb, :, xlb]], 0))
         d = high(jnp.concatenate([d_ref[ca, :, cla], d_ref[cb, :, clb]], 0))
-        w = jnp.concatenate([q, d], 0)
-        three_w = jnp.concatenate([q, d, d], 0)
-
-        def keys(n):
-            return x_ref[keys_of(plan, x_ref, h, n)].reshape(size, WIDE)
-
-        def one(n, m):
-            s = dot(keys(n), w, NT)
-            g_ref[chunk(n), :] = s
-            return jnp.maximum(m, jnp.max(s[:, : 2 * BLK], 0, keepdims=True))
-
-        m = lax.fori_loop(0, steps, one, jnp.full((1, 2 * BLK), -jnp.inf, F32), unroll=4)
-
-        def two(n, state):
-            l, eg = state
-            e = jnp.exp2(g_ref[chunk(n), : 2 * BLK] * c - m * c)
-            g_ref[chunk(n), : 2 * BLK] = e
-            return (
-                l + jnp.sum(e, 0, keepdims=True),
-                eg + jnp.sum(e * g_ref[chunk(n), 2 * BLK :], 0, keepdims=True),
+        ws.append(jnp.concatenate([q, d], 0))
+        threes.append(jnp.concatenate([q, d, d], 0))
+        ends.append(((xa, xla), (xb, xlb)))
+
+    def keys(h, n):
+        return x_ref[keys_of(plan, x_ref, h, n)].reshape(size, WIDE)
+
+    def one(n, ms):
+        out = []
+        for h in heads:
+            s = dot(keys(h, n), ws[h], NT)
+            g_ref[h, chunk(n), :] = s
+            out.append(jnp.maximum(ms[h], jnp.max(s[:, : 2 * BLK], 0, keepdims=True)))
+        return tuple(out)
+
+    ms = lax.fori_loop(0, steps, one, tuple(jnp.full((1, 2 * BLK), -jnp.inf, F32) for h in heads), unroll=2)
+
+    def two(n, state):
+        out = []
+        for h in heads:
+            l, eg = state[h]
+            e = jnp.exp2(g_ref[h, chunk(n), : 2 * BLK] * c - ms[h] * c)
+            g_ref[h, chunk(n), : 2 * BLK] = e
+            out.append(
+                (
+                    l + jnp.sum(e, 0, keepdims=True),
+                    eg + jnp.sum(e * g_ref[h, chunk(n), 2 * BLK :], 0, keepdims=True),
+                )
             )
-
-        l, eg = lax.fori_loop(0, steps, two, (jnp.zeros((1, 2 * BLK), F32),) * 2, unroll=4)
-        inv = 1.0 / l
-        delta = eg * inv
-
-        def three(n, dq):
-            p = g_ref[chunk(n), : 2 * BLK] * inv
-            ds = (p * (g_ref[chunk(n), 2 * BLK :] - delta)).astype(BF)
+        return tuple(out)
+
+    sums = lax.fori_loop(0, steps, two, tuple((jnp.zeros((1, 2 * BLK), F32),) * 2 for h in heads), unroll=2)
+    invs = [1.0 / l for l, _ in sums]
+    deltas = [eg * inv for (_, eg), inv in zip(sums, invs)]
+    q_ref[...] = jnp.zeros_like(q_ref)
+
+    def three(n, carry):
+        for h in heads:
+            p = g_ref[h, chunk(n), : 2 * BLK] * invs[h]
+            ds = (p * (g_ref[h, chunk(n), 2 * BLK :] - deltas[h])).astype(BF)
             hi = p.astype(BF)
             lo = (p - hi.astype(F32)).astype(BF)
-            dkv = dot(jnp.concatenate([ds, hi, lo], 1), three_w, NN)
+            dkv = dot(jnp.concatenate([ds, hi, lo], 1), threes[h], NN)
             where = keys_of(plan, x_ref, h, n)
             total = acc_ref[where].reshape(size, WIDE) + dkv
             o_ref[where] = (total * lane_scale).astype(BF).reshape(2 * plan.per, BLK, WIDE)
-            return dq + dot(ds, keys(n), TN)
-
-        dq = lax.fori_loop(0, steps, three, jnp.zeros((2 * BLK, WIDE), F32), unroll=4)
-        dq = (dq[:, :HD] * scale).astype(BF)
+            q_ref[h] += dot(ds, keys(h, n), TN)
+        return carry
+
+    lax.fori_loop(0, steps, three, 0, unroll=2)
+    for h in heads:
+        (xa, xla), (xb, xlb) = ends[h]
+        dq = (q_ref[h, :, :HD] * scale).astype(BF)
         o_ref[xa, :, xla] = dq[:BLK]
         o_ref[xb, :, xlb] = dq[BLK:]
 
@@ -334,7 +349,8 @@
             VMEM(flat.shape, F32),
             VMEM((2, plan.hp, KEYS, 4 * BLK), F32),
             VMEM((2, plan.hp, KEYS, 4 * BLK), BF),
-            VMEM((keys, 4 * BLK), F32),
+            VMEM((plan.hp, keys, 4 * BLK), F32),
+            VMEM((plan.hp, 2 * BLK, WIDE), F32),
         ],
         compiler_params=pltpu.CompilerParams(vmem_limit_bytes=56 << 20),
         cost_estimate=pl.CostEstimate(flops=46 * 10**9, bytes_accessed=12 * 10**6, transcendentals=6 * 10**6),
@@ -577,6 +593,15 @@
     )(hid, shard, small, ids)
 
 
+def put_own_grad(plan, item, acc_ref, sum_ref, o_ref):
+    share, own = D // item, plan.own
+    total = jnp.broadcast_to(jnp.sum(sum_ref[...], 0, keepdims=True), (16, own)).astype(BF)
+    for r in range(item):
+        o_ref[r, :share, :own] = acc_ref[r * share : (r + 1) * share].astype(BF)
+        o_ref[r, share:, :own] = total
+        o_ref[r, :, own:] = jnp.zeros((share + 16, o_ref.shape[2] - own), BF)
+
+
 def own_grad_kernel(plan, item, steps, a_ref, d_ref, o_ref, acc_ref, sum_ref):
     n = pl.program_id(0) * plan.chunks + pl.program_id(1)
 
@@ -591,13 +616,7 @@
 
     @pl.when(n == steps - 1)
     def _():
-        share = D // item
-        total = jnp.broadcast_to(jnp.sum(sum_ref[...], 0, keepdims=True), (16, sum_ref.shape[1])).astype(BF)
-        own = sum_ref.shape[1]
-        for r in range(item):
-            o_ref[r, :share, :own] = acc_ref[r * share : (r + 1) * share].astype(BF)
-            o_ref[r, share:, :own] = total
-            o_ref[r, :, own:] = jnp.zeros((share + 16, o_ref.shape[2] - own), BF)
+        put_own_grad(plan, item, acc_ref, sum_ref, o_ref)
 
 
 def own_grad(plan, item, hidden_all, dx):
@@ -708,9 +727,13 @@
         return pltpu.make_async_copy(self.src.at[self.me], self.buf.at[self.me], self.own.at[0])
 
     def step(self):
-        c, groups = pl.program_id(0), self.plan.groups
-
-        @pl.when(c == 0)
+        self.begin()
+        return self.arrived()
+
+    def begin(self):
+        groups = self.plan.groups
+
+        @pl.when(pl.program_id(0) == 0)
         def _():
             barrier = pltpu.get_barrier_semaphore()
             for k in range(1, groups):
@@ -723,7 +746,9 @@
                     self.copy(n, k).start()
             self.local().wait()
 
-        for k in range(1, groups):
+    def arrived(self):
+        c = pl.program_id(0)
+        for k in range(1, self.plan.groups):
             self.copy(c, k).wait_recv()
         return self.buf[:, c]
 
@@ -739,13 +764,129 @@
         return [VMEM(shape, BF), dma(sems), dma(sems), dma((1,))]
 
 
+class Give:
+    def __init__(self, plan, out, stage, send, recv, own):
+        self.plan, self.out, self.stage, self.send, self.recv, self.own = plan, out, stage, send, recv, own
+        self.me = lax.axis_index("seq")
+        self.rank = lax.axis_index("item")
+
+    def copy(self, c, k):
+        peer = lax.rem(self.me + k, self.plan.groups)
+        return pltpu.make_async_remote_copy(
+            src_ref=self.stage.at[c, peer],
+            dst_ref=self.out.at[self.me, c],
+            send_sem=self.send.at[c, k - 1],
+            recv_sem=self.recv.at[c, k - 1],
+            device_id=(peer, self.rank),
+            device_id_type=MESH,
+        )
+
+    def local(self, c):
+        return pltpu.make_async_copy(self.stage.at[c, self.me], self.out.at[self.me, c], self.own.at[c])
+
+    def step(self, fill):
+        c = pl.program_id(0)
+        fill(self.stage.at[c])
+        self.local(c).start()
+        for k in range(1, self.plan.groups):
+            self.copy(c, k).start()
+
+    def end(self):
+        @pl.when(pl.program_id(0) == self.plan.chunks - 1)
+        def _():
+            for n in range(self.plan.chunks):
+                self.local(n).wait()
+                for k in range(1, self.plan.groups):
+                    self.copy(n, k).wait()
+
+    @staticmethod
+    def scratch(plan, shape):
+        sems = (plan.chunks, plan.groups - 1)
+        dma = pltpu.SemaphoreType.DMA
+        return [VMEM((plan.chunks, plan.groups) + shape[2:], BF), dma(sems), dma(sems), dma((plan.chunks,))]
+
+
+class Spread:
+    def __init__(self, plan, out, stage, send, recv, own):
+        self.plan, self.out, self.stage, self.send, self.recv, self.own = plan, out, stage, send, recv, own
+        self.me = lax.axis_index("seq")
+        self.rank = lax.axis_index("item")
+        self.passing = plan.groups == 4
+        if self.passing:
+            self.peers = [self.me + 1 - 2 * lax.rem(self.me, 2), lax.rem(self.me + 2, 4)]
+        else:
+            self.peers = [lax.rem(self.me + k, plan.groups) for k in range(1, plan.groups)]
+
+    def rows(self, c):
+        half = self.plan.half
+        return pl.ds(pl.multiple_of(c * half, half), half)
+
+    def remote(self, src, dst, c, n, peer):
+        return pltpu.make_async_remote_copy(
+            src_ref=src,
+            dst_ref=dst,
+            send_sem=self.send.at[c, n],
+            recv_sem=self.recv.at[c, n],
+            device_id=(peer, self.rank),
+            device_id_type=MESH,
+        )
+
+    def copy(self, c, n):
+        return self.remote(self.stage.at[c], self.out.at[self.me, :, self.rows(c)], c, n, self.peers[n])
+
+    def onward(self, c, n):
+        part = self.out.at[self.peers[n], n, self.rows(c)]
+        return self.remote(part, part, c, 2 + n, self.peers[1 - n])
+
+    def local(self, c):
+        return pltpu.make_async_copy(self.stage.at[c], self.out.at[self.me, :, self.rows(c)], self.own.at[c])
+
+    def pass_on(self, c):
+        for n in range(2):
+            self.copy(c, n).wait_recv()
+            self.onward(c, n).start()
+
+    def step(self, value):
+        c = pl.program_id(0)
+        self.stage[c] = value.reshape(2, self.plan.half, value.shape[-1])
+        self.local(c).start()
+        for n in range(len(self.peers)):
+            self.copy(c, n).start()
+        if self.passing:
+
+            @pl.when(c > 0)
+            def _():
+                self.pass_on(c - 1)
+
+    def end(self):
+        @pl.when(pl.program_id(0) == self.plan.chunks - 1)
+        def _():
+            if self.passing:
+                self.pass_on(self.plan.chunks - 1)
+            for c in range(self.plan.chunks):
+                self.local(c).wait()
+                for n in range(len(self.peers)):
+                    self.copy(c, n).wait_send()
+                    if self.passing:
+                        self.onward(c, n).wait()
+                    else:
+                        self.copy(c, n).wait_recv()
+
+    @staticmethod
+    def scratch(plan):
+        sems = (plan.chunks, max(plan.groups - 1, 4))
+        dma = pltpu.SemaphoreType.DMA
+        return [VMEM((plan.chunks, 2, plan.half, D), BF), dma(sems), dma(sems), dma((plan.chunks,))]
+
+
 def swap_params(number):
     return pltpu.CompilerParams(collective_id=number, has_side_effects=True, vmem_limit_bytes=60 << 20)
 
 
 def fwd_kernel(plan, ff, c_ref, h_ref, w_ref, vec_ref, inner_ref,
-               next_ref, next_low_ref, r1_ref, r2_ref, u_ref, y_ref, ctx_ref, *swapping):
-    swap = Swap(plan, c_ref, *swapping)
+               all_ref, next_ref, r1_ref, r2_ref, u_ref, y_ref, ctx_ref, *swapping):
+    swap = Swap(plan, c_ref, *swapping[:4])
+    spread = Spread(plan, all_ref, *swapping[4:])
     w = Packed(w_ref, ff)
     ctx = pick_context(plan, swap.step())
     write(ctx_ref, ctx)
@@ -762,16 +903,36 @@
     nxt = unit2 * vec_ref[GAIN2 : GAIN2 + 1] + vec_ref[SHIFT2 : SHIFT2 + 1]
     low_ = nxt.astype(BF)
     write(next_ref, nxt)
-    write(next_low_ref, low_)
+    spread.step(low_)
     swap.end()
-
-
-def project_kernel(plan, a_ref, w_ref, bias_ref, x_ref):
-    a = read(a_ref)
-    y = [
-        (dot(a, column_part(w_ref, n), NN) + bias_ref[:, part_of(n)]).astype(BF) for n in range(plan.cols // D)
-    ]
-    put_heads(plan, jnp.concatenate(y, 1), x_ref.at[:, 0])
+    spread.end()
+
+
+def own_kernel(plan, a_ref, w_ref, o_ref):
+    share = D // w_ref.shape[0]
+    weight = w_ref[:, :share, : plan.own].reshape(D, plan.own)
+    bias = jnp.sum(w_ref[:, share : share + 1, : plan.own].astype(F32), 0)
+    y = (dot(a_ref[...].reshape(plan.rows, D), weight, NN) + bias).astype(BF)
+    one = Plan.__new__(Plan)
+    one.__dict__.update(plan.__dict__)
+    one.groups = 1
+    put_heads(one, y, o_ref.at[:, 0])
+
+
+def own_heads(plan, every, weight):
+    return pl.pallas_call(
+        partial(own_kernel, plan),
+        out_shape=jax.ShapeDtypeStruct(plan.x_shape(), BF),
+        grid=(plan.groups, plan.chunks),
+        in_specs=[
+            pl.BlockSpec((1, 2, 1, plan.half, D), lambda g, c: (g, 0, c, 0, 0)),
+            whole(weight.shape),
+        ],
+        out_specs=pl.BlockSpec((1, 1) + plan.x_shape()[2:], lambda g, c: (g, c, 0, 0, 0, 0)),
+        compiler_params=pltpu.CompilerParams(vmem_limit_bytes=48 << 20),
+        cost_estimate=pl.CostEstimate(flops=12 * 10**9, bytes_accessed=12 * 10**6, transcendentals=0),
+        name="own_heads",
+    )(every.reshape(plan.groups, 2, plan.chunks, plan.half, D), weight)
 
 
 def piece_spec(shape):
@@ -781,31 +942,18 @@
 def layer_fwd(plan, ctx, h, packed, vec, inner):
     t = (2, plan.tokens // 2)
     ff = inner.shape[-1]
-    shapes = [(D, F32), (D, BF), (D, F32), (D, F32), (ff, F32), (D, BF), (D, BF)]
+    shapes = [(D, F32), (D, F32), (D, F32), (ff, F32), (D, BF), (D, BF)]
     return pl.pallas_call(
         partial(fwd_kernel, plan, ff),
-        out_shape=[jax.ShapeDtypeStruct(t + (n,), d) for n, d in shapes],
+        out_shape=[jax.ShapeDtypeStruct((plan.groups,) + t + (D,), BF)] + [jax.ShapeDtypeStruct(t + (n,), d) for n, d in shapes],
         grid=(plan.chunks,),
         in_specs=[pl.BlockSpec(memory_space=pl.ANY), halves(plan, D)] + [whole(w.shape) for w in (packed, vec, inner)],
-        out_specs=[halves(plan, n) for n, _ in shapes],
-        scratch_shapes=Swap.scratch(plan, plan.c_shape()),
+        out_specs=[pl.BlockSpec(memory_space=pl.ANY)] + [halves(plan, n) for n, _ in shapes],
+        scratch_shapes=Swap.scratch(plan, plan.c_shape()) + Spread.scratch(plan),
         compiler_params=swap_params(2),
         cost_estimate=pl.CostEstimate(flops=24 * 10**9, bytes_accessed=50 * 10**6, transcendentals=3 * 10**6),
         name="layer_fwd",
     )(ctx, cut(plan, h), packed, vec, inner)
-
-
-def project(plan, a, columns, bias):
-    return pl.pallas_call(
-        partial(project_kernel, plan),
-        out_shape=jax.ShapeDtypeStruct(plan.x_shape(), BF),
-        grid=(plan.chunks,),
-        in_specs=[halves(plan, D), whole(columns.shape), whole(bias.shape)],
-        out_specs=piece_spec(plan.x_shape()),
-        compiler_params=pltpu.CompilerParams(vmem_limit_bytes=48 << 20),
-        cost_estimate=pl.CostEstimate(flops=8 * 10**9, bytes_accessed=10 * 10**6, transcendentals=0),
-        name="project",
-    )(a, columns, bias)
 
 
 SUM_DO, D_GAIN1, D_SHIFT1, SUM_DF, D_GAIN2, D_SHIFT2 = range(6)
@@ -893,18 +1041,32 @@
     )(ctx, cut(plan, h), cut(plan, gy), packed, vec, inner)
 
 
-def bwd_kernel(plan, ff, dx_ref, up_ref, r1_ref, r2_ref, u_ref, w_ref, cols_ref, vec_ref,
-               d_ref, dr1_ref, gz_ref, du_ref, df_ref, do_ref, dqkv_ref, sums_ref, inner_sum_ref, qkv_sum_ref, *swapping):
-    swap = Swap(plan, dx_ref, *swapping)
+def bwd_kernel(plan, ff, item, dx_ref, up_ref, r1_ref, r2_ref, u_ref, every_ref, own_ref, w_ref, cols_ref, vec_ref,
+               d_ref, dr1_ref, gz_ref, du_ref, df_ref, do_ref, own_grad_ref, sums_ref, inner_sum_ref, acc_ref, sum_ref, *swapping):
+    swap = Swap(plan, dx_ref, *swapping[:4])
+    give = Give(plan, d_ref, *swapping[4:])
     w = Packed(w_ref, ff)
-    dqkv = pick_heads(plan, swap.step())
-    write(dqkv_ref, dqkv)
-
-    @pl.when(pl.program_id(0) == 0)
+    swap.begin()
+    one = Plan.__new__(Plan)
+    one.__dict__.update(plan.__dict__)
+    one.groups = 1
+    c = pl.program_id(0)
+
+    @pl.when(c == 0)
     def _():
-        qkv_sum_ref[...] = jnp.zeros_like(qkv_sum_ref)
-
-    qkv_sum_ref[...] += jnp.sum(dqkv.astype(F32).reshape(-1, 8, dqkv.shape[-1]), 0)
+        acc_ref[...] = jnp.zeros_like(acc_ref)
+        sum_ref[...] = jnp.zeros_like(sum_ref)
+
+    for s in range(plan.groups):
+        d = pick_heads(one, own_ref[s : s + 1, 0])
+        acc_ref[...] += dot(every_ref[s].reshape(plan.rows, D), d, TN)
+        sum_ref[...] += jnp.sum(d.astype(F32).reshape(-1, 8, plan.own), 0)
+
+    @pl.when(c == plan.chunks - 1)
+    def _():
+        put_own_grad(plan, item, acc_ref, sum_ref, own_grad_ref)
+
+    dqkv = pick_heads(plan, swap.arrived())
     gy = read(up_ref)
     for n in range(plan.cols // D):
         gy = gy + dot(dqkv[:, part_of(n)], column_part(cols_ref, n), NT)
@@ -918,32 +1080,38 @@
         return value
 
     df, dr1, do, dc = back_chunk(plan, gy, unit1, inv1, unit2, inv2, gate, w, vec_ref, sums_ref, inner_sum_ref, du_ref)
-    put_context(plan, dc, d_ref.at[:, 0])
+    give.step(lambda ref: put_context(plan, dc, ref))
     write(dr1_ref, dr1)
     write(df_ref, df)
     write(do_ref, do)
     swap.end()
-
-
-def layer_bwd(plan, dx, up, r1, r2, u, packed, columns, vec):
+    give.end()
+
+
+def layer_bwd(plan, item, dx, up, r1, r2, u, every, packed, columns, vec):
     t = (2, plan.tokens // 2)
     ff = u.shape[-1]
-    shapes = [(D, F32), (ff, BF), (ff, BF), (D, BF), (D, BF), (plan.cols, BF)]
+    shapes = [(D, F32), (ff, BF), (ff, BF), (D, BF), (D, BF)]
     sums, sums_at = sum_specs(ff)
-    sums = sums + [jax.ShapeDtypeStruct((8, plan.cols), F32)]
-    sums_at = sums_at + [pl.BlockSpec((8, plan.cols), lambda c: (0, 0))]
+    own_grad_shape = (item, D // item + 16, D)
     return pl.pallas_call(
-        partial(bwd_kernel, plan, ff),
-        out_shape=[jax.ShapeDtypeStruct(plan.c_shape(), BF)] + [jax.ShapeDtypeStruct(t + (n,), d) for n, d in shapes] + sums,
+        partial(bwd_kernel, plan, ff, item),
+        out_shape=[jax.ShapeDtypeStruct(plan.c_shape(), BF)]
+        + [jax.ShapeDtypeStruct(t + (n,), d) for n, d in shapes]
+        + [jax.ShapeDtypeStruct(own_grad_shape, BF)]
+        + sums,
         grid=(plan.chunks,),
         in_specs=[pl.BlockSpec(memory_space=pl.ANY), halves(plan, D), halves(plan, D), halves(plan, D), halves(plan, ff)]
+        + [pl.BlockSpec((plan.groups, 2, plan.half, D), lambda c: (0, 0, c, 0)), piece_spec(plan.x_shape())]
         + [whole(w.shape) for w in (packed, columns, vec)],
-        out_specs=[piece_spec(plan.c_shape())] + [halves(plan, n) for n, _ in shapes] + sums_at,
-        scratch_shapes=Swap.scratch(plan, plan.x_shape()),
+        out_specs=[pl.BlockSpec(memory_space=pl.ANY)] + [halves(plan, n) for n, _ in shapes] + [whole(own_grad_shape)] + sums_at,
+        scratch_shapes=[VMEM((D, plan.own), F32), VMEM((8, plan.own), F32)]
+        + Swap.scratch(plan, plan.x_shape())
+        + Give.scratch(plan, plan.c_shape()),
         compiler_params=swap_params(4),
-        cost_estimate=pl.CostEstimate(flops=40 * 10**9, bytes_accessed=50 * 10**6, transcendentals=3 * 10**6),
+        cost_estimate=pl.CostEstimate(flops=70 * 10**9, bytes_accessed=60 * 10**6, transcendentals=3 * 10**6),
         name="layer_bwd",
-    )(dx, up, r1, r2, u, packed, columns, vec)
+    )(dx, up, r1, r2, u, every, dx, packed, columns, vec)
 
 
 def dense_grad_kernel(item, gz_ref, df_ref, y_ref, du_ref, ctx_ref, do_ref, vec_ref, fo_ref, rest_ref):
@@ -967,7 +1135,9 @@
     def _():
         at = parts * share
         rest_ref[:, at : at + share] = dot(ctx_ref[...], do_ref[...], TN).astype(BF).reshape(item, share, D)
-        rest_ref[:, at + share :] = vec_ref[...]
+        rest_ref[:, at + share : at + share + 16] = vec_ref[:, :16]
+        if vec_ref.shape[1] > 16:
+            rest_ref[:, at + share + 16 :] = vec_ref[:, 16:]
 
 
 def dense_grads(item, gz, df, y, du, ctx, do, vecs, cut_for=0):
@@ -992,33 +1162,6 @@
     )(gz, df, y, du, ctx, do, vecs)
 
 
-def column_grad_kernel(item, a_ref, d_ref, vec_ref, o_ref):
-    n = pl.program_id(0)
-    share = D // item
-    first = pl.multiple_of(n * share, 16)
-    o_ref[:, pl.ds(first, share)] = dot(a_ref[...], d_ref[...], TN).astype(BF).reshape(item, share, D)
-
-    @pl.when(n == pl.num_programs(0) - 1)
-    def _():
-        o_ref[:, o_ref.shape[1] - vec_ref.shape[1] :] = vec_ref[...]
-
-
-def column_grads(item, a, d, vecs):
-    tokens = a.shape[0]
-    parts = d.shape[1] // D
-    out = (item, parts * (D // item) + vecs.shape[1], D)
-    return pl.pallas_call(
-        partial(column_grad_kernel, item),
-        out_shape=jax.ShapeDtypeStruct(out, BF),
-        grid=(parts,),
-        in_specs=[whole(a.shape), pl.BlockSpec((tokens, D), lambda n: (0, n)), whole(vecs.shape)],
-        out_specs=whole(out),
-        compiler_params=pltpu.CompilerParams(vmem_limit_bytes=48 << 20),
-        cost_estimate=pl.CostEstimate(flops=6 * 10**9, bytes_accessed=10 * 10**6, transcendentals=0),
-        name="column_grads",
-    )(a, d, vecs)
-
-
 def tail_kernel(plan, dx_ref, up_ref, w_ref, o_ref):
     dqkv = pick_heads(plan, dx_ref[:, 0])
     out = read(up_ref)
@@ -1040,12 +1183,12 @@
     )(dx, up, w_qkv)
 
 
-def finish_kernel(plan, share, counts, seq_first, full_ref, owns_ref, *outs):
-    qkv_ref, bias0_ref, biasq_ref, biasv_ref, attn_ref, inner_ref, outer_ref = outs[:7]
-    small = outs[7:]
+def finish_kernel(plan, share, counts, seq_first, sizes, full_ref, *outs):
+    qkv_ref, bias_ref, attn_ref, inner_ref, outer_ref = outs[:5]
+    small = outs[5:]
     outer = outer_ref.shape[1]
     parts = inner_ref.shape[2] // D
-    hp, pairs, groups = plan.hp, plan.pairs, plan.groups
+    hp, groups = plan.hp, plan.groups
 
     def rest(layer, flat, at):
         for n in range(parts):
@@ -1060,61 +1203,46 @@
             first += n
         return at + 16
 
-    def in_order(pieces):
-        return jnp.concatenate([pieces[kind, head] for kind in "qkv" for head in range(H)], 1)
-
-    zero = full_ref[...].reshape(-1, D)
-    outer_ref[1] = zero[:outer].astype(F32)
-    zero = zero[rest(1, zero, outer) :]
-    columns = plan.cols // D
-    values = jnp.concatenate([zero[n * share : (n + 1) * share] for n in range(columns)], 1).astype(F32)
-    at = columns * share
-    vec = zero[at : at + 16].astype(F32)
-    biasq_ref[...] = vec[:1, :share]
-    biasv_ref[...] = vec[:1, share : 2 * share]
-    pieces = {}
-    for head in range(H):
-        g, i = head // hp, head % hp
-        pieces["k", head] = values[:, head * WIDE : head * WIDE + HD]
-        pieces["v", head] = values[:, head * WIDE + HD : (head + 1) * WIDE]
-        first = groups * hp * WIDE
-        if i < 2 * pairs:
-            first += (g * pairs + i // 2) * WIDE + (i % 2) * HD
-        else:
-            first += groups * pairs * WIDE + g * HD
-        pieces["q", head] = values[:, first : first + HD]
-    qkv_ref[1] = in_order(pieces)
-    at = rest(0, zero, at + 16)
-    own_at = 0
+    def own(layer, first):
+        pieces = {}
+        for head in range(H):
+            g, i = head // hp, head % hp
+            rows = full_ref[g, first : first + share + 16].astype(F32)
+            pieces["k", head] = rows[:, i * WIDE : i * WIDE + HD]
+            pieces["v", head] = rows[:, i * WIDE + HD : (i + 1) * WIDE]
+            pieces["q", head] = rows[:, (2 * hp + i) * HD : (2 * hp + i + 1) * HD]
+        value = jnp.concatenate([pieces[kind, head] for kind in "qkv" for head in range(H)], 1)
+        qkv_ref[layer] = value[:share]
+        bias_ref[layer : layer + 1, :] = value[share : share + 1]
+
+    first, second, third = sizes
+    one = full_ref[:, :first].reshape(-1, D)
+    outer_ref[1] = one[:outer].astype(F32)
+    rest(1, one, outer)
+    zero = full_ref[:, first : first + second].reshape(-1, D)
+    at = rest(0, zero, 0)
+    own(1, first + second)
+    own_at = first + second + third
     if seq_first:
-        own_at = outer // groups
+        here = outer // groups
         for g in range(groups):
-            outer_ref[0, g * own_at : (g + 1) * own_at] = owns_ref[g, :own_at].astype(F32)
+            outer_ref[0, g * here : (g + 1) * here] = full_ref[g, own_at : own_at + here].astype(F32)
+        own_at += here
     else:
         outer_ref[0] = zero[at : at + outer].astype(F32)
-    pieces = {}
-    for head in range(H):
-        g, i = head // hp, head % hp
-        rows = owns_ref[g, own_at : own_at + share + 16].astype(F32)
-        pieces["k", head] = rows[:, i * WIDE : i * WIDE + HD]
-        pieces["v", head] = rows[:, i * WIDE + HD : (i + 1) * WIDE]
-        pieces["q", head] = rows[:, (2 * hp + i) * HD : (2 * hp + i + 1) * HD]
-    value = in_order(pieces)
-    qkv_ref[0] = value[:share]
-    bias0_ref[...] = value[share : share + 1]
-
-
-def finish(plan, share, ff, item, counts, seq_first, full, owns):
-    out = [(LAYERS, share, 3 * D), (1, 3 * D), (1, share), (1, share), (LAYERS, share, D), (LAYERS, share, ff), (LAYERS, ff // item, D)]
-    out += [(LAYERS, n) for n in counts]
+    own(0, own_at)
+
+
+def finish(plan, share, ff, item, counts, seq_first, sizes, full):
+    out = [(share, 3 * D), (3 * D,), (share, D), (share, ff), (ff // item, D)] + [(n,) for n in counts]
     return pl.pallas_call(
-        partial(finish_kernel, plan, share, counts, seq_first),
-        out_shape=[jax.ShapeDtypeStruct(s, F32) for s in out],
-        in_specs=[pl.BlockSpec(memory_space=VMEM)] * 2,
+        partial(finish_kernel, plan, share, counts, seq_first, sizes),
+        out_shape=[jax.ShapeDtypeStruct((LAYERS,) + s, F32) for s in out],
+        in_specs=[pl.BlockSpec(memory_space=VMEM)],
         out_specs=[pl.BlockSpec(memory_space=VMEM)] * len(out),
         compiler_params=pltpu.CompilerParams(vmem_limit_bytes=48 << 20),
         name="finish",
-    )(full, owns)
+    )(full)
 
 
 def column_parts(plan, w):
@@ -1140,25 +1268,6 @@
     return jnp.concatenate(
         [lax.dynamic_index_in_dim(p, rank, axis, False) for p in column_parts(plan, w)], -1
     )
-
-
-def natural(plan, kv, pairs, last):
-    lead = kv.shape[:-2]
-    g, hp = plan.groups, plan.hp
-    kv = kv.reshape(lead + (g * hp, 2, HD))
-    q = jnp.concatenate(
-        [pairs.reshape(lead + (g, 2 * plan.pairs, HD)), last.reshape(lead + (g, plan.odd, HD))], -2
-    ).reshape(lead + (g * hp, HD))
-    return jnp.concatenate(
-        [p[..., :H, :].reshape(lead + (H * HD,)) for p in (q, kv[..., 0, :], kv[..., 1, :])], -1
-    )
-
-
-def from_all(plan, w):
-    lead = w.shape[:-1]
-    a = plan.groups * plan.hp * WIDE
-    b = a + plan.groups * plan.pairs * WIDE
-    return natural(plan, *(p.reshape(lead + (plan.groups, -1)) for p in (w[..., :a], w[..., a:b], w[..., b:])))
 
 
 def exchange(x):
@@ -1219,14 +1328,18 @@
     ids = jnp.pad(ids, ((0, 0), (0, -used % 1024))).reshape(groups, -1, 128)
     small = (bias_query, bias_value, bias_attn_out, norm1_gain, norm1_shift, bias_ffn_in, bias_ffn_out, norm2_gain, norm2_shift)
     flat_small = jnp.concatenate(small, 1).reshape(-1)
-    own_bias = lax.dynamic_update_slice(jnp.zeros((3 * D,), BF), bias_query[0], (item_rank * share,))
-    own_bias = lax.dynamic_update_slice(own_bias, bias_value[0], (2 * D + item_rank * share,))
-    shard = jnp.concatenate([w_qkv[0], own_bias[None], jnp.zeros((15, 3 * D), BF)])
+
+    def own_shard(layer):
+        bias = lax.dynamic_update_slice(jnp.zeros((3 * D,), BF), bias_query[layer], (item_rank * share,))
+        bias = lax.dynamic_update_slice(bias, bias_value[layer], (2 * D + item_rank * share,))
+        rows = jnp.concatenate([w_qkv[layer], bias[None], jnp.zeros((15, 3 * D), BF)])
+        return own_columns(plan, rows, seq_rank)
+
     hidden_all, x0, small_all, ids = start(
         plan,
         item,
         hidden[0].astype(BF),
-        own_columns(plan, shard, seq_rank),
+        own_shard(0),
         jnp.pad(flat_small, (0, SMALL * 128 - flat_small.shape[0])).reshape(SMALL, 128),
         ids,
     )
@@ -1243,7 +1356,6 @@
         vectors.append(out)
     stacked = [jnp.stack(v[2:5] + v[6:9] + [v[2]] * 2) for v in vectors]
     inner = [v[5][None] for v in vectors]
-    qkv_bias = [jnp.concatenate([v[0], jnp.zeros_like(v[0]), v[1]])[None] for v in vectors]
 
     columns = wide_parts(all_columns(plan, w_qkv[0])), wide_parts(all_columns(plan, w_qkv[1]))
 
@@ -1251,13 +1363,15 @@
         return [w_attn_out[layer], wide_parts(w_ffn_in[layer]), w_ffn_out[layer]]
 
     packed0 = lax.all_gather(jnp.concatenate(dense(0)), "item", axis=0)
+    own_weight1 = jnp.pad(own_shard(1), ((0, 0), (0, D - plan.own)))
+    own_weight1 = lax.all_gather(own_weight1, "item", axis=0)
+    packed1 = lax.all_gather(jnp.concatenate(dense(1)), "item", axis=0)
     columns1 = lax.all_gather(columns[1], "item", axis=0)
-    packed1 = lax.all_gather(jnp.concatenate(dense(1)), "item", axis=0)
     columns0 = lax.all_gather(columns[0], "item", axis=0)
 
     ctx0 = attn_fwd(plan, tables[0], x0)
-    h1, h1_low, r1, r2, u, y0, ctx0 = layer_fwd(plan, ctx0, hidden[0], packed0, stacked[0], inner[0])
-    x1 = exchange(project(plan, h1_low, columns1, all_columns(plan, qkv_bias[1])))
+    h1_all, h1, r1, r2, u, y0, ctx0 = layer_fwd(plan, ctx0, hidden[0], packed0, stacked[0], inner[0])
+    x1 = own_heads(plan, h1_all, own_weight1)
     ctx1 = attn_fwd(plan, tables[1], x1)
     d1, output, up1, gz1, du1, df1, do1, y1, ctx1, sums1, inner1 = layer_mid(
         plan, ctx1, h1, cotangent[0], packed1, stacked[1], inner[1]
@@ -1273,10 +1387,11 @@
         part = jnp.concatenate([v.reshape(item, -1) for v in vecs], 1)
         return jnp.pad(part, ((0, 0), (0, 16 * D - part.shape[1]))).reshape(item, 16, D).astype(BF)
 
-    def grads(gz, du, df, do, y, ctx, sums, inner_sum, cut_for=0):
+    def grads(gz, du, df, do, y, ctx, sums, inner_sum, cut_for=0, more=()):
         sums = jnp.sum(sums, 1)
         vecs = (sums[SUM_DO], sums[D_GAIN1], sums[D_SHIFT1], jnp.sum(inner_sum, 0), sums[SUM_DF], sums[D_GAIN2], sums[D_SHIFT2])
-        return dense_grads(item, flat(gz), flat(df), flat(y), flat(du), flat(ctx), flat(do), rows_for(vecs), cut_for)
+        rows = jnp.concatenate([rows_for(vecs)] + list(more), 1)
+        return dense_grads(item, flat(gz), flat(df), flat(y), flat(du), flat(ctx), flat(do), rows, cut_for)
 
     def seq_send(shares):
         rows = jnp.concatenate(shares)
@@ -1296,35 +1411,34 @@
     fo1, rest1 = scattered(fo1), scattered(rest1)
     dx1 = attn_bwd(plan, tables[1], x1, dc1)
     dx1, columns0 = tie(dx1, columns0)
-    d0, up0, gz0, du0, df0, do0, dqkv1, sums0, inner0, qkv_sum1 = layer_bwd(
-        plan, dx1, up1, r1, r2, u, packed0, columns1, stacked[0]
+    d0, up0, gz0, du0, df0, do0, own1, sums0, inner0 = layer_bwd(
+        plan, item, dx1, up1, r1, r2, u, h1_all, packed0, columns1, stacked[0]
     )
-    d0, fo1 = tie(d0, fo1)
-    dc0 = exchange(d0)
-    bias1 = from_all(plan, jnp.sum(qkv_sum1, 0))
-    qkv1 = column_grads(item, flat(h1_low), flat(dqkv1), rows_for((bias1[:D], bias1[2 * D :])))
+    dc0, fo1, rest1, own1 = tie(d0, fo1, rest1, own1)
+    own1 = scattered(own1)
+    sent1 = seq_send([fo1, rest1])
     seq_first = (w_ffn_out.shape[1] // groups) % 16 == 0
     fo0, rest0 = grads(gz0, du0, df0, do0, y0, ctx0, sums0, inner0, groups if seq_first else 0)
-    dc0, qkv1, fo0, rest0, rest1 = tie(dc0, qkv1, fo0, rest0, rest1)
-    qkv1, rest0 = scattered(qkv1), scattered(rest0)
+    dc0, fo0, rest0, sent1 = tie(dc0, fo0, rest0, sent1)
+    part1 = seq_sum(sent1)
+    rest0 = scattered(rest0)
     fo0 = exchange(fo0) if seq_first else scattered(fo0)
     dx0 = attn_bwd(plan, tables[0], x0, dc0)
-    dx0, fo0, qkv1 = tie(dx0, fo0, qkv1)
+    dx0, fo0, own1 = tie(dx0, fo0, own1)
     own0 = own_grad(plan, item, hidden_all, dx0)
     dx0 = exchange(dx0)
     if seq_first:
         own0 = jnp.concatenate([seq_sum(fo0), own0], 1)
+    own_share = scattered(own0)
     dx0, own0 = tie(dx0, own0)
-    own0 = scattered(own0)
-    sent = seq_send([fo1, rest1, qkv1, rest0] + ([] if seq_first else [fo0]))
+    part0 = seq_sum(seq_send([rest0] + ([] if seq_first else [fo0])))
     input_grad = layer_tail(plan, dx0, up0, columns0)
-    full = seq_gather(seq_sum(sent))
-    owns = seq_gather(own0)
-    qkv, bias0, biasq1, biasv1, attn, inner_grad, outer, *small_grads = finish(
-        plan, share, w_ffn_in.shape[2], item, counts, seq_first, full, owns
+    sizes = part1.shape[0], part0.shape[0], own1.shape[0]
+    full = seq_gather(jnp.concatenate([part1, part0, own1, own_share]))
+    qkv, bias, attn, inner_grad, outer, *small_grads = finish(
+        plan, share, w_ffn_in.shape[2], item, counts, seq_first, sizes, full
     )
-    biasq0, biasv0 = (lax.dynamic_slice_in_dim(bias0, part * D + item_rank * share, share, 1) for part in (0, 2))
-    bias_q, bias_v = jnp.concatenate([biasq0, biasq1]), jnp.concatenate([biasv0, biasv1])
+    bias_q, bias_v = (lax.dynamic_slice_in_dim(bias, part * D + item_rank * share, share, 1) for part in (0, 2))
     out_bias, gain1, shift1, inner_bias, ffn_bias, gain2, shift2 = small_grads
     return (
         output.reshape(hidden.shape),

time: 753 us -> 729 us (0.968)
  Pallas kernels: 452 us -> 511 us
  waiting for transfers between devices: 149 us -> 99.9 us
  blocking collectives: 33.5 us -> 12.8 us
  starting transfers between devices: 30.7 us -> 23 us
    all_to_all x7 -> x5, waiting for transfers between devices: 119 us -> 71.2 us  [exchange(): lax.all_to_all(y, 'seq', split_axis=0, concat_axis=0, tiled=True)]
    pallas_call x1, Pallas kernels: 32.9 us -> 79.1 us  [layer_fwd(): pl.pallas_call(partial(fwd_kernel, plan, ff), out_shape=[jax.ShapeDtypeSt...]
    all_to_all x1, blocking collectives: 33.5 us -> 12.8 us  [exchange(): lax.all_to_all(y, 'seq', split_axis=0, concat_axis=0, tiled=True)]
    reduce_scatter x5, waiting for transfers between devices: 0.05 us -> 20.6 us  [scattered(): return lax.psum_scatter(g, 'item', scatter_dimension=0, tiled=False)]
    pallas_call x4 -> x3, Pallas kernels: 87.6 us -> 102 us  [the longest x1 82.6 us: layer_bwd(): pl.pallas_call(partial(bwd_kernel, plan, ff, item), out_shape=[jax.ShapeD...]
    all_gather x1, waiting for transfers between devices: 9.22 us -> 0.01 us  [local(): columns1 = lax.all_gather(columns[1], 'item', axis=0)]
    all_gather x1, waiting for transfers between devices: 13.6 us -> 5.35 us  [local(): packed0 = lax.all_gather(jnp.concatenate(dense(0)), 'item', axis=0)]
    all_to_all x7 -> x5, starting transfers between devices: 30.4 us -> 22.5 us  [exchange(): lax.all_to_all(y, 'seq', split_axis=0, concat_axis=0, tiled=True)]
  transfers between devices with their start and end apart: 16 -> 15, of which waited for: 9 -> 8; matrix products, arithmetic and copies ran while one was open for 5% -> 4% of each run, Pallas kernels for 60% -> 70%
where the time goes in v6:
time: 729 us; the launch traced here: 721 us
  Pallas kernels  511 us (70%)
  waiting for transfers between devices  99.9 us (14%)
  local copies, waits for them, and re-layouts  43.7 us (6%)
  starting transfers between devices  23 us (3%)
  between operations  15.3 us (2%)
  other arithmetic  15.2 us (2%)
  blocking collectives  12.8 us (2%)
    pallas_call x2, Pallas kernels, attn_bwd(): pl.pallas_call(partial(attn_bwd_kernel, plan), out_shape=jax.ShapeDtypeSt...  97.1 us
    pallas_call x1, Pallas kernels, layer_bwd(): pl.pallas_call(partial(bwd_kernel, plan, ff, item), out_shape=[jax.ShapeD...  82.6 us
    pallas_call x1, Pallas kernels, layer_fwd(): pl.pallas_call(partial(fwd_kernel, plan, ff), out_shape=[jax.ShapeDtypeSt...  79.1 us
    all_to_all x5, waiting for transfers between devices, exchange(): lax.all_to_all(y, 'seq', split_axis=0, concat_axis=0, tiled=True)  71.2 us
    pallas_call x1, Pallas kernels, start(): pl.pallas_call(partial(start_kernel, plan, item), out_shape=[jax.ShapeDty...  67.6 us
    pallas_call x2, Pallas kernels, attn_fwd(): pl.pallas_call(partial(attn_fwd_kernel, plan), out_shape=jax.ShapeDtypeSt...  55.8 us
    pallas_call x1, Pallas kernels, layer_mid(): pl.pallas_call(partial(mid_kernel, plan, ff), out_shape=[jax.ShapeDtypeSt...  50.6 us
    pallas_call x2, Pallas kernels, dense_grads(): pl.pallas_call(partial(dense_grad_kernel, item), out_shape=[jax.ShapeDtyp...  37.9 us
  transfers between devices with their start and end apart: 15, of which 8 were waited for; matrix products, arithmetic and copies ran while one was open for 4% of the time, Pallas kernels for 70%

profile of v6, /device:TPU:0, one launch (start us, length us, event | category | flops | bytes accessed | tf_op | source)
XLA Modules:
  0.0 721.4 jit_solution(7734397469955713836)
XLA Ops:
  26.3 2.6 convert_element_type.33.hid_ref
  30.1 67.6 %start.1 = (bf16[4,2,512,768]{3,2,1,0:T(8,128)(2,1)S(1)}, bf16[4,4,9,2,64,128]{5,4,3,2,1,0:T(8,128)(2,1)S(1)}, bf16[8,32,128]{2,1,0:T(8,128)(2,1)S(1)}, s32[4,8,128]{2,1,0:T(8,128)S(1)}) custom-call(bf16[2,512,768]{2,1,0:T(8,128)(2,1)S(1)} %convert_element_type.33.hid_ref, bf16[112,576]{1,0:T(8,128)(2,1)S(1)} %pad_maximum_fusion.6.shard_ref, ...), custom_call_target="tpu_custom_call" | custom-call | flops 54999998464 | bytes 12000000 | tf_op jit(solution)/shard_map/start/pallas_call | solution.py:566
  97.7 2.6 copy-done.4
  103.4 2.3 fusion.12
  108.3 27.9 %attn_fwd.2 = bf16[96,64,128]{2,1,0:T(8,128)(2,1)S(1)} custom-call(s32[1536]{0:T(1024)S(1)} %reshape.286.lists_ref, bf16[288,64,128]{2,1,0:T(8,128)(2,1)} %bitcast.170), custom_call_target="tpu_custom_call" | custom-call | flops 25999998976 | bytes 6000000 | tf_op jit(solution)/shard_map/attn_fwd/pallas_call | solution.py:206
  138.6 5.4 all-gather.11.cloned.1.call-done
  144.0 79.1 %layer_fwd.1 = (bf16[4,2,512,768]{3,2,1,0:T(8,128)(2,1)}, f32[2,512,768]{2,1,0:T(8,128)}, f32[2,512,768]{2,1,0:T(8,128)}, f32[2,512,768]{2,1,0:T(8,128)}, f32[2,...) custom-call(bf16[4,4,3,2,64,128]{5,4,3,2,1,0:T(8,128)(2,1)} %bitcast.174, ...), custom_call_target="tpu_custom_call" | custom-call | flops 24000000000 | bytes 50000000 | tf_op jit(solution)/shard_map/layer_fwd/pallas_call | solution.py:946
  224.4 13.7 %own_heads.1 = bf16[4,4,9,2,64,128]{5,4,3,2,1,0:T(8,128)(2,1)S(1)} custom-call(bf16[4,2,4,128,768]{4,3,2,1,0:T(8,128)(2,1)} %bitcast.236, bf16[8,112,768]{2,1,0:T(8,128)(2,1)S(1)} %bitcast.168), custom_call_target="tpu_custom_call" | custom-call | flops 12000000000 | bytes 12000000 | tf_op jit(solution)/shard_map/own_heads/pallas_call | solution.py:923
  238.1 2.2 copy-done.6
  240.4 27.9 %attn_fwd.3 = bf16[96,64,128]{2,1,0:T(8,128)(2,1)S(1)} custom-call(s32[1536]{0:T(1024)S(1)} %reshape.285.lists_ref, bf16[288,64,128]{2,1,0:T(8,128)(2,1)} %bitcast.172), custom_call_target="tpu_custom_call" | custom-call | flops 25999998976 | bytes 6000000 | tf_op jit(solution)/shard_map/attn_fwd/pallas_call | solution.py:206
  270.6 50.6 %layer_mid.1 = (bf16[4,4,3,2,64,128]{5,4,3,2,1,0:T(8,128)(2,1)}, f32[2,512,768]{2,1,0:T(8,128)}, f32[2,512,768]{2,1,0:T(8,128)}, bf16[2,512,3072]{2,1,0:T(8,128)...) custom-call(bf16[4,4,3,2,64,128]{5,4,3,2,1,0:T(8,128)(2,1)} %bitcast, ...), custom_call_target="tpu_custom_call" | custom-call | flops 44999999488 | bytes 50000000 | tf_op jit(solution)/shard_map/layer_mid/pallas_call | solution.py:1030
  321.2 3.7 all-to-all-start
  326.5 18.9 %dense_grads.2 = (bf16[8,384,768]{2,1,0:T(8,128)(2,1)}, bf16[8,496,768]{2,1,0:T(8,128)(2,1)}) custom-call(bf16[1024,3072]{1,0:T(8,128)(2,1)} %bitcast.239, bf16[1024,768]{1,0:T(8,128)(2,1)} %bitcast.249, bf16[1024,768]{1,0:T(8,128)(2,1)} %bitcast.251, bf16[1024,3072]{1,0:T(8,128)(2,1)} %bitcast.240, bf16[1024,768]{1,0:T(8,128)(2,1)} %bitcast.252, ...), custom_call_target="tpu_custom_call" | custom-call | flops 14000000000 | bytes 30000000 | tf_op jit(solution)/shard_map/dense_grads/pallas_call | solution.py:1153
  347.4 48.6 %attn_bwd.2 = bf16[288,64,128]{2,1,0:T(8,128)(2,1)} custom-call(s32[1536]{0:T(1024)} %copy-done.2, bf16[288,64,128]{2,1,0:T(8,128)(2,1)} %bitcast.173, bf16[96,64,128]{2,1,0:T(8,128)(2,1)} %bitcast.185), custom_call_target="tpu_custom_call" | custom-call | flops 46000001024 | bytes 12000000 | tf_op jit(solution)/shard_map/attn_bwd/pallas_call | solution.py:343
  396.0 82.6 %layer_bwd.1 = (bf16[4,4,3,2,64,128]{5,4,3,2,1,0:T(8,128)(2,1)}, f32[2,512,768]{2,1,0:T(8,128)}, bf16[2,512,3072]{2,1,0:T(8,128)(2,1)}, bf16[2,512,3072]{2,1,0:T...) custom-call(bf16[4,4,9,2,64,128]{5,4,3,2,1,0:T(8,128)(2,1)} %bitcast, ...), custom_call_target="tpu_custom_call" | custom-call | flops 70000001024 | bytes 60000000 | tf_op jit(solution)/shard_map/layer_bwd/pallas_call | solution.py:1097
  482.5 3.6 all-to-all-start.1
  486.4 19.0 %dense_grads.3 = (bf16[4,8,96,768]{3,2,1,0:T(8,128)(2,1)}, bf16[8,496,768]{2,1,0:T(8,128)(2,1)}) custom-call(bf16[1024,3072]{1,0:T(8,128)(2,1)} %bitcast.237, bf16[1024,768]{1,0:T(8,128)(2,1)} %bitcast.247, bf16[1024,768]{1,0:T(8,128)(2,1)} %bitcast.244, bf16[1024,3072]{1,0:T(8,128)(2,1)} %bitcast.238, bf16[1024,768]{1,0:T(8,128)(2,1)} %bitcast.245, ...), custom_call_target="tpu_custom_call" | custom-call | flops 14000000000 | bytes 30000000 | tf_op jit(solution)/shard_map/dense_grads/pallas_call | solution.py:1153
  505.4 5.0 all-to-all-start.2
  510.5 48.5 %attn_bwd.3 = bf16[288,64,128]{2,1,0:T(8,128)(2,1)} custom-call(s32[1536]{0:T(1024)} %copy-done.1, bf16[288,64,128]{2,1,0:T(8,128)(2,1)} %bitcast.171, bf16[96,64,128]{2,1,0:T(8,128)(2,1)} %bitcast.246), custom_call_target="tpu_custom_call" | custom-call | flops 46000001024 | bytes 12000000 | tf_op jit(solution)/shard_map/attn_bwd/pallas_call | solution.py:343
  559.0 4.3 all-to-all-done.2
  563.3 3.3 reduce_sum.76
  566.6 2.4 copy-done
  569.0 13.3 %own_grad.1 = bf16[8,112,768]{2,1,0:T(8,128)(2,1)S(1)} custom-call(bf16[4,2,4,128,768]{4,3,2,1,0:T(8,128)(2,1)} %bitcast.169, bf16[4,4,9,2,64,128]{5,4,3,2,1,0:T(8,128)(2,1)S(1)} %bitcast.164), custom_call_target="tpu_custom_call" | custom-call | flops 7000000000 | bytes 12000000 | tf_op jit(solution)/shard_map/own_grad/pallas_call | solution.py:624
  585.6 12.8 %all_to_all.30 = bf16[4,128,768]{2,1,0:T(8,128)(2,1)S(1)} all-to-all(bf16[4,128,768]{2,1,0:T(8,128)(2,1)S(1)} %bitcast.184), channel_id=1, replica_groups=mesh['seq'=4,'item'=8] {'seq'}, dimensions={0} | all-to-all | bytes 1572864 | tf_op jit(solution)/shard_map/all_to_all | solution.py:1275
  598.3 5.0 all-to-all-start.3
  603.8 19.0 %reduce-scatter.14.cloned.1.call-done = bf16[1,208,768]{2,1,0:T(8,128)(2,1)} async-done(((bf16[8,208,768]{2,1,0:T(8,128)(2,1)}), bf16[1,208,768]{2,1,0:T(8,128)(2,1)}) %reduce-scatter.14.cloned.1.call-update) | async-done | bytes 319504 | tf_op jit(solution)/shard_map/reduce_scatter | solution.py:1384
  623.9 29.2 %all-to-all-done.3 = bf16[4,4608,128]{2,1,0:T(8,128)(2,1)} async-done(((bf16[4,4608,128]{2,1,0:T(8,128)(2,1)}), bf16[4,4608,128]{2,1,0:T(8,128)(2,1)}, u32[]{:S(2)}, u32[]{:S(2)}) %all-to-all-start.3) | async-done | bytes 4718624 | tf_op jit(solution)/shard_map/all_to_all | solution.py:1275
  653.0 2.3 broadcast_in_dim.8
  655.3 5.1 all-to-all-start.5
  660.4 8.4 %layer_tail.1 = f32[2,512,768]{2,1,0:T(8,128)} custom-call(bf16[4,4,9,2,64,128]{5,4,3,2,1,0:T(8,128)(2,1)} %bitcast.84.dx_ref, f32[2,512,768]{2,1,0:T(8,128)S(1)} %copy-done.9, bf16[8,288,768]{2,1,0:T(8,128)(2,1)} %bitcast.233), custom_call_target="tpu_custom_call" | custom-call | flops 8000000000 | bytes 12000000 | tf_op jit(solution)/shard_map/layer_tail/pallas_call | solution.py:1174
  668.8 37.8 %all-to-all-done.5.full_ref = bf16[4,672,768]{2,1,0:T(8,128)(2,1)} async-done(((bf16[4,672,768]{2,1,0:T(8,128)(2,1)}), bf16[4,672,768]{2,1,0:T(8,128)(2,1)}, u32[]{:S(2)}, u32[]{:S(2)}) %all-to-all-start.5) | async-done | bytes 4128800 | tf_op jit(solution)/shard_map/all_to_all | solution.py:1275
  706.6 5.5 finish.1
  (234 shorter events, 46.1 us)
Async XLA Ops:
  7.2 136.8 %all-gather.11.cloned.1.call-start = ((), (), s32[]{:S(2)}) async-start(), calls=%async_computation.16 | async-start | bytes 11943936 | tf_op jit(solution)/shard_map/all_gather | solution.py:1365
  10.2 2.8 copy-start.13
  13.0 2.1 copy-start.22
  13.0 2.3 copy-start.23
  15.0 208.1 %all-gather.13.cloned.1.call-start = ((), (), s32[]{:S(2)}) async-start(), calls=%async_computation.17 | async-start | bytes 1548288 | tf_op jit(solution)/shard_map/all_gather | solution.py:1367
  22.3 248.4 %all-gather.15.cloned.1.call-start = ((), (), s32[]{:S(2)}) async-start(), calls=%async_computation.18 | async-start | bytes 11943936 | tf_op jit(solution)/shard_map/all_gather | solution.py:1368
  23.0 373.0 %all-gather.17.cloned.1.call-start = ((), (), s32[]{:S(2)}) async-start(), calls=%async_computation.19 | async-start | bytes 3981312 | tf_op jit(solution)/shard_map/all_gather | solution.py:1370
  24.6 371.3 %all-gather.19.cloned.1.call-start = ((), (), s32[]{:S(2)}) async-start(), calls=%async_computation.20 | async-start | bytes 3981312 | tf_op jit(solution)/shard_map/all_gather | solution.py:1369
  97.7 2.6 copy-start.4
  100.3 2.2 copy-start.5
  105.8 134.5 %copy-start.2 = (s32[1536]{0:T(1024)}, s32[1536]{0:T(1024)S(1)}, u32[]{:S(2)}) copy-start(s32[1536]{0:T(1024)S(1)} %reshape.285.lists_ref) | copy-start | bytes 18436
  106.0 30.2 %copy-start.1 = (s32[1536]{0:T(1024)}, s32[1536]{0:T(1024)S(1)}, u32[]{:S(2)}) copy-start(s32[1536]{0:T(1024)S(1)} %reshape.286.lists_ref) | copy-start | bytes 18436
  238.1 2.3 copy-start.6
  321.2 3.8 copy-start.18
  321.2 4.2 copy-start.20
  321.2 24.2 %all-to-all-start = ((bf16[4,1536,128]{2,1,0:T(8,128)(2,1)}), bf16[4,1536,128]{2,1,0:T(8,128)(2,1)S(1)}, u32[]{:S(2)}, u32[]{:S(2)}) async-start(bf16[4,1536,128]{2,1,0:T(8,128)(2,1)} %bitcast.186), calls=%async_computation | async-start | bytes 3145728 | tf_op jit(solution)/shard_map/all_to_all | solution.py:1275
  325.0 153.7 %reduce-scatter.6.cloned.1.call-start = ((), (), s32[]{:S(2)}) async-start(), calls=%async_computation.11 | async-start | bytes 5308416 | tf_op jit(solution)/shard_map/reduce_scatter | solution.py:1384
  346.6 133.2 %reduce-scatter.8.cloned.1.call-start = ((), (), s32[]{:S(2)}) async-start(), calls=%async_computation.12 | async-start | bytes 6856704 | tf_op jit(solution)/shard_map/reduce_scatter | solution.py:1384
  347.3 211.6 %reduce-scatter.10.cloned.1.call-start = ((), (), s32[]{:S(2)}) async-start(), calls=%async_computation.13 | async-start | bytes 1548288 | tf_op jit(solution)/shard_map/reduce_scatter | solution.py:1384
  478.6 1.6 copy-start.19
  478.6 2.8 copy-start.15
  479.8 1.6 copy-start.14
  482.5 22.8 %all-to-all-start.1 = ((bf16[4,224,768]{2,1,0:T(8,128)(2,1)}), bf16[4,224,768]{2,1,0:T(8,128)(2,1)S(1)}, u32[]{:S(2)}, u32[]{:S(2)}) async-start(bf16[4,224,768]{2,1,0:T(8,128)(2,1)} %bitcast.77), calls=%async_computation.3 | async-start | bytes 2752512 | tf_op jit(solution)/shard_map/all_to_all | solution.py:1275
  486.2 98.2 %reduce-scatter.12.cloned.1.call-start = ((), (), s32[]{:S(2)}) async-start(), calls=%async_computation.14 | async-start | bytes 6856704 | tf_op jit(solution)/shard_map/reduce_scatter | solution.py:1384
  505.4 57.8 %all-to-all-start.2 = ((bf16[4,768,768]{2,1,0:T(8,128)(2,1)}), bf16[4,768,768]{2,1,0:T(8,128)(2,1)}, u32[]{:S(2)}, u32[]{:S(2)}) async-start(bf16[4,768,768]{2,1,0:T(8,128)(2,1)} %bitcast.180), calls=%async_computation.4 | async-start | bytes 9437184 | tf_op jit(solution)/shard_map/all_to_all | solution.py:1275
  510.4 112.4 %reduce-scatter.14.cloned.1.call-start = ((), (), s32[]{:S(2)}) async-start(), calls=%async_computation.15 | async-start | bytes 2875392 | tf_op jit(solution)/shard_map/reduce_scatter | solution.py:1384
  566.6 2.4 copy-start
  598.3 54.7 %all-to-all-start.3 = ((bf16[4,4608,128]{2,1,0:T(8,128)(2,1)}), bf16[4,4608,128]{2,1,0:T(8,128)(2,1)}, u32[]{:S(2)}, u32[]{:S(2)}) async-start(bf16[4,4608,128]{2,1,0:T(8,128)(2,1)} %bitcast.163), calls=%async_computation.6 | async-start | bytes 9437184 | tf_op jit(solution)/shard_map/all_to_all | solution.py:1275
  603.3 19.5 %copy-start.16 = (bf16[1,112,768]{2,1,0:T(8,128)(2,1)S(1)}, bf16[1,112,768]{2,1,0:T(8,128)(2,1)}, u32[]{:S(2)}) copy-start(bf16[1,112,768]{2,1,0:T(8,128)(2,1)} %reduce-scatter.10.cloned.1.call-done) | copy-start | bytes 516100
  655.3 5.1 copy-start.9
  655.3 51.3 %all-to-all-start.5 = ((bf16[4,672,768]{2,1,0:T(8,128)(2,1)}), bf16[4,672,768]{2,1,0:T(8,128)(2,1)}, u32[]{:S(2)}, u32[]{:S(2)}) async-start(bf16[4,672,768]{2,1,0:T(8,128)(2,1)} %broadcast_in_dim.8), calls=%async_computation.10 | async-start | bytes 8257536 | tf_op jit(solution)/shard_map/all_to_all | solution.py:1275
  668.8 43.9 %copy-start.10 = (f32[2,512,768]{2,1,0:T(8,128)S(1)}, f32[2,512,768]{2,1,0:T(8,128)}, u32[]{:S(2)}) copy-start(f32[2,512,768]{2,1,0:T(8,128)} %get-tuple-element.84) | copy-start | bytes 9437188
  (14 other events, 12.6 us)
Sparse Core Ops, SparseCore 0:
  15.1 128.8 all-gather.10
  146.2 22.3 all-gather.12
  170.8 99.7 all-gather.14
  272.7 39.8 all-gather.16
  314.7 40.3 all-gather.18
  357.3 53.8 reduce-scatter.5
  413.4 66.3 reduce-scatter.7
  482.2 33.7 reduce-scatter.9
  518.3 66.0 reduce-scatter.11
  587.3 35.5 reduce-scatter.13

commit v7 on v6

--- a/solution.py
+++ b/solution.py
@@ -1162,25 +1162,126 @@
     )(gz, df, y, du, ctx, do, vecs)
 
 
-def tail_kernel(plan, dx_ref, up_ref, w_ref, o_ref):
-    dqkv = pick_heads(plan, dx_ref[:, 0])
+def tail_kernel(plan, dx_ref, up_ref, w_ref, rows_ref, o_ref, got_ref, *scratch):
+    swap = Swap(plan, dx_ref, *scratch[:4])
+    send, recv, own = scratch[4:]
+    me, rank, groups = swap.me, swap.rank, plan.groups
+
+    def copy(k):
+        peer = lax.rem(me + k, groups)
+        return pltpu.make_async_remote_copy(
+            src_ref=rows_ref.at[peer],
+            dst_ref=got_ref.at[me],
+            send_sem=send.at[k - 1],
+            recv_sem=recv.at[k - 1],
+            device_id=(peer, rank),
+            device_id_type=MESH,
+        )
+
+    def local():
+        return pltpu.make_async_copy(rows_ref.at[me], got_ref.at[me], own.at[0])
+
+    swap.begin()
+
+    @pl.when(pl.program_id(0) == 0)
+    def _():
+        local().start()
+        for k in range(1, groups):
+            copy(k).start()
+
+    dqkv = pick_heads(plan, swap.arrived())
     out = read(up_ref)
     for n in range(plan.cols // D):
         out = out + dot(dqkv[:, part_of(n)], column_part(w_ref, n), NT)
     write(o_ref, out)
-
-
-def layer_tail(plan, dx, up, w_qkv):
+    swap.end()
+
+    @pl.when(pl.program_id(0) == plan.chunks - 1)
+    def _():
+        local().wait()
+        for k in range(1, groups):
+            copy(k).wait()
+
+
+def layer_tail(plan, dx, up, columns, rows):
+    dma = pltpu.SemaphoreType.DMA
     return pl.pallas_call(
         partial(tail_kernel, plan),
-        out_shape=jax.ShapeDtypeStruct(up.shape, F32),
+        out_shape=[jax.ShapeDtypeStruct(up.shape, F32), jax.ShapeDtypeStruct(rows.shape, BF)],
         grid=(plan.chunks,),
-        in_specs=[piece_spec(plan.x_shape()), halves(plan, D), whole(w_qkv.shape)],
-        out_specs=halves(plan, D),
-        compiler_params=pltpu.CompilerParams(vmem_limit_bytes=48 << 20),
-        cost_estimate=pl.CostEstimate(flops=8 * 10**9, bytes_accessed=12 * 10**6, transcendentals=0),
+        in_specs=[pl.BlockSpec(memory_space=pl.ANY), halves(plan, D), whole(columns.shape), pl.BlockSpec(memory_space=pl.ANY)],
+        out_specs=[halves(plan, D), pl.BlockSpec(memory_space=pl.ANY)],
+        scratch_shapes=Swap.scratch(plan, plan.x_shape()) + [dma((plan.groups - 1,)), dma((plan.groups - 1,)), dma((1,))],
+        compiler_params=swap_params(5),
+        cost_estimate=pl.CostEstimate(flops=55 * 10**9, bytes_accessed=12 * 10**6, transcendentals=0),
         name="layer_tail",
-    )(dx, up, w_qkv)
+    )(dx, up, columns, rows)
+
+
+def gather_kernel(groups, rows_ref, out_ref, send, recv, own):
+    me = lax.axis_index("seq")
+    rank = lax.axis_index("item")
+    barrier = pltpu.get_barrier_semaphore()
+    for k in range(1, groups):
+        pl.semaphore_signal(barrier, inc=1, device_id=(lax.rem(me + k, groups), rank), device_id_type=MESH)
+    pl.semaphore_wait(barrier, groups - 1)
+    count = rows_ref.shape[0]
+    first = count // 32 * 16
+    parts = [pl.ds(0, first), pl.ds(first, count - first)]
+    if groups == 4:
+        peers = [me + 1 - 2 * lax.rem(me, 2), lax.rem(me + 2, 4)]
+    else:
+        peers = [lax.rem(me + k, groups) for k in range(1, groups)]
+
+    def remote(src, dst, n, part, peer):
+        return pltpu.make_async_remote_copy(
+            src_ref=src, dst_ref=dst, send_sem=send.at[n, part], recv_sem=recv.at[n, part],
+            device_id=(peer, rank), device_id_type=MESH,
+        )
+
+    def copy(n, part):
+        return remote(rows_ref.at[parts[part]], out_ref.at[me, parts[part]], n, part, peers[n])
+
+    def onward(n):
+        piece = out_ref.at[peers[n], parts[n]]
+        return remote(piece, piece, 2, n, peers[1 - n])
+
+    local = pltpu.make_async_copy(rows_ref, out_ref.at[me], own.at[0])
+    if groups == 4:
+        order = [(0, 0), (1, 1), (0, 1), (1, 0)]
+    else:
+        order = [(n, part) for n in range(groups - 1) for part in range(2)]
+    for n, part in order:
+        copy(n, part).start()
+    local.start()
+    if groups == 4:
+        for n in range(2):
+            copy(n, n).wait_recv()
+            onward(n).start()
+        for n in range(2):
+            copy(n, 1 - n).wait_recv()
+            onward(n).wait()
+        for n, part in order:
+            copy(n, part).wait_send()
+    else:
+        for n, part in order:
+            copy(n, part).wait()
+    local.wait()
+
+
+def gather(groups, rows):
+    sems = (max(groups - 1, 3), 2)
+    dma = pltpu.SemaphoreType.DMA
+    return pl.pallas_call(
+        partial(gather_kernel, groups),
+        out_shape=jax.ShapeDtypeStruct((groups,) + rows.shape, BF),
+        in_specs=[pl.BlockSpec(memory_space=pl.ANY)],
+        out_specs=pl.BlockSpec(memory_space=pl.ANY),
+        scratch_shapes=[dma(sems), dma(sems), dma((1,))],
+        compiler_params=swap_params(6),
+        cost_estimate=pl.CostEstimate(flops=35 * 10**9, bytes_accessed=6 * 10**6, transcendentals=0),
+        name="gather",
+    )(rows)
 
 
 def finish_kernel(plan, share, counts, seq_first, sizes, full_ref, *outs):
@@ -1393,16 +1494,16 @@
         rows = jnp.concatenate([rows_for(vecs)] + list(more), 1)
         return dense_grads(item, flat(gz), flat(df), flat(y), flat(du), flat(ctx), flat(do), rows, cut_for)
 
-    def seq_send(shares):
+    def for_groups(shares):
         rows = jnp.concatenate(shares)
         rows = jnp.pad(rows, ((0, -rows.shape[0] % (16 * groups)), (0, 0)))
-        return exchange(rows.reshape(groups, -1, D))
+        return rows.reshape(groups, -1, D)
+
+    def seq_send(shares):
+        return exchange(for_groups(shares))
 
     def seq_sum(sent):
         return jnp.sum(sent.astype(F32), 0).astype(BF)
-
-    def seq_gather(part):
-        return exchange(jnp.broadcast_to(part[None], (groups,) + part.shape))
 
     counts = [share] * 3 + [w_ffn_in.shape[2] // item] + [share] * 3
     dc1 = exchange(d1)
@@ -1426,15 +1527,15 @@
     dx0 = attn_bwd(plan, tables[0], x0, dc0)
     dx0, fo0, own1 = tie(dx0, fo0, own1)
     own0 = own_grad(plan, item, hidden_all, dx0)
-    dx0 = exchange(dx0)
     if seq_first:
         own0 = jnp.concatenate([seq_sum(fo0), own0], 1)
     own_share = scattered(own0)
     dx0, own0 = tie(dx0, own0)
-    part0 = seq_sum(seq_send([rest0] + ([] if seq_first else [fo0])))
-    input_grad = layer_tail(plan, dx0, up0, columns0)
+    rows0 = for_groups([rest0] + ([] if seq_first else [fo0]))
+    input_grad, rows0 = layer_tail(plan, dx0, up0, columns0, rows0)
+    part0 = seq_sum(rows0)
     sizes = part1.shape[0], part0.shape[0], own1.shape[0]
-    full = seq_gather(jnp.concatenate([part1, part0, own1, own_share]))
+    full = gather(groups, jnp.concatenate([part1, part0, own1, own_share]))
     qkv, bias, attn, inner_grad, outer, *small_grads = finish(
         plan, share, w_ffn_in.shape[2], item, counts, seq_first, sizes, full
     )

time: 729 us -> 718 us (0.985)
  Pallas kernels: 511 us -> 600 us
  waiting for transfers between devices: 99.9 us -> 18.4 us
  blocking collectives: 12.8 us -> 0 us
  starting transfers between devices: 23 us -> 12.9 us
    pallas_call x1 -> x2, Pallas kernels: 8.36 us -> 101 us  [the longest x1 64.1 us: layer_tail(): pl.pallas_call(partial(tail_kernel, plan), out_shape=[jax.ShapeDtypeStruc...]
    all_to_all x5 -> x3, waiting for transfers between devices: 71.2 us -> 3.9 us  [exchange(): lax.all_to_all(y, 'seq', split_axis=0, concat_axis=0, tiled=True)]
    reduce_scatter x5, waiting for transfers between devices: 20.6 us -> 3.14 us  [scattered(): return lax.psum_scatter(g, 'item', scatter_dimension=0, tiled=False)]
    all_to_all x1 -> x0, blocking collectives: 12.8 us -> none  [exchange(): lax.all_to_all(y, 'seq', split_axis=0, concat_axis=0, tiled=True)]
    all_to_all x5 -> x3, starting transfers between devices: 22.5 us -> 12.4 us  [exchange(): lax.all_to_all(y, 'seq', split_axis=0, concat_axis=0, tiled=True)]
    unnamed x83 -> x88, local copies, waits for them, and re-layouts: 25 us -> 30.2 us
  transfers between devices with their start and end apart: 15 -> 13, of which waited for: 8 -> 5; matrix products, arithmetic and copies ran while one was open for 4% -> 4% of each run, Pallas kernels for 70% -> 79%
where the time goes in v7:
time: 718 us; the launch traced here: 710 us
  Pallas kernels  600 us (84%)
  local copies, waits for them, and re-layouts  46.4 us (6%)
  waiting for transfers between devices  18.4 us (3%)
  other arithmetic  17.1 us (2%)
  between operations  15.4 us (2%)
  starting transfers between devices  12.9 us (2%)
    pallas_call x2, Pallas kernels, attn_bwd(): pl.pallas_call(partial(attn_bwd_kernel, plan), out_shape=jax.ShapeDtypeSt...  97.1 us
    pallas_call x1, Pallas kernels, layer_bwd(): pl.pallas_call(partial(bwd_kernel, plan, ff, item), out_shape=[jax.ShapeD...  82.5 us
    pallas_call x1, Pallas kernels, layer_fwd(): pl.pallas_call(partial(fwd_kernel, plan, ff), out_shape=[jax.ShapeDtypeSt...  79.1 us
    pallas_call x1, Pallas kernels, start(): pl.pallas_call(partial(start_kernel, plan, item), out_shape=[jax.ShapeDty...  65.8 us
    pallas_call x1, Pallas kernels, layer_tail(): pl.pallas_call(partial(tail_kernel, plan), out_shape=[jax.ShapeDtypeStruc...  64.1 us
    pallas_call x2, Pallas kernels, attn_fwd(): pl.pallas_call(partial(attn_fwd_kernel, plan), out_shape=jax.ShapeDtypeSt...  55.8 us
    pallas_call x1, Pallas kernels, layer_mid(): pl.pallas_call(partial(mid_kernel, plan, ff), out_shape=[jax.ShapeDtypeSt...  50.6 us
    pallas_call x2, Pallas kernels, dense_grads(): pl.pallas_call(partial(dense_grad_kernel, item), out_shape=[jax.ShapeDtyp...  37.8 us
  transfers between devices with their start and end apart: 13, of which 5 were waited for; matrix products, arithmetic and copies ran while one was open for 4% of the time, Pallas kernels for 79%

profile of v7, /device:TPU:0, one launch (start us, length us, event | category | flops | bytes accessed | tf_op | source)
XLA Modules:
  0.0 710.4 jit_solution(10993618007512798770)
XLA Ops:
  25.2 2.4 convert_element_type.33.hid_ref
  28.8 65.8 %start.1 = (bf16[4,2,512,768]{3,2,1,0:T(8,128)(2,1)S(1)}, bf16[4,4,9,2,64,128]{5,4,3,2,1,0:T(8,128)(2,1)S(1)}, bf16[8,32,128]{2,1,0:T(8,128)(2,1)S(1)}, s32[4,8,128]{2,1,0:T(8,128)S(1)}) custom-call(bf16[2,512,768]{2,1,0:T(8,128)(2,1)S(1)} %convert_element_type.33.hid_ref, bf16[112,576]{1,0:T(8,128)(2,1)S(1)} %pad_maximum_fusion.6.shard_ref, ...), custom_call_target="tpu_custom_call" | custom-call | flops 54999998464 | bytes 12000000 | tf_op jit(solution)/shard_map/start/pallas_call | solution.py:566
  94.6 2.6 copy-done.4
  97.2 2.2 copy-done.5
  100.3 2.3 fusion.12
  105.2 27.9 %attn_fwd.2 = bf16[96,64,128]{2,1,0:T(8,128)(2,1)S(1)} custom-call(s32[1536]{0:T(1024)S(1)} %reshape.279.lists_ref, bf16[288,64,128]{2,1,0:T(8,128)(2,1)} %bitcast.166), custom_call_target="tpu_custom_call" | custom-call | flops 25999998976 | bytes 6000000 | tf_op jit(solution)/shard_map/attn_fwd/pallas_call | solution.py:206
  135.6 8.5 %all-gather.11.cloned.1.call-done = bf16[6912,768]{1,0:T(8,128)(2,1)} async-done(((bf16[864,768]{1,0:T(8,128)(2,1)}), bf16[6912,768]{1,0:T(8,128)(2,1)}) %all-gather.11.cloned.1.call-update) | async-done | bytes 10616848 | tf_op jit(solution)/shard_map/all_gather | solution.py:1466
  144.0 79.1 %layer_fwd.1 = (bf16[4,2,512,768]{3,2,1,0:T(8,128)(2,1)}, f32[2,512,768]{2,1,0:T(8,128)}, f32[2,512,768]{2,1,0:T(8,128)}, f32[2,512,768]{2,1,0:T(8,128)}, f32[2,...) custom-call(bf16[4,4,3,2,64,128]{5,4,3,2,1,0:T(8,128)(2,1)} %bitcast.172, ...), custom_call_target="tpu_custom_call" | custom-call | flops 24000000000 | bytes 50000000 | tf_op jit(solution)/shard_map/layer_fwd/pallas_call | solution.py:946
  224.5 13.7 %own_heads.1 = bf16[4,4,9,2,64,128]{5,4,3,2,1,0:T(8,128)(2,1)S(1)} custom-call(bf16[4,2,4,128,768]{4,3,2,1,0:T(8,128)(2,1)} %bitcast.235, bf16[8,112,768]{2,1,0:T(8,128)(2,1)S(1)} %bitcast.164), custom_call_target="tpu_custom_call" | custom-call | flops 12000000000 | bytes 12000000 | tf_op jit(solution)/shard_map/own_heads/pallas_call | solution.py:923
  238.2 2.3 copy-done.6
  240.4 27.9 %attn_fwd.3 = bf16[96,64,128]{2,1,0:T(8,128)(2,1)S(1)} custom-call(s32[1536]{0:T(1024)S(1)} %reshape.278.lists_ref, bf16[288,64,128]{2,1,0:T(8,128)(2,1)} %bitcast.168), custom_call_target="tpu_custom_call" | custom-call | flops 25999998976 | bytes 6000000 | tf_op jit(solution)/shard_map/attn_fwd/pallas_call | solution.py:206
  270.9 50.6 %layer_mid.1 = (bf16[4,4,3,2,64,128]{5,4,3,2,1,0:T(8,128)(2,1)}, f32[2,512,768]{2,1,0:T(8,128)}, f32[2,512,768]{2,1,0:T(8,128)}, bf16[2,512,3072]{2,1,0:T(8,128)...) custom-call(bf16[4,4,3,2,64,128]{5,4,3,2,1,0:T(8,128)(2,1)} %bitcast, ...), custom_call_target="tpu_custom_call" | custom-call | flops 44999999488 | bytes 50000000 | tf_op jit(solution)/shard_map/layer_mid/pallas_call | solution.py:1030
  321.5 3.7 all-to-all-start
  326.8 18.9 %dense_grads.2 = (bf16[8,384,768]{2,1,0:T(8,128)(2,1)}, bf16[8,496,768]{2,1,0:T(8,128)(2,1)}) custom-call(bf16[1024,3072]{1,0:T(8,128)(2,1)} %bitcast.238, bf16[1024,768]{1,0:T(8,128)(2,1)} %bitcast.247, bf16[1024,768]{1,0:T(8,128)(2,1)} %bitcast.249, bf16[1024,3072]{1,0:T(8,128)(2,1)} %bitcast.239, bf16[1024,768]{1,0:T(8,128)(2,1)} %bitcast.250, ...), custom_call_target="tpu_custom_call" | custom-call | flops 14000000000 | bytes 30000000 | tf_op jit(solution)/shard_map/dense_grads/pallas_call | solution.py:1153
  347.6 48.6 %attn_bwd.2 = bf16[288,64,128]{2,1,0:T(8,128)(2,1)} custom-call(s32[1536]{0:T(1024)} %copy-done.2, bf16[288,64,128]{2,1,0:T(8,128)(2,1)} %bitcast.169, bf16[96,64,128]{2,1,0:T(8,128)(2,1)} %bitcast.183), custom_call_target="tpu_custom_call" | custom-call | flops 46000001024 | bytes 12000000 | tf_op jit(solution)/shard_map/attn_bwd/pallas_call | solution.py:343
  396.2 82.5 %layer_bwd.1 = (bf16[4,4,3,2,64,128]{5,4,3,2,1,0:T(8,128)(2,1)}, f32[2,512,768]{2,1,0:T(8,128)}, bf16[2,512,3072]{2,1,0:T(8,128)(2,1)}, bf16[2,512,3072]{2,1,0:T...) custom-call(bf16[4,4,9,2,64,128]{5,4,3,2,1,0:T(8,128)(2,1)} %bitcast, ...), custom_call_target="tpu_custom_call" | custom-call | flops 70000001024 | bytes 60000000 | tf_op jit(solution)/shard_map/layer_bwd/pallas_call | solution.py:1097
  482.8 3.6 all-to-all-start.1
  486.6 18.9 %dense_grads.3 = (bf16[4,8,96,768]{3,2,1,0:T(8,128)(2,1)}, bf16[8,496,768]{2,1,0:T(8,128)(2,1)}) custom-call(bf16[1024,3072]{1,0:T(8,128)(2,1)} %bitcast.236, bf16[1024,768]{1,0:T(8,128)(2,1)} %bitcast.245, bf16[1024,768]{1,0:T(8,128)(2,1)} %bitcast.242, bf16[1024,3072]{1,0:T(8,128)(2,1)} %bitcast.237, bf16[1024,768]{1,0:T(8,128)(2,1)} %bitcast.243, ...), custom_call_target="tpu_custom_call" | custom-call | flops 14000000000 | bytes 30000000 | tf_op jit(solution)/shard_map/dense_grads/pallas_call | solution.py:1153
  505.6 5.0 all-to-all-start.2
  511.0 48.5 %attn_bwd.3 = bf16[288,64,128]{2,1,0:T(8,128)(2,1)} custom-call(s32[1536]{0:T(1024)} %copy-done.1, bf16[288,64,128]{2,1,0:T(8,128)(2,1)} %bitcast.167, bf16[96,64,128]{2,1,0:T(8,128)(2,1)} %bitcast.244), custom_call_target="tpu_custom_call" | custom-call | flops 46000001024 | bytes 12000000 | tf_op jit(solution)/shard_map/attn_bwd/pallas_call | solution.py:343
  559.5 3.9 all-to-all-done.2
  563.4 3.3 reduce_sum.76
  566.7 2.4 copy-done.7
  569.1 13.3 %own_grad.1 = bf16[8,112,768]{2,1,0:T(8,128)(2,1)S(1)} custom-call(bf16[4,2,4,128,768]{4,3,2,1,0:T(8,128)(2,1)} %bitcast.165, bf16[4,4,9,2,64,128]{5,4,3,2,1,0:T(8,128)(2,1)S(1)} %bitcast.171), custom_call_target="tpu_custom_call" | custom-call | flops 7000000000 | bytes 12000000 | tf_op jit(solution)/shard_map/own_grad/pallas_call | solution.py:624
  584.1 1.9 reduce-scatter.12.cloned.1.call-done
  586.0 2.1 pad.35
  588.1 64.1 %layer_tail.1 = (f32[2,512,768]{2,1,0:T(8,128)}, bf16[4,128,768]{2,1,0:T(8,128)(2,1)}) custom-call(bf16[4,4,9,2,64,128]{5,4,3,2,1,0:T(8,128)(2,1)} %bitcast.170, f32[2,512,768]{2,1,0:T(8,128)} %get-tuple-element.128.up_ref, bf16[8,288,768]{2,1,0:T(8,128)(2,1)} %bitcast.232, bf16[4,128,768]{2,1,0:T(8,128)(2,1)} %bitcast.188), custom_call_target="tpu_custom_call" | custom-call | flops 54999998464 | bytes 12000000 | tf_op jit(solution)/shard_map/layer_tail/pallas_call | solution.py:1208
  653.4 2.0 pad_maximum_fusion.1.rows_ref
  655.4 37.0 %gather.1.full_ref = bf16[4,672,768]{2,1,0:T(8,128)(2,1)} custom-call(bf16[672,768]{1,0:T(8,128)(2,1)} %pad_maximum_fusion.1.rows_ref), custom_call_target="tpu_custom_call" | custom-call | flops 35000000512 | bytes 6000000 | tf_op jit(solution)/shard_map/gather/pallas_call | solution.py:1275
  692.5 2.2 copy-done
  694.6 3.4 finish.1
  698.6 1.7 copy.162
  (234 shorter events, 42.9 us)
Async XLA Ops:
  7.2 136.8 %all-gather.11.cloned.1.call-start = ((), (), s32[]{:S(2)}) async-start(), calls=%async_computation.13 | async-start | bytes 11943936 | tf_op jit(solution)/shard_map/all_gather | solution.py:1466
  10.2 2.8 copy-start.14
  13.0 2.1 copy-start.24
  13.0 2.3 copy-start.25
  13.9 2.7 copy-start.15
  15.0 208.1 %all-gather.13.cloned.1.call-start = ((), (), s32[]{:S(2)}) async-start(), calls=%async_computation.14 | async-start | bytes 1548288 | tf_op jit(solution)/shard_map/all_gather | solution.py:1468
  21.1 249.7 %all-gather.15.cloned.1.call-start = ((), (), s32[]{:S(2)}) async-start(), calls=%async_computation.15 | async-start | bytes 11943936 | tf_op jit(solution)/shard_map/all_gather | solution.py:1469
  21.9 374.4 %all-gather.17.cloned.1.call-start = ((), (), s32[]{:S(2)}) async-start(), calls=%async_computation.16 | async-start | bytes 3981312 | tf_op jit(solution)/shard_map/all_gather | solution.py:1471
  23.5 372.7 %all-gather.19.cloned.1.call-start = ((), (), s32[]{:S(2)}) async-start(), calls=%async_computation.17 | async-start | bytes 3981312 | tf_op jit(solution)/shard_map/all_gather | solution.py:1470
  94.6 2.6 copy-start.4
  97.2 2.2 copy-start.5
  102.8 137.6 %copy-start.2 = (s32[1536]{0:T(1024)}, s32[1536]{0:T(1024)S(1)}, u32[]{:S(2)}) copy-start(s32[1536]{0:T(1024)S(1)} %reshape.278.lists_ref) | copy-start | bytes 18436
  103.0 30.1 %copy-start.1 = (s32[1536]{0:T(1024)}, s32[1536]{0:T(1024)S(1)}, u32[]{:S(2)}) copy-start(s32[1536]{0:T(1024)S(1)} %reshape.279.lists_ref) | copy-start | bytes 18436
  238.2 2.3 copy-start.6
  321.4 3.8 copy-start.20
  321.4 4.2 copy-start.22
  321.5 24.2 %all-to-all-start = ((bf16[4,1536,128]{2,1,0:T(8,128)(2,1)}), bf16[4,1536,128]{2,1,0:T(8,128)(2,1)S(1)}, u32[]{:S(2)}, u32[]{:S(2)}) async-start(bf16[4,1536,128]{2,1,0:T(8,128)(2,1)} %bitcast.184), calls=%async_computation | async-start | bytes 3145728 | tf_op jit(solution)/shard_map/all_to_all | solution.py:1376
  325.2 153.7 %reduce-scatter.6.cloned.1.call-start = ((), (), s32[]{:S(2)}) async-start(), calls=%async_computation.8 | async-start | bytes 5308416 | tf_op jit(solution)/shard_map/reduce_scatter | solution.py:1485
  346.8 133.2 %reduce-scatter.8.cloned.1.call-start = ((), (), s32[]{:S(2)}) async-start(), calls=%async_computation.9 | async-start | bytes 6856704 | tf_op jit(solution)/shard_map/reduce_scatter | solution.py:1485
  347.6 211.9 %reduce-scatter.10.cloned.1.call-start = ((), (), s32[]{:S(2)}) async-start(), calls=%async_computation.10 | async-start | bytes 1548288 | tf_op jit(solution)/shard_map/reduce_scatter | solution.py:1485
  478.8 1.7 copy-start.21
  478.8 2.8 copy-start.17
  480.0 1.6 copy-start.16
  482.8 22.8 %all-to-all-start.1 = ((bf16[4,224,768]{2,1,0:T(8,128)(2,1)}), bf16[4,224,768]{2,1,0:T(8,128)(2,1)S(1)}, u32[]{:S(2)}, u32[]{:S(2)}) async-start(bf16[4,224,768]{2,1,0:T(8,128)(2,1)} %bitcast.77), calls=%async_computation.3 | async-start | bytes 2752512 | tf_op jit(solution)/shard_map/all_to_all | solution.py:1376
  486.4 99.6 %reduce-scatter.12.cloned.1.call-start = ((), (), s32[]{:S(2)}) async-start(), calls=%async_computation.11 | async-start | bytes 6856704 | tf_op jit(solution)/shard_map/reduce_scatter | solution.py:1485
  505.6 57.8 %all-to-all-start.2 = ((bf16[4,768,768]{2,1,0:T(8,128)(2,1)}), bf16[4,768,768]{2,1,0:T(8,128)(2,1)}, u32[]{:S(2)}, u32[]{:S(2)}) async-start(bf16[4,768,768]{2,1,0:T(8,128)(2,1)} %bitcast.178), calls=%async_computation.4 | async-start | bytes 9437184 | tf_op jit(solution)/shard_map/all_to_all | solution.py:1376
  510.6 142.8 %reduce-scatter.14.cloned.1.call-start = ((), (), s32[]{:S(2)}) async-start(), calls=%async_computation.12 | async-start | bytes 2875392 | tf_op jit(solution)/shard_map/reduce_scatter | solution.py:1485
  566.7 2.4 copy-start.7
  588.1 65.4 %copy-start.18 = (bf16[1,112,768]{2,1,0:T(8,128)(2,1)S(1)}, bf16[1,112,768]{2,1,0:T(8,128)(2,1)}, u32[]{:S(2)}) copy-start(bf16[1,112,768]{2,1,0:T(8,128)(2,1)} %reduce-scatter.10.cloned.1.call-done) | copy-start | bytes 516100
  692.5 2.2 copy-start
  694.6 4.0 copy-start.10
  698.6 3.0 copy-start.11
  (14 other events, 12.8 us)
Sparse Core Ops, SparseCore 0:
  15.1 128.8 all-gather.10
  146.2 22.3 all-gather.12
  170.8 99.9 all-gather.14
  272.9 39.9 all-gather.16
  314.9 40.3 all-gather.18
  357.5 53.8 reduce-scatter.5
  413.7 66.2 reduce-scatter.7
  482.4 35.0 reduce-scatter.9
  519.9 66.0 reduce-scatter.11
  588.9 35.9 reduce-scatter.13

commit v8 on v7

--- a/solution.py
+++ b/solution.py
@@ -603,15 +603,19 @@
 
 
 def own_grad_kernel(plan, item, steps, a_ref, d_ref, o_ref, acc_ref, sum_ref):
-    n = pl.program_id(0) * plan.chunks + pl.program_id(1)
+    n = pl.program_id(0)
+    one = Plan.__new__(Plan)
+    one.__dict__.update(plan.__dict__)
+    one.groups = 1
 
     @pl.when(n == 0)
     def _():
         acc_ref[...] = jnp.zeros_like(acc_ref)
         sum_ref[...] = jnp.zeros_like(sum_ref)
 
-    d = pick_heads(plan, d_ref[:, 0])
-    acc_ref[...] += dot(a_ref[...].reshape(plan.rows, D), d, TN)
+    d = jnp.concatenate([pick_heads(one, d_ref[:, c]) for c in range(plan.chunks)], 0)
+    a = jnp.concatenate([a_ref[0, :, c].reshape(plan.rows, D) for c in range(plan.chunks)], 0)
+    acc_ref[...] += dot(a, d, TN)
     sum_ref[...] += jnp.sum(d.astype(F32).reshape(-1, 8, d.shape[1]), 0)
 
     @pl.when(n == steps - 1)
@@ -622,12 +626,12 @@
 def own_grad(plan, item, hidden_all, dx):
     a = hidden_all.reshape(plan.groups, 2, plan.chunks, plan.half, D)
     return pl.pallas_call(
-        partial(own_grad_kernel, plan, item, plan.groups * plan.chunks),
+        partial(own_grad_kernel, plan, item, plan.groups),
         out_shape=jax.ShapeDtypeStruct((item, D // item + 16, D), BF),
-        grid=(plan.groups, plan.chunks),
+        grid=(plan.groups,),
         in_specs=[
-            pl.BlockSpec((1, 2, 1, plan.half, D), lambda g, c: (g, 0, c, 0, 0)),
-            pl.BlockSpec((1, 1) + plan.x_shape()[2:], lambda g, c: (g, c, 0, 0, 0, 0)),
+            pl.BlockSpec((1, 2, plan.chunks, plan.half, D), lambda g: (g, 0, 0, 0, 0)),
+            pl.BlockSpec((1,) + plan.x_shape()[1:], lambda g: (g, 0, 0, 0, 0, 0)),
         ],
         out_specs=whole((item, D // item + 16, D)),
         scratch_shapes=[VMEM((D, plan.own), F32), VMEM((8, plan.own), F32)],
@@ -1516,7 +1520,6 @@
         plan, item, dx1, up1, r1, r2, u, h1_all, packed0, columns1, stacked[0]
     )
     dc0, fo1, rest1, own1 = tie(d0, fo1, rest1, own1)
-    own1 = scattered(own1)
     sent1 = seq_send([fo1, rest1])
     seq_first = (w_ffn_out.shape[1] // groups) % 16 == 0
     fo0, rest0 = grads(gz0, du0, df0, do0, y0, ctx0, sums0, inner0, groups if seq_first else 0)
@@ -1527,15 +1530,14 @@
     dx0 = attn_bwd(plan, tables[0], x0, dc0)
     dx0, fo0, own1 = tie(dx0, fo0, own1)
     own0 = own_grad(plan, item, hidden_all, dx0)
-    if seq_first:
-        own0 = jnp.concatenate([seq_sum(fo0), own0], 1)
+    own0 = jnp.concatenate([own1] + ([seq_sum(fo0)] if seq_first else []) + [own0], 1)
     own_share = scattered(own0)
     dx0, own0 = tie(dx0, own0)
     rows0 = for_groups([rest0] + ([] if seq_first else [fo0]))
     input_grad, rows0 = layer_tail(plan, dx0, up0, columns0, rows0)
     part0 = seq_sum(rows0)
-    sizes = part1.shape[0], part0.shape[0], own1.shape[0]
-    full = gather(groups, jnp.concatenate([part1, part0, own1, own_share]))
+    sizes = part1.shape[0], part0.shape[0], own1.shape[1]
+    full = gather(groups, jnp.concatenate([part1, part0, own_share]))
     qkv, bias, attn, inner_grad, outer, *small_grads = finish(
         plan, share, w_ffn_in.shape[2], item, counts, seq_first, sizes, full
     )

time: 718 us -> 715 us (level)
    unnamed x88 -> x80, local copies, waits for them, and re-layouts: 30.2 us -> 30.2 us
  transfers between devices with their start and end apart: 13 -> 12, of which waited for: 5 -> 3; matrix products, arithmetic and copies ran while one was open for 4% -> 5% of each run, Pallas kernels for 79% -> 79%
where the time goes in v8:
time: 715 us; the launch traced here: 705 us
  Pallas kernels  594 us (83%)
  local copies, waits for them, and re-layouts  46.4 us (6%)
  other arithmetic  20.8 us (3%)
  waiting for transfers between devices  16.2 us (2%)
  between operations  15 us (2%)
  starting transfers between devices  12.8 us (2%)
    pallas_call x2, Pallas kernels, attn_bwd(): pl.pallas_call(partial(attn_bwd_kernel, plan), out_shape=jax.ShapeDtypeSt...  97 us
    pallas_call x1, Pallas kernels, layer_bwd(): pl.pallas_call(partial(bwd_kernel, plan, ff, item), out_shape=[jax.ShapeD...  82.5 us
    pallas_call x1, Pallas kernels, layer_fwd(): pl.pallas_call(partial(fwd_kernel, plan, ff), out_shape=[jax.ShapeDtypeSt...  79 us
    pallas_call x1, Pallas kernels, start(): pl.pallas_call(partial(start_kernel, plan, item), out_shape=[jax.ShapeDty...  65.8 us
    pallas_call x1, Pallas kernels, layer_tail(): pl.pallas_call(partial(tail_kernel, plan), out_shape=[jax.ShapeDtypeStruc...  65.4 us
    pallas_call x2, Pallas kernels, attn_fwd(): pl.pallas_call(partial(attn_fwd_kernel, plan), out_shape=jax.ShapeDtypeSt...  55.8 us
    pallas_call x1, Pallas kernels, layer_mid(): pl.pallas_call(partial(mid_kernel, plan, ff), out_shape=[jax.ShapeDtypeSt...  50.6 us
    pallas_call x2, Pallas kernels, dense_grads(): pl.pallas_call(partial(dense_grad_kernel, item), out_shape=[jax.ShapeDtyp...  37.7 us
  transfers between devices with their start and end apart: 12, of which 3 were waited for; matrix products, arithmetic and copies ran while one was open for 5% of the time, Pallas kernels for 79%

profile of v8, /device:TPU:0, one launch (start us, length us, event | category | flops | bytes accessed | tf_op | source)
XLA Modules:
  0.0 705.4 jit_solution(12292558987548800302)
XLA Ops:
  25.2 2.4 convert_element_type.33.hid_ref
  28.8 65.8 %start.1 = (bf16[4,2,512,768]{3,2,1,0:T(8,128)(2,1)S(1)}, bf16[4,4,9,2,64,128]{5,4,3,2,1,0:T(8,128)(2,1)S(1)}, bf16[8,32,128]{2,1,0:T(8,128)(2,1)S(1)}, s32[4,8,128]{2,1,0:T(8,128)S(1)}) custom-call(bf16[2,512,768]{2,1,0:T(8,128)(2,1)S(1)} %convert_element_type.33.hid_ref, bf16[112,576]{1,0:T(8,128)(2,1)S(1)} %pad_maximum_fusion.6.shard_ref, ...), custom_call_target="tpu_custom_call" | custom-call | flops 54999998464 | bytes 12000000 | tf_op jit(solution)/shard_map/start/pallas_call | solution.py:566
  94.6 2.6 copy-done.4
  97.3 2.2 copy-done.5
  100.3 2.3 fusion.12
  105.3 27.9 %attn_fwd.2 = bf16[96,64,128]{2,1,0:T(8,128)(2,1)S(1)} custom-call(s32[1536]{0:T(1024)S(1)} %reshape.279.lists_ref, bf16[288,64,128]{2,1,0:T(8,128)(2,1)} %bitcast.165), custom_call_target="tpu_custom_call" | custom-call | flops 25999998976 | bytes 6000000 | tf_op jit(solution)/shard_map/attn_fwd/pallas_call | solution.py:206
  135.6 8.4 %all-gather.11.cloned.1.call-done = bf16[6912,768]{1,0:T(8,128)(2,1)} async-done(((bf16[864,768]{1,0:T(8,128)(2,1)}), bf16[6912,768]{1,0:T(8,128)(2,1)}) %all-gather.11.cloned.1.call-update) | async-done | bytes 10616848 | tf_op jit(solution)/shard_map/all_gather | solution.py:1470
  144.0 79.0 %layer_fwd.1 = (bf16[4,2,512,768]{3,2,1,0:T(8,128)(2,1)}, f32[2,512,768]{2,1,0:T(8,128)}, f32[2,512,768]{2,1,0:T(8,128)}, f32[2,512,768]{2,1,0:T(8,128)}, f32[2,...) custom-call(bf16[4,4,3,2,64,128]{5,4,3,2,1,0:T(8,128)(2,1)} %bitcast.171, ...), custom_call_target="tpu_custom_call" | custom-call | flops 24000000000 | bytes 50000000 | tf_op jit(solution)/shard_map/layer_fwd/pallas_call | solution.py:950
  224.4 13.7 %own_heads.1 = bf16[4,4,9,2,64,128]{5,4,3,2,1,0:T(8,128)(2,1)S(1)} custom-call(bf16[4,2,4,128,768]{4,3,2,1,0:T(8,128)(2,1)} %bitcast.233, bf16[8,112,768]{2,1,0:T(8,128)(2,1)S(1)} %bitcast.163), custom_call_target="tpu_custom_call" | custom-call | flops 12000000000 | bytes 12000000 | tf_op jit(solution)/shard_map/own_heads/pallas_call | solution.py:927
  238.1 2.3 copy-done.6
  240.4 27.9 %attn_fwd.3 = bf16[96,64,128]{2,1,0:T(8,128)(2,1)S(1)} custom-call(s32[1536]{0:T(1024)S(1)} %reshape.278.lists_ref, bf16[288,64,128]{2,1,0:T(8,128)(2,1)} %bitcast.167), custom_call_target="tpu_custom_call" | custom-call | flops 25999998976 | bytes 6000000 | tf_op jit(solution)/shard_map/attn_fwd/pallas_call | solution.py:206
  270.9 50.6 %layer_mid.1 = (bf16[4,4,3,2,64,128]{5,4,3,2,1,0:T(8,128)(2,1)}, f32[2,512,768]{2,1,0:T(8,128)}, f32[2,512,768]{2,1,0:T(8,128)}, bf16[2,512,3072]{2,1,0:T(8,128)...) custom-call(bf16[4,4,3,2,64,128]{5,4,3,2,1,0:T(8,128)(2,1)} %bitcast, ...), custom_call_target="tpu_custom_call" | custom-call | flops 44999999488 | bytes 50000000 | tf_op jit(solution)/shard_map/layer_mid/pallas_call | solution.py:1034
  321.5 3.7 all-to-all-start
  326.8 18.9 %dense_grads.2 = (bf16[8,384,768]{2,1,0:T(8,128)(2,1)}, bf16[8,496,768]{2,1,0:T(8,128)(2,1)}) custom-call(bf16[1024,3072]{1,0:T(8,128)(2,1)} %bitcast.236, bf16[1024,768]{1,0:T(8,128)(2,1)} %bitcast.245, bf16[1024,768]{1,0:T(8,128)(2,1)} %bitcast.247, bf16[1024,3072]{1,0:T(8,128)(2,1)} %bitcast.237, bf16[1024,768]{1,0:T(8,128)(2,1)} %bitcast.248, ...), custom_call_target="tpu_custom_call" | custom-call | flops 14000000000 | bytes 30000000 | tf_op jit(solution)/shard_map/dense_grads/pallas_call | solution.py:1157
  347.6 48.6 %attn_bwd.2 = bf16[288,64,128]{2,1,0:T(8,128)(2,1)} custom-call(s32[1536]{0:T(1024)} %copy-done.2, bf16[288,64,128]{2,1,0:T(8,128)(2,1)} %bitcast.168, bf16[96,64,128]{2,1,0:T(8,128)(2,1)} %bitcast.182), custom_call_target="tpu_custom_call" | custom-call | flops 46000001024 | bytes 12000000 | tf_op jit(solution)/shard_map/attn_bwd/pallas_call | solution.py:343
  396.2 82.5 %layer_bwd.1 = (bf16[4,4,3,2,64,128]{5,4,3,2,1,0:T(8,128)(2,1)}, f32[2,512,768]{2,1,0:T(8,128)}, bf16[2,512,3072]{2,1,0:T(8,128)(2,1)}, bf16[2,512,3072]{2,1,0:T...) custom-call(bf16[4,4,9,2,64,128]{5,4,3,2,1,0:T(8,128)(2,1)} %bitcast, ...), custom_call_target="tpu_custom_call" | custom-call | flops 70000001024 | bytes 60000000 | tf_op jit(solution)/shard_map/layer_bwd/pallas_call | solution.py:1101
  482.0 2.5 fusion.2
  484.5 3.6 all-to-all-start.1
  488.3 18.8 %dense_grads.3 = (bf16[4,8,96,768]{3,2,1,0:T(8,128)(2,1)}, bf16[8,496,768]{2,1,0:T(8,128)(2,1)}) custom-call(bf16[1024,3072]{1,0:T(8,128)(2,1)} %bitcast.234, bf16[1024,768]{1,0:T(8,128)(2,1)} %bitcast.243, bf16[1024,768]{1,0:T(8,128)(2,1)} %bitcast.240, bf16[1024,3072]{1,0:T(8,128)(2,1)} %bitcast.235, bf16[1024,768]{1,0:T(8,128)(2,1)} %bitcast.241, ...), custom_call_target="tpu_custom_call" | custom-call | flops 14000000000 | bytes 30000000 | tf_op jit(solution)/shard_map/dense_grads/pallas_call | solution.py:1157
  507.2 5.0 all-to-all-start.2
  512.2 48.4 %attn_bwd.3 = bf16[288,64,128]{2,1,0:T(8,128)(2,1)} custom-call(s32[1536]{0:T(1024)} %copy-done.1, bf16[288,64,128]{2,1,0:T(8,128)(2,1)} %bitcast.166, bf16[96,64,128]{2,1,0:T(8,128)(2,1)} %bitcast.242), custom_call_target="tpu_custom_call" | custom-call | flops 46000001024 | bytes 12000000 | tf_op jit(solution)/shard_map/attn_bwd/pallas_call | solution.py:343
  560.6 4.8 all-to-all-done.2
  565.4 3.3 reduce_sum.76
  568.8 2.4 copy-done.7
  571.2 7.5 %own_grad.1 = bf16[8,112,768]{2,1,0:T(8,128)(2,1)S(1)} custom-call(bf16[4,2,4,128,768]{4,3,2,1,0:T(8,128)(2,1)} %bitcast.164, bf16[4,4,9,2,64,128]{5,4,3,2,1,0:T(8,128)(2,1)S(1)} %bitcast.170), custom_call_target="tpu_custom_call" | custom-call | flops 7000000000 | bytes 12000000 | tf_op jit(solution)/shard_map/own_grad/pallas_call | solution.py:628
  578.7 2.1 pad_maximum_fusion
  581.2 2.1 pad.35
  583.2 65.4 %layer_tail.1 = (f32[2,512,768]{2,1,0:T(8,128)}, bf16[4,128,768]{2,1,0:T(8,128)(2,1)}) custom-call(bf16[4,4,9,2,64,128]{5,4,3,2,1,0:T(8,128)(2,1)} %bitcast.169, f32[2,512,768]{2,1,0:T(8,128)} %get-tuple-element.129.up_ref, bf16[8,288,768]{2,1,0:T(8,128)(2,1)} %bitcast.230, bf16[4,128,768]{2,1,0:T(8,128)(2,1)} %bitcast.187), custom_call_target="tpu_custom_call" | custom-call | flops 54999998464 | bytes 12000000 | tf_op jit(solution)/shard_map/layer_tail/pallas_call | solution.py:1212
  649.9 2.1 pad_maximum_fusion.1.rows_ref
  652.0 35.8 %gather.1.full_ref = bf16[4,672,768]{2,1,0:T(8,128)(2,1)} custom-call(bf16[672,768]{1,0:T(8,128)(2,1)} %pad_maximum_fusion.1.rows_ref), custom_call_target="tpu_custom_call" | custom-call | flops 35000000512 | bytes 6000000 | tf_op jit(solution)/shard_map/gather/pallas_call | solution.py:1279
  687.8 2.2 copy-done
  690.0 3.4 finish.1
  (223 shorter events, 42.3 us)
Async XLA Ops:
  7.2 136.8 %all-gather.11.cloned.1.call-start = ((), (), s32[]{:S(2)}) async-start(), calls=%async_computation.11 | async-start | bytes 11943936 | tf_op jit(solution)/shard_map/all_gather | solution.py:1470
  10.2 2.8 copy-start.15
  13.0 2.1 copy-start.20
  13.0 2.3 copy-start.21
  13.9 2.7 copy-start.16
  15.0 208.1 %all-gather.13.cloned.1.call-start = ((), (), s32[]{:S(2)}) async-start(), calls=%async_computation.12 | async-start | bytes 1548288 | tf_op jit(solution)/shard_map/all_gather | solution.py:1472
  21.1 249.7 %all-gather.15.cloned.1.call-start = ((), (), s32[]{:S(2)}) async-start(), calls=%async_computation.13 | async-start | bytes 11943936 | tf_op jit(solution)/shard_map/all_gather | solution.py:1473
  21.9 374.3 %all-gather.17.cloned.1.call-start = ((), (), s32[]{:S(2)}) async-start(), calls=%async_computation.14 | async-start | bytes 3981312 | tf_op jit(solution)/shard_map/all_gather | solution.py:1475
  23.5 372.7 %all-gather.19.cloned.1.call-start = ((), (), s32[]{:S(2)}) async-start(), calls=%async_computation.15 | async-start | bytes 3981312 | tf_op jit(solution)/shard_map/all_gather | solution.py:1474
  94.6 2.6 copy-start.4
  97.3 2.2 copy-start.5
  102.8 137.6 %copy-start.2 = (s32[1536]{0:T(1024)}, s32[1536]{0:T(1024)S(1)}, u32[]{:S(2)}) copy-start(s32[1536]{0:T(1024)S(1)} %reshape.278.lists_ref) | copy-start | bytes 18436
  103.0 30.1 %copy-start.1 = (s32[1536]{0:T(1024)}, s32[1536]{0:T(1024)S(1)}, u32[]{:S(2)}) copy-start(s32[1536]{0:T(1024)S(1)} %reshape.279.lists_ref) | copy-start | bytes 18436
  133.1 1.1 copy-start.8
  223.1 1.3 copy-start.3
  238.1 2.3 copy-start.6
  268.3 1.1 copy-start.9
  321.5 3.8 copy-start.17
  321.5 4.2 copy-start.18
  321.5 24.2 %all-to-all-start = ((bf16[4,1536,128]{2,1,0:T(8,128)(2,1)}), bf16[4,1536,128]{2,1,0:T(8,128)(2,1)S(1)}, u32[]{:S(2)}, u32[]{:S(2)}) async-start(bf16[4,1536,128]{2,1,0:T(8,128)(2,1)} %bitcast.183), calls=%async_computation | async-start | bytes 3145728 | tf_op jit(solution)/shard_map/all_to_all | solution.py:1380
  325.2 156.8 %reduce-scatter.5.cloned.1.call-start = ((), (), s32[]{:S(2)}) async-start(), calls=%async_computation.7 | async-start | bytes 5308416 | tf_op jit(solution)/shard_map/reduce_scatter | solution.py:1489
  345.7 1.1 copy-start.13
  346.9 135.1 %reduce-scatter.7.cloned.1.call-start = ((), (), s32[]{:S(2)}) async-start(), calls=%async_computation.8 | async-start | bytes 6856704 | tf_op jit(solution)/shard_map/reduce_scatter | solution.py:1489
  484.5 22.7 %all-to-all-start.1 = ((bf16[4,224,768]{2,1,0:T(8,128)(2,1)}), bf16[4,224,768]{2,1,0:T(8,128)(2,1)S(1)}, u32[]{:S(2)}, u32[]{:S(2)}) async-start(bf16[4,224,768]{2,1,0:T(8,128)(2,1)} %bitcast.77), calls=%async_computation.3 | async-start | bytes 2752512 | tf_op jit(solution)/shard_map/all_to_all | solution.py:1380
  488.1 93.1 %reduce-scatter.9.cloned.1.call-start = ((), (), s32[]{:S(2)}) async-start(), calls=%async_computation.9 | async-start | bytes 6856704 | tf_op jit(solution)/shard_map/reduce_scatter | solution.py:1489
  507.2 58.2 %all-to-all-start.2 = ((bf16[4,768,768]{2,1,0:T(8,128)(2,1)}), bf16[4,768,768]{2,1,0:T(8,128)(2,1)}, u32[]{:S(2)}, u32[]{:S(2)}) async-start(bf16[4,768,768]{2,1,0:T(8,128)(2,1)} %bitcast.177), calls=%async_computation.4 | async-start | bytes 9437184 | tf_op jit(solution)/shard_map/all_to_all | solution.py:1380
  512.2 137.8 %reduce-scatter.11.cloned.1.call-start = ((), (), s32[]{:S(2)}) async-start(), calls=%async_computation.10 | async-start | bytes 4423680 | tf_op jit(solution)/shard_map/reduce_scatter | solution.py:1489
  568.8 2.4 copy-start.7
  571.1 7.5 %copy-start.14 = (bf16[8,112,768]{2,1,0:T(8,128)(2,1)S(1)}, bf16[8,112,768]{2,1,0:T(8,128)(2,1)}, u32[]{:S(2)}) copy-start(bf16[8,112,768]{2,1,0:T(8,128)(2,1)} %get-tuple-element.125) | copy-start | bytes 4128772
  687.8 2.2 copy-start
  690.0 4.0 copy-start.10
  694.0 3.0 copy-start.11
  (9 other events, 6.8 us)
Sparse Core Ops, SparseCore 0:
  15.1 128.8 all-gather.10
  146.2 22.3 all-gather.12
  170.8 99.9 all-gather.14
  272.9 39.8 all-gather.16
  314.9 40.3 all-gather.18
  357.5 53.8 reduce-scatter.4
  413.7 66.2 reduce-scatter.6
  507.3 73.3 reduce-scatter.8
  583.1 48.8 reduce-scatter.10
